TPU v7x, 32 devices: a whole 2x2x4 slice. The times are simulated.
32 devices in a mesh: ctx: 4 (over z), fsdp: 8 (over y, x, core).
Axes of the slice: x: 2, y: 2, z: 4, core: 2. Of those that a mesh axis runs over, the one named last changes fastest.
Arguments:
- tokens: bfloat16 [16, 1024, 1024], P('fsdp', 'ctx'), may hold values from -6 to 6
- cotangent: bfloat16 [16, 1024, 1024], P('fsdp', 'ctx'), may hold values from -6 to 6
- sequence_lengths: int32 [16], replicated, may hold values from 1 to 1024, 10240 in all
- slot_sequence: int32 [16], replicated, may hold values from 0 to 15, each once
- offset_bucket: int32 [2047], replicated, may hold values from 0 to 31
- first_gain: bfloat16 [1024], P('fsdp'), may hold values from 0.5 to 1.5
- second_gain: bfloat16 [1024], P('fsdp'), may hold values from 0.5 to 1.5
- query_weight: bfloat16 [1024, 1024], P('fsdp'), may hold values from -0.09375 to 0.09375
- key_weight: bfloat16 [1024, 1024], P('fsdp'), may hold values from -0.09375 to 0.09375
- value_weight: bfloat16 [1024, 1024], P('fsdp'), may hold values from -0.1875 to 0.1875
- output_weight: bfloat16 [1024, 1024], P('fsdp'), may hold values from -0.75 to 0.75
- expand_weight: bfloat16 [1024, 4096], P('fsdp'), may hold values from -0.1875 to 0.1875
- contract_weight: bfloat16 [1024, 4096], P('fsdp'), may hold values from -0.125 to 0.125
- bias_table: bfloat16 [32, 16], replicated, may hold values from -4 to 4
- clip_limit: float32 [16], replicated, may hold values from 0.5 to 6
Outputs:
- output: bfloat16 [16, 1024, 1024], P('fsdp', 'ctx')
- input_gradient: float32 [16, 1024, 1024], P('fsdp', 'ctx')
- first_gain_gradient: float32 [1024], P('fsdp')
- second_gain_gradient: float32 [1024], P('fsdp')
- query_weight_gradient: float32 [1024, 1024], P('fsdp')
- key_weight_gradient: float32 [1024, 1024], P('fsdp')
- value_weight_gradient: float32 [1024, 1024], P('fsdp')
- output_weight_gradient: float32 [1024, 1024], P('fsdp')
- expand_weight_gradient: float32 [1024, 4096], P('fsdp')
- contract_weight_gradient: float32 [1024, 4096], P('fsdp')
- bias_table_gradient: float32 [32, 16], P('fsdp')
- head_maximum: float32 [16], replicated
- new_query_weight: float32 [1024, 1024], P('fsdp')
- new_key_weight: float32 [1024, 1024], P('fsdp')
Inputs may be any that keep to these rules, and one draw needn't show every extreme that they name: `sequence_lengths`: the longest sequence has exactly 1024 valid positions. `slot_sequence`: every sequence number appears in exactly one slot.
All inputs are finite; a program needn't handle non-finite values.
Results may differ from a plain program's by a relative error of at most 0.015.
The roundings to bfloat16 on the way count: a program that leaves them out, or rounds other values in their place, can miss the bound.
Values may be sent and summed in bfloat16 or wider, within the bound.
No kernel may reach another device: no remote copies, remote signals or barrier semaphores. Data moves between devices by JAX's collectives and lax.ppermute only.
A program may use at most 512 MiB of HBM per device.

v0:
```python
import math

import jax
import jax.numpy as jnp
from jax import lax
from jax.sharding import PartitionSpec as P

epsilon = 1e-06
masked = -1e30


def normalize(values):
    scaled = lax.rsqrt(jnp.mean(values * values, axis=-1, keepdims=True) + epsilon)
    return (values * scaled, scaled)


def normalize_back(values, scaled, upstream):
    unit_rows = values * scaled
    return scaled * (upstream - unit_rows * jnp.mean(upstream * unit_rows, axis=-1, keepdims=True))


def gelu_slope(values):
    cumulative = 0.5 * (1.0 + jax.scipy.special.erf(values / math.sqrt(2.0)))
    density = jnp.exp(-0.5 * values * values) / math.sqrt(2.0 * math.pi)
    return cumulative + values * density


def scaled_rows(weight, scaling):
    return (scaling.astype(jnp.float32)[:, None] * weight.astype(jnp.float32)).astype(jnp.bfloat16)


def weight_rows(weight, operand):
    whole = lax.all_gather(weight, "fsdp", axis=0, tiled=True)
    return jnp.dot(operand, whole, preferred_element_type=jnp.float32)


def weight_columns(weight, operand):
    return lax.dot_general(
        operand,
        lax.all_gather(weight, "fsdp", axis=0, tiled=True),
        (((1,), (1,)), ((), ())),
        preferred_element_type=jnp.float32,
    )


def build_bias(table_values, offset_bucket, first_query, local_length):
    bucket_count = table_values.shape[0]
    total_length = (offset_bucket.shape[0] + 1) // 2
    matching = offset_bucket[:, None] == jnp.arange(bucket_count)[None, :]
    per_offset = jnp.sum(jnp.where(matching[:, :, None], table_values[None, :, :], 0.0), axis=1)
    offsets = (
        jnp.arange(total_length)[None, :]
        - (first_query + jnp.arange(local_length))[:, None]
        + total_length
        - 1
    )
    return jnp.take(per_offset.T, offsets, axis=1)


def attend_block(queries, key_block, value_block, position_bias, query_okay, key_okay):
    products = jnp.einsum("bqhd,bkhd->bhqk", queries, key_block, preferred_element_type=jnp.float32)
    both_okay = query_okay[:, None, :, None] & key_okay[:, None, None, :]
    largest = jnp.max(jnp.where(both_okay, products, masked), axis=(0, 2, 3))
    scores = jnp.where(key_okay[:, None, None, :], products + position_bias[None], masked)
    row_max = jnp.max(scores, axis=-1, keepdims=True)
    exponent = jnp.exp(scores - row_max)
    summed = jnp.sum(exponent, axis=-1, keepdims=True)
    weights_low = (exponent / summed).astype(jnp.bfloat16)
    context = jnp.einsum(
        "bhqk,bkhd->bqhd", weights_low, value_block, preferred_element_type=jnp.float32
    )
    return (context.astype(jnp.bfloat16), (row_max + jnp.log(summed))[..., 0], largest)


def attend_back(queries, key_block, value_block, position_bias, key_okay, log_total, context_grad):
    products = jnp.einsum("bqhd,bkhd->bhqk", queries, key_block, preferred_element_type=jnp.float32)
    scores = jnp.where(key_okay[:, None, None, :], products + position_bias[None], masked)
    probs = jnp.exp(scores - log_total[..., None])
    weights_low = probs.astype(jnp.bfloat16)
    value_grad = jnp.einsum(
        "bhqk,bqhd->bkhd", weights_low, context_grad, preferred_element_type=jnp.float32
    )
    probs_grad = jnp.einsum(
        "bqhd,bkhd->bhqk", context_grad, value_block, preferred_element_type=jnp.float32
    )
    row_inner = jnp.sum(probs * probs_grad, axis=-1, keepdims=True)
    score_grad = (probs * (probs_grad - row_inner)).astype(jnp.bfloat16)
    query_grad = jnp.einsum(
        "bhqk,bkhd->bqhd", score_grad, key_block, preferred_element_type=jnp.float32
    )
    key_grad = jnp.einsum(
        "bhqk,bqhd->bkhd", score_grad, queries, preferred_element_type=jnp.float32
    )
    bias_grad = jnp.sum(score_grad.astype(jnp.float32), axis=0)
    return (query_grad.astype(jnp.bfloat16), key_grad, value_grad, bias_grad)


def local(
    tokens,
    cotangent,
    sequence_lengths,
    slot_sequence,
    offset_bucket,
    first_gain,
    second_gain,
    query_weight,
    key_weight,
    value_weight,
    output_weight,
    expand_weight,
    contract_weight,
    bias_table,
    clip_limit,
):
    held_count, local_length, model_width = tokens.shape
    shard_index = lax.axis_index("fsdp")
    context_index = lax.axis_index("ctx")
    context_count = lax.axis_size("ctx")
    shard_count = lax.axis_size("fsdp")
    total_length = local_length * context_count
    row_count = held_count * local_length
    head_count = bias_table.shape[1]
    inner_width = query_weight.shape[1]
    head_size = inner_width // head_count
    hidden_width = expand_weight.shape[1]
    total_sequences = sequence_lengths.shape[0]
    block_count = held_count // 2
    first_query = context_index * local_length
    held_ids = lax.dynamic_slice_in_dim(slot_sequence, shard_index * held_count, held_count)
    length_here = jnp.sum(
        jnp.where(
            held_ids[:, None] == jnp.arange(total_sequences)[None, :], sequence_lengths[None, :], 0
        ),
        axis=1,
    )
    query_okay = (first_query + jnp.arange(local_length))[None, :] < length_here[:, None]
    key_okay = jnp.arange(total_length)[None, :] < length_here[:, None]

    def blocked(array):
        return array.reshape((block_count, 2) + array.shape[1:])

    token_rows = tokens.reshape(row_count, model_width).astype(jnp.float32)
    unit_one, scale_one = normalize(token_rows)
    normed_one = unit_one.astype(jnp.bfloat16)
    stacked = jnp.concatenate([query_weight, key_weight, value_weight], axis=1)
    effective_qkv = scaled_rows(stacked, first_gain)
    qkv_low = weight_rows(effective_qkv, normed_one).astype(jnp.bfloat16)
    query_heads = qkv_low[:, :inner_width].reshape(held_count, local_length, head_count, head_size)
    key_local = qkv_low[:, inner_width : 2 * inner_width].reshape(
        held_count, local_length, inner_width
    )
    value_local = qkv_low[:, 2 * inner_width :].reshape(held_count, local_length, inner_width)
    key_all, value_all = (
        lax.all_gather(key_local, "ctx", axis=1, tiled=True),
        lax.all_gather(value_local, "ctx", axis=1, tiled=True),
    )
    key_heads = key_all.reshape(held_count, total_length, head_count, head_size)
    value_heads = value_all.reshape(held_count, total_length, head_count, head_size)
    table_float = bias_table.astype(jnp.float32)
    position_bias = build_bias(table_float, offset_bucket, first_query, local_length)

    def forward_step(largest, block_inputs):
        queries, key_block, value_block, query_block_okay, key_block_okay = block_inputs
        context, log_total, peak = attend_block(
            queries, key_block, value_block, position_bias, query_block_okay, key_block_okay
        )
        return (jnp.maximum(largest, peak), (context, log_total))

    largest, (context_blocks, log_totals) = lax.scan(
        forward_step,
        jnp.full((head_count,), masked, jnp.float32),
        (
            blocked(query_heads),
            blocked(key_heads),
            blocked(value_heads),
            blocked(query_okay),
            blocked(key_okay),
        ),
    )
    largest = lax.pmax(largest, ("ctx", "fsdp"))
    context_rows = context_blocks.reshape(row_count, inner_width)
    attended = weight_columns(output_weight, context_rows)
    hidden_one = token_rows + attended
    unit_two, scale_two = normalize(hidden_one)
    normed_two = unit_two.astype(jnp.bfloat16)
    effective_expand = scaled_rows(expand_weight, second_gain)
    pre_act = weight_rows(effective_expand, normed_two)
    activated = jax.nn.gelu(pre_act, approximate=False).astype(jnp.bfloat16)
    mixed = weight_columns(contract_weight, activated)
    row_okay = query_okay.reshape(row_count, 1)
    result = (
        jnp.where(row_okay, hidden_one + mixed, 0.0)
        .astype(jnp.bfloat16)
        .reshape(held_count, local_length, model_width)
    )
    wanted = shard_index * held_count + jnp.arange(held_count)
    picker = (slot_sequence[None, :] == wanted[:, None]).astype(jnp.bfloat16)
    output = jnp.einsum(
        "rt,tpd->rpd",
        picker,
        lax.all_gather(result, "fsdp", axis=0, tiled=True),
        preferred_element_type=jnp.float32,
    ).astype(jnp.bfloat16)
    out_grad = jnp.where(
        row_okay, cotangent.reshape(row_count, model_width).astype(jnp.float32), 0.0
    )
    out_low = out_grad.astype(jnp.bfloat16)
    act_grad = weight_rows(contract_weight, out_low).astype(jnp.bfloat16).astype(jnp.float32)
    pre_grad = (act_grad * gelu_slope(pre_act)).astype(jnp.bfloat16)
    normed_two_grad = weight_columns(effective_expand, pre_grad)
    hidden_grad = out_grad + normalize_back(hidden_one, scale_two, normed_two_grad)
    attended_grad = hidden_grad.astype(jnp.bfloat16)
    context_grad = weight_rows(output_weight, attended_grad).astype(jnp.bfloat16)
    context_grad_heads = context_grad.reshape(held_count, local_length, head_count, head_size)

    def backward_step(bias_total, block_inputs):
        queries, key_block, value_block, key_block_okay, log_total, grad_block = block_inputs
        query_grad, key_grad, value_grad, bias_grad = attend_back(
            queries, key_block, value_block, position_bias, key_block_okay, log_total, grad_block
        )
        return (bias_total + bias_grad, (query_grad, key_grad, value_grad))

    bias_total, (query_grads, key_grads, value_grads) = lax.scan(
        backward_step,
        jnp.zeros(position_bias.shape, jnp.float32),
        (
            blocked(query_heads),
            blocked(key_heads),
            blocked(value_heads),
            blocked(key_okay),
            log_totals,
            blocked(context_grad_heads),
        ),
    )
    key_part = key_grads.reshape(held_count, total_length, inner_width)
    value_part = value_grads.reshape(held_count, total_length, inner_width)
    key_sum, value_sum = (
        lax.psum_scatter(key_part, "ctx", scatter_dimension=1, tiled=True),
        lax.psum_scatter(value_part, "ctx", scatter_dimension=1, tiled=True),
    )
    qkv_grad = jnp.concatenate(
        [
            query_grads.reshape(row_count, inner_width),
            key_sum.astype(jnp.bfloat16).reshape(row_count, inner_width),
            value_sum.astype(jnp.bfloat16).reshape(row_count, inner_width),
        ],
        axis=1,
    )
    normed_one_grad = weight_columns(effective_qkv, qkv_grad)
    input_gradient = (hidden_grad + normalize_back(token_rows, scale_one, normed_one_grad)).reshape(
        held_count, local_length, model_width
    )
    unused_bias, bias_pull = jax.vjp(
        lambda table_values: build_bias(table_values, offset_bucket, first_query, local_length),
        table_float,
    )
    table_grad = bias_pull(bias_total)[0]

    def term(operand, partner):
        return lax.dot_general(
            operand, partner, (((0,), (0,)), ((), ())), preferred_element_type=jnp.float32
        )

    shard_terms = lax.psum_scatter(
        jnp.concatenate(
            [
                term(normed_one, qkv_grad),
                term(attended_grad, context_rows),
                term(normed_two, pre_grad),
                term(out_low, activated),
            ],
            axis=1,
        ),
        "fsdp",
        scatter_dimension=0,
        tiled=True,
    )
    summed_terms = lax.psum(shard_terms, "ctx")
    raw_one = summed_terms[:, : 3 * inner_width]
    output_weight_gradient = summed_terms[:, 3 * inner_width : 4 * inner_width]
    raw_two = summed_terms[:, 4 * inner_width : 4 * inner_width + hidden_width]
    contract_weight_gradient = summed_terms[:, 4 * inner_width + hidden_width :]
    first_scale = first_gain.astype(jnp.float32)[:, None]
    second_scale = second_gain.astype(jnp.float32)[:, None]
    first_gain_gradient = jnp.sum(stacked.astype(jnp.float32) * raw_one, axis=1)
    second_gain_gradient = jnp.sum(expand_weight.astype(jnp.float32) * raw_two, axis=1)
    query_weight_gradient = first_scale * raw_one[:, :inner_width]
    key_weight_gradient = first_scale * raw_one[:, inner_width : 2 * inner_width]
    value_weight_gradient = first_scale * raw_one[:, 2 * inner_width :]
    expand_weight_gradient = second_scale * raw_two
    table_whole = lax.psum(table_grad, ("ctx", "fsdp"))
    table_rows = bias_table.shape[0] // shard_count
    bias_table_gradient = lax.dynamic_slice_in_dim(
        table_whole, shard_index * table_rows, table_rows, 0
    )
    shrink = clip_limit / jnp.maximum(clip_limit, largest)
    column_scale = jnp.repeat(jnp.sqrt(shrink), head_size)
    new_query_weight = query_weight.astype(jnp.float32) * column_scale[None, :]
    new_key_weight = key_weight.astype(jnp.float32) * column_scale[None, :]
    return (
        output,
        input_gradient,
        first_gain_gradient,
        second_gain_gradient,
        query_weight_gradient,
        key_weight_gradient,
        value_weight_gradient,
        output_weight_gradient,
        expand_weight_gradient,
        contract_weight_gradient,
        bias_table_gradient,
        largest,
        new_query_weight,
        new_key_weight,
    )


def solution(mesh):
    return jax.shard_map(
        local,
        mesh=mesh,
        in_specs=(
            P("fsdp", "ctx", None),
            P("fsdp", "ctx", None),
            P(),
            P(),
            P(),
            P("fsdp"),
            P("fsdp"),
            P("fsdp", None),
            P("fsdp", None),
            P("fsdp", None),
            P("fsdp", None),
            P("fsdp", None),
            P("fsdp", None),
            P(),
            P(),
        ),
        out_specs=(
            P("fsdp", "ctx", None),
            P("fsdp", "ctx", None),
            P("fsdp"),
            P("fsdp"),
            P("fsdp", None),
            P("fsdp", None),
            P("fsdp", None),
            P("fsdp", None),
            P("fsdp", None),
            P("fsdp", None),
            P("fsdp", None),
            P(),
            P("fsdp", None),
            P("fsdp", None),
        ),
        check_vma=False,
    )
```

profile of v0, /device:TPU:0, one launch (start us, length us, event | category | flops | bytes accessed | tf_op | source)
XLA Modules:
  0.0 3383.2 jit_solution(13022539884463617970)
XLA Ops:
  8.4 2.2 fusion.36
  10.7 1.5 fusion.35
  12.8 1.5 fusion.30
  14.2 44.7 %all-gather.8.cloned.1.call-done = bf16[1024,3072]{1,0:T(8,128)(2,1)} async-done(((bf16[128,3072]{1,0:T(8,128)(2,1)}), bf16[1024,3072]{1,0:T(8,128)(2,1)}) %all-gather.8.cloned.1.call-update) | async-done | bytes 6291472 | tf_op jit(solution)/shard_map/all_gather | solution.py:33
  59.0 6.4 convolution_convert_fusion.1
  65.5 1.7 fusion.67
  68.6 1.2 fusion.24
  73.5 1.0 copy-done.10
  74.7 866.0 %gather_fusion = f32[262144,16]{1,0:T(8,128)} fusion(f32[16,2047]{0,1:T(8,128)S(1)} %bitcast.94, s32[262144]{0:T(1024)S(1)} %broadcast_clamp_fusion), kind=kCustom, calls=%fused_computation | custom fusion | bytes 34603008 | tf_op jit(solution)/shard_map/jit(_take)/gather | solution.py:57
  940.6 75.3 %copy.85 = f32[256,1024,16]{1,0,2:T(8,128)} copy(f32[256,1024,16]{2,1,0:T(8,128)} %bitcast.7) | data formatting | bytes 33554432 | tf_op jit(solution)/shard_map/jit(_take)/gather | solution.py:57
  1015.9 1.1 broadcast_and_fusion
  1017.0 12.5 select_bitcast_fusion
  1029.5 1.3 fusion.27
  1030.8 1.3 reshape.297
  1032.1 1.7 copy.82
  1033.9 6.6 copy.81
  1040.5 22.1 fusion.65
  1062.7 6.2 copy.79
  1068.9 14.3 fusion
  1083.2 15.3 fusion.43
  1098.5 1.1 copy.86
  1099.8 4.6 multiply_reduce_fusion.2
  1104.5 26.0 fusion.8
  1130.6 11.6 fusion.14
  1142.2 7.1 multiply_reduce_fusion.1
  1150.0 1.3 convolution_convert_fusion.3
  1151.2 2.3 reshape.298
  1153.5 2.8 copy.89
  1156.3 16.8 fusion.2
  1173.1 8.7 copy.94
  1182.0 24.3 multiply_reduce_fusion
  1206.2 35.0 %convert_reduce_fusion = (f32[16,256,1024]{2,1,0:T(8,128)}, bf16[2,16,256,1024]{3,2,1,0:T(8,128)(2,1)}) fusion(f32[2,16,256,1024]{3,2,1,0:T(8,128)} %get-tuple-element.160, f32[2,16,256]{2,1,0:T(8,128)S(1)} %get-tuple-element.159, f32[2,16,256,1024]{3,2,1,0:T(8,128)} %get-tuple-element.139, f32[2,16,256]{2,1,0:T(8,128)S(1)} %log_add_fusion), kind=kLoop, calls=%fused_computation.4 | loop fusion | flops 46137344 | bytes 100728832 | tf_op jit(solution)/shard_map/while/body/eval_jaxpr/reduce_sum | solution.py:94
  1241.2 12.4 fusion.68
  1253.6 8.8 copy.92
  1262.7 13.3 fusion.42
  1276.0 2.5 copy.90
  1278.5 1.2 copy.110
  1279.7 3.3 fusion.52
  1283.0 8.5 fusion.69
  1291.5 8.3 fusion.63
  1299.8 26.8 reduce-scatter.6.cloned.1.call-done
  1326.6 1.7 convert_element_type.151
  1328.3 1.3 copy.96
  1329.6 144.5 %reduce-scatter.4.cloned.1.call-done = f32[2,256,1024]{2,1,0:T(8,128)} async-done(((f32[2,1024,1024]{2,1,0:T(8,128)}), f32[2,256,1024]{2,1,0:T(8,128)}) %reduce-scatter.4.cloned.1.call-update) | async-done | bytes 2097168 | tf_op jit(solution)/shard_map/reduce_scatter | solution.py:238
  1474.2 1.7 convert_element_type.149
  1475.9 1.3 copy.95
  1477.2 10.1 fusion.44
  1487.4 33.2 pad_maximum_fusion
  1521.2 10.7 select_convert_fusion
  1532.0 275.4 %reduce-scatter.8.cloned.1.call-done = f32[128,12288]{1,0:T(8,128)} async-done(((f32[1024,12288]{1,0:T(8,128)}), f32[128,12288]{1,0:T(8,128)}) %reduce-scatter.8.cloned.1.call-update) | async-done | bytes 6291472 | tf_op jit(solution)/shard_map/reduce_scatter | solution.py:264
  1807.5 39.8 %pmax.7 = f32[16]{0:T(128)S(1)} all-reduce(f32[16]{0:T(128)S(1)} %broadcast_maximum_fusion), channel_id=1, replica_groups=mesh['ctx'=4,'fsdp'=8] {'ctx','fsdp'}, use_global_device_ids=true, to_apply=%region_20.21 | all-reduce | flops 16 | bytes 128 | tf_op jit(solution)/shard_map/pmax | solution.py:180
  1847.3 65.0 %copy.102 = f32[256,1024,16]{2,1,0:T(8,128)} copy(f32[256,1024,16]{1,0,2:T(8,128)} %bitcast.95) | data formatting | bytes 33554432 | tf_op jit(solution)/shard_map/while/body/eval_jaxpr/reduce_sum | solution.py:94
  1912.3 1387.4 %scatter_custom_fusion = f32[16,2047]{0,1:T(8,128)} fusion(s32[262144]{0:T(1024)} %bitcast.107, f32[262144,16]{1,0:T(8,128)} %bitcast.21, f32[]{:T(128)} %constant.56.clone.1), kind=kCustom, calls=%fused_computation.99 | custom fusion | flops 4194304 | bytes 131520 | tf_op jit(solution)/shard_map/transpose(jvp(jit(_take)))/scatter-add | solution.py:57
  3299.7 2.2 copy.99
  3302.1 1.5 select_reduce_fusion.1
  3303.5 41.3 %psum.15 = f32[32,16]{1,0:T(8,128)S(1)} all-reduce(f32[32,16]{1,0:T(8,128)S(1)} %select_reduce_fusion.1), channel_id=1, replica_groups=mesh['ctx'=4,'fsdp'=8] {'ctx','fsdp'}, use_global_device_ids=true, to_apply=%region_18.19 | all-reduce | flops 512 | bytes 4096 | tf_op jit(solution)/shard_map/psum | solution.py:291
  3345.4 2.0 convert_multiply_fusion.5
  3347.5 8.5 fusion.38
  3356.0 1.2 copy.100
  3357.3 6.6 fusion.31
  3363.9 1.8 fusion.34
  3365.8 2.3 fusion.37
  3368.0 5.5 fusion.66
  3373.5 2.9 slice_multiply_fusion.1
  (148 shorter events, 9.8 us)
Async XLA Ops:
  7.2 51.8 %all-gather.8.cloned.1.call-start = ((), (), s32[]{:S(2)}) async-start(), calls=%async_computation.3 | async-start | bytes 7077888 | tf_op jit(solution)/shard_map/all_gather | solution.py:33
  7.9 0.5 copy-start.28
  10.6 1023.3 %all-gather.12.cloned.1.call-start = ((), (), s32[]{:S(2)}) async-start(), calls=%async_computation.5 | async-start | bytes 5242880 | tf_op jit(solution)/shard_map/all_gather | solution.py:154
  12.2 0.6 copy-start.24
  14.2 44.8 %copy-start.18 = (bf16[512,1024]{1,0:T(8,128)(2,1)}, bf16[512,1024]{1,0:T(8,128)(2,1)S(1)}, u32[]{:S(2)}) copy-start(bf16[512,1024]{1,0:T(8,128)(2,1)S(1)} %fusion.30) | copy-start | bytes 3145732
  65.4 3.2 copy-start.40
  65.4 3.2 copy-start.7
  65.4 5.8 copy-start.36
  65.4 5.9 copy-start.41
  65.5 6.2 copy-start.27
  65.5 6.3 copy-start.26
  67.2 995.4 %all-gather.10.cloned.1.call-start = ((), (), s32[]{:S(2)}) async-start(), calls=%async_computation.4 | async-start | bytes 5242880 | tf_op jit(solution)/shard_map/all_gather | solution.py:155
  68.0 1031.9 %all-gather.14.cloned.1.call-start = ((), (), s32[]{:S(2)}) async-start(), calls=%async_computation.6 | async-start | bytes 2359296 | tf_op jit(solution)/shard_map/all_gather | solution.py:40
  68.5 1035.9 %all-gather.16.cloned.1.call-start = ((), (), s32[]{:S(2)}) async-start(), calls=%async_computation.7 | async-start | bytes 9437184 | tf_op jit(solution)/shard_map/all_gather | solution.py:33
  68.6 1.9 copy-start.30
  69.9 1060.7 %all-gather.18.cloned.1.call-start = ((), (), s32[]{:S(2)}) async-start(), calls=%async_computation.8 | async-start | bytes 9437184 | tf_op jit(solution)/shard_map/all_gather | solution.py:40
  70.5 1256.1 %reduce-scatter.6.cloned.1.call-start = ((), (), s32[]{:S(2)}) async-start(), calls=%async_computation.11 | async-start | bytes 10485760 | tf_op jit(solution)/shard_map/reduce_scatter | solution.py:239
  71.8 0.6 copy-start.22
  73.5 1.0 copy-start.10
  1015.9 13.6 copy-start.32
  1017.0 12.5 copy-start.5
  1017.0 13.8 copy-start.11
  1033.8 28.8 copy-start
  1033.8 6.7 copy-start.4
  1083.2 16.7 copy-start.2
  1099.8 30.7 copy-start.8
  1104.5 26.1 copy-start.13
  1130.5 11.6 copy-start.16
  1130.6 11.6 copy-start.38
  1142.1 7.2 copy-start.6
  1142.1 7.2 copy-start.33
  1142.1 7.8 copy-start.39
  1181.9 292.2 %reduce-scatter.4.cloned.1.call-start = ((), (), s32[]{:S(2)}) async-start(), calls=%async_computation.10 | async-start | bytes 10485760 | tf_op jit(solution)/shard_map/reduce_scatter | solution.py:238
  1206.2 35.0 %copy-start.1 = (bf16[2,256,16,64]{1,3,2,0:T(8,128)(2,1)S(1)}, bf16[2,256,16,64]{1,3,2,0:T(8,128)(2,1)}, u32[]{:S(2)}) copy-start(bf16[2,256,16,64]{1,3,2,0:T(8,128)(2,1)} %copy-done) | copy-start | bytes 3145732
  1262.4 17.3 copy-start.9
  1262.4 545.0 %reduce-scatter.8.cloned.1.call-start = ((), (), s32[]{:S(2)}) async-start(), calls=%async_computation.12 | async-start | bytes 56623104 | tf_op jit(solution)/shard_map/reduce_scatter | solution.py:264
  1276.0 7.0 copy-start.12
  1276.0 7.0 copy-start.14
  1283.0 8.5 copy-start.17
  1283.0 8.5 copy-start.44
  1520.6 0.7 copy-start.34
  1520.6 286.8 %copy-start.35 = (f32[16]{0:T(128)S(1)}, f32[16]{0:T(128)}, u32[]{:S(2)}) copy-start(f32[16]{0:T(128)} %get-tuple-element.140) | copy-start | bytes 196
  1520.6 1826.9 %all-gather.20.cloned.1.call-start = ((), (), s32[]{:S(2)}) async-start(), calls=%async_computation.9 | async-start | bytes 9437184 | tf_op jit(solution)/shard_map/all_gather | solution.py:201
  1531.9 1833.8 %all-reduce.2.cloned.1.call-start = ((), (), s32[]{:S(2)}) async-start(), calls=%async_computation.13 | async-start | bytes 12582912 | tf_op jit(solution)/shard_map/psum | solution.py:278
  1847.2 1454.7 %copy-start.43 = (f32[16]{0:T(128)}, f32[16]{0:T(128)S(1)}, u32[]{:S(2)}) copy-start(f32[16]{0:T(128)S(1)} %pmax.7) | copy-start | bytes 196
  1847.2 1454.7 %copy-start.42 = (f32[16]{0:T(128)S(1)}, f32[16]{0:T(128)}, u32[]{:S(2)}) copy-start(f32[16]{0:T(128)} %param.29) | copy-start | bytes 196
  1847.2 1454.8 %copy-start.23 = (pred[2047,32]{0,1:T(8,128)(4,1)S(1)}, pred[2047,32]{0,1:T(8,128)(4,1)}, u32[]{:S(2)}) copy-start(pred[2047,32]{0,1:T(8,128)(4,1)} %copy-done.22) | copy-start | bytes 196516
  1847.2 1498.2 %copy-start.15 = (bf16[128,1024]{1,0:T(8,128)(2,1)S(1)}, bf16[128,1024]{1,0:T(8,128)(2,1)}, u32[]{:S(2)}) copy-start(bf16[128,1024]{1,0:T(8,128)(2,1)} %param.23) | copy-start | bytes 786436
  1847.3 1500.2 %copy-start.37 = (s32[16]{0:T(128)S(1)}, s32[16]{0:T(128)}, u32[]{:S(2)}) copy-start(s32[16]{0:T(128)} %param.18) | copy-start | bytes 196
  1912.3 1445.0 %copy-start.3 = (bf16[2,256,1024]{2,1,0:T(8,128)(2,1)S(1)}, bf16[2,256,1024]{2,1,0:T(8,128)(2,1)}, u32[]{:S(2)}) copy-start(bf16[2,256,1024]{2,1,0:T(8,128)(2,1)} %param.15) | copy-start | bytes 3145732
  1912.3 1445.0 %copy-start.25 = (f32[1,2,2,128]{3,1,2,0:T(2,128)S(1)}, f32[1,2,2,128]{3,1,2,0:T(2,128)}, u32[]{:S(2)}) copy-start(f32[1,2,2,128]{3,1,2,0:T(2,128)} %copy-done.24) | copy-start | bytes 6148
  3347.5 9.8 copy-start.19
  3347.5 9.8 copy-start.20
  3347.5 9.8 copy-start.21
  3363.9 4.1 copy-start.31
  3363.9 9.6 copy-start.29
Sparse Core Ops, SparseCore 0:
  10.7 48.2 all-gather.7
  67.3 80.7 all-gather.11
  150.3 79.2 all-gather.9
  231.4 26.4 all-gather.13
  260.1 54.3 all-gather.15
  316.3 54.3 all-gather.17
  1182.0 144.4 reduce-scatter.5
  1328.9 145.1 reduce-scatter.3
  1520.7 286.6 reduce-scatter.7
  1809.9 55.0 all-gather.19
  1867.5 222.8 all-reduce.1
where the time goes:
time: 3390 us; the launch traced here: 3380 us
  other arithmetic  1510 us (45%)
  local copies, waits for them, and re-layouts  1060 us (31%)
  waiting for transfers between devices  493 us (15%)
  matrix products  217 us (6%)
  blocking collectives  81.1 us (2%)
    scatter-add x1, other arithmetic, build_bias(): return jnp.take(per_offset.T, offsets, axis=1)  1390 us
    gather x2, local copies, waits for them, and re-layouts, build_bias(): return jnp.take(per_offset.T, offsets, axis=1)  941 us
    reduce_scatter x1, waiting for transfers between devices, local(): lax.psum_scatter(jnp.concatenate([term(normed_one, qkv_grad), term(attend...  275 us
    reduce_scatter x1, waiting for transfers between devices, local(): lax.psum_scatter(key_part, 'ctx', scatter_dimension=1, tiled=True)  145 us
  transfers between devices with their start and end apart: 11, of which 4 were waited for; matrix products, arithmetic and copies ran while one was open for 79% of the time, Pallas kernels for 0%

commit v1 on v0

v1 whole, which is shorter than its diff:
```python
import functools
import math

import jax
import jax.numpy as jnp
from jax import lax
from jax.experimental import pallas as pl
from jax.experimental.pallas import tpu as pltpu
from jax.sharding import PartitionSpec as P

epsilon = 1e-06
masked = -1e30
tile = 128
half_tile = 64
wide = jnp.float32
low = jnp.bfloat16


def dot(left, right, left_dim, right_dim):
    return lax.dot_general(
        left, right, (((left_dim,), (right_dim,)), ((), ())), preferred_element_type=wide
    )


def strip_kernel(line_ref, strip_ref):
    width = line_ref.shape[-1]
    rows = jnp.broadcast_to(line_ref[0], (tile, width))
    strip_ref[0] = pltpu.roll(rows, width - (tile - 1), 1, stride=1, stride_axis=0)


def bias_strips(lines):
    heads, _, width = lines.shape
    return pl.pallas_call(
        strip_kernel,
        grid=(heads,),
        in_specs=[pl.BlockSpec((1, 1, width), lambda h: (h, 0, 0))],
        out_specs=pl.BlockSpec((1, tile, width), lambda h: (h, 0, 0)),
        out_shape=jax.ShapeDtypeStruct((heads, tile, width), wide),
        compiler_params=pltpu.CompilerParams(vmem_limit_bytes=32 << 20),
        name="bias_strips",
    )(lines)


def diagonal_kernel(strip_ref, line_ref):
    strip = strip_ref[0]
    rows = tile
    while rows > 1:
        rows //= 2
        strip = pltpu.roll(strip[:rows], rows, 1) + strip[rows:]
    line_ref[0] = strip


def diagonal_sums(strips):
    heads, _, width = strips.shape
    return pl.pallas_call(
        diagonal_kernel,
        grid=(heads,),
        in_specs=[pl.BlockSpec((1, tile, width), lambda h: (h, 0, 0))],
        out_specs=pl.BlockSpec((1, 1, width), lambda h: (h, 0, 0)),
        out_shape=jax.ShapeDtypeStruct((heads, 1, width), wide),
        compiler_params=pltpu.CompilerParams(vmem_limit_bytes=32 << 20),
        name="diagonal_sums",
    )(strips)


def one_head(block, head, extra=None):
    lane = lax.broadcasted_iota(jnp.int32, block.shape, 1)
    kept = jnp.where((lane >= half_tile) if head else (lane < half_tile), block, 0)
    if extra is None:
        return kept
    return jnp.where(lane == (0 if head else half_tile), extra, kept)


def key_masks(total, length):
    position = lax.broadcasted_iota(jnp.int32, (total, tile), 0)
    return jnp.where(position < length, 0.0, masked).astype(low)


def strip_columns(total, first, width):
    return [
        pl.ds(pl.multiple_of(total - tile - row + first, tile), width)
        for row in range(0, total, tile)
    ]


def add_bias(products, strip_ref, head, columns):
    return jnp.concatenate(
        [
            products[block * tile : (block + 1) * tile] + strip_ref[head, :, where]
            for block, where in enumerate(columns)
        ],
        axis=0,
    )


def forward_kernel(
    length_ref, query_ref, key_ref, value_ref, strip_ref, context_ref, total_ref, top_ref, *, step
):
    length = length_ref[0]
    total = query_ref.shape[0]
    masks = key_masks(total, length)
    ones = jnp.ones((step, tile), low)
    keys = [one_head(key_ref[...], head, masks) for head in (0, 1)]
    values = [one_head(value_ref[...], head).astype(wide).T.astype(low) for head in (0, 1)]

    def body(index, tops):
        first = pl.multiple_of(index * step, step)
        queries = query_ref[pl.ds(first, step), :]
        columns = strip_columns(total, first, step)
        query_okay = first + lax.broadcasted_iota(jnp.int32, (1, step), 1) < length
        context = None
        peaks = []
        for head in (0, 1):
            products = dot(keys[head], one_head(queries, head, ones), 1, 1)
            scores = add_bias(products, strip_ref, head, columns)
            row_max = jnp.max(scores, axis=0, keepdims=True)
            exponent = jnp.exp(scores - row_max)
            summed = jnp.sum(exponent, axis=0, keepdims=True)
            part = dot(values[head], exponent.astype(low), 1, 0) * (1.0 / summed)
            context = part if context is None else context + part
            total_ref[0, head : head + 1, pl.ds(first, step)] = row_max + jnp.log(summed)
            peaks.append(
                jnp.where(query_okay, jnp.max(products, axis=0, keepdims=True), masked)
            )
        context_ref[pl.ds(first, step), :] = context.T.astype(low)
        return tuple(jnp.maximum(top, peak) for top, peak in zip(tops, peaks))

    tops = lax.fori_loop(
        0, total // step, body, tuple(jnp.full((1, step), masked, wide) for _ in (0, 1))
    )
    for head in (0, 1):
        peak = jnp.max(tops[head], axis=1, keepdims=True)
        top_ref[0, head : head + 1, :] = jnp.broadcast_to(peak, (1, tile))


def attention_forward(length, qkv, strips, step=512):
    total = qkv.shape[0]
    pairs = qkv.shape[1] // (3 * tile)
    strip_width = strips.shape[2]

    def columns(which):
        return pl.BlockSpec((total, tile), lambda p, _: (0, which * pairs + p))

    return pl.pallas_call(
        functools.partial(forward_kernel, step=step),
        grid_spec=pltpu.PrefetchScalarGridSpec(
            num_scalar_prefetch=1,
            grid=(pairs,),
            in_specs=[
                columns(0),
                columns(1),
                columns(2),
                pl.BlockSpec((2, tile, strip_width), lambda p, _: (p, 0, 0)),
            ],
            out_specs=[
                columns(0),
                pl.BlockSpec((1, 2, total), lambda p, _: (p, 0, 0)),
                pl.BlockSpec((1, 2, tile), lambda p, _: (p, 0, 0)),
            ],
        ),
        out_shape=[
            jax.ShapeDtypeStruct((total, pairs * tile), low),
            jax.ShapeDtypeStruct((pairs, 2, total), wide),
            jax.ShapeDtypeStruct((pairs, 2, tile), wide),
        ],
        compiler_params=pltpu.CompilerParams(vmem_limit_bytes=48 << 20),
        cost_estimate=pl.CostEstimate(
            flops=40_000_000_000, bytes_accessed=12 << 20, transcendentals=0
        ),
        name="attention_forward",
    )(length, qkv, qkv, qkv, strips)


def backward_kernel(
    length_ref,
    query_ref,
    key_ref,
    value_ref,
    context_ref,
    grad_ref,
    total_ref,
    strip_ref,
    query_grad_ref,
    key_grad_ref,
    value_grad_ref,
    strip_grad_ref,
    key_sum,
    value_sum,
    *,
    step,
):
    length = length_ref[0]
    total = query_ref.shape[0]
    masks = key_masks(total, length)
    ones = jnp.ones((step, tile), low)
    keys = [one_head(key_ref[...], head, masks) for head in (0, 1)]
    plain_keys = [one_head(key_ref[...], head) for head in (0, 1)]
    values = [one_head(value_ref[...], head) for head in (0, 1)]
    key_sum[...] = jnp.zeros_like(key_sum)
    value_sum[...] = jnp.zeros_like(value_sum)
    strip_grad_ref[...] = jnp.zeros_like(strip_grad_ref)

    def body(index, carry):
        first = pl.multiple_of(index * step, step)
        queries = query_ref[pl.ds(first, step), :]
        grads = grad_ref[pl.ds(first, step), :]
        columns = strip_columns(total, first, step)
        inner = grads.astype(wide) * context_ref[pl.ds(first, step), :].astype(wide)
        query_grad = None
        for head in (0, 1):
            head_grads = one_head(grads, head)
            pick = one_head(jnp.ones((8, tile), wide), head)
            row_inner = lax.dot_general(
                pick,
                inner,
                (((1,), (1,)), ((), ())),
                precision=lax.Precision.HIGHEST,
                preferred_element_type=wide,
            )[:1]
            log_total = total_ref[0, head : head + 1, pl.ds(first, step)]
            products = dot(keys[head], one_head(queries, head, ones), 1, 1)
            probs = jnp.exp(add_bias(products, strip_ref, head, columns) - log_total)
            value_sum[...] += dot(probs.astype(low), head_grads, 1, 0)
            score_grad = probs * (dot(values[head], head_grads, 1, 1) - row_inner)
            for block, where in enumerate(columns):
                strip_grad_ref[head, :, where] += score_grad[block * tile : (block + 1) * tile]
            score_low = score_grad.astype(low)
            key_sum[...] += dot(score_low, one_head(queries, head), 1, 0)
            part = dot(score_low, plain_keys[head], 0, 0)
            query_grad = part if query_grad is None else query_grad + part
        query_grad_ref[pl.ds(first, step), :] = query_grad.astype(low)
        return carry

    lax.fori_loop(0, total // step, body, 0)
    key_grad_ref[...] = key_sum[...].astype(low)
    value_grad_ref[...] = value_sum[...].astype(low)


def attention_backward(length, qkv, context, context_grad, log_totals, strips, step=256):
    total = qkv.shape[0]
    pairs = qkv.shape[1] // (3 * tile)
    strip_width = strips.shape[2]

    def columns(which):
        return pl.BlockSpec((total, tile), lambda p, _: (0, which * pairs + p))

    strip_block = pl.BlockSpec((2, tile, strip_width), lambda p, _: (p, 0, 0))
    return pl.pallas_call(
        functools.partial(backward_kernel, step=step),
        grid_spec=pltpu.PrefetchScalarGridSpec(
            num_scalar_prefetch=1,
            grid=(pairs,),
            in_specs=[
                columns(0),
                columns(1),
                columns(2),
                columns(0),
                columns(0),
                pl.BlockSpec((1, 2, total), lambda p, _: (p, 0, 0)),
                strip_block,
            ],
            out_specs=[columns(0), columns(0), columns(0), strip_block],
            scratch_shapes=[pltpu.VMEM((total, tile), wide), pltpu.VMEM((total, tile), wide)],
        ),
        out_shape=[jax.ShapeDtypeStruct((total, pairs * tile), low)] * 3
        + [jax.ShapeDtypeStruct((2 * pairs, tile, strip_width), wide)],
        compiler_params=pltpu.CompilerParams(vmem_limit_bytes=48 << 20),
        cost_estimate=pl.CostEstimate(
            flops=60_000_000_000, bytes_accessed=24 << 20, transcendentals=0
        ),
        name="attention_backward",
    )(length, qkv, qkv, qkv, context, context_grad, log_totals, strips)


def gelu_and_slope(values):
    distance = jnp.abs(values) * math.sqrt(0.5)
    ratio = 1.0 / (1.0 + 0.3275911 * distance)
    density = jnp.exp(-distance * distance)
    poly = 1.061405429 * ratio - 1.453152027
    poly = poly * ratio + 1.421413741
    poly = poly * ratio - 0.284496736
    poly = poly * ratio + 0.254829592
    tail = (0.5 * ratio) * poly * density
    cumulative = jnp.where(values >= 0, 1.0 - tail, tail)
    slope = cumulative + values * density * (1.0 / math.sqrt(2.0 * math.pi))
    return values * cumulative, slope


def feed_forward_kernel(
    normed_ref,
    normed_t_ref,
    grad_ref,
    grad_t_ref,
    expand_ref,
    contract_ref,
    mixed_ref,
    normed_grad_ref,
    expand_grad_ref,
    contract_grad_ref,
    mixed_sum,
    normed_sum,
):
    index = pl.program_id(0)
    pre_act = dot(normed_ref[...], expand_ref[...], 1, 0)
    act_grad = dot(grad_ref[...], contract_ref[...], 1, 0).astype(low).astype(wide)
    activated, slope = gelu_and_slope(pre_act)
    activated = activated.astype(low)
    pre_grad = (act_grad * slope).astype(low)
    contract_grad_ref[...] = dot(grad_t_ref[...], activated, 1, 0).astype(low)
    expand_grad_ref[...] = dot(normed_t_ref[...], pre_grad, 1, 0).astype(low)
    mixed = dot(activated, contract_ref[...], 1, 1)
    normed_grad = dot(pre_grad, expand_ref[...], 1, 1)

    @pl.when(index == 0)
    def _():
        mixed_sum[...] = mixed
        normed_sum[...] = normed_grad

    @pl.when(index > 0)
    def _():
        mixed_sum[...] += mixed
        normed_sum[...] += normed_grad

    @pl.when(index == pl.num_programs(0) - 1)
    def _():
        mixed_ref[...] = mixed_sum[...].astype(low)
        normed_grad_ref[...] = normed_sum[...].astype(low)


def feed_forward(normed, normed_t, grad, grad_t, expand, contract, step=512):
    rows, width = normed.shape
    hidden = expand.shape[1]
    whole = pl.BlockSpec((rows, width), lambda i: (0, 0), pipeline_mode=pl.Buffered(1))
    whole_t = pl.BlockSpec((width, rows), lambda i: (0, 0), pipeline_mode=pl.Buffered(1))
    block = pl.BlockSpec((width, step), lambda i: (0, i))
    whole_out = pl.BlockSpec((rows, width), lambda i: (0, 0))
    return pl.pallas_call(
        feed_forward_kernel,
        grid=(hidden // step,),
        in_specs=[whole, whole_t, whole, whole_t, block, block],
        out_specs=[whole_out, whole_out, block, block],
        out_shape=[jax.ShapeDtypeStruct((rows, width), low)] * 2
        + [jax.ShapeDtypeStruct((width, hidden), low)] * 2,
        scratch_shapes=[pltpu.VMEM((rows, width), wide), pltpu.VMEM((rows, width), wide)],
        compiler_params=pltpu.CompilerParams(vmem_limit_bytes=56 << 20),
        cost_estimate=pl.CostEstimate(
            flops=12 * rows * width * hidden * 3 // 2, bytes_accessed=40 << 20, transcendentals=0
        ),
        name="feed_forward",
    )(normed, normed_t, grad, grad_t, expand, contract)


def normalize(values):
    scaled = lax.rsqrt(jnp.mean(values * values, axis=-1, keepdims=True) + epsilon)
    return (values * scaled, scaled)


def normalize_back(values, scaled, upstream):
    unit_rows = values * scaled
    return scaled * (upstream - unit_rows * jnp.mean(upstream * unit_rows, axis=-1, keepdims=True))


def scaled_rows(weight, scaling):
    return (scaling.astype(wide)[:, None] * weight.astype(wide)).astype(low)


def take(array, index):
    return lax.dynamic_index_in_dim(array, index, 0, keepdims=False)


def put(array, part, index):
    return lax.dynamic_update_slice_in_dim(array, part[None], index, 0)


def after(array, *others):
    return lax.optimization_barrier((array, *others))[0]


class Links:
    def __init__(self):
        self.shards = lax.axis_size("fsdp")
        self.depth = lax.axis_size("ctx")
        self.shard = lax.axis_index("fsdp")
        self.level = lax.axis_index("ctx")
        self.chips = self.shards // 2
        self.chip = self.shard // 2
        self.core = self.shard % 2
        self.groups = [list(range(core, self.shards, 2)) for core in (0, 1)]

    def sibling(self, array):
        return lax.ppermute(array, "fsdp", [(i, i ^ 1) for i in range(self.shards)])

    def across(self, array, bit):
        return lax.ppermute(array, "fsdp", [(i, i ^ (2 * bit)) for i in range(self.shards)])

    def vertical(self, array, distance):
        count = self.depth
        return lax.ppermute(array, "ctx", [(i, (i + distance) % count) for i in range(count)])

    def in_order(self, mine, other, axis):
        return jnp.concatenate(
            [jnp.where(self.core == 0, mine, other), jnp.where(self.core == 0, other, mine)],
            axis=axis,
        )

    def gather(self, shard, behind=()):
        if self.chips != 4:
            return (
                lax.all_gather(shard, "fsdp", axis=0, tiled=True, axis_index_groups=self.groups),
                (),
            )
        if behind:
            shard = after(shard, *behind)
        half = shard.shape[0] // 2
        first = self.across(shard, 1)
        second = self.across(shard, 2)
        upper = self.across(first[:half], 2)
        lower = self.across(second[half:], 1)
        whole = jnp.zeros((4,) + shard.shape, shard.dtype)
        whole = put(whole, shard, self.chip)
        whole = put(whole, first, self.chip ^ 1)
        whole = put(whole, second, self.chip ^ 2)
        whole = put(whole, jnp.concatenate([upper, lower], axis=0), self.chip ^ 3)
        return whole.reshape((4 * shard.shape[0],) + shard.shape[1:]), (first, second)

    def scatter(self, terms, behind=()):
        if self.chips != 4:
            summed = lax.psum_scatter(
                terms, "fsdp", scatter_dimension=0, tiled=True, axis_index_groups=self.groups
            )
            return summed.astype(wide), ()
        if behind:
            terms = after(terms, *behind)
        parts = terms.reshape((4, terms.shape[0] // 4) + terms.shape[1:])
        half = parts.shape[1] // 2
        corner = take(parts, self.chip ^ 3)
        upper = self.across(corner[:half], 1)
        lower = self.across(corner[half:], 2)
        beside = take(parts, self.chip ^ 1).astype(wide)
        below = take(parts, self.chip ^ 2).astype(wide)
        beside = jnp.concatenate([beside[:half], beside[half:] + lower.astype(wide)], axis=0)
        below = jnp.concatenate([below[:half] + upper.astype(wide), below[half:]], axis=0)
        first = self.across(beside.astype(low), 1)
        second = self.across(below.astype(low), 2)
        own = take(parts, self.chip).astype(wide)
        return own + first.astype(wide) + second.astype(wide), (first, second)

    def level_sum(self, terms):
        count = self.depth
        parts = terms.reshape((count, terms.shape[0] // count) + terms.shape[1:])
        total = take(parts, self.level).astype(wide)
        for distance in range(1, count):
            part = take(parts, (self.level + distance) % count)
            total = total + self.vertical(part, distance).astype(wide)
        total = total.astype(low)
        whole = put(jnp.zeros_like(parts), total, self.level)
        for distance in range(1, count):
            part = self.vertical(total, distance)
            whole = put(whole, part, (self.level - distance) % count)
        return whole.reshape(terms.shape)

    def exchange_rows(self, rows):
        parts = rows.reshape((2, rows.shape[0] // 2) + rows.shape[1:])
        mine = take(parts, self.core)
        other = self.sibling(take(parts, 1 - self.core))
        return self.in_order(mine[None], other[None], 0)

    def trade(self, array, outward, swapped):
        pairs = []
        for level in range(self.depth):
            for shard in range(self.shards):
                chip, core = divmod(shard, 2)
                side, odd = divmod(level, 2)
                slot = odd if not swapped else 1 - odd
                held = level * self.shards + shard
                worked = (2 * core + slot) * self.shards + 2 * chip + side
                pairs.append((held, worked) if outward else (worked, held))
        return lax.ppermute(array, ("ctx", "fsdp"), pairs)

    def to_slots(self, blocks):
        odd = self.level % 2
        first = self.trade(take(blocks, odd), True, False)
        second = self.trade(take(blocks, 1 - odd), True, True)
        flip = odd == 0
        return jnp.concatenate(
            [jnp.where(flip, first, second), jnp.where(flip, second, first)], axis=0
        )

    def from_slots(self, rows):
        odd = self.level % 2
        blocks = rows.reshape((2, rows.shape[0] // 2) + rows.shape[1:])
        first = self.trade(take(blocks, odd), False, False)
        second = self.trade(take(blocks, 1 - odd), False, True)
        flip = odd == 0
        return jnp.stack([jnp.where(flip, first, second), jnp.where(flip, second, first)])


def local(
    tokens,
    cotangent,
    sequence_lengths,
    slot_sequence,
    offset_bucket,
    first_gain,
    second_gain,
    query_weight,
    key_weight,
    value_weight,
    output_weight,
    expand_weight,
    contract_weight,
    bias_table,
    clip_limit,
):
    links = Links()
    core = links.core
    held_count, local_length, model_width = tokens.shape
    total_length = local_length * links.depth
    half_length = total_length // 2
    bucket_count, head_count = bias_table.shape
    inner_width = query_weight.shape[1]
    head_size = inner_width // head_count
    hidden_width = expand_weight.shape[1]
    row_share = query_weight.shape[0]
    own_heads = head_count // 2
    own_inner = inner_width // 2
    own_hidden = hidden_width // 2
    slot_count = slot_sequence.shape[0]
    assert held_count == 2 and links.depth == 4

    slots = jnp.arange(slot_count)
    slot = links.chip * (2 * held_count) + links.level
    sequence = jnp.sum(jnp.where(slots == slot, slot_sequence, 0))
    length = jnp.sum(jnp.where(slots == sequence, sequence_lengths, 0))
    row_okay = jnp.arange(total_length)[:, None] < length

    stacked = jnp.concatenate([query_weight, key_weight, value_weight], axis=1)
    effective_qkv = scaled_rows(stacked, first_gain)
    effective_expand = scaled_rows(expand_weight, second_gain)

    def side_columns(which):
        def cut(weight, blocks):
            parts = weight.reshape(row_share, blocks, 2, weight.shape[1] // (2 * blocks))
            return lax.dynamic_index_in_dim(parts, which, 2, keepdims=False).reshape(row_share, -1)

        return jnp.concatenate(
            [
                cut(effective_qkv, 3),
                cut(output_weight, 1),
                cut(effective_expand, 1),
                cut(contract_weight, 1),
            ],
            axis=1,
        )

    mine = side_columns(core)
    other = links.sibling(side_columns(1 - core))
    chip_rows = links.in_order(mine, other, 0)
    cuts = [0, 3 * own_inner, 4 * own_inner, 4 * own_inner + own_hidden]
    cuts.append(cuts[-1] + own_hidden)
    qkv_shard, output_shard, expand_shard, contract_shard = (
        chip_rows[:, start:stop] for start, stop in zip(cuts[:-1], cuts[1:])
    )

    token_half = links.to_slots(tokens)
    token_low = links.in_order(token_half, links.sibling(token_half), 0)
    cotangent_half = links.to_slots(after(cotangent, token_low))
    cotangent_low = links.in_order(cotangent_half, links.sibling(cotangent_half), 0)

    whole_qkv, sent = links.gather(qkv_shard)
    whole_output, sent = links.gather(output_shard, sent)
    whole_expand, sent = links.gather(expand_shard, sent)
    whole_contract, sent = links.gather(contract_shard, sent)

    line_width = 2 * total_length
    falling = jnp.concatenate([jnp.flip(offset_bucket), jnp.full((1,), -1, jnp.int32)])
    matching = falling[:, None] == jnp.arange(bucket_count)[None, :]
    own_table = lax.dynamic_slice_in_dim(bias_table, core * own_heads, own_heads, 1)
    lines = dot(own_table, matching.astype(low), 0, 1)
    strips = bias_strips(lines.reshape(own_heads, 1, line_width))

    token_rows = token_low.astype(wide)
    unit_one, scale_one = normalize(token_rows)
    normed_one = unit_one.astype(low)
    qkv = dot(normed_one, whole_qkv, 1, 0).astype(low)
    length_line = length.reshape(1).astype(jnp.int32)
    context, log_totals, tops = attention_forward(length_line, qkv, strips)
    attended = dot(context, whole_output, 1, 1).astype(low)
    hidden_one = token_rows + (
        attended.astype(wide) + links.sibling(attended).astype(wide)
    )
    unit_two, scale_two = normalize(hidden_one)
    normed_two = unit_two.astype(low)
    out_low = jnp.where(row_okay, cotangent_low, 0)
    mixed, normed_two_part, expand_terms, contract_terms = feed_forward(
        normed_two, normed_two.T, out_low, out_low.T, whole_expand, whole_contract
    )
    normed_two_grad = normed_two_part.astype(wide) + links.sibling(normed_two_part).astype(wide)
    hidden_grad = out_low.astype(wide) + normalize_back(hidden_one, scale_two, normed_two_grad)
    attended_grad = hidden_grad.astype(low)

    def own_half(array, which):
        return lax.dynamic_slice_in_dim(array, which * half_length, half_length, 0)

    mixed_half = own_half(mixed, core).astype(wide) + links.sibling(
        own_half(mixed, 1 - core)
    ).astype(wide)
    result_half = jnp.where(
        own_half(row_okay, core), own_half(hidden_one, core) + mixed_half, 0.0
    ).astype(low)
    result = links.from_slots(result_half)

    context_grad = dot(attended_grad, whole_output, 1, 0).astype(low)
    output_terms = dot(attended_grad, context, 0, 0).astype(low)
    query_grad, key_grad, value_grad, strip_grads = attention_backward(
        length_line, qkv, context, context_grad, log_totals, strips
    )
    qkv_grad = jnp.concatenate([query_grad, key_grad, value_grad], axis=1)
    qkv_terms = dot(normed_one, qkv_grad, 0, 0).astype(low)
    normed_one_part = dot(qkv_grad, whole_qkv, 1, 1)
    normed_one_grad = own_half(normed_one_part, core) + links.sibling(
        own_half(normed_one_part, 1 - core).astype(low)
    ).astype(wide)
    input_half = own_half(hidden_grad, core) + normalize_back(
        own_half(token_rows, core), own_half(scale_one, core), normed_one_grad
    )
    input_gradient = links.from_slots(input_half.astype(low)).astype(wide)

    contract_sum, sent = links.scatter(contract_terms)
    expand_sum, sent = links.scatter(expand_terms, sent)
    output_sum, sent = links.scatter(output_terms, sent)
    qkv_sum, sent = links.scatter(qkv_terms, sent)
    gathered, _ = links.gather(result.reshape(held_count * local_length, model_width), sent)

    def finished(summed):
        parts = links.exchange_rows(summed.astype(low))
        flat = parts.reshape(2 * row_share, -1)
        return links.level_sum(flat).reshape(parts.shape)

    contract_parts = finished(contract_sum)
    expand_parts = finished(expand_sum)
    output_parts = finished(output_sum)
    qkv_parts = finished(qkv_sum)

    def columns_of(parts, blocks):
        width = parts.shape[2] // blocks
        shaped = parts.reshape(2, row_share, blocks, width).transpose(1, 2, 0, 3)
        return shaped.reshape(row_share, 2 * blocks * width).astype(wide)

    contract_weight_gradient = columns_of(contract_parts, 1)
    raw_two = columns_of(expand_parts, 1)
    output_weight_gradient = columns_of(output_parts, 1)
    raw_one = columns_of(qkv_parts, 3)
    first_scale = first_gain.astype(wide)[:, None]
    second_scale = second_gain.astype(wide)[:, None]
    first_gain_gradient = jnp.sum(stacked.astype(wide) * raw_one, axis=1)
    second_gain_gradient = jnp.sum(expand_weight.astype(wide) * raw_two, axis=1)
    query_weight_gradient = first_scale * raw_one[:, :inner_width]
    key_weight_gradient = first_scale * raw_one[:, inner_width : 2 * inner_width]
    value_weight_gradient = first_scale * raw_one[:, 2 * inner_width :]
    expand_weight_gradient = second_scale * raw_two

    gathered = gathered.reshape(links.chips * held_count, local_length, model_width)

    def slot_of(wanted):
        return jnp.sum(jnp.where(slot_sequence == wanted, slots, 0))

    def place_of(found):
        return (found // 4) * held_count + found % 2

    own_slots = [slot_of(links.shard * held_count + row) for row in range(held_count)]
    other_slots = [slot_of((links.shard ^ 1) * held_count + row) for row in range(held_count)]
    from_other = links.sibling(jnp.stack([take(gathered, place_of(s)) for s in other_slots]))
    output = jnp.stack(
        [
            jnp.where((s // 2) % 2 == core, take(gathered, place_of(s)), from_other[row])
            for row, s in enumerate(own_slots)
        ]
    )

    diagonals = diagonal_sums(strip_grads).reshape(own_heads, line_width)
    table_grad = lax.dot_general(
        diagonals,
        matching.astype(wide),
        (((1,), (0,)), ((), ())),
        precision=lax.Precision.HIGHEST,
        preferred_element_type=wide,
    )
    small = jnp.concatenate([table_grad, tops.reshape(own_heads, -1)[:, :1]], axis=1)

    def joined(left, right):
        return jnp.concatenate(
            [
                left[:, :bucket_count] + right[:, :bucket_count],
                jnp.maximum(left[:, bucket_count:], right[:, bucket_count:]),
            ],
            axis=1,
        )

    bit = 1
    while bit < links.chips:
        small = joined(small, links.across(small, bit))
        bit *= 2
    bit = 1
    while bit < links.depth:
        swap = [(i, i ^ bit) for i in range(links.depth)]
        small = joined(small, lax.ppermute(small, "ctx", swap))
        bit *= 2
    small = links.in_order(small, links.sibling(small), 0)
    table_rows = bucket_count // links.shards
    bias_table_gradient = lax.dynamic_slice_in_dim(
        small[:, :bucket_count].T, links.shard * table_rows, table_rows, 0
    )
    largest = small[:, bucket_count]
    shrink = clip_limit / jnp.maximum(clip_limit, largest)
    column_scale = jnp.repeat(jnp.sqrt(shrink), head_size)
    new_query_weight = query_weight.astype(wide) * column_scale[None, :]
    new_key_weight = key_weight.astype(wide) * column_scale[None, :]
    return (
        output,
        input_gradient,
        first_gain_gradient,
        second_gain_gradient,
        query_weight_gradient,
        key_weight_gradient,
        value_weight_gradient,
        output_weight_gradient,
        expand_weight_gradient,
        contract_weight_gradient,
        bias_table_gradient,
        largest,
        new_query_weight,
        new_key_weight,
    )


def solution(mesh):
    return jax.shard_map(
        local,
        mesh=mesh,
        in_specs=(
            P("fsdp", "ctx", None),
            P("fsdp", "ctx", None),
            P(),
            P(),
            P(),
            P("fsdp"),
            P("fsdp"),
            P("fsdp", None),
            P("fsdp", None),
            P("fsdp", None),
            P("fsdp", None),
            P("fsdp", None),
            P("fsdp", None),
            P(),
            P(),
        ),
        out_specs=(
            P("fsdp", "ctx", None),
            P("fsdp", "ctx", None),
            P("fsdp"),
            P("fsdp"),
            P("fsdp", None),
            P("fsdp", None),
            P("fsdp", None),
            P("fsdp", None),
            P("fsdp", None),
            P("fsdp", None),
            P("fsdp", None),
            P(),
            P("fsdp", None),
            P("fsdp", None),
        ),
        check_vma=False,
    )
```

time: 3390 us -> 682 us (0.20)
  other arithmetic: 1510 us -> 91.1 us
  local copies, waits for them, and re-layouts: 1060 us -> 123 us
  waiting for transfers between devices: 493 us -> 143 us
  matrix products: 217 us -> 25.5 us
  starting transfers between devices: 1.12 us -> 169 us
  Pallas kernels: 0 us -> 107 us
  blocking collectives: 81.1 us -> 0 us
    scatter-add x1 -> x0, other arithmetic: 1390 us -> none  [build_bias(): return jnp.take(per_offset.T, offsets, axis=1)]
    gather x2 -> x0, local copies, waits for them, and re-layouts: 941 us -> none  [build_bias(): return jnp.take(per_offset.T, offsets, axis=1)]
    reduce_scatter x3 -> x0, waiting for transfers between devices: 447 us -> none  [the longest x1 275 us: local(): lax.psum_scatter(jnp.concatenate([term(normed_one, qkv_grad), term(attend...]
    dot_general x19 -> x8, matrix products: 217 us -> 25.5 us  [the longest x7 24.9 us: dot(): lax.dot_general(left, right, (((left_dim,), (right_dim,)), ((), ())), pre...]
    ppermute x0 -> x85, starting transfers between devices: none -> 169 us  [the longest x24 82.3 us: vertical(): lax.ppermute(array, 'ctx', [(i, (i + distance) % count) for i in range(co...]
    ppermute x0 -> x85, waiting for transfers between devices: none -> 143 us  [the longest x38 78.7 us: across(): lax.ppermute(array, 'fsdp', [(i, i ^ 2 * bit) for i in range(self.shards)])]
    pallas_call x0 -> x5, Pallas kernels: none -> 107 us  [the longest x1 40.2 us: feed_forward(): pl.pallas_call(feed_forward_kernel, grid=(hidden // step,), in_specs=[who...]
    reduce_sum x2 -> x0, local copies, waits for them, and re-layouts: 65.4 us -> none  [the longest x1 65 us: attend_back(): bias_grad = jnp.sum(score_grad.astype(jnp.float32), axis=0)]
  transfers between devices with their start and end apart: 11 -> 85, of which waited for: 4 -> 29; matrix products, arithmetic and copies ran while one was open for 79% -> 31% of each run, Pallas kernels for 0% -> 10%
where the time goes in v1:
time: 682 us; the launch traced here: 671 us
  starting transfers between devices  169 us (25%)
  waiting for transfers between devices  143 us (21%)
  local copies, waits for them, and re-layouts  123 us (18%)
  Pallas kernels  107 us (16%)
  other arithmetic  91.1 us (13%)
  matrix products  25.5 us (4%)
  between operations  13.2 us (2%)
    ppermute x24, starting transfers between devices, vertical(): lax.ppermute(array, 'ctx', [(i, (i + distance) % count) for i in range(co...  82.3 us
    ppermute x38, waiting for transfers between devices, across(): lax.ppermute(array, 'fsdp', [(i, i ^ 2 * bit) for i in range(self.shards)])  78.7 us
    ppermute x24, waiting for transfers between devices, vertical(): lax.ppermute(array, 'ctx', [(i, (i + distance) % count) for i in range(co...  57.7 us
    pallas_call x1, Pallas kernels, feed_forward(): pl.pallas_call(feed_forward_kernel, grid=(hidden // step,), in_specs=[who...  40.2 us
    ppermute x38, starting transfers between devices, across(): lax.ppermute(array, 'fsdp', [(i, i ^ 2 * bit) for i in range(self.shards)])  39 us
    pallas_call x1, Pallas kernels, attention_backward(): pl.pallas_call(functools.partial(backward_kernel, step=step), grid_spec=p...  36.3 us
    unnamed x160, local copies, waits for them, and re-layouts  30.6 us
    dot_general x7, matrix products, dot(): lax.dot_general(left, right, (((left_dim,), (right_dim,)), ((), ())), pre...  24.9 us
  transfers between devices with their start and end apart: 85, of which 29 were waited for; matrix products, arithmetic and copies ran while one was open for 31% of the time, Pallas kernels for 10%

profile of v1, /device:TPU:0, one launch (start us, length us, event | category | flops | bytes accessed | tf_op | source)
XLA Modules:
  0.0 670.6 jit_solution(16264174343401989376)
XLA Ops:
  3.1 5.4 collective-permute-start
  9.4 3.0 collective-permute-start.1
  13.5 5.3 collective-permute-start.13
  33.5 2.9 collective-permute-done.14
  38.7 13.7 %collective-permute-start.15 = (bf16[512,1024]{0,1:T(8,128)(2,1)}, bf16[512,1024]{0,1:T(8,128)(2,1)}, u32[]{:S(2)}, u32[]{:S(2)}) collective-permute-start(bf16[512,1024]{0,1:T(8,128)(2,1)} %pad_maximum_fusion.5), channel_id=1, source_target_pairs={{0,1},{1,0},{2,3},{3,2},{4,5},{5,4},{6,7},{7,6},{8,9},{9,8},{10,11... | collective-permute-start | bytes 3145736 | tf_op jit(solution)/shard_map/ppermute | solution.py:391
  58.2 2.8 bias_strips.1.strip_ref
  61.0 3.4 copy-done.2
  67.2 3.0 broadcast_select_fusion.5
  82.1 3.9 copy.97.grad_ref
  88.3 8.8 %collective-permute-done.4 = bf16[256,1536]{1,0:T(8,128)(2,1)} collective-permute-done((bf16[256,1536]{1,0:T(8,128)(2,1)}, bf16[256,1536]{1,0:T(8,128)(2,1)}, u32[]{:S(2)}, u32[]{:S(2)}) %collective-permute-start.4) | collective-permute-done | bytes 786464 | tf_op jit(solution)/shard_map/ppermute | solution.py:394
  119.0 5.7 convolution_convert_fusion.1.query_ref.key_ref.value_ref
  124.7 22.6 %attention_forward.1 = (bf16[1024,512]{1,0:T(8,128)(2,1)S(1)}, f32[4,2,1024]{2,1,0:T(2,128)S(1)}, f32[4,2,128]{2,1,0:T(2,128)S(1)}) custom-call(s32[1]{0:T(128)} %bitcast.2.length_ref, bf16[1024,1536]{1,0:T(8,128)(2,1)S(1)} %convolution_convert_fusion.1.query_ref.key_ref.value_ref, ...), custom_call_target="tpu_custom_call" | custom-call | flops 40000000000 | bytes 12582912 | tf_op jit(solution)/shard_map/attention_forward/pallas_call | solution.py:144
  148.0 2.5 convolution_convert_fusion.2
  155.8 31.8 %collective-permute-done.18 = bf16[128,2048]{1,0:T(8,128)(2,1)S(1)} collective-permute-done((bf16[128,2048]{1,0:T(8,128)(2,1)S(1)}, bf16[128,2048]{1,0:T(8,128)(2,1)S(1)}, u32[]{:S(2)}, u32[]{:S(2)}) %collective-permute-start.18) | collective-permute-done | bytes 524320 | tf_op jit(solution)/shard_map/ppermute | solution.py:394
  198.8 2.6 copy.96.normed_ref
  201.3 4.1 fusion.73.normed_t_ref
  207.7 40.2 %feed_forward.1 = (bf16[1024,1024]{1,0:T(8,128)(2,1)}, bf16[1024,1024]{1,0:T(8,128)(2,1)}, bf16[1024,2048]{1,0:T(8,128)(2,1)}, bf16[1024,2048]{1,0:T(8,128)(2,1)}) custom-call(bf16[1024,1024]{1,0:T(8,128)(2,1)} %copy.96.normed_ref, bf16[1024,1024]{1,0:T(8,128)(2,1)} %fusion.73.normed_t_ref, bf16[1024,1024]{1,0:T(8,128)(2,1)} %copy.97.grad_ref, ...), custom_call_target="tpu_custom_call" | custom-call | flops 38654705664 | bytes 41943040 | tf_op jit(solution)/shard_map/feed_forward/pallas_call | solution.py:337
  247.9 2.9 dynamic-slice_bitcast_fusion.7
  251.9 2.9 copy.105
  254.9 3.9 copy.98
  281.5 4.3 fusion.58
  285.8 2.7 select_convert_fusion
  288.4 2.4 copy.129
  292.2 2.9 dynamic-slice_bitcast_fusion.1
  297.2 2.9 multiply_reduce_fusion
  300.1 3.3 multiply_add_fusion
  303.5 3.3 convolution_convert_fusion.4.grad_ref
  306.8 36.3 %attention_backward.1 = (bf16[1024,512]{1,0:T(8,128)(2,1)S(1)}, bf16[1024,512]{1,0:T(8,128)(2,1)S(1)}, bf16[1024,512]{1,0:T(8,128)(2,1)S(1)}, f32[8,128,2048]{2,1,0:T(8,128)}) custom-call(s32[1]{0:T(128)} %bitcast.2.length_ref, bf16[1024,1536]{1,0:T(8,128)(2,1)} %copy-done.4, bf16[1024,1536]{1,0:T(8,128)(2,1)} %copy-done.4, bf16[1024,1536]{1,0:T(8,128)(2,1)} %copy-done.4, ...), custom_call_target="tpu_custom_call" | custom-call | flops 60000002048 | bytes 25165824 | tf_op jit(solution)/shard_map/attention_backward/pallas_call | solution.py:248
  343.1 3.4 copy-done.3
  346.5 4.8 diagonal_sums.1
  353.2 5.5 fusion.64
  358.7 5.1 convolution_convert_fusion
  369.7 6.4 collective-permute-start.82
  377.8 4.3 collective-permute-start.83
  389.3 7.4 %collective-permute-done.35 = bf16[256,2048]{1,0:T(8,128)(2,1)S(1)} collective-permute-done((bf16[256,2048]{1,0:T(8,128)(2,1)S(1)}, bf16[256,2048]{1,0:T(8,128)(2,1)S(1)}, u32[]{:S(2)}, u32[]{:S(2)}) %collective-permute-start.35) | collective-permute-done | bytes 1048608 | tf_op jit(solution)/shard_map/ppermute | solution.py:394
  396.6 6.1 collective-permute-done.33
  402.8 3.9 fusion.3
  411.1 2.4 collective-permute-done.36
  433.0 2.4 dynamic-slice_bitcast_fusion.19
  438.5 2.6 collective-permute-start.66
  445.4 2.9 collective-permute-done.51
  448.3 21.6 %collective-permute-start.68 = (bf16[64,512]{1,0:T(8,128)(2,1)S(1)}, bf16[64,512]{1,0:T(8,128)(2,1)S(1)}, u32[]{:S(2)}, u32[]{:S(2)}) collective-permute-start(bf16[64,512]{1,0:T(8,128)(2,1)S(1)} %get-tuple-element.193), channel_id=1, source_target_pairs={{0,16},{8,24},{16,0},{24,8},{1,17},{9,25},{17,1},{25,9},{2,18},{10... | collective-permute-start | bytes 196616 | tf_op jit(solution)/shard_map/ppermute | solution.py:398
  472.2 9.3 %collective-permute-done.68 = bf16[64,512]{1,0:T(8,128)(2,1)S(1)} collective-permute-done((bf16[64,512]{1,0:T(8,128)(2,1)S(1)}, bf16[64,512]{1,0:T(8,128)(2,1)S(1)}, u32[]{:S(2)}, u32[]{:S(2)}) %collective-permute-start.68) | collective-permute-done | bytes 65568 | tf_op jit(solution)/shard_map/ppermute | solution.py:398
  489.8 4.3 collective-permute-done.70
  494.1 7.6 %collective-permute-start.71 = (bf16[64,512]{1,0:T(8,128)(2,1)}, bf16[64,512]{1,0:T(8,128)(2,1)S(1)}, u32[]{:S(2)}, u32[]{:S(2)}) collective-permute-start(bf16[64,512]{1,0:T(8,128)(2,1)} %get-tuple-element.102), channel_id=1, source_target_pairs={{0,16},{8,24},{16,0},{24,8},{1,17},{9,25},{17,1},{25,9},{2,18},{10... | collective-permute-start | bytes 196616 | tf_op jit(solution)/shard_map/ppermute | solution.py:398
  503.2 2.9 collective-permute-done.71
  506.7 3.8 collective-permute-done.72
  519.3 4.4 collective-permute-start.62
  527.4 14.3 %collective-permute-done.61 = bf16[64,2048]{1,0:T(8,128)(2,1)S(1)} collective-permute-done((bf16[64,2048]{1,0:T(8,128)(2,1)S(1)}, bf16[64,2048]{1,0:T(8,128)(2,1)S(1)}, u32[]{:S(2)}, u32[]{:S(2)}) %collective-permute-start.61) | collective-permute-done | bytes 262176 | tf_op jit(solution)/shard_map/ppermute | solution.py:398
  541.7 4.4 collective-permute-start.79
  548.2 7.2 %collective-permute-start.63 = (bf16[64,2048]{1,0:T(8,128)(2,1)}, bf16[64,2048]{1,0:T(8,128)(2,1)}, u32[]{:S(2)}, u32[]{:S(2)}) collective-permute-start(bf16[64,2048]{1,0:T(8,128)(2,1)} %get-tuple-element.104), channel_id=1, source_target_pairs={{0,8},{8,16},{16,24},{24,0},{1,9},{9,17},{17,25},{25,1},{2,10},{10... | collective-permute-start | bytes 786440 | tf_op jit(solution)/shard_map/ppermute | solution.py:398
  560.4 2.8 collective-permute-start.65
  563.3 5.5 collective-permute-done.78
  572.3 2.9 copy.124
  576.2 5.0 collective-permute-done.64
  588.9 13.8 %collective-permute-start.53 = (bf16[64,1536]{1,0:T(8,128)(2,1)S(1)}, bf16[64,1536]{1,0:T(8,128)(2,1)}, u32[]{:S(2)}, u32[]{:S(2)}) collective-permute-start(bf16[64,1536]{1,0:T(8,128)(2,1)S(1)} %get-tuple-element.184), channel_id=1, source_target_pairs={{0,8},{8,16},{16,24},{24,0},{1,9},{9,17},{17,25},{25,1},{2,10},{10... | collective-permute-start | bytes 589832 | tf_op jit(solution)/shard_map/ppermute | solution.py:398
  602.8 3.4 collective-permute-start.54
  608.5 3.0 copy.123
  613.0 6.6 collective-permute-done.54
  622.5 4.7 collective-permute-start.56
  627.9 2.4 collective-permute-start.58
  633.2 3.2 collective-permute-done.44
  638.4 10.8 %collective-permute-done.46 = bf16[256,1024]{1,0:T(8,128)(2,1)S(1)} collective-permute-done((bf16[256,1024]{1,0:T(8,128)(2,1)S(1)}, bf16[256,1024]{1,0:T(8,128)(2,1)S(1)}, u32[]{:S(2)}, u32[]{:S(2)}) %collective-permute-start.46) | collective-permute-done | bytes 524320 | tf_op jit(solution)/shard_map/ppermute | solution.py:394
  654.0 2.7 reshape.330
  (479 shorter events, 224.2 us)
Async XLA Ops:
  3.1 27.6 %collective-permute-start = (bf16[256,1024]{0,1:T(8,128)(2,1)}, bf16[256,1024]{0,1:T(8,128)(2,1)}, u32[]{:S(2)}, u32[]{:S(2)}) collective-permute-start(bf16[256,1024]{0,1:T(8,128)(2,1)} %bitcast), channel_id=1, source_target_pairs={{0,0},{1,16},{2,2},{3,18},{4,4},{5,20},{6,6},{7,22},{8,8},{9,24},{... | collective-permute-start | bytes 1572872 | tf_op jit(solution)/shard_map/ppermute | solution.py:478
  9.4 21.2 %collective-permute-start.1 = (bf16[256,1024]{0,1:T(8,128)(2,1)}, bf16[256,1024]{0,1:T(8,128)(2,1)}, u32[]{:S(2)}, u32[]{:S(2)}) collective-permute-start(bf16[256,1024]{0,1:T(8,128)(2,1)} %bitcast.1), channel_id=1, source_target_pairs={{0,8},{1,24},{2,10},{3,26},{4,12},{5,28},{6,14},{7,30},{8,0},{9,16... | collective-permute-start | bytes 1572872 | tf_op jit(solution)/shard_map/ppermute | solution.py:478
  13.5 19.9 %collective-permute-start.13 = (bf16[256,1024]{0,1:T(8,128)(2,1)}, bf16[256,1024]{0,1:T(8,128)(2,1)}, u32[]{:S(2)}, u32[]{:S(2)}) collective-permute-start(bf16[256,1024]{0,1:T(8,128)(2,1)} %bitcast.28), channel_id=1, source_target_pairs={{0,0},{1,16},{2,2},{3,18},{4,4},{5,20},{6,6},{7,22},{8,8},{9,24},{... | collective-permute-start | bytes 1572872 | tf_op jit(solution)/shard_map/ppermute | solution.py:478
  19.9 16.5 %collective-permute-start.14 = (bf16[256,1024]{0,1:T(8,128)(2,1)}, bf16[256,1024]{0,1:T(8,128)(2,1)}, u32[]{:S(2)}, u32[]{:S(2)}) collective-permute-start(bf16[256,1024]{0,1:T(8,128)(2,1)} %bitcast.29), channel_id=1, source_target_pairs={{0,8},{1,24},{2,10},{3,26},{4,12},{5,28},{6,14},{7,30},{8,0},{9,16... | collective-permute-start | bytes 1572872 | tf_op jit(solution)/shard_map/ppermute | solution.py:478
  30.6 41.3 %collective-permute-start.3 = (bf16[128,6144]{1,0:T(8,128)(2,1)}, bf16[128,6144]{1,0:T(8,128)(2,1)}, u32[]{:S(2)}, u32[]{:S(2)}) collective-permute-start(bf16[128,6144]{1,0:T(8,128)(2,1)} %pad_maximum_fusion.2), channel_id=1, source_target_pairs={{0,1},{1,0},{2,3},{3,2},{4,5},{5,4},{6,7},{7,6},{8,9},{9,8},{10,11... | collective-permute-start | bytes 4718600 | tf_op jit(solution)/shard_map/ppermute | solution.py:391
  33.0 34.2 %collective-permute-start.2 = (bf16[512,1024]{0,1:T(8,128)(2,1)}, bf16[512,1024]{0,1:T(8,128)(2,1)}, u32[]{:S(2)}, u32[]{:S(2)}) collective-permute-start(bf16[512,1024]{0,1:T(8,128)(2,1)} %pad_maximum_fusion.4), channel_id=1, source_target_pairs={{0,1},{1,0},{2,3},{3,2},{4,5},{5,4},{6,7},{7,6},{8,9},{9,8},{10,11... | collective-permute-start | bytes 3145736 | tf_op jit(solution)/shard_map/ppermute | solution.py:391
  38.7 31.5 %collective-permute-start.15 = (bf16[512,1024]{0,1:T(8,128)(2,1)}, bf16[512,1024]{0,1:T(8,128)(2,1)}, u32[]{:S(2)}, u32[]{:S(2)}) collective-permute-start(bf16[512,1024]{0,1:T(8,128)(2,1)} %pad_maximum_fusion.5), channel_id=1, source_target_pairs={{0,1},{1,0},{2,3},{3,2},{4,5},{5,4},{6,7},{7,6},{8,9},{9,8},{10,11... | collective-permute-start | bytes 3145736 | tf_op jit(solution)/shard_map/ppermute | solution.py:391
  77.3 19.8 %collective-permute-start.4 = (bf16[256,1536]{1,0:T(8,128)(2,1)}, bf16[256,1536]{1,0:T(8,128)(2,1)}, u32[]{:S(2)}, u32[]{:S(2)}) collective-permute-start(bf16[256,1536]{1,0:T(8,128)(2,1)} %get-tuple-element.110), channel_id=1, source_target_pairs={{0,2},{1,3},{2,0},{3,1},{4,6},{5,7},{6,4},{7,5},{8,10},{9,11},{10,... | collective-permute-start | bytes 2359304 | tf_op jit(solution)/shard_map/ppermute | solution.py:394
  78.8 19.5 %collective-permute-start.5 = (bf16[256,1536]{1,0:T(8,128)(2,1)}, bf16[256,1536]{1,0:T(8,128)(2,1)}, u32[]{:S(2)}, u32[]{:S(2)}) collective-permute-start(bf16[256,1536]{1,0:T(8,128)(2,1)} %get-tuple-element.110), channel_id=1, source_target_pairs={{0,4},{1,5},{2,6},{3,7},{4,0},{5,1},{6,2},{7,3},{8,12},{9,13},{10,... | collective-permute-start | bytes 2359304 | tf_op jit(solution)/shard_map/ppermute | solution.py:394
  101.3 15.1 %collective-permute-start.6 = (bf16[128,1536]{1,0:T(8,128)(2,1)S(1)}, bf16[128,1536]{1,0:T(8,128)(2,1)S(1)}, u32[]{:S(2)}, u32[]{:S(2)}) collective-permute-start(bf16[128,1536]{1,0:T(8,128)(2,1)S(1)} %slice.362), channel_id=1, source_target_pairs={{0,4},{1,5},{2,6},{3,7},{4,0},{5,1},{6,2},{7,3},{8,12},{9,13},{10,... | collective-permute-start | bytes 1179656 | tf_op jit(solution)/shard_map/ppermute | solution.py:394
  102.9 15.1 %collective-permute-start.7 = (bf16[128,1536]{1,0:T(8,128)(2,1)S(1)}, bf16[128,1536]{1,0:T(8,128)(2,1)S(1)}, u32[]{:S(2)}, u32[]{:S(2)}) collective-permute-start(bf16[128,1536]{1,0:T(8,128)(2,1)S(1)} %slice.363), channel_id=1, source_target_pairs={{0,2},{1,3},{2,0},{3,1},{4,6},{5,7},{6,4},{7,5},{8,10},{9,11},{10,... | collective-permute-start | bytes 1179656 | tf_op jit(solution)/shard_map/ppermute | solution.py:394
  110.5 40.2 %collective-permute-start.16 = (bf16[256,2048]{1,0:T(8,128)(2,1)S(1)}, bf16[256,2048]{1,0:T(8,128)(2,1)S(1)}, u32[]{:S(2)}, u32[]{:S(2)}) collective-permute-start(bf16[256,2048]{1,0:T(8,128)(2,1)S(1)} %get-tuple-element.36), channel_id=1, source_target_pairs={{0,2},{1,3},{2,0},{3,1},{4,6},{5,7},{6,4},{7,5},{8,10},{9,11},{10,... | collective-permute-start | bytes 3145736 | tf_op jit(solution)/shard_map/ppermute | solution.py:394
  111.0 39.7 %collective-permute-start.17 = (bf16[256,2048]{1,0:T(8,128)(2,1)S(1)}, bf16[256,2048]{1,0:T(8,128)(2,1)S(1)}, u32[]{:S(2)}, u32[]{:S(2)}) collective-permute-start(bf16[256,2048]{1,0:T(8,128)(2,1)S(1)} %get-tuple-element.36), channel_id=1, source_target_pairs={{0,4},{1,5},{2,6},{3,7},{4,0},{5,1},{6,2},{7,3},{8,12},{9,13},{10,... | collective-permute-start | bytes 3145736 | tf_op jit(solution)/shard_map/ppermute | solution.py:394
  112.5 34.8 %collective-permute-start.10 = (bf16[128,512]{1,0:T(8,128)(2,1)S(1)}, bf16[128,512]{1,0:T(8,128)(2,1)S(1)}, u32[]{:S(2)}, u32[]{:S(2)}) collective-permute-start(bf16[128,512]{1,0:T(8,128)(2,1)S(1)} %slice.366), channel_id=1, source_target_pairs={{0,4},{1,5},{2,6},{3,7},{4,0},{5,1},{6,2},{7,3},{8,12},{9,13},{10,... | collective-permute-start | bytes 393224 | tf_op jit(solution)/shard_map/ppermute | solution.py:394
  116.5 30.8 %collective-permute-start.11 = (bf16[128,512]{1,0:T(8,128)(2,1)S(1)}, bf16[128,512]{1,0:T(8,128)(2,1)S(1)}, u32[]{:S(2)}, u32[]{:S(2)}) collective-permute-start(bf16[128,512]{1,0:T(8,128)(2,1)S(1)} %slice.367), channel_id=1, source_target_pairs={{0,2},{1,3},{2,0},{3,1},{4,6},{5,7},{6,4},{7,5},{8,10},{9,11},{10,... | collective-permute-start | bytes 393224 | tf_op jit(solution)/shard_map/ppermute | solution.py:394
  150.5 44.3 %collective-permute-start.12 = (bf16[1024,1024]{0,1:T(8,128)(2,1)S(1)}, bf16[1024,1024]{0,1:T(8,128)(2,1)S(1)}, u32[]{:S(2)}, u32[]{:S(2)}) collective-permute-start(bf16[1024,1024]{0,1:T(8,128)(2,1)S(1)} %convolution_convert_fusion.2), channel_id=1, source_target_pairs={{0,1},{1,0},{2,3},{3,2},{4,5},{5,4},{6,7},{7,6},{8,9},{9,8},{10,11... | collective-permute-start | bytes 6291464 | tf_op jit(solution)/shard_map/ppermute | solution.py:391
  150.6 37.1 %collective-permute-start.20 = (bf16[256,2048]{1,0:T(8,128)(2,1)S(1)}, bf16[256,2048]{1,0:T(8,128)(2,1)S(1)}, u32[]{:S(2)}, u32[]{:S(2)}) collective-permute-start(bf16[256,2048]{1,0:T(8,128)(2,1)S(1)} %get-tuple-element.37), channel_id=1, source_target_pairs={{0,2},{1,3},{2,0},{3,1},{4,6},{5,7},{6,4},{7,5},{8,10},{9,11},{10,... | collective-permute-start | bytes 3145736 | tf_op jit(solution)/shard_map/ppermute | solution.py:394
  151.2 39.0 %collective-permute-start.21 = (bf16[256,2048]{1,0:T(8,128)(2,1)S(1)}, bf16[256,2048]{1,0:T(8,128)(2,1)S(1)}, u32[]{:S(2)}, u32[]{:S(2)}) collective-permute-start(bf16[256,2048]{1,0:T(8,128)(2,1)S(1)} %get-tuple-element.37), channel_id=1, source_target_pairs={{0,4},{1,5},{2,6},{3,7},{4,0},{5,1},{6,2},{7,3},{8,12},{9,13},{10,... | collective-permute-start | bytes 3145736 | tf_op jit(solution)/shard_map/ppermute | solution.py:394
  153.4 34.2 %collective-permute-start.18 = (bf16[128,2048]{1,0:T(8,128)(2,1)S(1)}, bf16[128,2048]{1,0:T(8,128)(2,1)S(1)}, u32[]{:S(2)}, u32[]{:S(2)}) collective-permute-start(bf16[128,2048]{1,0:T(8,128)(2,1)S(1)} %slice.370), channel_id=1, source_target_pairs={{0,4},{1,5},{2,6},{3,7},{4,0},{5,1},{6,2},{7,3},{8,12},{9,13},{10,... | collective-permute-start | bytes 1572872 | tf_op jit(solution)/shard_map/ppermute | solution.py:394
  154.0 33.6 %collective-permute-start.19 = (bf16[128,2048]{1,0:T(8,128)(2,1)S(1)}, bf16[128,2048]{1,0:T(8,128)(2,1)S(1)}, u32[]{:S(2)}, u32[]{:S(2)}) collective-permute-start(bf16[128,2048]{1,0:T(8,128)(2,1)S(1)} %slice.371), channel_id=1, source_target_pairs={{0,2},{1,3},{2,0},{3,1},{4,6},{5,7},{6,4},{7,5},{8,10},{9,11},{10,... | collective-permute-start | bytes 1572872 | tf_op jit(solution)/shard_map/ppermute | solution.py:394
  188.7 16.8 %collective-permute-start.22 = (bf16[128,2048]{1,0:T(8,128)(2,1)}, bf16[128,2048]{1,0:T(8,128)(2,1)}, u32[]{:S(2)}, u32[]{:S(2)}) collective-permute-start(bf16[128,2048]{1,0:T(8,128)(2,1)} %slice.372), channel_id=1, source_target_pairs={{0,4},{1,5},{2,6},{3,7},{4,0},{5,1},{6,2},{7,3},{8,12},{9,13},{10,... | collective-permute-start | bytes 1572872 | tf_op jit(solution)/shard_map/ppermute | solution.py:394
  191.0 14.4 %collective-permute-start.23 = (bf16[128,2048]{1,0:T(8,128)(2,1)}, bf16[128,2048]{1,0:T(8,128)(2,1)}, u32[]{:S(2)}, u32[]{:S(2)}) collective-permute-start(bf16[128,2048]{1,0:T(8,128)(2,1)} %slice.373), channel_id=1, source_target_pairs={{0,2},{1,3},{2,0},{3,1},{4,6},{5,7},{6,4},{7,5},{8,10},{9,11},{10,... | collective-permute-start | bytes 1572872 | tf_op jit(solution)/shard_map/ppermute | solution.py:394
  250.7 12.9 %collective-permute-start.28 = (bf16[128,2048]{1,0:T(8,128)(2,1)}, bf16[128,2048]{1,0:T(8,128)(2,1)}, u32[]{:S(2)}, u32[]{:S(2)}) collective-permute-start(bf16[128,2048]{1,0:T(8,128)(2,1)} %get-tuple-element.124), channel_id=1, source_target_pairs={{0,4},{1,5},{2,6},{3,7},{4,0},{5,1},{6,2},{7,3},{8,12},{9,13},{10,... | collective-permute-start | bytes 1572872 | tf_op jit(solution)/shard_map/ppermute | solution.py:394
  254.8 42.5 %collective-permute-start.27 = (bf16[1024,1024]{0,1:T(8,128)(2,1)S(1)}, bf16[1024,1024]{0,1:T(8,128)(2,1)}, u32[]{:S(2)}, u32[]{:S(2)}) collective-permute-start(bf16[1024,1024]{0,1:T(8,128)(2,1)S(1)} %copy.105), channel_id=1, source_target_pairs={{0,1},{1,0},{2,3},{3,2},{4,5},{5,4},{6,7},{7,6},{8,9},{9,8},{10,11... | collective-permute-start | bytes 6291464 | tf_op jit(solution)/shard_map/ppermute | solution.py:391
  261.1 24.7 %collective-permute-start.24 = (bf16[512,1024]{0,1:T(8,128)(2,1)}, bf16[512,1024]{0,1:T(8,128)(2,1)}, u32[]{:S(2)}, u32[]{:S(2)}) collective-permute-start(bf16[512,1024]{0,1:T(8,128)(2,1)} %constant_dynamic-slice_fusion.4), channel_id=1, source_target_pairs={{0,1},{1,0},{2,3},{3,2},{4,5},{5,4},{6,7},{7,6},{8,9},{9,8},{10,11... | collective-permute-start | bytes 3145736 | tf_op jit(solution)/shard_map/ppermute | solution.py:391
  267.2 23.6 %collective-permute-start.31 = (bf16[256,2048]{1,0:T(8,128)(2,1)}, bf16[256,2048]{1,0:T(8,128)(2,1)}, u32[]{:S(2)}, u32[]{:S(2)}) collective-permute-start(bf16[256,2048]{1,0:T(8,128)(2,1)} %pad_maximum_fusion.8), channel_id=1, source_target_pairs={{0,4},{1,5},{2,6},{3,7},{4,0},{5,1},{6,2},{7,3},{8,12},{9,13},{10,... | collective-permute-start | bytes 3145736 | tf_op jit(solution)/shard_map/ppermute | solution.py:394
  269.5 22.7 %collective-permute-start.29 = (bf16[256,2048]{1,0:T(8,128)(2,1)}, bf16[256,2048]{1,0:T(8,128)(2,1)}, u32[]{:S(2)}, u32[]{:S(2)}) collective-permute-start(bf16[256,2048]{1,0:T(8,128)(2,1)} %pad_maximum_fusion.7), channel_id=1, source_target_pairs={{0,2},{1,3},{2,0},{3,1},{4,6},{5,7},{6,4},{7,5},{8,10},{9,11},{10,... | collective-permute-start | bytes 3145736 | tf_op jit(solution)/shard_map/ppermute | solution.py:394
  295.1 68.7 %collective-permute-start.32 = (bf16[128,2048]{1,0:T(8,128)(2,1)}, bf16[128,2048]{1,0:T(8,128)(2,1)}, u32[]{:S(2)}, u32[]{:S(2)}) collective-permute-start(bf16[128,2048]{1,0:T(8,128)(2,1)} %get-tuple-element.118), channel_id=1, source_target_pairs={{0,4},{1,5},{2,6},{3,7},{4,0},{5,1},{6,2},{7,3},{8,12},{9,13},{10,... | collective-permute-start | bytes 1572872 | tf_op jit(solution)/shard_map/ppermute | solution.py:394
  296.2 67.6 %collective-permute-start.34 = (bf16[128,2048]{1,0:T(8,128)(2,1)}, bf16[128,2048]{1,0:T(8,128)(2,1)}, u32[]{:S(2)}, u32[]{:S(2)}) collective-permute-start(bf16[128,2048]{1,0:T(8,128)(2,1)} %get-tuple-element.117), channel_id=1, source_target_pairs={{0,2},{1,3},{2,0},{3,1},{4,6},{5,7},{6,4},{7,5},{8,10},{9,11},{10,... | collective-permute-start | bytes 1572872 | tf_op jit(solution)/shard_map/ppermute | solution.py:394
  352.0 13.8 %collective-permute-start.80 = (f32[8,33]{1,0:T(8,128)S(1)}, f32[8,33]{1,0:T(8,128)S(1)}, u32[]{:S(2)}, u32[]{:S(2)}) collective-permute-start(f32[8,33]{1,0:T(8,128)S(1)} %pad_maximum_fusion.23), channel_id=1, source_target_pairs={{0,2},{1,3},{2,0},{3,1},{4,6},{5,7},{6,4},{7,5},{8,10},{9,11},{10,... | collective-permute-start | bytes 3176 | tf_op jit(solution)/shard_map/ppermute | solution.py:394
  376.2 20.5 %collective-permute-start.35 = (bf16[256,2048]{1,0:T(8,128)(2,1)S(1)}, bf16[256,2048]{1,0:T(8,128)(2,1)S(1)}, u32[]{:S(2)}, u32[]{:S(2)}) collective-permute-start(bf16[256,2048]{1,0:T(8,128)(2,1)S(1)} %pad_maximum_fusion.10), channel_id=1, source_target_pairs={{0,4},{1,5},{2,6},{3,7},{4,0},{5,1},{6,2},{7,3},{8,12},{9,13},{10,... | collective-permute-start | bytes 3145736 | tf_op jit(solution)/shard_map/ppermute | solution.py:394
  383.2 19.6 %collective-permute-start.33 = (bf16[256,2048]{1,0:T(8,128)(2,1)}, bf16[256,2048]{1,0:T(8,128)(2,1)}, u32[]{:S(2)}, u32[]{:S(2)}) collective-permute-start(bf16[256,2048]{1,0:T(8,128)(2,1)} %pad_maximum_fusion.9), channel_id=1, source_target_pairs={{0,2},{1,3},{2,0},{3,1},{4,6},{5,7},{6,4},{7,5},{8,10},{9,11},{10,... | collective-permute-start | bytes 3145736 | tf_op jit(solution)/shard_map/ppermute | solution.py:394
  385.5 25.1 %collective-permute-start.49 = (bf16[512,1024]{0,1:T(8,128)(2,1)}, bf16[512,1024]{0,1:T(8,128)(2,1)S(1)}, u32[]{:S(2)}, u32[]{:S(2)}) collective-permute-start(bf16[512,1024]{0,1:T(8,128)(2,1)} %dynamic-slice_convert_fusion), channel_id=1, source_target_pairs={{0,1},{1,0},{2,3},{3,2},{4,5},{5,4},{6,7},{7,6},{8,9},{9,8},{10,11... | collective-permute-start | bytes 3145736 | tf_op jit(solution)/shard_map/ppermute | solution.py:391
  407.5 27.9 %collective-permute-start.73 = (bf16[128,2048]{1,0:T(8,128)(2,1)}, bf16[128,2048]{1,0:T(8,128)(2,1)}, u32[]{:S(2)}, u32[]{:S(2)}) collective-permute-start(bf16[128,2048]{1,0:T(8,128)(2,1)} %dynamic-slice_bitcast_fusion.12), channel_id=1, source_target_pairs={{0,1},{1,0},{2,3},{3,2},{4,5},{5,4},{6,7},{7,6},{8,9},{9,8},{10,11... | collective-permute-start | bytes 1572872 | tf_op jit(solution)/shard_map/ppermute | solution.py:391
  410.6 27.8 %collective-permute-start.59 = (bf16[128,2048]{1,0:T(8,128)(2,1)}, bf16[128,2048]{1,0:T(8,128)(2,1)}, u32[]{:S(2)}, u32[]{:S(2)}) collective-permute-start(bf16[128,2048]{1,0:T(8,128)(2,1)} %dynamic-slice_bitcast_fusion.13), channel_id=1, source_target_pairs={{0,1},{1,0},{2,3},{3,2},{4,5},{5,4},{6,7},{7,6},{8,9},{9,8},{10,11... | collective-permute-start | bytes 1572872 | tf_op jit(solution)/shard_map/ppermute | solution.py:391
  414.0 15.7 %collective-permute-start.39 = (bf16[256,512]{1,0:T(8,128)(2,1)S(1)}, bf16[256,512]{1,0:T(8,128)(2,1)}, u32[]{:S(2)}, u32[]{:S(2)}) collective-permute-start(bf16[256,512]{1,0:T(8,128)(2,1)S(1)} %pad_maximum_fusion.20), channel_id=1, source_target_pairs={{0,4},{1,5},{2,6},{3,7},{4,0},{5,1},{6,2},{7,3},{8,12},{9,13},{10,... | collective-permute-start | bytes 786440 | tf_op jit(solution)/shard_map/ppermute | solution.py:394
  416.2 13.9 %collective-permute-start.37 = (bf16[256,512]{1,0:T(8,128)(2,1)}, bf16[256,512]{1,0:T(8,128)(2,1)}, u32[]{:S(2)}, u32[]{:S(2)}) collective-permute-start(bf16[256,512]{1,0:T(8,128)(2,1)} %pad_maximum_fusion.19), channel_id=1, source_target_pairs={{0,2},{1,3},{2,0},{3,1},{4,6},{5,7},{6,4},{7,5},{8,10},{9,11},{10,... | collective-permute-start | bytes 786440 | tf_op jit(solution)/shard_map/ppermute | solution.py:394
  424.8 20.2 %collective-permute-start.50 = (bf16[256,1024]{0,1:T(8,128)(2,1)}, bf16[256,1024]{0,1:T(8,128)(2,1)S(1)}, u32[]{:S(2)}, u32[]{:S(2)}) collective-permute-start(bf16[256,1024]{0,1:T(8,128)(2,1)} %copy.110), channel_id=1, source_target_pairs={{0,0},{16,1},{2,2},{18,3},{4,4},{20,5},{6,6},{22,7},{8,8},{24,9},{... | collective-permute-start | bytes 1572872 | tf_op jit(solution)/shard_map/ppermute | solution.py:478
  429.7 18.5 %collective-permute-start.51 = (bf16[256,1024]{0,1:T(8,128)(2,1)}, bf16[256,1024]{0,1:T(8,128)(2,1)S(1)}, u32[]{:S(2)}, u32[]{:S(2)}) collective-permute-start(bf16[256,1024]{0,1:T(8,128)(2,1)} %copy.112), channel_id=1, source_target_pairs={{8,0},{24,1},{10,2},{26,3},{12,4},{28,5},{14,6},{30,7},{0,8},{16,9... | collective-permute-start | bytes 1572872 | tf_op jit(solution)/shard_map/ppermute | solution.py:478
  430.1 18.3 %collective-permute-start.25 = (bf16[256,1024]{0,1:T(8,128)(2,1)}, bf16[256,1024]{0,1:T(8,128)(2,1)S(1)}, u32[]{:S(2)}, u32[]{:S(2)}) collective-permute-start(bf16[256,1024]{0,1:T(8,128)(2,1)} %copy.101), channel_id=1, source_target_pairs={{0,0},{16,1},{2,2},{18,3},{4,4},{20,5},{6,6},{22,7},{8,8},{24,9},{... | collective-permute-start | bytes 1572872 | tf_op jit(solution)/shard_map/ppermute | solution.py:478
  435.4 34.5 %collective-permute-start.26 = (bf16[256,1024]{0,1:T(8,128)(2,1)S(1)}, bf16[256,1024]{0,1:T(8,128)(2,1)S(1)}, u32[]{:S(2)}, u32[]{:S(2)}) collective-permute-start(bf16[256,1024]{0,1:T(8,128)(2,1)S(1)} %copy.103), channel_id=1, source_target_pairs={{8,0},{24,1},{10,2},{26,3},{12,4},{28,5},{14,6},{30,7},{0,8},{16,9... | collective-permute-start | bytes 1572872 | tf_op jit(solution)/shard_map/ppermute | solution.py:478
  443.3 104.8 %collective-permute-start.40 = (bf16[128,1536]{1,0:T(8,128)(2,1)}, bf16[128,1536]{1,0:T(8,128)(2,1)}, u32[]{:S(2)}, u32[]{:S(2)}) collective-permute-start(bf16[128,1536]{1,0:T(8,128)(2,1)} %get-tuple-element.130), channel_id=1, source_target_pairs={{0,4},{1,5},{2,6},{3,7},{4,0},{5,1},{6,2},{7,3},{8,12},{9,13},{10,... | collective-permute-start | bytes 1179656 | tf_op jit(solution)/shard_map/ppermute | solution.py:394
  444.9 110.5 %collective-permute-start.42 = (bf16[128,1536]{1,0:T(8,128)(2,1)}, bf16[128,1536]{1,0:T(8,128)(2,1)}, u32[]{:S(2)}, u32[]{:S(2)}) collective-permute-start(bf16[128,1536]{1,0:T(8,128)(2,1)} %get-tuple-element.129), channel_id=1, source_target_pairs={{0,2},{1,3},{2,0},{3,1},{4,6},{5,7},{6,4},{7,5},{8,10},{9,11},{10,... | collective-permute-start | bytes 1179656 | tf_op jit(solution)/shard_map/ppermute | solution.py:394
  448.3 22.8 %collective-permute-start.67 = (bf16[64,512]{1,0:T(8,128)(2,1)S(1)}, bf16[64,512]{1,0:T(8,128)(2,1)S(1)}, u32[]{:S(2)}, u32[]{:S(2)}) collective-permute-start(bf16[64,512]{1,0:T(8,128)(2,1)S(1)} %get-tuple-element.191), channel_id=1, source_target_pairs={{0,8},{8,16},{16,24},{24,0},{1,9},{9,17},{17,25},{25,1},{2,10},{10... | collective-permute-start | bytes 196616 | tf_op jit(solution)/shard_map/ppermute | solution.py:398
  448.3 33.2 %collective-permute-start.68 = (bf16[64,512]{1,0:T(8,128)(2,1)S(1)}, bf16[64,512]{1,0:T(8,128)(2,1)S(1)}, u32[]{:S(2)}, u32[]{:S(2)}) collective-permute-start(bf16[64,512]{1,0:T(8,128)(2,1)S(1)} %get-tuple-element.193), channel_id=1, source_target_pairs={{0,16},{8,24},{16,0},{24,8},{1,17},{9,25},{17,1},{25,9},{2,18},{10... | collective-permute-start | bytes 196616 | tf_op jit(solution)/shard_map/ppermute | solution.py:398
  471.1 44.2 %collective-permute-start.74 = (bf16[64,2048]{1,0:T(8,128)(2,1)}, bf16[64,2048]{1,0:T(8,128)(2,1)}, u32[]{:S(2)}, u32[]{:S(2)}) collective-permute-start(bf16[64,2048]{1,0:T(8,128)(2,1)} %get-tuple-element.152), channel_id=1, source_target_pairs={{0,8},{8,16},{16,24},{24,0},{1,9},{9,17},{17,25},{25,1},{2,10},{10... | collective-permute-start | bytes 786440 | tf_op jit(solution)/shard_map/ppermute | solution.py:398
  481.5 33.9 %collective-permute-start.75 = (bf16[64,2048]{1,0:T(8,128)(2,1)}, bf16[64,2048]{1,0:T(8,128)(2,1)}, u32[]{:S(2)}, u32[]{:S(2)}) collective-permute-start(bf16[64,2048]{1,0:T(8,128)(2,1)} %get-tuple-element.154), channel_id=1, source_target_pairs={{0,16},{8,24},{16,0},{24,8},{1,17},{9,25},{17,1},{25,9},{2,18},{10... | collective-permute-start | bytes 786440 | tf_op jit(solution)/shard_map/ppermute | solution.py:398
  515.4 26.3 %collective-permute-start.61 = (bf16[64,2048]{1,0:T(8,128)(2,1)S(1)}, bf16[64,2048]{1,0:T(8,128)(2,1)S(1)}, u32[]{:S(2)}, u32[]{:S(2)}) collective-permute-start(bf16[64,2048]{1,0:T(8,128)(2,1)S(1)} %copy-done.54), channel_id=1, source_target_pairs={{0,16},{8,24},{16,0},{24,8},{1,17},{9,25},{17,1},{25,9},{2,18},{10... | collective-permute-start | bytes 786440 | tf_op jit(solution)/shard_map/ppermute | solution.py:398
  519.3 22.5 %collective-permute-start.62 = (bf16[64,2048]{1,0:T(8,128)(2,1)S(1)}, bf16[64,2048]{1,0:T(8,128)(2,1)S(1)}, u32[]{:S(2)}, u32[]{:S(2)}) collective-permute-start(bf16[64,2048]{1,0:T(8,128)(2,1)S(1)} %copy-done.53), channel_id=1, source_target_pairs={{0,24},{8,0},{16,8},{24,16},{1,25},{9,1},{17,9},{25,17},{2,26},{10... | collective-permute-start | bytes 786440 | tf_op jit(solution)/shard_map/ppermute | solution.py:398
  526.5 33.9 %collective-permute-start.77 = (bf16[64,2048]{1,0:T(8,128)(2,1)S(1)}, bf16[64,2048]{1,0:T(8,128)(2,1)S(1)}, u32[]{:S(2)}, u32[]{:S(2)}) collective-permute-start(bf16[64,2048]{1,0:T(8,128)(2,1)S(1)} %get-tuple-element.100), channel_id=1, source_target_pairs={{0,8},{8,16},{16,24},{24,0},{1,9},{9,17},{17,25},{25,1},{2,10},{10... | collective-permute-start | bytes 786440 | tf_op jit(solution)/shard_map/ppermute | solution.py:398
  541.7 27.1 %collective-permute-start.78 = (bf16[64,2048]{1,0:T(8,128)(2,1)S(1)}, bf16[64,2048]{1,0:T(8,128)(2,1)S(1)}, u32[]{:S(2)}, u32[]{:S(2)}) collective-permute-start(bf16[64,2048]{1,0:T(8,128)(2,1)S(1)} %get-tuple-element.100), channel_id=1, source_target_pairs={{0,16},{8,24},{16,0},{24,8},{1,17},{9,25},{17,1},{25,9},{2,18},{10... | collective-permute-start | bytes 786440 | tf_op jit(solution)/shard_map/ppermute | solution.py:398
  541.7 28.0 %collective-permute-start.79 = (bf16[64,2048]{1,0:T(8,128)(2,1)S(1)}, bf16[64,2048]{1,0:T(8,128)(2,1)S(1)}, u32[]{:S(2)}, u32[]{:S(2)}) collective-permute-start(bf16[64,2048]{1,0:T(8,128)(2,1)S(1)} %get-tuple-element.100), channel_id=1, source_target_pairs={{0,24},{8,0},{16,8},{24,16},{1,25},{9,1},{17,9},{25,17},{2,26},{10... | collective-permute-start | bytes 786440 | tf_op jit(solution)/shard_map/ppermute | solution.py:398
  548.2 27.0 %collective-permute-start.63 = (bf16[64,2048]{1,0:T(8,128)(2,1)}, bf16[64,2048]{1,0:T(8,128)(2,1)}, u32[]{:S(2)}, u32[]{:S(2)}) collective-permute-start(bf16[64,2048]{1,0:T(8,128)(2,1)} %get-tuple-element.104), channel_id=1, source_target_pairs={{0,8},{8,16},{16,24},{24,0},{1,9},{9,17},{17,25},{25,1},{2,10},{10... | collective-permute-start | bytes 786440 | tf_op jit(solution)/shard_map/ppermute | solution.py:398
  555.4 25.8 %collective-permute-start.64 = (bf16[64,2048]{1,0:T(8,128)(2,1)}, bf16[64,2048]{1,0:T(8,128)(2,1)}, u32[]{:S(2)}, u32[]{:S(2)}) collective-permute-start(bf16[64,2048]{1,0:T(8,128)(2,1)} %get-tuple-element.104), channel_id=1, source_target_pairs={{0,16},{8,24},{16,0},{24,8},{1,17},{9,25},{17,1},{25,9},{2,18},{10... | collective-permute-start | bytes 786440 | tf_op jit(solution)/shard_map/ppermute | solution.py:398
  560.4 21.7 %collective-permute-start.65 = (bf16[64,2048]{1,0:T(8,128)(2,1)}, bf16[64,2048]{1,0:T(8,128)(2,1)S(1)}, u32[]{:S(2)}, u32[]{:S(2)}) collective-permute-start(bf16[64,2048]{1,0:T(8,128)(2,1)} %get-tuple-element.104), channel_id=1, source_target_pairs={{0,24},{8,0},{16,8},{24,16},{1,25},{9,1},{17,9},{25,17},{2,26},{10... | collective-permute-start | bytes 786440 | tf_op jit(solution)/shard_map/ppermute | solution.py:398
  568.8 13.4 %collective-permute-start.43 = (bf16[256,1536]{1,0:T(8,128)(2,1)}, bf16[256,1536]{1,0:T(8,128)(2,1)}, u32[]{:S(2)}, u32[]{:S(2)}) collective-permute-start(bf16[256,1536]{1,0:T(8,128)(2,1)} %pad_maximum_fusion.17), channel_id=1, source_target_pairs={{0,4},{1,5},{2,6},{3,7},{4,0},{5,1},{6,2},{7,3},{8,12},{9,13},{10,... | collective-permute-start | bytes 2359304 | tf_op jit(solution)/shard_map/ppermute | solution.py:394
  588.9 24.1 %collective-permute-start.53 = (bf16[64,1536]{1,0:T(8,128)(2,1)S(1)}, bf16[64,1536]{1,0:T(8,128)(2,1)}, u32[]{:S(2)}, u32[]{:S(2)}) collective-permute-start(bf16[64,1536]{1,0:T(8,128)(2,1)S(1)} %get-tuple-element.184), channel_id=1, source_target_pairs={{0,8},{8,16},{16,24},{24,0},{1,9},{9,17},{17,25},{25,1},{2,10},{10... | collective-permute-start | bytes 589832 | tf_op jit(solution)/shard_map/ppermute | solution.py:398
  602.8 16.9 %collective-permute-start.54 = (bf16[64,1536]{1,0:T(8,128)(2,1)S(1)}, bf16[64,1536]{1,0:T(8,128)(2,1)}, u32[]{:S(2)}, u32[]{:S(2)}) collective-permute-start(bf16[64,1536]{1,0:T(8,128)(2,1)S(1)} %get-tuple-element.186), channel_id=1, source_target_pairs={{0,16},{8,24},{16,0},{24,8},{1,17},{9,25},{17,1},{25,9},{2,18},{10... | collective-permute-start | bytes 589832 | tf_op jit(solution)/shard_map/ppermute | solution.py:398
  606.1 13.5 %collective-permute-start.55 = (bf16[64,1536]{1,0:T(8,128)(2,1)S(1)}, bf16[64,1536]{1,0:T(8,128)(2,1)}, u32[]{:S(2)}, u32[]{:S(2)}) collective-permute-start(bf16[64,1536]{1,0:T(8,128)(2,1)S(1)} %get-tuple-element.185), channel_id=1, source_target_pairs={{0,24},{8,0},{16,8},{24,16},{1,25},{9,1},{17,9},{25,17},{2,26},{10... | collective-permute-start | bytes 589832 | tf_op jit(solution)/shard_map/ppermute | solution.py:398
  611.5 24.9 %collective-permute-start.44 = (bf16[512,1024]{1,0:T(8,128)(2,1)S(1)}, bf16[512,1024]{1,0:T(8,128)(2,1)S(1)}, u32[]{:S(2)}, u32[]{:S(2)}) collective-permute-start(bf16[512,1024]{1,0:T(8,128)(2,1)S(1)} %bitcast.333), channel_id=1, source_target_pairs={{0,2},{1,3},{2,0},{3,1},{4,6},{5,7},{6,4},{7,5},{8,10},{9,11},{10,... | collective-permute-start | bytes 3145736 | tf_op jit(solution)/shard_map/ppermute | solution.py:394
  611.9 25.7 %collective-permute-start.45 = (bf16[512,1024]{1,0:T(8,128)(2,1)S(1)}, bf16[512,1024]{1,0:T(8,128)(2,1)S(1)}, u32[]{:S(2)}, u32[]{:S(2)}) collective-permute-start(bf16[512,1024]{1,0:T(8,128)(2,1)S(1)} %bitcast.334), channel_id=1, source_target_pairs={{0,4},{1,5},{2,6},{3,7},{4,0},{5,1},{6,2},{7,3},{8,12},{9,13},{10,... | collective-permute-start | bytes 3145736 | tf_op jit(solution)/shard_map/ppermute | solution.py:394
  627.8 24.7 %collective-permute-start.57 = (bf16[64,1536]{1,0:T(8,128)(2,1)S(1)}, bf16[64,1536]{1,0:T(8,128)(2,1)S(1)}, u32[]{:S(2)}, u32[]{:S(2)}) collective-permute-start(bf16[64,1536]{1,0:T(8,128)(2,1)S(1)} %get-tuple-element.106), channel_id=1, source_target_pairs={{0,16},{8,24},{16,0},{24,8},{1,17},{9,25},{17,1},{25,9},{2,18},{10... | collective-permute-start | bytes 589832 | tf_op jit(solution)/shard_map/ppermute | solution.py:398
  627.9 25.3 %collective-permute-start.58 = (bf16[64,1536]{1,0:T(8,128)(2,1)S(1)}, bf16[64,1536]{1,0:T(8,128)(2,1)S(1)}, u32[]{:S(2)}, u32[]{:S(2)}) collective-permute-start(bf16[64,1536]{1,0:T(8,128)(2,1)S(1)} %get-tuple-element.106), channel_id=1, source_target_pairs={{0,24},{8,0},{16,8},{24,16},{1,25},{9,1},{17,9},{25,17},{2,26},{10... | collective-permute-start | bytes 589832 | tf_op jit(solution)/shard_map/ppermute | solution.py:398
  652.6 14.9 %collective-permute-start.48 = (bf16[2,256,1024]{2,1,0:T(8,128)(2,1)}, bf16[2,256,1024]{2,1,0:T(8,128)(2,1)}, u32[]{:S(2)}, u32[]{:S(2)}) collective-permute-start(bf16[2,256,1024]{2,1,0:T(8,128)(2,1)} %pad_maximum_fusion.11), channel_id=1, source_target_pairs={{0,1},{1,0},{2,3},{3,2},{4,5},{5,4},{6,7},{7,6},{8,9},{9,8},{10,11... | collective-permute-start | bytes 3145736 | tf_op jit(solution)/shard_map/ppermute | solution.py:391
  (92 other events, 730.8 us)

commit v2 on v1

--- a/solution.py
+++ b/solution.py
@@ -286,68 +286,532 @@
     return values * cumulative, slope
 
 
+def block_copies(index_ref, offset, pieces, target, semaphores):
+    copies = []
+    for number, piece in enumerate(pieces):
+        rows = piece.shape[-2]
+        where = pl.ds(pl.multiple_of(index_ref[offset + number] * rows, rows), rows)
+        place = target.at[where, :] if len(piece.shape) == 2 else target.at[:, where, :]
+        copies.append(pltpu.make_async_copy(piece, place, semaphores.at[offset + number]))
+    return copies
+
+
+anywhere = pl.BlockSpec(memory_space=pl.ANY)
+
+
+def cost(flops, moved):
+    return pl.CostEstimate(flops=flops, bytes_accessed=moved, transcendentals=0)
+
+
+def side_kernel(
+    core_ref, q_ref, k_ref, v_ref, o_ref, e_ref, c_ref, first_ref, second_ref, *outs
+):
+    def scaled(block, gain_ref):
+        return (gain_ref[...] * block.astype(wide)).astype(low)
+
+    for side in (0, 1):
+        core = core_ref[0] if side == 0 else 1 - core_ref[0]
+        qkv_ref, out_ref, early_ref, late_ref = outs[4 * side : 4 * side + 4]
+        inner = out_ref.shape[1]
+        hidden = early_ref.shape[2]
+        columns = pl.ds(pl.multiple_of(core * inner, inner), inner)
+        for block, ref in enumerate((q_ref, k_ref, v_ref)):
+            qkv_ref[:, block * inner : (block + 1) * inner] = scaled(ref[:, columns], first_ref)
+        out_ref[...] = o_ref[:, columns]
+        for part, ref in enumerate((early_ref, late_ref)):
+            columns = pl.ds(pl.multiple_of((2 * core + part) * hidden, hidden), hidden)
+            ref[0] = scaled(e_ref[:, columns], second_ref)
+            ref[1] = c_ref[:, columns]
+
+
+def weight_sides(core, query, key, value, output, expand, contract, first_gain, second_gain):
+    rows, inner = query.shape
+    hidden = expand.shape[1] // 4
+    one_side = [
+        jax.ShapeDtypeStruct((rows, 3 * inner // 2), low),
+        jax.ShapeDtypeStruct((rows, inner // 2), low),
+        jax.ShapeDtypeStruct((2, rows, hidden), low),
+        jax.ShapeDtypeStruct((2, rows, hidden), low),
+    ]
+    vmem = pl.BlockSpec(memory_space=pltpu.VMEM)
+    outs = pl.pallas_call(
+        side_kernel,
+        in_specs=[pl.BlockSpec(memory_space=pltpu.SMEM)] + [vmem] * 8,
+        out_specs=[vmem] * 8,
+        out_shape=one_side * 2,
+        compiler_params=pltpu.CompilerParams(vmem_limit_bytes=32 << 20),
+        cost_estimate=cost(0, 7 << 20),
+        name="weight_sides",
+    )(
+        core,
+        query,
+        key,
+        value,
+        output,
+        expand,
+        contract,
+        first_gain.astype(wide)[:, None],
+        second_gain.astype(wide)[:, None],
+    )
+    return outs[:4], outs[4:]
+
+
+def token_kernel(place_ref, *refs, normed):
+    pieces = refs[:4]
+    plain_ref, first_ref, first_t_ref, semaphores = refs[4:]
+    copies = block_copies(place_ref, 0, pieces, plain_ref, semaphores)
+    for copy in copies:
+        copy.start()
+    for copy in copies:
+        copy.wait()
+    total = plain_ref.shape[0]
+    step = total // 4
+    for block in range(4):
+        rows = slice(block * step, (block + 1) * step)
+        values = plain_ref[rows, :].astype(wide)
+        if normed:
+            values = normalize(values)[0]
+        else:
+            position = block * step + lax.broadcasted_iota(jnp.int32, values.shape, 0)
+            values = jnp.where(position < place_ref[4], values, 0.0)
+        first_ref[rows, :] = values.astype(low)
+        first_t_ref[:, rows] = values.T.astype(low)
+
+
+def token_rows_of(places, pieces, normed):
+    total, width = 4 * pieces[0].shape[0], pieces[0].shape[1]
+    vmem = pl.BlockSpec(memory_space=pltpu.VMEM)
+    return pl.pallas_call(
+        functools.partial(token_kernel, normed=normed),
+        in_specs=[pl.BlockSpec(memory_space=pltpu.SMEM)] + [anywhere] * 4,
+        out_specs=[vmem] * 3,
+        out_shape=[
+            jax.ShapeDtypeStruct((total, width), low),
+            jax.ShapeDtypeStruct((total, width), low),
+            jax.ShapeDtypeStruct((width, total), low),
+        ],
+        scratch_shapes=[pltpu.SemaphoreType.DMA((4,))],
+        compiler_params=pltpu.CompilerParams(vmem_limit_bytes=40 << 20),
+        cost_estimate=cost(0, 12 << 20),
+        name="token_rows" if normed else "cotangent_rows",
+    )(places, *pieces)
+
+
+def rows_product_kernel(place_ref, rows_ref, *refs, count, across):
+    pieces = refs[:count]
+    out_ref, weight, semaphores = refs[count:]
+
+    @pl.when(pl.program_id(0) == 0)
+    def _():
+        copies = block_copies(place_ref, 0, pieces, weight, semaphores)
+        for copy in copies:
+            copy.start()
+        for copy in copies:
+            copy.wait()
+
+    out_ref[...] = dot(rows_ref[...], weight[...], 1, 1 if across else 0).astype(low)
+
+
+def rows_product(places, rows, pieces, across, name, step=256):
+    total, depth = rows.shape
+    count = len(pieces)
+    whole = (count * pieces[0].shape[0], pieces[0].shape[1])
+    width = whole[0] if across else whole[1]
+    return pl.pallas_call(
+        functools.partial(rows_product_kernel, count=count, across=across),
+        grid_spec=pltpu.PrefetchScalarGridSpec(
+            num_scalar_prefetch=1,
+            grid=(total // step,),
+            in_specs=[pl.BlockSpec((step, depth), lambda i, _: (i, 0))] + [anywhere] * count,
+            out_specs=pl.BlockSpec((step, width), lambda i, _: (i, 0)),
+            scratch_shapes=[pltpu.VMEM(whole, low), pltpu.SemaphoreType.DMA((count,))],
+        ),
+        out_shape=jax.ShapeDtypeStruct((total, width), low),
+        compiler_params=pltpu.CompilerParams(vmem_limit_bytes=40 << 20),
+        cost_estimate=cost(3 * total * whole[0] * whole[1], 8 << 20),
+        name=name,
+    )(places, rows, *pieces)
+
+
+def second_norm_kernel(token_ref, mine_ref, other_ref, hidden_ref, normed_ref, normed_t_ref):
+    attended = mine_ref[...].astype(wide) + other_ref[...].astype(wide)
+    hidden = token_ref[...].astype(wide) + attended
+    hidden_ref[...] = hidden
+    normed = normalize(hidden)[0]
+    normed_ref[...] = normed.astype(low)
+    normed_t_ref[...] = normed.T.astype(low)
+
+
+def second_norm(tokens, mine, other, step=256):
+    total, width = tokens.shape
+    block = pl.BlockSpec((step, width), lambda i: (i, 0))
+    return pl.pallas_call(
+        second_norm_kernel,
+        grid=(total // step,),
+        in_specs=[block] * 3,
+        out_specs=[block, block, pl.BlockSpec((width, step), lambda i: (0, i))],
+        out_shape=[
+            jax.ShapeDtypeStruct((total, width), wide),
+            jax.ShapeDtypeStruct((total, width), low),
+            jax.ShapeDtypeStruct((width, total), low),
+        ],
+        compiler_params=pltpu.CompilerParams(vmem_limit_bytes=40 << 20),
+        cost_estimate=cost(0, 16 << 20),
+        name="second_norm",
+    )(tokens, mine, other)
+
+
 def feed_forward_kernel(
-    normed_ref,
-    normed_t_ref,
-    grad_ref,
-    grad_t_ref,
-    expand_ref,
-    contract_ref,
-    mixed_ref,
-    normed_grad_ref,
-    expand_grad_ref,
-    contract_grad_ref,
-    mixed_sum,
-    normed_sum,
+    place_ref, normed_ref, normed_t_ref, grad_ref, grad_t_ref, *refs, count, first
 ):
+    pieces = refs[:count]
+    refs = refs[count:]
+    if first:
+        mixed_sum, normed_sum, terms_ref, upper_ref, lower_ref, weight, semaphores = refs
+        before = ()
+    else:
+        before = refs[:2]
+        own_ref, other_ref, normed_grad_ref, terms_ref, upper_ref, lower_ref = refs[2:8]
+        weight, semaphores, mixed_sum, normed_sum = refs[8:]
     index = pl.program_id(0)
-    pre_act = dot(normed_ref[...], expand_ref[...], 1, 0)
-    act_grad = dot(grad_ref[...], contract_ref[...], 1, 0).astype(low).astype(wide)
+    step = terms_ref.shape[2]
+
+    @pl.when(index == 0)
+    def _():
+        copies = block_copies(place_ref, 0, pieces, weight, semaphores)
+        for number, (source, target) in enumerate(zip(before, (mixed_sum, normed_sum))):
+            copies.append(
+                pltpu.make_async_copy(source, target, semaphores.at[count + number])
+            )
+        for copy in copies:
+            copy.start()
+        for copy in copies:
+            copy.wait()
+
+    columns = pl.ds(pl.multiple_of(index * step, step), step)
+    expand = weight[0, :, columns]
+    contract = weight[1, :, columns]
+    pre_act = dot(normed_ref[...], expand, 1, 0)
+    act_grad = dot(grad_ref[...], contract, 1, 0).astype(low).astype(wide)
     activated, slope = gelu_and_slope(pre_act)
     activated = activated.astype(low)
     pre_grad = (act_grad * slope).astype(low)
-    contract_grad_ref[...] = dot(grad_t_ref[...], activated, 1, 0).astype(low)
-    expand_grad_ref[...] = dot(normed_t_ref[...], pre_grad, 1, 0).astype(low)
-    mixed = dot(activated, contract_ref[...], 1, 1)
-    normed_grad = dot(pre_grad, expand_ref[...], 1, 1)
+    terms_ref[1] = dot(grad_t_ref[...], activated, 1, 0).astype(low)
+    terms_ref[0] = dot(normed_t_ref[...], pre_grad, 1, 0).astype(low)
+    half = upper_ref.shape[1]
+    corner = pl.multiple_of(place_ref[count] * (2 * half), 2 * half)
+    for part in (0, 1):
+        upper_ref[part] = terms_ref[part, pl.ds(corner, half), :]
+        lower_ref[part] = terms_ref[part, pl.ds(corner + half, half), :]
+    mixed = dot(activated, contract, 1, 1)
+    normed_grad = dot(pre_grad, expand, 1, 1)
+    if first:
+
+        @pl.when(index == 0)
+        def _():
+            mixed_sum[...] = mixed
+            normed_sum[...] = normed_grad
+
+        @pl.when(index > 0)
+        def _():
+            mixed_sum[...] += mixed
+            normed_sum[...] += normed_grad
+
+    else:
+        mixed_sum[...] += mixed
+        normed_sum[...] += normed_grad
+
+        @pl.when(index == pl.num_programs(0) - 1)
+        def _():
+            rows = own_ref.shape[0]
+            core = place_ref[count + 1]
+            own = pl.multiple_of(core * rows, rows)
+            away = pl.multiple_of((1 - core) * rows, rows)
+            own_ref[...] = mixed_sum[pl.ds(own, rows), :].astype(low)
+            other_ref[...] = mixed_sum[pl.ds(away, rows), :].astype(low)
+            normed_grad_ref[...] = normed_sum[...].astype(low)
+
+
+def feed_forward(places, normed, normed_t, grad, grad_t, pieces, chips, before=None, step=512):
+    rows, width = normed.shape
+    count = len(pieces)
+    hidden = pieces[0].shape[2]
+    half = width // chips // 2
+    first = before is None
+
+    def fixed(shape):
+        return pl.BlockSpec(shape, lambda i, _: (0,) * len(shape), pipeline_mode=pl.Buffered(1))
+
+    def moving(leading):
+        return pl.BlockSpec((2, leading, step), lambda i, _: (0, 0, i))
+
+    whole = fixed((rows, width))
+    term_specs = [moving(width), moving(half), moving(half)]
+    term_shapes = [jax.ShapeDtypeStruct((2, n, hidden), low) for n in (width, half, half)]
+    scratch = [
+        pltpu.VMEM((2, width, hidden), low),
+        pltpu.SemaphoreType.DMA((count + 2,)),
+    ]
+    if first:
+        out_specs = [whole, whole] + term_specs
+        out_shape = [jax.ShapeDtypeStruct((rows, width), wide)] * 2 + term_shapes
+    else:
+        part = fixed((rows // 2, width))
+        out_specs = [part, part, whole] + term_specs
+        out_shape = [
+            jax.ShapeDtypeStruct((rows // 2, width), low),
+            jax.ShapeDtypeStruct((rows // 2, width), low),
+            jax.ShapeDtypeStruct((rows, width), low),
+        ] + term_shapes
+        scratch += [pltpu.VMEM((rows, width), wide)] * 2
+    return pl.pallas_call(
+        functools.partial(feed_forward_kernel, count=count, first=first),
+        grid_spec=pltpu.PrefetchScalarGridSpec(
+            num_scalar_prefetch=1,
+            grid=(hidden // step,),
+            in_specs=[whole, fixed((width, rows))] * 2
+            + [anywhere] * (count + (0 if first else 2)),
+            out_specs=out_specs,
+            scratch_shapes=scratch,
+        ),
+        out_shape=out_shape,
+        compiler_params=pltpu.CompilerParams(vmem_limit_bytes=58 << 20),
+        cost_estimate=cost(20 * rows * width * hidden, 40 << 20),
+        name="feed_forward",
+    )(places, normed, normed_t, grad, grad_t, *pieces, *(() if first else before))
+
+
+def hidden_back_kernel(place_ref, mine_ref, other_ref, hidden_ref, grad_ref, *refs, count):
+    pieces = refs[:count]
+    hidden_grad_ref, low_ref, low_t_ref, context_grad_ref, weight, semaphores = refs[count:]
+
+    @pl.when(pl.program_id(0) == 0)
+    def _():
+        copies = block_copies(place_ref, 0, pieces, weight, semaphores)
+        for copy in copies:
+            copy.start()
+        for copy in copies:
+            copy.wait()
+
+    upstream = mine_ref[...].astype(wide) + other_ref[...].astype(wide)
+    hidden = hidden_ref[...]
+    scale = normalize(hidden)[1]
+    hidden_grad = grad_ref[...].astype(wide) + normalize_back(hidden, scale, upstream)
+    hidden_grad_ref[...] = hidden_grad
+    attended_grad = hidden_grad.astype(low)
+    low_ref[...] = attended_grad
+    low_t_ref[...] = hidden_grad.T.astype(low)
+    context_grad_ref[...] = dot(attended_grad, weight[...], 1, 0).astype(low)
+
+
+def hidden_back(places, mine, other, hidden, grad, pieces, step=256):
+    total, width = hidden.shape
+    count = len(pieces)
+    inner = pieces[0].shape[1]
+    block = pl.BlockSpec((step, width), lambda i, _: (i, 0))
+    return pl.pallas_call(
+        functools.partial(hidden_back_kernel, count=count),
+        grid_spec=pltpu.PrefetchScalarGridSpec(
+            num_scalar_prefetch=1,
+            grid=(total // step,),
+            in_specs=[block] * 4 + [anywhere] * count,
+            out_specs=[
+                block,
+                block,
+                pl.BlockSpec((width, step), lambda i, _: (0, i)),
+                pl.BlockSpec((step, inner), lambda i, _: (i, 0)),
+            ],
+            scratch_shapes=[pltpu.VMEM((width, inner), low), pltpu.SemaphoreType.DMA((count,))],
+        ),
+        out_shape=[
+            jax.ShapeDtypeStruct((total, width), wide),
+            jax.ShapeDtypeStruct((total, width), low),
+            jax.ShapeDtypeStruct((width, total), low),
+            jax.ShapeDtypeStruct((total, inner), low),
+        ],
+        compiler_params=pltpu.CompilerParams(vmem_limit_bytes=40 << 20),
+        cost_estimate=cost(4 * total * width * inner, 24 << 20),
+        name="hidden_back",
+    )(places, mine, other, hidden, grad, *pieces)
+
+
+def attention_terms_kernel(
+    corner_ref, grad_t_ref, normed_t_ref, context_ref, q_ref, k_ref, v_ref, terms_ref, upper_ref, lower_ref
+):
+    inner = context_ref.shape[1]
+    terms_ref[0, :, :inner] = dot(grad_t_ref[...], context_ref[...], 1, 0).astype(low)
+    for number, ref in enumerate((q_ref, k_ref, v_ref)):
+        columns = slice((number + 1) * inner, (number + 2) * inner)
+        terms_ref[0, :, columns] = dot(normed_t_ref[...], ref[...], 1, 0).astype(low)
+
+    @pl.when(pl.program_id(0) == corner_ref[0])
+    def _():
+        half = upper_ref.shape[0]
+        upper_ref[...] = terms_ref[0, :half, :]
+        lower_ref[...] = terms_ref[0, half:, :]
+
+
+def attention_terms(corner, grad_t, normed_t, context, query_grad, key_grad, value_grad, chips):
+    width, total = normed_t.shape
+    inner = context.shape[1]
+    share = width // chips
+    block = pl.BlockSpec((share, total), lambda i, _: (i, 0))
+    whole = pl.BlockSpec((total, inner), lambda i, _: (0, 0), pipeline_mode=pl.Buffered(1))
+    corner_block = pl.BlockSpec((share // 2, 4 * inner), lambda i, _: (0, 0))
+    return pl.pallas_call(
+        attention_terms_kernel,
+        grid_spec=pltpu.PrefetchScalarGridSpec(
+            num_scalar_prefetch=1,
+            grid=(chips,),
+            in_specs=[block, block] + [whole] * 4,
+            out_specs=[
+                pl.BlockSpec((1, share, 4 * inner), lambda i, _: (i, 0, 0)),
+                corner_block,
+                corner_block,
+            ],
+        ),
+        out_shape=[
+            jax.ShapeDtypeStruct((chips, share, 4 * inner), low),
+            jax.ShapeDtypeStruct((share // 2, 4 * inner), low),
+            jax.ShapeDtypeStruct((share // 2, 4 * inner), low),
+        ],
+        compiler_params=pltpu.CompilerParams(vmem_limit_bytes=40 << 20),
+        cost_estimate=cost(4 * total * width * 4 * inner, 16 << 20),
+        name="attention_terms",
+    )(corner, grad_t, normed_t, context, query_grad, key_grad, value_grad)
+
+
+def input_product_kernel(place_ref, q_ref, k_ref, v_ref, *refs, count):
+    pieces = refs[:count]
+    own_ref, other_ref, weight, semaphores = refs[count:]
+    index = pl.program_id(0)
 
     @pl.when(index == 0)
     def _():
-        mixed_sum[...] = mixed
-        normed_sum[...] = normed_grad
-
-    @pl.when(index > 0)
+        copies = block_copies(place_ref, 0, pieces, weight, semaphores)
+        for copy in copies:
+            copy.start()
+        for copy in copies:
+            copy.wait()
+
+    inner = q_ref.shape[1]
+    product = dot(q_ref[...], weight[:, :inner], 1, 1)
+    product += dot(k_ref[...], weight[:, inner : 2 * inner], 1, 1)
+    product += dot(v_ref[...], weight[:, 2 * inner :], 1, 1)
+
+    @pl.when(index < 2)
     def _():
-        mixed_sum[...] += mixed
-        normed_sum[...] += normed_grad
-
-    @pl.when(index == pl.num_programs(0) - 1)
+        other_ref[...] = product.astype(low)
+
+    @pl.when(index >= 2)
     def _():
-        mixed_ref[...] = mixed_sum[...].astype(low)
-        normed_grad_ref[...] = normed_sum[...].astype(low)
-
-
-def feed_forward(normed, normed_t, grad, grad_t, expand, contract, step=512):
-    rows, width = normed.shape
-    hidden = expand.shape[1]
-    whole = pl.BlockSpec((rows, width), lambda i: (0, 0), pipeline_mode=pl.Buffered(1))
-    whole_t = pl.BlockSpec((width, rows), lambda i: (0, 0), pipeline_mode=pl.Buffered(1))
-    block = pl.BlockSpec((width, step), lambda i: (0, i))
-    whole_out = pl.BlockSpec((rows, width), lambda i: (0, 0))
+        own_ref[...] = product
+
+
+def input_product(places, query_grad, key_grad, value_grad, pieces):
+    total, inner = query_grad.shape
+    count = len(pieces)
+    width = count * pieces[0].shape[0]
+    step = total // 4
+
+    def rows(i, place_ref):
+        core = place_ref[count]
+        return (jnp.where(i < 2, 2 * (1 - core) + i, 2 * core + i - 2), 0)
+
     return pl.pallas_call(
-        feed_forward_kernel,
-        grid=(hidden // step,),
-        in_specs=[whole, whole_t, whole, whole_t, block, block],
-        out_specs=[whole_out, whole_out, block, block],
-        out_shape=[jax.ShapeDtypeStruct((rows, width), low)] * 2
-        + [jax.ShapeDtypeStruct((width, hidden), low)] * 2,
-        scratch_shapes=[pltpu.VMEM((rows, width), wide), pltpu.VMEM((rows, width), wide)],
-        compiler_params=pltpu.CompilerParams(vmem_limit_bytes=56 << 20),
-        cost_estimate=pl.CostEstimate(
-            flops=12 * rows * width * hidden * 3 // 2, bytes_accessed=40 << 20, transcendentals=0
+        functools.partial(input_product_kernel, count=count),
+        grid_spec=pltpu.PrefetchScalarGridSpec(
+            num_scalar_prefetch=1,
+            grid=(4,),
+            in_specs=[pl.BlockSpec((step, inner), rows)] * 3 + [anywhere] * count,
+            out_specs=[
+                pl.BlockSpec((step, width), lambda i, _: (jnp.maximum(i - 2, 0), 0)),
+                pl.BlockSpec((step, width), lambda i, _: (jnp.minimum(i, 1), 0)),
+            ],
+            scratch_shapes=[
+                pltpu.VMEM((width, 3 * inner), low),
+                pltpu.SemaphoreType.DMA((count,)),
+            ],
         ),
-        name="feed_forward",
-    )(normed, normed_t, grad, grad_t, expand, contract)
+        out_shape=[
+            jax.ShapeDtypeStruct((total // 2, width), wide),
+            jax.ShapeDtypeStruct((total // 2, width), low),
+        ],
+        compiler_params=pltpu.CompilerParams(vmem_limit_bytes=40 << 20),
+        cost_estimate=cost(4 * total * width * 3 * inner, 16 << 20),
+        name="input_product",
+    )(places, query_grad, key_grad, value_grad, *pieces)
+
+
+def finish_kernel(place_ref, own_ref, other_ref, base_ref, token_ref, first_ref, second_ref, *, back):
+    index = pl.program_id(0)
+    summed = own_ref[...].astype(wide) + other_ref[...].astype(wide)
+    if back:
+        tokens = token_ref[...].astype(wide)
+        values = base_ref[...] + normalize_back(tokens, normalize(tokens)[1], summed)
+    else:
+        row = (2 * place_ref[0] + index) * summed.shape[0]
+        position = row + lax.broadcasted_iota(jnp.int32, summed.shape, 0)
+        values = jnp.where(position < place_ref[2], base_ref[...] + summed, 0.0)
+    values = values.astype(low)
+
+    @pl.when(index == place_ref[1])
+    def _():
+        first_ref[...] = values
+
+    @pl.when(index != place_ref[1])
+    def _():
+        second_ref[...] = values
+
+
+def finish_half(core, odd, length, own, other, base, tokens, back):
+    rows, width = own.shape
+    step = rows // 2
+    half = pl.BlockSpec((step, width), lambda i, _: (i, 0))
+    whole = pl.BlockSpec((step, width), lambda i, place_ref: (2 * place_ref[0] + i, 0))
+    quarter = pl.BlockSpec((step, width), lambda i, _: (0, 0))
+    return pl.pallas_call(
+        functools.partial(finish_kernel, back=back),
+        grid_spec=pltpu.PrefetchScalarGridSpec(
+            num_scalar_prefetch=1,
+            grid=(2,),
+            in_specs=[half, half, whole, whole],
+            out_specs=[quarter, quarter],
+        ),
+        out_shape=[jax.ShapeDtypeStruct((step, width), low)] * 2,
+        compiler_params=pltpu.CompilerParams(vmem_limit_bytes=32 << 20),
+        cost_estimate=cost(0, 8 << 20),
+        name="input_gradient_rows" if back else "result_rows",
+    )(jnp.stack([core, odd, length]).astype(jnp.int32), own, other, base, tokens)
+
+
+def pick_kernel(slot_ref, *refs, count):
+    pieces = refs[:count]
+    own_ref, other_ref, semaphores = refs[count:]
+    for row in range(4):
+        target = (own_ref if row < 2 else other_ref).at[row % 2]
+        for number in range(count):
+
+            @pl.when(slot_ref[row] == slot_ref[4 + number])
+            def _():
+                copy = pltpu.make_async_copy(pieces[number], target, semaphores.at[row])
+                copy.start()
+                copy.wait()
+
+
+def pick_slots(slots, pieces):
+    count = len(pieces)
+    shape = (2,) + pieces[0].shape
+    return pl.pallas_call(
+        functools.partial(pick_kernel, count=count),
+        in_specs=[pl.BlockSpec(memory_space=pltpu.SMEM)] + [anywhere] * count,
+        out_specs=[anywhere] * 2,
+        out_shape=[jax.ShapeDtypeStruct(shape, low)] * 2,
+        scratch_shapes=[pltpu.SemaphoreType.DMA((4,))],
+        compiler_params=pltpu.CompilerParams(vmem_limit_bytes=32 << 20),
+        cost_estimate=cost(0, 8 << 20),
+        name="pick_slots",
+    )(slots, *pieces)
 
 
 def normalize(values):
@@ -386,16 +850,13 @@
         self.chip = self.shard // 2
         self.core = self.shard % 2
         self.groups = [list(range(core, self.shards, 2)) for core in (0, 1)]
+        self.square = self.chips == 4
 
     def sibling(self, array):
         return lax.ppermute(array, "fsdp", [(i, i ^ 1) for i in range(self.shards)])
 
     def across(self, array, bit):
         return lax.ppermute(array, "fsdp", [(i, i ^ (2 * bit)) for i in range(self.shards)])
-
-    def vertical(self, array, distance):
-        count = self.depth
-        return lax.ppermute(array, "ctx", [(i, (i + distance) % count) for i in range(count)])
 
     def in_order(self, mine, other, axis):
         return jnp.concatenate(
@@ -403,67 +864,72 @@
             axis=axis,
         )
 
-    def gather(self, shard, behind=()):
-        if self.chips != 4:
-            return (
-                lax.all_gather(shard, "fsdp", axis=0, tiled=True, axis_index_groups=self.groups),
-                (),
+    def gather(self, parts, behind=()):
+        if not self.square:
+            whole = [
+                lax.all_gather(part, "fsdp", axis=0, axis_index_groups=self.groups)
+                for part in parts
+            ]
+            return [tuple(w[chip] for w in whole) for chip in range(self.chips)], ()
+        if behind:
+            parts = tuple(after(part, *behind) for part in parts)
+        first = tuple(self.across(part, 1) for part in parts)
+        second = tuple(self.across(part, 2) for part in parts)
+        corner = (self.across(first[0], 2), self.across(second[1], 1))
+        return [parts, first, second, corner], (*first, *second)
+
+    def chip_numbers(self):
+        return [self.chip ^ k for k in range(4)] if self.square else list(range(self.chips))
+
+    def gather_weight(self, mine, behind=(), other=None):
+        pairs, sent = self.gather((mine, other), behind)
+        return [piece for pair in pairs for piece in pair], sent
+
+    def weight_places(self):
+        return [2 * chip + side for chip in self.chip_numbers() for side in (self.core, 1 - self.core)]
+
+    def scatter(self, terms, upper, lower, behind=()):
+        dim = terms.ndim - 2
+        if not self.square:
+            summed = lax.psum_scatter(
+                terms, "fsdp", scatter_dimension=dim, tiled=True, axis_index_groups=self.groups
             )
+            return summed.astype(low), ()
+        share = terms.shape[dim] // 4
+        half = share // 2
+
+        def rows(chip):
+            return lax.dynamic_slice_in_dim(terms, chip * share, share, dim).astype(wide)
+
         if behind:
-            shard = after(shard, *behind)
-        half = shard.shape[0] // 2
-        first = self.across(shard, 1)
-        second = self.across(shard, 2)
-        upper = self.across(first[:half], 2)
-        lower = self.across(second[half:], 1)
-        whole = jnp.zeros((4,) + shard.shape, shard.dtype)
-        whole = put(whole, shard, self.chip)
-        whole = put(whole, first, self.chip ^ 1)
-        whole = put(whole, second, self.chip ^ 2)
-        whole = put(whole, jnp.concatenate([upper, lower], axis=0), self.chip ^ 3)
-        return whole.reshape((4 * shard.shape[0],) + shard.shape[1:]), (first, second)
-
-    def scatter(self, terms, behind=()):
-        if self.chips != 4:
-            summed = lax.psum_scatter(
-                terms, "fsdp", scatter_dimension=0, tiled=True, axis_index_groups=self.groups
-            )
-            return summed.astype(wide), ()
-        if behind:
-            terms = after(terms, *behind)
-        parts = terms.reshape((4, terms.shape[0] // 4) + terms.shape[1:])
-        half = parts.shape[1] // 2
-        corner = take(parts, self.chip ^ 3)
-        upper = self.across(corner[:half], 1)
-        lower = self.across(corner[half:], 2)
-        beside = take(parts, self.chip ^ 1).astype(wide)
-        below = take(parts, self.chip ^ 2).astype(wide)
-        beside = jnp.concatenate([beside[:half], beside[half:] + lower.astype(wide)], axis=0)
-        below = jnp.concatenate([below[:half] + upper.astype(wide), below[half:]], axis=0)
-        first = self.across(beside.astype(low), 1)
-        second = self.across(below.astype(low), 2)
-        own = take(parts, self.chip).astype(wide)
-        return own + first.astype(wide) + second.astype(wide), (first, second)
+            upper, lower = after(upper, *behind), after(lower, *behind)
+        upper = self.across(upper, 1).astype(wide)
+        lower = self.across(lower, 2).astype(wide)
+        top = [(0, 0, 0)] * dim + [(0, half, 0), (0, 0, 0)]
+        bottom = [(0, 0, 0)] * dim + [(half, 0, 0), (0, 0, 0)]
+        zero = jnp.zeros((), wide)
+        beside = (rows(self.chip ^ 1) + lax.pad(lower, zero, bottom)).astype(low)
+        below = (rows(self.chip ^ 2) + lax.pad(upper, zero, top)).astype(low)
+        first = self.across(beside, 1)
+        second = self.across(below, 2)
+        summed = rows(self.chip) + first.astype(wide) + second.astype(wide)
+        return summed.astype(low), (first, second)
 
     def level_sum(self, terms):
-        count = self.depth
-        parts = terms.reshape((count, terms.shape[0] // count) + terms.shape[1:])
-        total = take(parts, self.level).astype(wide)
-        for distance in range(1, count):
-            part = take(parts, (self.level + distance) % count)
-            total = total + self.vertical(part, distance).astype(wide)
-        total = total.astype(low)
-        whole = put(jnp.zeros_like(parts), total, self.level)
-        for distance in range(1, count):
-            part = self.vertical(total, distance)
-            whole = put(whole, part, (self.level - distance) % count)
-        return whole.reshape(terms.shape)
+        inward = lax.ppermute(terms, "ctx", [(0, 1), (3, 2)])
+        joined = (terms.astype(wide) + inward.astype(wide)).astype(low)
+        across = lax.ppermute(joined, "ctx", [(1, 2), (2, 1)])
+        total = (joined.astype(wide) + across.astype(wide)).astype(low)
+        outward = lax.ppermute(total, "ctx", [(1, 0), (2, 3)])
+        inner = (self.level == 1) | (self.level == 2)
+        return jnp.where(inner, total, outward)
 
     def exchange_rows(self, rows):
-        parts = rows.reshape((2, rows.shape[0] // 2) + rows.shape[1:])
-        mine = take(parts, self.core)
-        other = self.sibling(take(parts, 1 - self.core))
-        return self.in_order(mine[None], other[None], 0)
+        dim = rows.ndim - 2
+        half = rows.shape[dim] // 2
+        mine = lax.dynamic_slice_in_dim(rows, self.core * half, half, dim)
+        other = self.sibling(lax.dynamic_slice_in_dim(rows, (1 - self.core) * half, half, dim))
+        return jnp.where(self.core == 0, mine, other), jnp.where(self.core == 0, other, mine)
 
     def trade(self, array, outward, swapped):
         pairs = []
@@ -477,22 +943,22 @@
                 pairs.append((held, worked) if outward else (worked, held))
         return lax.ppermute(array, ("ctx", "fsdp"), pairs)
 
-    def to_slots(self, blocks):
+    def to_slot(self, blocks):
         odd = self.level % 2
         first = self.trade(take(blocks, odd), True, False)
         second = self.trade(take(blocks, 1 - odd), True, True)
-        flip = odd == 0
-        return jnp.concatenate(
-            [jnp.where(flip, first, second), jnp.where(flip, second, first)], axis=0
-        )
-
-    def from_slots(self, rows):
+        return [first, second, self.sibling(first), self.sibling(second)]
+
+    def quarter_places(self):
         odd = self.level % 2
-        blocks = rows.reshape((2, rows.shape[0] // 2) + rows.shape[1:])
-        first = self.trade(take(blocks, odd), False, False)
-        second = self.trade(take(blocks, 1 - odd), False, True)
-        flip = odd == 0
-        return jnp.stack([jnp.where(flip, first, second), jnp.where(flip, second, first)])
+        near, far = 2 * self.core, 2 * (1 - self.core)
+        return [near + odd, near + 1 - odd, far + odd, far + 1 - odd]
+
+    def from_slot(self, quarters):
+        first = self.trade(quarters[0], False, False)
+        second = self.trade(quarters[1], False, True)
+        flip = self.level % 2 == 0
+        return jnp.where(flip, first, second), jnp.where(flip, second, first)
 
 
 def local(
@@ -516,61 +982,47 @@
     core = links.core
     held_count, local_length, model_width = tokens.shape
     total_length = local_length * links.depth
-    half_length = total_length // 2
     bucket_count, head_count = bias_table.shape
     inner_width = query_weight.shape[1]
     head_size = inner_width // head_count
-    hidden_width = expand_weight.shape[1]
-    row_share = query_weight.shape[0]
     own_heads = head_count // 2
     own_inner = inner_width // 2
-    own_hidden = hidden_width // 2
     slot_count = slot_sequence.shape[0]
     assert held_count == 2 and links.depth == 4
 
     slots = jnp.arange(slot_count)
     slot = links.chip * (2 * held_count) + links.level
     sequence = jnp.sum(jnp.where(slots == slot, slot_sequence, 0))
-    length = jnp.sum(jnp.where(slots == sequence, sequence_lengths, 0))
-    row_okay = jnp.arange(total_length)[:, None] < length
-
-    stacked = jnp.concatenate([query_weight, key_weight, value_weight], axis=1)
-    effective_qkv = scaled_rows(stacked, first_gain)
-    effective_expand = scaled_rows(expand_weight, second_gain)
-
-    def side_columns(which):
-        def cut(weight, blocks):
-            parts = weight.reshape(row_share, blocks, 2, weight.shape[1] // (2 * blocks))
-            return lax.dynamic_index_in_dim(parts, which, 2, keepdims=False).reshape(row_share, -1)
-
-        return jnp.concatenate(
-            [
-                cut(effective_qkv, 3),
-                cut(output_weight, 1),
-                cut(effective_expand, 1),
-                cut(contract_weight, 1),
-            ],
-            axis=1,
-        )
-
-    mine = side_columns(core)
-    other = links.sibling(side_columns(1 - core))
-    chip_rows = links.in_order(mine, other, 0)
-    cuts = [0, 3 * own_inner, 4 * own_inner, 4 * own_inner + own_hidden]
-    cuts.append(cuts[-1] + own_hidden)
-    qkv_shard, output_shard, expand_shard, contract_shard = (
-        chip_rows[:, start:stop] for start, stop in zip(cuts[:-1], cuts[1:])
-    )
-
-    token_half = links.to_slots(tokens)
-    token_low = links.in_order(token_half, links.sibling(token_half), 0)
-    cotangent_half = links.to_slots(after(cotangent, token_low))
-    cotangent_low = links.in_order(cotangent_half, links.sibling(cotangent_half), 0)
-
-    whole_qkv, sent = links.gather(qkv_shard)
-    whole_output, sent = links.gather(output_shard, sent)
-    whole_expand, sent = links.gather(expand_shard, sent)
-    whole_contract, sent = links.gather(contract_shard, sent)
+    length = jnp.sum(jnp.where(slots == sequence, sequence_lengths, 0)).astype(jnp.int32)
+    odd = links.level % 2
+
+    def numbers(*values):
+        return jnp.stack([jnp.asarray(value, jnp.int32) for value in values])
+
+    token_quarters = links.to_slot(tokens)
+    mine, other = weight_sides(
+        numbers(core),
+        query_weight,
+        key_weight,
+        value_weight,
+        output_weight,
+        expand_weight,
+        contract_weight,
+        first_gain,
+        second_gain,
+    )
+    arrived = [links.sibling(array) for array in other]
+    sent = ()
+    gathered = []
+    for own_part, arrived_part in zip(mine, arrived):
+        pieces, sent = links.gather_weight(own_part, sent, arrived_part)
+        gathered.append(pieces)
+    qkv_pieces, output_pieces, early_pieces, late_pieces = gathered
+    weight_places = links.weight_places()
+    corner = links.chip ^ 3 if links.square else 0
+    places = numbers(*weight_places, corner, core)
+    core_places = numbers(*weight_places, core)
+    slot_places = numbers(*links.quarter_places(), length)
 
     line_width = 2 * total_length
     falling = jnp.concatenate([jnp.flip(offset_bucket), jnp.full((1,), -1, jnp.int32)])
@@ -579,104 +1031,117 @@
     lines = dot(own_table, matching.astype(low), 0, 1)
     strips = bias_strips(lines.reshape(own_heads, 1, line_width))
 
-    token_rows = token_low.astype(wide)
-    unit_one, scale_one = normalize(token_rows)
-    normed_one = unit_one.astype(low)
-    qkv = dot(normed_one, whole_qkv, 1, 0).astype(low)
-    length_line = length.reshape(1).astype(jnp.int32)
+    token_low, normed_one, normed_one_t = token_rows_of(slot_places, token_quarters, True)
+    cotangent_quarters = links.to_slot(after(cotangent, *token_quarters))
+    _, out_low, out_low_t = token_rows_of(slot_places, cotangent_quarters, False)
+
+    qkv = rows_product(places, normed_one, qkv_pieces, False, "qkv_product")
+    length_line = length.reshape(1)
     context, log_totals, tops = attention_forward(length_line, qkv, strips)
-    attended = dot(context, whole_output, 1, 1).astype(low)
-    hidden_one = token_rows + (
-        attended.astype(wide) + links.sibling(attended).astype(wide)
-    )
-    unit_two, scale_two = normalize(hidden_one)
-    normed_two = unit_two.astype(low)
-    out_low = jnp.where(row_okay, cotangent_low, 0)
-    mixed, normed_two_part, expand_terms, contract_terms = feed_forward(
-        normed_two, normed_two.T, out_low, out_low.T, whole_expand, whole_contract
-    )
-    normed_two_grad = normed_two_part.astype(wide) + links.sibling(normed_two_part).astype(wide)
-    hidden_grad = out_low.astype(wide) + normalize_back(hidden_one, scale_two, normed_two_grad)
-    attended_grad = hidden_grad.astype(low)
-
-    def own_half(array, which):
-        return lax.dynamic_slice_in_dim(array, which * half_length, half_length, 0)
-
-    mixed_half = own_half(mixed, core).astype(wide) + links.sibling(
-        own_half(mixed, 1 - core)
-    ).astype(wide)
-    result_half = jnp.where(
-        own_half(row_okay, core), own_half(hidden_one, core) + mixed_half, 0.0
-    ).astype(low)
-    result = links.from_slots(result_half)
-
-    context_grad = dot(attended_grad, whole_output, 1, 0).astype(low)
-    output_terms = dot(attended_grad, context, 0, 0).astype(low)
+    attended = rows_product(places, context, output_pieces, True, "attended_product")
+    hidden_one, normed_two, normed_two_t = second_norm(
+        token_low, attended, links.sibling(attended)
+    )
+    operands = (normed_two, normed_two_t, out_low, out_low_t)
+    mixed_sum, normed_sum, early_terms, early_upper, early_lower = feed_forward(
+        places, *operands, early_pieces, links.chips
+    )
+    mixed_own, mixed_away, normed_two_part, late_terms, late_upper, late_lower = feed_forward(
+        places, *operands, late_pieces, links.chips, (mixed_sum, normed_sum)
+    )
+    hidden_grad, attended_grad, attended_grad_t, context_grad = hidden_back(
+        places,
+        normed_two_part,
+        links.sibling(normed_two_part),
+        hidden_one,
+        out_low,
+        output_pieces,
+    )
     query_grad, key_grad, value_grad, strip_grads = attention_backward(
         length_line, qkv, context, context_grad, log_totals, strips
     )
-    qkv_grad = jnp.concatenate([query_grad, key_grad, value_grad], axis=1)
-    qkv_terms = dot(normed_one, qkv_grad, 0, 0).astype(low)
-    normed_one_part = dot(qkv_grad, whole_qkv, 1, 1)
-    normed_one_grad = own_half(normed_one_part, core) + links.sibling(
-        own_half(normed_one_part, 1 - core).astype(low)
-    ).astype(wide)
-    input_half = own_half(hidden_grad, core) + normalize_back(
-        own_half(token_rows, core), own_half(scale_one, core), normed_one_grad
-    )
-    input_gradient = links.from_slots(input_half.astype(low)).astype(wide)
-
-    contract_sum, sent = links.scatter(contract_terms)
-    expand_sum, sent = links.scatter(expand_terms, sent)
-    output_sum, sent = links.scatter(output_terms, sent)
-    qkv_sum, sent = links.scatter(qkv_terms, sent)
-    gathered, _ = links.gather(result.reshape(held_count * local_length, model_width), sent)
-
-    def finished(summed):
-        parts = links.exchange_rows(summed.astype(low))
-        flat = parts.reshape(2 * row_share, -1)
-        return links.level_sum(flat).reshape(parts.shape)
-
-    contract_parts = finished(contract_sum)
-    expand_parts = finished(expand_sum)
-    output_parts = finished(output_sum)
-    qkv_parts = finished(qkv_sum)
-
-    def columns_of(parts, blocks):
-        width = parts.shape[2] // blocks
-        shaped = parts.reshape(2, row_share, blocks, width).transpose(1, 2, 0, 3)
-        return shaped.reshape(row_share, 2 * blocks * width).astype(wide)
-
-    contract_weight_gradient = columns_of(contract_parts, 1)
-    raw_two = columns_of(expand_parts, 1)
-    output_weight_gradient = columns_of(output_parts, 1)
-    raw_one = columns_of(qkv_parts, 3)
+    attention_parts, attention_upper, attention_lower = attention_terms(
+        numbers(corner),
+        attended_grad_t,
+        normed_one_t,
+        context,
+        query_grad,
+        key_grad,
+        value_grad,
+        links.chips,
+    )
+    attention_parts = attention_parts.reshape(model_width, -1)
+
+    early_sum, sent = links.scatter(early_terms, early_upper, early_lower)
+    late_sum, sent = links.scatter(late_terms, late_upper, late_lower, sent)
+    attention_sum, sent = links.scatter(
+        attention_parts, attention_upper, attention_lower, sent
+    )
+    early_left, early_right = links.exchange_rows(links.level_sum(early_sum))
+    late_left, late_right = links.exchange_rows(links.level_sum(late_sum))
+    attention_left, attention_right = links.exchange_rows(links.level_sum(attention_sum))
+
+    own_part, away_part = input_product(core_places, query_grad, key_grad, value_grad, qkv_pieces)
+    input_quarters = finish_half(
+        core, odd, length, own_part, links.sibling(away_part), hidden_grad, token_low, True
+    )
+    input_gradient = jnp.stack(links.from_slot(input_quarters)).astype(wide)
+
+    result_quarters = finish_half(
+        core, odd, length, mixed_own, links.sibling(mixed_away), hidden_one, token_low, False
+    )
+    results = links.from_slot(result_quarters)
+    result_pairs, _ = links.gather(results, sent)
+
+    def slot_of(wanted):
+        return jnp.sum(jnp.where(slot_sequence == wanted, slots, 0))
+
+    own_slots = [slot_of(links.shard * held_count + row) for row in range(held_count)]
+    other_slots = [slot_of((links.shard ^ 1) * held_count + row) for row in range(held_count)]
+    piece_slots = [
+        (2 * chip + core) * held_count + row
+        for chip in links.chip_numbers()
+        for row in range(held_count)
+    ]
+    picked, picked_other = pick_slots(
+        numbers(*own_slots, *other_slots, *piece_slots),
+        [piece for pair in result_pairs for piece in pair],
+    )
+    from_other = links.sibling(picked_other)
+    output = jnp.stack(
+        [
+            jnp.where((s // held_count) % 2 == core, picked[row], from_other[row])
+            for row, s in enumerate(own_slots)
+        ]
+    )
+
+    def side_by_side(*parts):
+        return jnp.concatenate(parts, axis=1).astype(wide)
+
+    raw_two = side_by_side(early_left[0], late_left[0], early_right[0], late_right[0])
+    contract_weight_gradient = side_by_side(
+        early_left[1], late_left[1], early_right[1], late_right[1]
+    )
+
+    def inner_columns(block):
+        columns = slice(block * own_inner, (block + 1) * own_inner)
+        return side_by_side(attention_left[:, columns], attention_right[:, columns])
+
+    output_weight_gradient = inner_columns(0)
+    raw_query, raw_key, raw_value = (inner_columns(block) for block in (1, 2, 3))
     first_scale = first_gain.astype(wide)[:, None]
     second_scale = second_gain.astype(wide)[:, None]
-    first_gain_gradient = jnp.sum(stacked.astype(wide) * raw_one, axis=1)
+    first_gain_gradient = jnp.sum(
+        query_weight.astype(wide) * raw_query
+        + key_weight.astype(wide) * raw_key
+        + value_weight.astype(wide) * raw_value,
+        axis=1,
+    )
     second_gain_gradient = jnp.sum(expand_weight.astype(wide) * raw_two, axis=1)
-    query_weight_gradient = first_scale * raw_one[:, :inner_width]
-    key_weight_gradient = first_scale * raw_one[:, inner_width : 2 * inner_width]
-    value_weight_gradient = first_scale * raw_one[:, 2 * inner_width :]
+    query_weight_gradient = first_scale * raw_query
+    key_weight_gradient = first_scale * raw_key
+    value_weight_gradient = first_scale * raw_value
     expand_weight_gradient = second_scale * raw_two
-
-    gathered = gathered.reshape(links.chips * held_count, local_length, model_width)
-
-    def slot_of(wanted):
-        return jnp.sum(jnp.where(slot_sequence == wanted, slots, 0))
-
-    def place_of(found):
-        return (found // 4) * held_count + found % 2
-
-    own_slots = [slot_of(links.shard * held_count + row) for row in range(held_count)]
-    other_slots = [slot_of((links.shard ^ 1) * held_count + row) for row in range(held_count)]
-    from_other = links.sibling(jnp.stack([take(gathered, place_of(s)) for s in other_slots]))
-    output = jnp.stack(
-        [
-            jnp.where((s // 2) % 2 == core, take(gathered, place_of(s)), from_other[row])
-            for row, s in enumerate(own_slots)
-        ]
-    )
 
     diagonals = diagonal_sums(strip_grads).reshape(own_heads, line_width)
     table_grad = lax.dot_general(

time: 682 us -> 504 us (0.74)
  starting transfers between devices: 169 us -> 83.6 us
  local copies, waits for them, and re-layouts: 123 us -> 41.4 us
  Pallas kernels: 107 us -> 168 us
  other arithmetic: 91.1 us -> 39.4 us
  matrix products: 25.5 us -> 1.22 us
  waiting for transfers between devices: 143 us -> 155 us
    ppermute x24 -> x9, starting transfers between devices: 82.3 us -> 16.5 us  [the longest x3 8.36 us: level_sum(): inward = lax.ppermute(terms, 'ctx', [(0, 1), (3, 2)])]
    pallas_call x1 -> x14, Pallas kernels: 40.2 us -> 102 us  [the longest x2 54.2 us: feed_forward(): pl.pallas_call(functools.partial(feed_forward_kernel, count=count, first=...]
    dot_general x7 -> x1, matrix products: 24.9 us -> 0.64 us  [dot(): lax.dot_general(left, right, (((left_dim,), (right_dim,)), ((), ())), pre...]
    dynamic_slice x18 -> x3, local copies, waits for them, and re-layouts: 15.5 us -> 0.14 us  [exchange_rows(): lax.dynamic_slice_in_dim(rows, (1 - self.core) * half, half, dim)]
    dynamic_update_slice x26 -> x0, local copies, waits for them, and re-layouts: 14.1 us -> none  [put(): return lax.dynamic_update_slice_in_dim(array, part[None], index, 0)]
    convert_element_type x8 -> x0, local copies, waits for them, and re-layouts: 13.8 us -> none  [the longest x6 10.1 us: columns_of(): return shaped.reshape(row_share, 2 * blocks * width).astype(wide)]
    slice x14 -> x1, local copies, waits for them, and re-layouts: 12.1 us -> 0.07 us  [inner_columns(): return side_by_side(attention_left[:, columns], attention_right[:, columns])]
    ppermute x2, waiting for transfers between devices: 0.38 us -> 12.3 us  [local(): small = joined(small, lax.ppermute(small, 'ctx', swap))]
  transfers between devices with their start and end apart: 85 -> 80, of which waited for: 29 -> 24; matrix products, arithmetic and copies ran while one was open for 31% -> 9% of each run, Pallas kernels for 10% -> 28%
where the time goes in v2:
time: 504 us; the launch traced here: 497 us
  Pallas kernels  168 us (33%)
  waiting for transfers between devices  155 us (31%)
  starting transfers between devices  83.6 us (17%)
  local copies, waits for them, and re-layouts  41.4 us (8%)
  other arithmetic  39.4 us (8%)
  between operations  7.41 us (1%)
    ppermute x44, waiting for transfers between devices, across(): lax.ppermute(array, 'fsdp', [(i, i ^ 2 * bit) for i in range(self.shards)])  88.4 us
    pallas_call x2, Pallas kernels, feed_forward(): pl.pallas_call(functools.partial(feed_forward_kernel, count=count, first=...  54.2 us
    ppermute x44, starting transfers between devices, across(): lax.ppermute(array, 'fsdp', [(i, i ^ 2 * bit) for i in range(self.shards)])  46.8 us
    ppermute x3, waiting for transfers between devices, level_sum(): outward = lax.ppermute(total, 'ctx', [(1, 0), (2, 3)])  39.5 us
    pallas_call x1, Pallas kernels, attention_backward(): pl.pallas_call(functools.partial(backward_kernel, step=step), grid_spec=p...  36.1 us
    unnamed x189, local copies, waits for them, and re-layouts  34.6 us
    pallas_call x1, Pallas kernels, attention_forward(): pl.pallas_call(functools.partial(forward_kernel, step=step), grid_spec=pl...  22.4 us
    ppermute x2, waiting for transfers between devices, local(): small = joined(small, lax.ppermute(small, 'ctx', swap))  12.3 us
  transfers between devices with their start and end apart: 80, of which 24 were waited for; matrix products, arithmetic and copies ran while one was open for 9% of the time, Pallas kernels for 28%

profile of v2, /device:TPU:0, one launch (start us, length us, event | category | flops | bytes accessed | tf_op | source)
XLA Modules:
  0.0 496.6 jit_solution(8710280223367432811)
XLA Ops:
  0.7 2.4 dynamic-slice_bitcast_fusion.2
  3.1 3.0 collective-permute-start.1
  14.9 2.1 collective-permute-start.4
  17.0 1.7 collective-permute-start
  23.6 7.3 %collective-permute-done.7.refs_4_ = bf16[128,1536]{1,0:T(8,128)(2,1)S(1)} collective-permute-done((bf16[128,1536]{1,0:T(8,128)(2,1)}, bf16[128,1536]{1,0:T(8,128)(2,1)S(1)}, u32[]{:S(2)}, u32[]{:S(2)}) %collective-permute-start.7) | collective-permute-done | bytes 393248 | tf_op jit(solution)/shard_map/ppermute | solution.py:859
  33.3 1.5 collective-permute-start.9
  34.9 4.5 collective-permute-done.8.refs_5_
  46.2 2.8 bias_strips.1.strip_ref
  49.1 3.4 copy-done.3
  57.5 1.9 token_rows.1
  65.8 6.5 %qkv_product.1.query_ref.key_ref.value_ref = bf16[1024,1536]{1,0:T(8,128)(2,1)S(1)} custom-call(s32[10]{0:T(128)S(1)} %stack.156.place_ref, bf16[1024,1024]{1,0:T(8,128)(2,1)S(1)} %get-tuple-element.76.rows_ref, bf16[128,1536]{1,0:T(8,128)(2,1)} %get-tuple-element.77.refs_0_, bf16[128,1536]{1,0:T(8,128)(2,1)S(1)} %copy-done.48, ...), custom_call_target="tpu_custom_call" | custom-call | flops 4831838208 | bytes 8388608 | tf_op jit(solution)/shard_map/qkv_product/pallas_call | solution.py:420
  72.3 22.4 %attention_forward.1 = (bf16[1024,512]{1,0:T(8,128)(2,1)S(1)}, f32[4,2,1024]{2,1,0:T(2,128)S(1)}, f32[4,2,128]{2,1,0:T(2,128)S(1)}) custom-call(s32[1]{0:T(128)} %bitcast.14.length_ref, bf16[1024,1536]{1,0:T(8,128)(2,1)S(1)} %qkv_product.1.query_ref.key_ref.value_ref, bf16[1024,1536]{1,0:T(8,128)(2,1)S(1)} %qkv_product.1.query_ref.key_ref.value_ref, ...), custom_call_target="tpu_custom_call" | custom-call | flops 40000000000 | bytes 12582912 | tf_op jit(solution)/shard_map/attention_forward/pallas_call | solution.py:144
  95.5 4.3 attended_product.1.mine_ref
  103.7 11.5 %collective-permute-done.26.refs_4_ = bf16[2,128,1024]{2,1,0:T(8,128)(2,1)S(1)} collective-permute-done((bf16[2,128,1024]{2,1,0:T(8,128)(2,1)S(1)}, bf16[2,128,1024]{2,1,0:T(8,128)(2,1)S(1)}, u32[]{:S(2)}, u32[]{:S(2)}) %collective-permute-start.26) | collective-permute-done | bytes 524320 | tf_op jit(solution)/shard_map/ppermute | solution.py:859
  116.9 9.2 %collective-permute-done.27.refs_5_ = bf16[2,128,1024]{2,1,0:T(8,128)(2,1)S(1)} collective-permute-done((bf16[2,128,1024]{2,1,0:T(8,128)(2,1)S(1)}, bf16[2,128,1024]{2,1,0:T(8,128)(2,1)S(1)}, u32[]{:S(2)}, u32[]{:S(2)}) %collective-permute-start.27) | collective-permute-done | bytes 524320 | tf_op jit(solution)/shard_map/ppermute | solution.py:859
  126.5 5.7 %collective-permute-start.21 = (bf16[256,1024]{1,0:T(8,128)(2,1)S(1)}, bf16[256,1024]{1,0:T(8,128)(2,1)S(1)}, u32[]{:S(2)}, u32[]{:S(2)}) collective-permute-start(bf16[256,1024]{1,0:T(8,128)(2,1)S(1)} %collective-permute-done.19.refs_0_), channel_id=1, source_target_pairs={{0,1},{1,0},{2,3},{3,2},{4,5},{5,4},{6,7},{7,6},{8,9},{9,8},{10,11... | collective-permute-start | bytes 1572872 | tf_op jit(solution)/shard_map/ppermute | solution.py:856
  136.4 2.1 cotangent_rows.1
  142.3 3.0 second_norm.1
  150.4 8.7 %collective-permute-done.32.refs_5_ = bf16[2,128,1024]{2,1,0:T(8,128)(2,1)} collective-permute-done((bf16[2,128,1024]{2,1,0:T(8,128)(2,1)S(1)}, bf16[2,128,1024]{2,1,0:T(8,128)(2,1)}, u32[]{:S(2)}, u32[]{:S(2)}) %collective-permute-start.32) | collective-permute-done | bytes 524320 | tf_op jit(solution)/shard_map/ppermute | solution.py:859
  161.3 26.6 %feed_forward.2 = (f32[1024,1024]{1,0:T(8,128)}, f32[1024,1024]{1,0:T(8,128)}, bf16[2,1024,1024]{2,1,0:T(8,128)(2,1)}, bf16[2,128,1024]{2,1,0:T(8,128)(2,1)}, bf16[2,128,1024]{2,1,0:T(8,128)(2,1)}) custom-call(s32[10]{0:T(128)} %copy-done.34, bf16[1024,1024]{1,0:T(8,128)(2,1)} %copy-done.39, bf16[1024,1024]{1,0:T(8,128)(2,1)} %copy-done.40, ...), custom_call_target="tpu_custom_call" | custom-call | flops 21474836480 | bytes 41943040 | tf_op jit(solution)/shard_map/feed_forward/pallas_call | solution.py:567
  189.1 27.7 %feed_forward.3 = (bf16[512,1024]{1,0:T(8,128)(2,1)}, bf16[512,1024]{1,0:T(8,128)(2,1)}, bf16[1024,1024]{1,0:T(8,128)(2,1)}, bf16[2,1024,1024]{2,1,0:T(8,128)(2,...) custom-call(s32[10]{0:T(128)} %copy-done.34, bf16[1024,1024]{1,0:T(8,128)(2,1)} %copy-done.39, ...), custom_call_target="tpu_custom_call" | custom-call | flops 21474836480 | bytes 41943040 | tf_op jit(solution)/shard_map/feed_forward/pallas_call | solution.py:567
  218.5 12.7 %collective-permute-done.41 = bf16[2,128,1024]{2,1,0:T(8,128)(2,1)} collective-permute-done((bf16[2,128,1024]{2,1,0:T(8,128)(2,1)S(1)}, bf16[2,128,1024]{2,1,0:T(8,128)(2,1)}, u32[]{:S(2)}, u32[]{:S(2)}) %collective-permute-start.41) | collective-permute-done | bytes 524320 | tf_op jit(solution)/shard_map/ppermute | solution.py:859
  232.2 3.8 add_convert_fusion.13
  242.7 2.7 stack.142.slot_ref
  246.1 2.2 copy-done.2
  248.4 2.8 result_rows.1
  251.9 8.8 %collective-permute-done.44 = bf16[2,256,1024]{2,1,0:T(8,128)(2,1)} collective-permute-done((bf16[2,256,1024]{2,1,0:T(8,128)(2,1)}, bf16[2,256,1024]{2,1,0:T(8,128)(2,1)}, u32[]{:S(2)}, u32[]{:S(2)}) %collective-permute-start.44) | collective-permute-done | bytes 1048608 | tf_op jit(solution)/shard_map/ppermute | solution.py:859
  263.0 9.4 %hidden_back.1 = (f32[1024,1024]{1,0:T(8,128)}, bf16[1024,1024]{1,0:T(8,128)(2,1)}, bf16[1024,1024]{1,0:T(8,128)(2,1)S(1)}, bf16[1024,512]{1,0:T(8,128)(2,1)S(1)}) custom-call(s32[10]{0:T(128)S(1)} %copy-done.35, bf16[1024,1024]{1,0:T(8,128)(2,1)S(1)} %copy-done.12, bf16[1024,1024]{1,0:T(8,128)(2,1)} %collective-permute-done.40.other_ref, ...), custom_call_target="tpu_custom_call" | custom-call | flops 2147483648 | bytes 25165824 | tf_op jit(solution)/shard_map/hidden_back/pallas_call | solution.py:612
  272.4 36.1 %attention_backward.1 = (bf16[1024,512]{1,0:T(8,128)(2,1)S(1)}, bf16[1024,512]{1,0:T(8,128)(2,1)S(1)}, bf16[1024,512]{1,0:T(8,128)(2,1)S(1)}, f32[8,128,2048]{2,1,0:T(8,128)}) custom-call(s32[1]{0:T(128)} %bitcast.14.length_ref, bf16[1024,1536]{1,0:T(8,128)(2,1)} %copy-done.59, bf16[1024,1536]{1,0:T(8,128)(2,1)} %copy-done.59, ...), custom_call_target="tpu_custom_call" | custom-call | flops 60000002048 | bytes 25165824 | tf_op jit(solution)/shard_map/attention_backward/pallas_call | solution.py:248
  308.5 3.8 copy-done.4
  312.3 4.8 diagonal_sums.1
  317.8 1.6 collective-permute-start.75
  319.4 2.6 add_convert_fusion.5
  322.0 1.8 collective-permute-start.67
  324.9 2.7 collective-permute-done.76
  327.8 1.8 add_convert_fusion.11
  331.4 12.3 %collective-permute-done.77 = f32[8,33]{1,0:T(8,128)S(1)} collective-permute-done((f32[8,33]{1,0:T(8,128)S(1)}, f32[8,33]{1,0:T(8,128)S(1)}, u32[]{:S(2)}, u32[]{:S(2)}) %collective-permute-start.77) | collective-permute-done | bytes 1088 | tf_op jit(solution)/shard_map/ppermute | solution.py:1172
  343.9 3.4 collective-permute-start.78
  347.2 5.3 %attention_terms.1 = (bf16[4,256,2048]{2,1,0:T(8,128)(2,1)S(1)}, bf16[128,2048]{1,0:T(8,128)(2,1)S(1)}, bf16[128,2048]{1,0:T(8,128)(2,1)S(1)}) custom-call(s32[1]{0:T(128)} %bitcast.23.corner_ref, bf16[1024,1024]{1,0:T(8,128)(2,1)S(1)} %get-tuple-element.105.grad_t_ref, bf16[1024,1024]{1,0:T(8,128)(2,1)S(1)} %copy-done.37, bf16[1024,512]{1,0:T(8,128)(2,1)S(1)} %copy-done.58, ...), custom_call_target="tpu_custom_call" | custom-call | flops 8589934592 | bytes 16777216 | tf_op jit(solution)/shard_map/attention_terms/pallas_call | solution.py:661
  354.6 1.6 collective-permute-start.68
  356.3 1.9 add_convert_fusion.2
  358.1 4.3 collective-permute-start.71
  362.5 4.6 collective-permute-done.51
  369.7 1.7 collective-permute-start.50
  371.4 7.7 %input_product.1 = (f32[512,1024]{1,0:T(8,128)S(1)}, bf16[512,1024]{1,0:T(8,128)(2,1)}) custom-call(s32[9]{0:T(128)S(1)} %stack.163.place_ref, bf16[1024,512]{1,0:T(8,128)(2,1)S(1)} %get-tuple-element.109.q_ref, bf16[1024,512]{1,0:T(8,128)(2,1)S(1)} %get-tuple-element.110.k_ref, bf16[1024,512]{1,0:T(8,128)(2,1)S(1)} %copy-done.61, ...), custom_call_target="tpu_custom_call" | custom-call | flops 6442450944 | bytes 16777216 | tf_op jit(solution)/shard_map/input_product/pallas_call | solution.py:721
  379.5 3.0 add_convert_fusion.3
  385.2 2.0 collective-permute-start.72
  387.1 6.3 %collective-permute-done.52 = bf16[256,2048]{1,0:T(8,128)(2,1)S(1)} collective-permute-done((bf16[256,2048]{1,0:T(8,128)(2,1)}, bf16[256,2048]{1,0:T(8,128)(2,1)S(1)}, u32[]{:S(2)}, u32[]{:S(2)}) %collective-permute-start.52) | collective-permute-done | bytes 1048608 | tf_op jit(solution)/shard_map/ppermute | solution.py:859
  395.6 2.3 collective-permute-start.63
  398.8 2.2 copy-done.5
  401.0 1.6 copy-done.9
  402.6 2.8 input_gradient_rows.1
  406.1 3.8 collective-permute-done.69
  411.8 1.9 add_convert_fusion
  413.7 7.1 %collective-permute-done.63 = bf16[256,2048]{1,0:T(8,128)(2,1)} collective-permute-done((bf16[256,2048]{1,0:T(8,128)(2,1)}, bf16[256,2048]{1,0:T(8,128)(2,1)}, u32[]{:S(2)}, u32[]{:S(2)}) %collective-permute-start.63) | collective-permute-done | bytes 1048608 | tf_op jit(solution)/shard_map/ppermute | solution.py:919
  422.1 2.0 add_convert_fusion.7
  425.0 6.9 %collective-permute-done.62 = bf16[256,1024]{1,0:T(8,128)(2,1)S(1)} collective-permute-done((bf16[256,1024]{1,0:T(8,128)(2,1)S(1)}, bf16[256,1024]{1,0:T(8,128)(2,1)S(1)}, u32[]{:S(2)}, u32[]{:S(2)}) %collective-permute-start.62) | collective-permute-done | bytes 524320 | tf_op jit(solution)/shard_map/ppermute | solution.py:944
  438.0 11.1 %collective-permute-done.73 = bf16[2,256,1024]{2,1,0:T(8,128)(2,1)S(1)} collective-permute-done((bf16[2,256,1024]{2,1,0:T(8,128)(2,1)S(1)}, bf16[2,256,1024]{2,1,0:T(8,128)(2,1)S(1)}, u32[]{:S(2)}, u32[]{:S(2)}) %collective-permute-start.73) | collective-permute-done | bytes 1048608 | tf_op jit(solution)/shard_map/ppermute | solution.py:923
  452.5 5.9 %collective-permute-done.57.refs_6_ = bf16[256,1024]{1,0:T(8,128)(2,1)S(1)} collective-permute-done((bf16[256,1024]{1,0:T(8,128)(2,1)S(1)}, bf16[256,1024]{1,0:T(8,128)(2,1)S(1)}, u32[]{:S(2)}, u32[]{:S(2)}) %collective-permute-start.57) | collective-permute-done | bytes 524320 | tf_op jit(solution)/shard_map/ppermute | solution.py:859
  458.4 3.0 collective-permute-done.58.refs_7_
  462.9 1.5 maximum_convert_fusion.1
  464.4 24.6 %collective-permute-done.65 = bf16[256,2048]{1,0:T(8,128)(2,1)S(1)} collective-permute-done((bf16[256,2048]{1,0:T(8,128)(2,1)S(1)}, bf16[256,2048]{1,0:T(8,128)(2,1)S(1)}, u32[]{:S(2)}, u32[]{:S(2)}) %collective-permute-start.65) | collective-permute-done | bytes 1048608 | tf_op jit(solution)/shard_map/ppermute | solution.py:923
  489.3 2.4 convert_multiply_fusion
  494.0 2.3 convert_multiply_fusion.6
  (373 shorter events, 98.1 us)
Async XLA Ops:
  3.1 20.5 %collective-permute-start.1 = (bf16[256,1024]{1,0:T(8,128)(2,1)}, bf16[256,1024]{1,0:T(8,128)(2,1)S(1)}, u32[]{:S(2)}, u32[]{:S(2)}) collective-permute-start(bf16[256,1024]{1,0:T(8,128)(2,1)} %get-tuple-element.191), channel_id=1, source_target_pairs={{0,8},{1,24},{2,10},{3,26},{4,12},{5,28},{6,14},{7,30},{8,0},{9,16... | collective-permute-start | bytes 1572872 | tf_op jit(solution)/shard_map/ppermute | solution.py:944
  17.0 16.2 %collective-permute-start = (bf16[256,1024]{1,0:T(8,128)(2,1)}, bf16[256,1024]{1,0:T(8,128)(2,1)S(1)}, u32[]{:S(2)}, u32[]{:S(2)}) collective-permute-start(bf16[256,1024]{1,0:T(8,128)(2,1)} %get-tuple-element.192), channel_id=1, source_target_pairs={{0,0},{1,16},{2,2},{3,18},{4,4},{5,20},{6,6},{7,22},{8,8},{9,24},{... | collective-permute-start | bytes 1572872 | tf_op jit(solution)/shard_map/ppermute | solution.py:944
  23.1 16.3 %collective-permute-start.8 = (bf16[128,1536]{1,0:T(8,128)(2,1)S(1)}, bf16[128,1536]{1,0:T(8,128)(2,1)}, u32[]{:S(2)}, u32[]{:S(2)}) collective-permute-start(bf16[128,1536]{1,0:T(8,128)(2,1)S(1)} %collective-permute-done.4.refs_1_), channel_id=1, source_target_pairs={{0,4},{1,5},{2,6},{3,7},{4,0},{5,1},{6,2},{7,3},{8,12},{9,13},{10,... | collective-permute-start | bytes 1179656 | tf_op jit(solution)/shard_map/ppermute | solution.py:859
  23.6 20.3 %collective-permute-start.3 = (bf16[256,1024]{1,0:T(8,128)(2,1)S(1)}, bf16[256,1024]{1,0:T(8,128)(2,1)S(1)}, u32[]{:S(2)}, u32[]{:S(2)}) collective-permute-start(bf16[256,1024]{1,0:T(8,128)(2,1)S(1)} %collective-permute-done.1.refs_1_), channel_id=1, source_target_pairs={{0,1},{1,0},{2,3},{3,2},{4,5},{5,4},{6,7},{7,6},{8,9},{9,8},{10,11... | collective-permute-start | bytes 1572872 | tf_op jit(solution)/shard_map/ppermute | solution.py:856
  33.2 21.3 %collective-permute-start.2 = (bf16[256,1024]{1,0:T(8,128)(2,1)S(1)}, bf16[256,1024]{1,0:T(8,128)(2,1)S(1)}, u32[]{:S(2)}, u32[]{:S(2)}) collective-permute-start(bf16[256,1024]{1,0:T(8,128)(2,1)S(1)} %collective-permute-done.refs_0_), channel_id=1, source_target_pairs={{0,1},{1,0},{2,3},{3,2},{4,5},{5,4},{6,7},{7,6},{8,9},{9,8},{10,11... | collective-permute-start | bytes 1572872 | tf_op jit(solution)/shard_map/ppermute | solution.py:856
  33.3 27.4 %collective-permute-start.9 = (bf16[128,1536]{1,0:T(8,128)(2,1)}, bf16[128,1536]{1,0:T(8,128)(2,1)}, u32[]{:S(2)}, u32[]{:S(2)}) collective-permute-start(bf16[128,1536]{1,0:T(8,128)(2,1)} %collective-permute-done.5.refs_2_), channel_id=1, source_target_pairs={{0,4},{1,5},{2,6},{3,7},{4,0},{5,1},{6,2},{7,3},{8,12},{9,13},{10,... | collective-permute-start | bytes 1179656 | tf_op jit(solution)/shard_map/ppermute | solution.py:859
  39.4 23.9 %collective-permute-start.10 = (bf16[128,1536]{1,0:T(8,128)(2,1)}, bf16[128,1536]{1,0:T(8,128)(2,1)}, u32[]{:S(2)}, u32[]{:S(2)}) collective-permute-start(bf16[128,1536]{1,0:T(8,128)(2,1)} %collective-permute-done.8.refs_5_), channel_id=1, source_target_pairs={{0,2},{1,3},{2,0},{3,1},{4,6},{5,7},{6,4},{7,5},{8,10},{9,11},{10,... | collective-permute-start | bytes 1179656 | tf_op jit(solution)/shard_map/ppermute | solution.py:859
  42.4 18.9 %collective-permute-start.12 = (bf16[128,512]{1,0:T(8,128)(2,1)S(1)}, bf16[128,512]{1,0:T(8,128)(2,1)S(1)}, u32[]{:S(2)}, u32[]{:S(2)}) collective-permute-start(bf16[128,512]{1,0:T(8,128)(2,1)S(1)} %get-tuple-element.81.refs_0_), channel_id=1, source_target_pairs={{0,2},{1,3},{2,0},{3,1},{4,6},{5,7},{6,4},{7,5},{8,10},{9,11},{10,... | collective-permute-start | bytes 393224 | tf_op jit(solution)/shard_map/ppermute | solution.py:859
  43.9 17.9 %collective-permute-start.15 = (bf16[128,512]{1,0:T(8,128)(2,1)S(1)}, bf16[128,512]{1,0:T(8,128)(2,1)}, u32[]{:S(2)}, u32[]{:S(2)}) collective-permute-start(bf16[128,512]{1,0:T(8,128)(2,1)S(1)} %collective-permute-done.11.refs_1_), channel_id=1, source_target_pairs={{0,4},{1,5},{2,6},{3,7},{4,0},{5,1},{6,2},{7,3},{8,12},{9,13},{10,... | collective-permute-start | bytes 393224 | tf_op jit(solution)/shard_map/ppermute | solution.py:859
  55.4 46.2 %collective-permute-start.24 = (bf16[2,128,1024]{2,1,0:T(8,128)(2,1)}, bf16[2,128,1024]{2,1,0:T(8,128)(2,1)S(1)}, u32[]{:S(2)}, u32[]{:S(2)}) collective-permute-start(bf16[2,128,1024]{2,1,0:T(8,128)(2,1)} %get-tuple-element.92), channel_id=1, source_target_pairs={{0,1},{1,0},{2,3},{3,2},{4,5},{5,4},{6,7},{7,6},{8,9},{9,8},{10,11... | collective-permute-start | bytes 1572872 | tf_op jit(solution)/shard_map/ppermute | solution.py:856
  60.7 34.7 %collective-permute-start.14 = (bf16[128,512]{1,0:T(8,128)(2,1)S(1)}, bf16[128,512]{1,0:T(8,128)(2,1)S(1)}, u32[]{:S(2)}, u32[]{:S(2)}) collective-permute-start(bf16[128,512]{1,0:T(8,128)(2,1)S(1)} %get-tuple-element.81.refs_0_), channel_id=1, source_target_pairs={{0,4},{1,5},{2,6},{3,7},{4,0},{5,1},{6,2},{7,3},{8,12},{9,13},{10,... | collective-permute-start | bytes 393224 | tf_op jit(solution)/shard_map/ppermute | solution.py:859
  61.2 34.2 %collective-permute-start.13 = (bf16[128,512]{1,0:T(8,128)(2,1)S(1)}, bf16[128,512]{1,0:T(8,128)(2,1)S(1)}, u32[]{:S(2)}, u32[]{:S(2)}) collective-permute-start(bf16[128,512]{1,0:T(8,128)(2,1)S(1)} %collective-permute-done.11.refs_1_), channel_id=1, source_target_pairs={{0,2},{1,3},{2,0},{3,1},{4,6},{5,7},{6,4},{7,5},{8,10},{9,11},{10,... | collective-permute-start | bytes 393224 | tf_op jit(solution)/shard_map/ppermute | solution.py:859
  61.8 33.6 %collective-permute-start.16 = (bf16[128,512]{1,0:T(8,128)(2,1)S(1)}, bf16[128,512]{1,0:T(8,128)(2,1)S(1)}, u32[]{:S(2)}, u32[]{:S(2)}) collective-permute-start(bf16[128,512]{1,0:T(8,128)(2,1)S(1)} %collective-permute-done.12.refs_2_), channel_id=1, source_target_pairs={{0,4},{1,5},{2,6},{3,7},{4,0},{5,1},{6,2},{7,3},{8,12},{9,13},{10,... | collective-permute-start | bytes 393224 | tf_op jit(solution)/shard_map/ppermute | solution.py:859
  63.3 32.1 %collective-permute-start.17 = (bf16[128,512]{1,0:T(8,128)(2,1)}, bf16[128,512]{1,0:T(8,128)(2,1)S(1)}, u32[]{:S(2)}, u32[]{:S(2)}) collective-permute-start(bf16[128,512]{1,0:T(8,128)(2,1)} %collective-permute-done.15.refs_5_), channel_id=1, source_target_pairs={{0,2},{1,3},{2,0},{3,1},{4,6},{5,7},{6,4},{7,5},{8,10},{9,11},{10,... | collective-permute-start | bytes 393224 | tf_op jit(solution)/shard_map/ppermute | solution.py:859
  100.4 40.7 %collective-permute-start.18 = (bf16[1024,1024]{1,0:T(8,128)(2,1)S(1)}, bf16[1024,1024]{1,0:T(8,128)(2,1)S(1)}, u32[]{:S(2)}, u32[]{:S(2)}) collective-permute-start(bf16[1024,1024]{1,0:T(8,128)(2,1)S(1)} %attended_product.1.mine_ref), channel_id=1, source_target_pairs={{0,1},{1,0},{2,3},{3,2},{4,5},{5,4},{6,7},{7,6},{8,9},{9,8},{10,11... | collective-permute-start | bytes 6291464 | tf_op jit(solution)/shard_map/ppermute | solution.py:856
  100.4 14.8 %collective-permute-start.26 = (bf16[2,128,1024]{2,1,0:T(8,128)(2,1)S(1)}, bf16[2,128,1024]{2,1,0:T(8,128)(2,1)S(1)}, u32[]{:S(2)}, u32[]{:S(2)}) collective-permute-start(bf16[2,128,1024]{2,1,0:T(8,128)(2,1)S(1)} %copy-done.44), channel_id=1, source_target_pairs={{0,4},{1,5},{2,6},{3,7},{4,0},{5,1},{6,2},{7,3},{8,12},{9,13},{10,... | collective-permute-start | bytes 1572872 | tf_op jit(solution)/shard_map/ppermute | solution.py:859
  101.0 15.2 %collective-permute-start.23 = (bf16[2,128,1024]{2,1,0:T(8,128)(2,1)S(1)}, bf16[2,128,1024]{2,1,0:T(8,128)(2,1)S(1)}, u32[]{:S(2)}, u32[]{:S(2)}) collective-permute-start(bf16[2,128,1024]{2,1,0:T(8,128)(2,1)S(1)} %copy-done.44), channel_id=1, source_target_pairs={{0,2},{1,3},{2,0},{3,1},{4,6},{5,7},{6,4},{7,5},{8,10},{9,11},{10,... | collective-permute-start | bytes 1572872 | tf_op jit(solution)/shard_map/ppermute | solution.py:859
  101.6 24.5 %collective-permute-start.27 = (bf16[2,128,1024]{2,1,0:T(8,128)(2,1)S(1)}, bf16[2,128,1024]{2,1,0:T(8,128)(2,1)S(1)}, u32[]{:S(2)}, u32[]{:S(2)}) collective-permute-start(bf16[2,128,1024]{2,1,0:T(8,128)(2,1)S(1)} %collective-permute-done.24.refs_1_), channel_id=1, source_target_pairs={{0,4},{1,5},{2,6},{3,7},{4,0},{5,1},{6,2},{7,3},{8,12},{9,13},{10,... | collective-permute-start | bytes 1572872 | tf_op jit(solution)/shard_map/ppermute | solution.py:859
  103.2 22.9 %collective-permute-start.20 = (bf16[256,1024]{1,0:T(8,128)(2,1)S(1)}, bf16[256,1024]{1,0:T(8,128)(2,1)S(1)}, u32[]{:S(2)}, u32[]{:S(2)}) collective-permute-start(bf16[256,1024]{1,0:T(8,128)(2,1)S(1)} %get-tuple-element.189), channel_id=1, source_target_pairs={{0,8},{1,24},{2,10},{3,26},{4,12},{5,28},{6,14},{7,30},{8,0},{9,16... | collective-permute-start | bytes 1572872 | tf_op jit(solution)/shard_map/ppermute | solution.py:944
  116.2 16.0 %collective-permute-start.25 = (bf16[2,128,1024]{2,1,0:T(8,128)(2,1)S(1)}, bf16[2,128,1024]{2,1,0:T(8,128)(2,1)S(1)}, u32[]{:S(2)}, u32[]{:S(2)}) collective-permute-start(bf16[2,128,1024]{2,1,0:T(8,128)(2,1)S(1)} %collective-permute-done.24.refs_1_), channel_id=1, source_target_pairs={{0,2},{1,3},{2,0},{3,1},{4,6},{5,7},{6,4},{7,5},{8,10},{9,11},{10,... | collective-permute-start | bytes 1572872 | tf_op jit(solution)/shard_map/ppermute | solution.py:859
  132.3 16.9 %collective-permute-start.29 = (bf16[2,128,1024]{2,1,0:T(8,128)(2,1)S(1)}, bf16[2,128,1024]{2,1,0:T(8,128)(2,1)S(1)}, u32[]{:S(2)}, u32[]{:S(2)}) collective-permute-start(bf16[2,128,1024]{2,1,0:T(8,128)(2,1)S(1)} %copy-done.42), channel_id=1, source_target_pairs={{0,2},{1,3},{2,0},{3,1},{4,6},{5,7},{6,4},{7,5},{8,10},{9,11},{10,... | collective-permute-start | bytes 1572872 | tf_op jit(solution)/shard_map/ppermute | solution.py:859
  132.9 15.1 %collective-permute-start.35 = (bf16[2,128,1024]{2,1,0:T(8,128)(2,1)S(1)}, bf16[2,128,1024]{2,1,0:T(8,128)(2,1)S(1)}, u32[]{:S(2)}, u32[]{:S(2)}) collective-permute-start(bf16[2,128,1024]{2,1,0:T(8,128)(2,1)S(1)} %collective-permute-done.23.refs_2_), channel_id=1, source_target_pairs={{0,4},{1,5},{2,6},{3,7},{4,0},{5,1},{6,2},{7,3},{8,12},{9,13},{10,... | collective-permute-start | bytes 1572872 | tf_op jit(solution)/shard_map/ppermute | solution.py:859
  134.0 25.1 %collective-permute-start.32 = (bf16[2,128,1024]{2,1,0:T(8,128)(2,1)S(1)}, bf16[2,128,1024]{2,1,0:T(8,128)(2,1)}, u32[]{:S(2)}, u32[]{:S(2)}) collective-permute-start(bf16[2,128,1024]{2,1,0:T(8,128)(2,1)S(1)} %collective-permute-done.28.refs_1_), channel_id=1, source_target_pairs={{0,4},{1,5},{2,6},{3,7},{4,0},{5,1},{6,2},{7,3},{8,12},{9,13},{10,... | collective-permute-start | bytes 1572872 | tf_op jit(solution)/shard_map/ppermute | solution.py:859
  134.9 25.6 %collective-permute-start.36 = (bf16[2,128,1024]{2,1,0:T(8,128)(2,1)S(1)}, bf16[2,128,1024]{2,1,0:T(8,128)(2,1)S(1)}, u32[]{:S(2)}, u32[]{:S(2)}) collective-permute-start(bf16[2,128,1024]{2,1,0:T(8,128)(2,1)S(1)} %collective-permute-done.27.refs_5_), channel_id=1, source_target_pairs={{0,2},{1,3},{2,0},{3,1},{4,6},{5,7},{6,4},{7,5},{8,10},{9,11},{10,... | collective-permute-start | bytes 1572872 | tf_op jit(solution)/shard_map/ppermute | solution.py:859
  141.1 46.8 %collective-permute-start.31 = (bf16[2,128,1024]{2,1,0:T(8,128)(2,1)S(1)}, bf16[2,128,1024]{2,1,0:T(8,128)(2,1)S(1)}, u32[]{:S(2)}, u32[]{:S(2)}) collective-permute-start(bf16[2,128,1024]{2,1,0:T(8,128)(2,1)S(1)} %copy-done.42), channel_id=1, source_target_pairs={{0,4},{1,5},{2,6},{3,7},{4,0},{5,1},{6,2},{7,3},{8,12},{9,13},{10,... | collective-permute-start | bytes 1572872 | tf_op jit(solution)/shard_map/ppermute | solution.py:859
  148.0 40.0 %collective-permute-start.30 = (bf16[2,128,1024]{2,1,0:T(8,128)(2,1)S(1)}, bf16[2,128,1024]{2,1,0:T(8,128)(2,1)S(1)}, u32[]{:S(2)}, u32[]{:S(2)}) collective-permute-start(bf16[2,128,1024]{2,1,0:T(8,128)(2,1)S(1)} %collective-permute-done.28.refs_1_), channel_id=1, source_target_pairs={{0,2},{1,3},{2,0},{3,1},{4,6},{5,7},{6,4},{7,5},{8,10},{9,11},{10,... | collective-permute-start | bytes 1572872 | tf_op jit(solution)/shard_map/ppermute | solution.py:859
  149.2 38.7 %collective-permute-start.33 = (bf16[2,128,1024]{2,1,0:T(8,128)(2,1)S(1)}, bf16[2,128,1024]{2,1,0:T(8,128)(2,1)S(1)}, u32[]{:S(2)}, u32[]{:S(2)}) collective-permute-start(bf16[2,128,1024]{2,1,0:T(8,128)(2,1)S(1)} %collective-permute-done.29.refs_2_), channel_id=1, source_target_pairs={{0,4},{1,5},{2,6},{3,7},{4,0},{5,1},{6,2},{7,3},{8,12},{9,13},{10,... | collective-permute-start | bytes 1572872 | tf_op jit(solution)/shard_map/ppermute | solution.py:859
  159.1 28.9 %collective-permute-start.34 = (bf16[2,128,1024]{2,1,0:T(8,128)(2,1)}, bf16[2,128,1024]{2,1,0:T(8,128)(2,1)}, u32[]{:S(2)}, u32[]{:S(2)}) collective-permute-start(bf16[2,128,1024]{2,1,0:T(8,128)(2,1)} %collective-permute-done.32.refs_5_), channel_id=1, source_target_pairs={{0,2},{1,3},{2,0},{3,1},{4,6},{5,7},{6,4},{7,5},{8,10},{9,11},{10,... | collective-permute-start | bytes 1572872 | tf_op jit(solution)/shard_map/ppermute | solution.py:859
  216.8 46.1 %collective-permute-start.40 = (bf16[1024,1024]{1,0:T(8,128)(2,1)}, bf16[1024,1024]{1,0:T(8,128)(2,1)}, u32[]{:S(2)}, u32[]{:S(2)}) collective-permute-start(bf16[1024,1024]{1,0:T(8,128)(2,1)} %get-tuple-element.104.mine_ref), channel_id=1, source_target_pairs={{0,1},{1,0},{2,3},{3,2},{4,5},{5,4},{6,7},{7,6},{8,9},{9,8},{10,11... | collective-permute-start | bytes 6291464 | tf_op jit(solution)/shard_map/ppermute | solution.py:856
  216.8 14.4 %collective-permute-start.41 = (bf16[2,128,1024]{2,1,0:T(8,128)(2,1)S(1)}, bf16[2,128,1024]{2,1,0:T(8,128)(2,1)}, u32[]{:S(2)}, u32[]{:S(2)}) collective-permute-start(bf16[2,128,1024]{2,1,0:T(8,128)(2,1)S(1)} %copy-done.83), channel_id=1, source_target_pairs={{0,4},{1,5},{2,6},{3,7},{4,0},{5,1},{6,2},{7,3},{8,12},{9,13},{10,... | collective-permute-start | bytes 1572872 | tf_op jit(solution)/shard_map/ppermute | solution.py:859
  218.1 14.1 %collective-permute-start.43 = (bf16[2,128,1024]{2,1,0:T(8,128)(2,1)S(1)}, bf16[2,128,1024]{2,1,0:T(8,128)(2,1)}, u32[]{:S(2)}, u32[]{:S(2)}) collective-permute-start(bf16[2,128,1024]{2,1,0:T(8,128)(2,1)S(1)} %copy-done.82), channel_id=1, source_target_pairs={{0,2},{1,3},{2,0},{3,1},{4,6},{5,7},{6,4},{7,5},{8,10},{9,11},{10,... | collective-permute-start | bytes 1572872 | tf_op jit(solution)/shard_map/ppermute | solution.py:859
  218.5 27.6 %collective-permute-start.37 = (bf16[512,1024]{1,0:T(8,128)(2,1)}, bf16[512,1024]{1,0:T(8,128)(2,1)}, u32[]{:S(2)}, u32[]{:S(2)}) collective-permute-start(bf16[512,1024]{1,0:T(8,128)(2,1)} %get-tuple-element.100), channel_id=1, source_target_pairs={{0,1},{1,0},{2,3},{3,2},{4,5},{5,4},{6,7},{7,6},{8,9},{9,8},{10,11... | collective-permute-start | bytes 3145736 | tf_op jit(solution)/shard_map/ppermute | solution.py:856
  236.0 24.7 %collective-permute-start.44 = (bf16[2,256,1024]{2,1,0:T(8,128)(2,1)}, bf16[2,256,1024]{2,1,0:T(8,128)(2,1)}, u32[]{:S(2)}, u32[]{:S(2)}) collective-permute-start(bf16[2,256,1024]{2,1,0:T(8,128)(2,1)} %get-tuple-element.173), channel_id=1, source_target_pairs={{0,4},{1,5},{2,6},{3,7},{4,0},{5,1},{6,2},{7,3},{8,12},{9,13},{10,... | collective-permute-start | bytes 3145736 | tf_op jit(solution)/shard_map/ppermute | solution.py:859
  236.8 24.4 %collective-permute-start.42 = (bf16[2,256,1024]{2,1,0:T(8,128)(2,1)}, bf16[2,256,1024]{2,1,0:T(8,128)(2,1)}, u32[]{:S(2)}, u32[]{:S(2)}) collective-permute-start(bf16[2,256,1024]{2,1,0:T(8,128)(2,1)} %get-tuple-element.174), channel_id=1, source_target_pairs={{0,2},{1,3},{2,0},{3,1},{4,6},{5,7},{6,4},{7,5},{8,10},{9,11},{10,... | collective-permute-start | bytes 3145736 | tf_op jit(solution)/shard_map/ppermute | solution.py:859
  251.1 72.9 %collective-permute-start.38 = (bf16[256,1024]{1,0:T(8,128)(2,1)S(1)}, bf16[256,1024]{1,0:T(8,128)(2,1)S(1)}, u32[]{:S(2)}, u32[]{:S(2)}) collective-permute-start(bf16[256,1024]{1,0:T(8,128)(2,1)S(1)} %get-tuple-element.102), channel_id=1, source_target_pairs={{0,0},{16,1},{2,2},{18,3},{4,4},{20,5},{6,6},{22,7},{8,8},{24,9},{... | collective-permute-start | bytes 1572872 | tf_op jit(solution)/shard_map/ppermute | solution.py:944
  251.8 73.0 %collective-permute-start.39 = (bf16[256,1024]{1,0:T(8,128)(2,1)S(1)}, bf16[256,1024]{1,0:T(8,128)(2,1)S(1)}, u32[]{:S(2)}, u32[]{:S(2)}) collective-permute-start(bf16[256,1024]{1,0:T(8,128)(2,1)S(1)} %get-tuple-element.103), channel_id=1, source_target_pairs={{8,0},{24,1},{10,2},{26,3},{12,4},{28,5},{14,6},{30,7},{0,8},{16,9... | collective-permute-start | bytes 1572872 | tf_op jit(solution)/shard_map/ppermute | solution.py:944
  261.3 66.5 %collective-permute-start.45 = (bf16[2,128,1024]{2,1,0:T(8,128)(2,1)S(1)}, bf16[2,128,1024]{2,1,0:T(8,128)(2,1)S(1)}, u32[]{:S(2)}, u32[]{:S(2)}) collective-permute-start(bf16[2,128,1024]{2,1,0:T(8,128)(2,1)S(1)} %copy-done.74), channel_id=1, source_target_pairs={{0,4},{1,5},{2,6},{3,7},{4,0},{5,1},{6,2},{7,3},{8,12},{9,13},{10,... | collective-permute-start | bytes 1572872 | tf_op jit(solution)/shard_map/ppermute | solution.py:859
  262.4 65.3 %collective-permute-start.47 = (bf16[2,128,1024]{2,1,0:T(8,128)(2,1)S(1)}, bf16[2,128,1024]{2,1,0:T(8,128)(2,1)S(1)}, u32[]{:S(2)}, u32[]{:S(2)}) collective-permute-start(bf16[2,128,1024]{2,1,0:T(8,128)(2,1)S(1)} %copy-done.73), channel_id=1, source_target_pairs={{0,2},{1,3},{2,0},{3,1},{4,6},{5,7},{6,4},{7,5},{8,10},{9,11},{10,... | collective-permute-start | bytes 1572872 | tf_op jit(solution)/shard_map/ppermute | solution.py:859
  322.0 32.2 %collective-permute-start.67 = (bf16[2,256,1024]{2,1,0:T(8,128)(2,1)S(1)}, bf16[2,256,1024]{2,1,0:T(8,128)(2,1)S(1)}, u32[]{:S(2)}, u32[]{:S(2)}) collective-permute-start(bf16[2,256,1024]{2,1,0:T(8,128)(2,1)S(1)} %add_convert_fusion.5), channel_id=1, source_target_pairs={{0,8},{24,16},{1,9},{25,17},{2,10},{26,18},{3,11},{27,19},{4,12},{... | collective-permute-start | bytes 3145736 | tf_op jit(solution)/shard_map/ppermute | solution.py:919
  327.8 15.9 %collective-permute-start.77 = (f32[8,33]{1,0:T(8,128)S(1)}, f32[8,33]{1,0:T(8,128)S(1)}, u32[]{:S(2)}, u32[]{:S(2)}) collective-permute-start(f32[8,33]{1,0:T(8,128)S(1)} %pad_maximum_fusion.8), channel_id=1, source_target_pairs={{0,8},{8,0},{16,24},{24,16},{1,9},{9,1},{17,25},{25,17},{2,10},{10... | collective-permute-start | bytes 3176 | tf_op jit(solution)/shard_map/ppermute | solution.py:1172
  329.7 23.0 %collective-permute-start.48 = (bf16[2,256,1024]{2,1,0:T(8,128)(2,1)}, bf16[2,256,1024]{2,1,0:T(8,128)(2,1)S(1)}, u32[]{:S(2)}, u32[]{:S(2)}) collective-permute-start(bf16[2,256,1024]{2,1,0:T(8,128)(2,1)} %get-tuple-element.171), channel_id=1, source_target_pairs={{0,4},{1,5},{2,6},{3,7},{4,0},{5,1},{6,2},{7,3},{8,12},{9,13},{10,... | collective-permute-start | bytes 3145736 | tf_op jit(solution)/shard_map/ppermute | solution.py:859
  330.5 22.2 %collective-permute-start.46 = (bf16[2,256,1024]{2,1,0:T(8,128)(2,1)}, bf16[2,256,1024]{2,1,0:T(8,128)(2,1)}, u32[]{:S(2)}, u32[]{:S(2)}) collective-permute-start(bf16[2,256,1024]{2,1,0:T(8,128)(2,1)} %get-tuple-element.172), channel_id=1, source_target_pairs={{0,2},{1,3},{2,0},{3,1},{4,6},{5,7},{6,4},{7,5},{8,10},{9,11},{10,... | collective-permute-start | bytes 3145736 | tf_op jit(solution)/shard_map/ppermute | solution.py:859
  352.7 26.5 %collective-permute-start.79 = (f32[8,33]{1,0:T(8,128)S(1)}, f32[8,33]{1,0:T(8,128)S(1)}, u32[]{:S(2)}, u32[]{:S(2)}) collective-permute-start(f32[8,33]{1,0:T(8,128)S(1)} %pad_maximum_fusion.10), channel_id=1, source_target_pairs={{0,1},{1,0},{2,3},{3,2},{4,5},{5,4},{6,7},{7,6},{8,9},{9,8},{10,11... | collective-permute-start | bytes 3176 | tf_op jit(solution)/shard_map/ppermute | solution.py:856
  352.7 14.3 %collective-permute-start.51 = (bf16[128,2048]{1,0:T(8,128)(2,1)S(1)}, bf16[128,2048]{1,0:T(8,128)(2,1)S(1)}, u32[]{:S(2)}, u32[]{:S(2)}) collective-permute-start(bf16[128,2048]{1,0:T(8,128)(2,1)S(1)} %get-tuple-element.124), channel_id=1, source_target_pairs={{0,2},{1,3},{2,0},{3,1},{4,6},{5,7},{6,4},{7,5},{8,10},{9,11},{10,... | collective-permute-start | bytes 1572872 | tf_op jit(solution)/shard_map/ppermute | solution.py:859
  353.3 14.0 %collective-permute-start.49 = (bf16[128,2048]{1,0:T(8,128)(2,1)S(1)}, bf16[128,2048]{1,0:T(8,128)(2,1)S(1)}, u32[]{:S(2)}, u32[]{:S(2)}) collective-permute-start(bf16[128,2048]{1,0:T(8,128)(2,1)S(1)} %get-tuple-element.122), channel_id=1, source_target_pairs={{0,4},{1,5},{2,6},{3,7},{4,0},{5,1},{6,2},{7,3},{8,12},{9,13},{10,... | collective-permute-start | bytes 1572872 | tf_op jit(solution)/shard_map/ppermute | solution.py:859
  354.6 24.9 %collective-permute-start.68 = (bf16[2,256,1024]{2,1,0:T(8,128)(2,1)S(1)}, bf16[2,256,1024]{2,1,0:T(8,128)(2,1)}, u32[]{:S(2)}, u32[]{:S(2)}) collective-permute-start(bf16[2,256,1024]{2,1,0:T(8,128)(2,1)S(1)} %add_convert_fusion.4), channel_id=1, source_target_pairs={{8,16},{16,8},{9,17},{17,9},{10,18},{18,10},{11,19},{19,11},{12,20... | collective-permute-start | bytes 3145736 | tf_op jit(solution)/shard_map/ppermute | solution.py:921
  358.1 25.6 %collective-permute-start.71 = (bf16[2,256,1024]{2,1,0:T(8,128)(2,1)S(1)}, bf16[2,256,1024]{2,1,0:T(8,128)(2,1)S(1)}, u32[]{:S(2)}, u32[]{:S(2)}) collective-permute-start(bf16[2,256,1024]{2,1,0:T(8,128)(2,1)S(1)} %add_convert_fusion.2), channel_id=1, source_target_pairs={{0,8},{24,16},{1,9},{25,17},{2,10},{26,18},{3,11},{27,19},{4,12},{... | collective-permute-start | bytes 3145736 | tf_op jit(solution)/shard_map/ppermute | solution.py:919
  368.7 24.7 %collective-permute-start.52 = (bf16[256,2048]{1,0:T(8,128)(2,1)}, bf16[256,2048]{1,0:T(8,128)(2,1)S(1)}, u32[]{:S(2)}, u32[]{:S(2)}) collective-permute-start(bf16[256,2048]{1,0:T(8,128)(2,1)} %get-tuple-element.169), channel_id=1, source_target_pairs={{0,4},{1,5},{2,6},{3,7},{4,0},{5,1},{6,2},{7,3},{8,12},{9,13},{10,... | collective-permute-start | bytes 3145736 | tf_op jit(solution)/shard_map/ppermute | solution.py:859
  369.7 24.4 %collective-permute-start.50 = (bf16[256,2048]{1,0:T(8,128)(2,1)S(1)}, bf16[256,2048]{1,0:T(8,128)(2,1)S(1)}, u32[]{:S(2)}, u32[]{:S(2)}) collective-permute-start(bf16[256,2048]{1,0:T(8,128)(2,1)S(1)} %get-tuple-element.170), channel_id=1, source_target_pairs={{0,2},{1,3},{2,0},{3,1},{4,6},{5,7},{6,4},{7,5},{8,10},{9,11},{10,... | collective-permute-start | bytes 3145736 | tf_op jit(solution)/shard_map/ppermute | solution.py:859
  379.1 19.6 %collective-permute-start.60 = (bf16[512,1024]{1,0:T(8,128)(2,1)}, bf16[512,1024]{1,0:T(8,128)(2,1)}, u32[]{:S(2)}, u32[]{:S(2)}) collective-permute-start(bf16[512,1024]{1,0:T(8,128)(2,1)} %get-tuple-element.130), channel_id=1, source_target_pairs={{0,1},{1,0},{2,3},{3,2},{4,5},{5,4},{6,7},{7,6},{8,9},{9,8},{10,11... | collective-permute-start | bytes 3145736 | tf_op jit(solution)/shard_map/ppermute | solution.py:856
  382.5 27.4 %collective-permute-start.69 = (bf16[2,256,1024]{2,1,0:T(8,128)(2,1)}, bf16[2,256,1024]{2,1,0:T(8,128)(2,1)}, u32[]{:S(2)}, u32[]{:S(2)}) collective-permute-start(bf16[2,256,1024]{2,1,0:T(8,128)(2,1)} %add_convert_fusion.3), channel_id=1, source_target_pairs={{8,0},{16,24},{9,1},{17,25},{10,2},{18,26},{11,3},{19,27},{12,4},{... | collective-permute-start | bytes 3145736 | tf_op jit(solution)/shard_map/ppermute | solution.py:923
  385.2 26.2 %collective-permute-start.72 = (bf16[2,256,1024]{2,1,0:T(8,128)(2,1)}, bf16[2,256,1024]{2,1,0:T(8,128)(2,1)}, u32[]{:S(2)}, u32[]{:S(2)}) collective-permute-start(bf16[2,256,1024]{2,1,0:T(8,128)(2,1)} %add_convert_fusion.1), channel_id=1, source_target_pairs={{8,16},{16,8},{9,17},{17,9},{10,18},{18,10},{11,19},{19,11},{12,20... | collective-permute-start | bytes 3145736 | tf_op jit(solution)/shard_map/ppermute | solution.py:921
  395.6 25.2 %collective-permute-start.63 = (bf16[256,2048]{1,0:T(8,128)(2,1)}, bf16[256,2048]{1,0:T(8,128)(2,1)}, u32[]{:S(2)}, u32[]{:S(2)}) collective-permute-start(bf16[256,2048]{1,0:T(8,128)(2,1)} %add_convert_fusion.8), channel_id=1, source_target_pairs={{0,8},{24,16},{1,9},{25,17},{2,10},{26,18},{3,11},{27,19},{4,12},{... | collective-permute-start | bytes 3145736 | tf_op jit(solution)/shard_map/ppermute | solution.py:919
  405.3 18.8 %collective-permute-start.61 = (bf16[256,1024]{1,0:T(8,128)(2,1)S(1)}, bf16[256,1024]{1,0:T(8,128)(2,1)S(1)}, u32[]{:S(2)}, u32[]{:S(2)}) collective-permute-start(bf16[256,1024]{1,0:T(8,128)(2,1)S(1)} %get-tuple-element.132), channel_id=1, source_target_pairs={{0,0},{16,1},{2,2},{18,3},{4,4},{20,5},{6,6},{22,7},{8,8},{24,9},{... | collective-permute-start | bytes 1572872 | tf_op jit(solution)/shard_map/ppermute | solution.py:944
  406.0 25.9 %collective-permute-start.62 = (bf16[256,1024]{1,0:T(8,128)(2,1)S(1)}, bf16[256,1024]{1,0:T(8,128)(2,1)S(1)}, u32[]{:S(2)}, u32[]{:S(2)}) collective-permute-start(bf16[256,1024]{1,0:T(8,128)(2,1)S(1)} %get-tuple-element.133), channel_id=1, source_target_pairs={{8,0},{24,1},{10,2},{26,3},{12,4},{28,5},{14,6},{30,7},{0,8},{16,9... | collective-permute-start | bytes 1572872 | tf_op jit(solution)/shard_map/ppermute | solution.py:944
  411.3 22.9 %collective-permute-start.70 = (bf16[2,128,1024]{2,1,0:T(8,128)(2,1)S(1)}, bf16[2,128,1024]{2,1,0:T(8,128)(2,1)S(1)}, u32[]{:S(2)}, u32[]{:S(2)}) collective-permute-start(bf16[2,128,1024]{2,1,0:T(8,128)(2,1)S(1)} %constant_dynamic-slice_fusion.1), channel_id=1, source_target_pairs={{0,1},{1,0},{2,3},{3,2},{4,5},{5,4},{6,7},{7,6},{8,9},{9,8},{10,11... | collective-permute-start | bytes 1572872 | tf_op jit(solution)/shard_map/ppermute | solution.py:856
  411.4 23.9 %collective-permute-start.53 = (bf16[256,1024]{1,0:T(8,128)(2,1)S(1)}, bf16[256,1024]{1,0:T(8,128)(2,1)S(1)}, u32[]{:S(2)}, u32[]{:S(2)}) collective-permute-start(bf16[256,1024]{1,0:T(8,128)(2,1)S(1)} %get-tuple-element.125.refs_0_), channel_id=1, source_target_pairs={{0,2},{1,3},{2,0},{3,1},{4,6},{5,7},{6,4},{7,5},{8,10},{9,11},{10,... | collective-permute-start | bytes 1572872 | tf_op jit(solution)/shard_map/ppermute | solution.py:859
  420.8 28.3 %collective-permute-start.73 = (bf16[2,256,1024]{2,1,0:T(8,128)(2,1)S(1)}, bf16[2,256,1024]{2,1,0:T(8,128)(2,1)S(1)}, u32[]{:S(2)}, u32[]{:S(2)}) collective-permute-start(bf16[2,256,1024]{2,1,0:T(8,128)(2,1)S(1)} %add_convert_fusion), channel_id=1, source_target_pairs={{8,0},{16,24},{9,1},{17,25},{10,2},{18,26},{11,3},{19,27},{12,4},{... | collective-permute-start | bytes 3145736 | tf_op jit(solution)/shard_map/ppermute | solution.py:923
  431.9 18.6 %collective-permute-start.64 = (bf16[256,2048]{1,0:T(8,128)(2,1)S(1)}, bf16[256,2048]{1,0:T(8,128)(2,1)S(1)}, u32[]{:S(2)}, u32[]{:S(2)}) collective-permute-start(bf16[256,2048]{1,0:T(8,128)(2,1)S(1)} %add_convert_fusion.7), channel_id=1, source_target_pairs={{8,16},{16,8},{9,17},{17,9},{10,18},{18,10},{11,19},{19,11},{12,20... | collective-permute-start | bytes 3145736 | tf_op jit(solution)/shard_map/ppermute | solution.py:921
  434.2 16.9 %collective-permute-start.55 = (bf16[256,1024]{1,0:T(8,128)(2,1)S(1)}, bf16[256,1024]{1,0:T(8,128)(2,1)S(1)}, u32[]{:S(2)}, u32[]{:S(2)}) collective-permute-start(bf16[256,1024]{1,0:T(8,128)(2,1)S(1)} %get-tuple-element.125.refs_0_), channel_id=1, source_target_pairs={{0,4},{1,5},{2,6},{3,7},{4,0},{5,1},{6,2},{7,3},{8,12},{9,13},{10,... | collective-permute-start | bytes 1572872 | tf_op jit(solution)/shard_map/ppermute | solution.py:859
  435.3 17.1 %collective-permute-start.54 = (bf16[256,1024]{1,0:T(8,128)(2,1)S(1)}, bf16[256,1024]{1,0:T(8,128)(2,1)S(1)}, u32[]{:S(2)}, u32[]{:S(2)}) collective-permute-start(bf16[256,1024]{1,0:T(8,128)(2,1)S(1)} %get-tuple-element.126.refs_1_), channel_id=1, source_target_pairs={{0,2},{1,3},{2,0},{3,1},{4,6},{5,7},{6,4},{7,5},{8,10},{9,11},{10,... | collective-permute-start | bytes 1572872 | tf_op jit(solution)/shard_map/ppermute | solution.py:859
  436.8 21.6 %collective-permute-start.57 = (bf16[256,1024]{1,0:T(8,128)(2,1)S(1)}, bf16[256,1024]{1,0:T(8,128)(2,1)S(1)}, u32[]{:S(2)}, u32[]{:S(2)}) collective-permute-start(bf16[256,1024]{1,0:T(8,128)(2,1)S(1)} %collective-permute-done.53.refs_2_), channel_id=1, source_target_pairs={{0,4},{1,5},{2,6},{3,7},{4,0},{5,1},{6,2},{7,3},{8,12},{9,13},{10,... | collective-permute-start | bytes 1572872 | tf_op jit(solution)/shard_map/ppermute | solution.py:859
  451.1 37.9 %collective-permute-start.65 = (bf16[256,2048]{1,0:T(8,128)(2,1)S(1)}, bf16[256,2048]{1,0:T(8,128)(2,1)S(1)}, u32[]{:S(2)}, u32[]{:S(2)}) collective-permute-start(bf16[256,2048]{1,0:T(8,128)(2,1)S(1)} %add_convert_fusion.6), channel_id=1, source_target_pairs={{8,0},{16,24},{9,1},{17,25},{10,2},{18,26},{11,3},{19,27},{12,4},{... | collective-permute-start | bytes 3145736 | tf_op jit(solution)/shard_map/ppermute | solution.py:923
  462.3 29.3 %collective-permute-start.59 = (bf16[2,256,1024]{2,1,0:T(8,128)(2,1)S(1)}, bf16[2,256,1024]{2,1,0:T(8,128)(2,1)S(1)}, u32[]{:S(2)}, u32[]{:S(2)}) collective-permute-start(bf16[2,256,1024]{2,1,0:T(8,128)(2,1)S(1)} %get-tuple-element.128), channel_id=1, source_target_pairs={{0,1},{1,0},{2,3},{3,2},{4,5},{5,4},{6,7},{7,6},{8,9},{9,8},{10,11... | collective-permute-start | bytes 3145736 | tf_op jit(solution)/shard_map/ppermute | solution.py:856
  (109 other events, 1131.3 us)

commit v3 on v1

v3 whole, which is shorter than its diff:
```python
import functools
import math

import jax
import jax.numpy as jnp
from jax import lax
from jax.experimental import pallas as pl
from jax.experimental.pallas import tpu as pltpu
from jax.sharding import PartitionSpec as P

epsilon = 1e-06
masked = -1e30
tile = 128
half_tile = 64
wide = jnp.float32
low = jnp.bfloat16
anywhere = pl.BlockSpec(memory_space=pl.ANY)
in_vmem = pl.BlockSpec(memory_space=pltpu.VMEM)
in_hbm = pl.BlockSpec(memory_space=pltpu.HBM)


class Steps:
    def __init__(self):
        self.behind = ()

    def wait(self, *arrays):
        self.behind += arrays

    def launch(
        self,
        name,
        kernel,
        operands,
        in_specs,
        out_specs,
        out_shape,
        grid=(1,),
        prefetch=1,
        scratch=(),
        estimate=(0, 1 << 20),
        memory=24,
        stored=(),
    ):
        inputs, idle = len(operands), self.behind

        def run(*refs):
            refs = list(refs)
            mark_ref = refs.pop(inputs + len(idle) + len(out_specs))
            mark_ref[...] = jnp.zeros_like(mark_ref)
            kernel(*refs[:inputs], *refs[inputs + len(idle) :])

        out_specs, out_shape = list(out_specs), list(out_shape)
        outs = pl.pallas_call(
            run,
            grid_spec=pltpu.PrefetchScalarGridSpec(
                num_scalar_prefetch=prefetch,
                grid=grid,
                in_specs=list(in_specs) + [anywhere] * len(idle),
                out_specs=out_specs + [pl.BlockSpec((8, tile), lambda *_: (0, 0))],
                scratch_shapes=list(scratch),
            ),
            out_shape=[
                pltpu.HBM(shape, kind) if number in stored else jax.ShapeDtypeStruct(shape, kind)
                for number, (shape, kind) in enumerate(out_shape + [((8, tile), wide)])
            ],
            compiler_params=pltpu.CompilerParams(vmem_limit_bytes=memory << 20),
            cost_estimate=pl.CostEstimate(
                flops=int(estimate[0]), bytes_accessed=int(estimate[1]), transcendentals=0
            ),
            name=name,
        )(*operands, *idle)
        self.behind = (outs[-1],)
        return outs[:-1]


def dot(left, right, left_dim, right_dim):
    return lax.dot_general(
        left, right, (((left_dim,), (right_dim,)), ((), ())), preferred_element_type=wide
    )


def strip_kernel(line_ref, strip_ref):
    width = line_ref.shape[-1]
    rows = jnp.broadcast_to(line_ref[0], (tile, width))
    strip_ref[0] = pltpu.roll(rows, width - (tile - 1), 1, stride=1, stride_axis=0)


def bias_strips(steps, lines):
    heads, _, width = lines.shape
    return steps.launch(
        "bias_strips",
        strip_kernel,
        [lines],
        [pl.BlockSpec((1, 1, width), lambda h: (h, 0, 0))],
        [pl.BlockSpec((1, tile, width), lambda h: (h, 0, 0))],
        [((heads, tile, width), wide)],
        grid=(heads,),
        prefetch=0,
        memory=16,
        stored=(0,),
        estimate=(0, 8 << 20),
    )[0]


def diagonal_kernel(strip_ref, line_ref):
    strip = strip_ref[0]
    rows = tile
    while rows > 1:
        rows //= 2
        strip = pltpu.roll(strip[:rows], rows, 1) + strip[rows:]
    line_ref[0] = strip


def diagonal_sums(steps, strips):
    heads, _, width = strips.shape
    return steps.launch(
        "diagonal_sums",
        diagonal_kernel,
        [strips],
        [pl.BlockSpec((1, tile, width), lambda h: (h, 0, 0))],
        [pl.BlockSpec((1, 1, width), lambda h: (h, 0, 0))],
        [((heads, 1, width), wide)],
        grid=(heads,),
        prefetch=0,
        memory=16,
        estimate=(0, 2 << 20),
    )[0]


def one_head(block, head, extra=None):
    lane = lax.broadcasted_iota(jnp.int32, block.shape, 1)
    kept = jnp.where((lane >= half_tile) if head else (lane < half_tile), block, 0)
    if extra is None:
        return kept
    return jnp.where(lane == (0 if head else half_tile), extra, kept)


def key_masks(total, length):
    position = lax.broadcasted_iota(jnp.int32, (total, tile), 0)
    return jnp.where(position < length, 0.0, masked).astype(low)


def strip_columns(total, first, width):
    return [
        pl.ds(pl.multiple_of(total - tile - row + first, tile), width)
        for row in range(0, total, tile)
    ]


def add_bias(products, strip_ref, head, columns):
    return jnp.concatenate(
        [
            products[block * tile : (block + 1) * tile] + strip_ref[head, :, where]
            for block, where in enumerate(columns)
        ],
        axis=0,
    )


def forward_kernel(
    length_ref, query_ref, key_ref, value_ref, strip_ref, context_ref, total_ref, top_ref, *, step
):
    length = length_ref[0]
    total = query_ref.shape[0]
    masks = key_masks(total, length)
    ones = jnp.ones((step, tile), low)
    keys = [one_head(key_ref[...], head, masks) for head in (0, 1)]
    values = [one_head(value_ref[...], head).astype(wide).T.astype(low) for head in (0, 1)]

    def body(index, tops):
        first = pl.multiple_of(index * step, step)
        queries = query_ref[pl.ds(first, step), :]
        columns = strip_columns(total, first, step)
        query_okay = first + lax.broadcasted_iota(jnp.int32, (1, step), 1) < length
        context = None
        peaks = []
        for head in (0, 1):
            products = dot(keys[head], one_head(queries, head, ones), 1, 1)
            scores = add_bias(products, strip_ref, head, columns)
            row_max = jnp.max(scores, axis=0, keepdims=True)
            exponent = jnp.exp(scores - row_max)
            summed = jnp.sum(exponent, axis=0, keepdims=True)
            part = dot(values[head], exponent.astype(low), 1, 0) * (1.0 / summed)
            context = part if context is None else context + part
            total_ref[0, head : head + 1, pl.ds(first, step)] = row_max + jnp.log(summed)
            peaks.append(
                jnp.where(query_okay, jnp.max(products, axis=0, keepdims=True), masked)
            )
        context_ref[pl.ds(first, step), :] = context.T.astype(low)
        return tuple(jnp.maximum(top, peak) for top, peak in zip(tops, peaks))

    tops = lax.fori_loop(
        0, total // step, body, tuple(jnp.full((1, step), masked, wide) for _ in (0, 1))
    )
    for head in (0, 1):
        peak = jnp.max(tops[head], axis=1, keepdims=True)
        top_ref[0, head : head + 1, :] = jnp.broadcast_to(peak, (1, tile))


def attention_forward(steps, length, qkv, strips, start, count, step=512):
    total = qkv.shape[0]
    pairs = qkv.shape[1] // (3 * tile)
    strip_width = strips.shape[2]

    def columns(which):
        return pl.BlockSpec((total, tile), lambda p, _: (0, which * pairs + start + p))

    return steps.launch(
        "attention_forward",
        functools.partial(forward_kernel, step=step),
        [length, qkv, qkv, qkv, strips],
        [columns(which) for which in range(3)]
        + [pl.BlockSpec((2, tile, strip_width), lambda p, _: (start + p, 0, 0))],
        [
            pl.BlockSpec((total, tile), lambda p, _: (0, p)),
            pl.BlockSpec((1, 2, total), lambda p, _: (p, 0, 0)),
            pl.BlockSpec((1, 2, tile), lambda p, _: (p, 0, 0)),
        ],
        [((total, count * tile), low), ((count, 2, total), wide), ((count, 2, tile), wide)],
        grid=(count,),
        memory=32,
        estimate=(6e9 * count, (3 << 20) * count),
    )


def backward_kernel(
    length_ref,
    query_ref,
    key_ref,
    value_ref,
    context_ref,
    grad_ref,
    total_ref,
    strip_ref,
    query_grad_ref,
    key_grad_ref,
    value_grad_ref,
    strip_grad_ref,
    key_sum,
    value_sum,
    *,
    step,
):
    length = length_ref[0]
    total = query_ref.shape[0]
    masks = key_masks(total, length)
    ones = jnp.ones((step, tile), low)
    keys = [one_head(key_ref[...], head, masks) for head in (0, 1)]
    plain_keys = [one_head(key_ref[...], head) for head in (0, 1)]
    values = [one_head(value_ref[...], head) for head in (0, 1)]
    key_sum[...] = jnp.zeros_like(key_sum)
    value_sum[...] = jnp.zeros_like(value_sum)
    strip_grad_ref[...] = jnp.zeros_like(strip_grad_ref)

    def body(index, carry):
        first = pl.multiple_of(index * step, step)
        queries = query_ref[pl.ds(first, step), :]
        grads = grad_ref[pl.ds(first, step), :]
        columns = strip_columns(total, first, step)
        inner = grads.astype(wide) * context_ref[pl.ds(first, step), :].astype(wide)
        query_grad = None
        for head in (0, 1):
            head_grads = one_head(grads, head)
            pick = one_head(jnp.ones((8, tile), wide), head)
            row_inner = lax.dot_general(
                pick,
                inner,
                (((1,), (1,)), ((), ())),
                precision=lax.Precision.HIGHEST,
                preferred_element_type=wide,
            )[:1]
            log_total = total_ref[0, head : head + 1, pl.ds(first, step)]
            products = dot(keys[head], one_head(queries, head, ones), 1, 1)
            probs = jnp.exp(add_bias(products, strip_ref, head, columns) - log_total)
            value_sum[...] += dot(probs.astype(low), head_grads, 1, 0)
            score_grad = probs * (dot(values[head], head_grads, 1, 1) - row_inner)
            for block, where in enumerate(columns):
                strip_grad_ref[head, :, where] += score_grad[block * tile : (block + 1) * tile]
            score_low = score_grad.astype(low)
            key_sum[...] += dot(score_low, one_head(queries, head), 1, 0)
            part = dot(score_low, plain_keys[head], 0, 0)
            query_grad = part if query_grad is None else query_grad + part
        query_grad_ref[pl.ds(first, step), :] = query_grad.astype(low)
        return carry

    lax.fori_loop(0, total // step, body, 0)
    key_grad_ref[...] = key_sum[...].astype(low)
    value_grad_ref[...] = value_sum[...].astype(low)


def attention_backward(
    steps, length, qkv, context, context_grad, log_totals, strips, start, held, step=256
):
    total = qkv.shape[0]
    pairs = qkv.shape[1] // (3 * tile)
    strip_width = strips.shape[2]

    def columns(which, first=start):
        return pl.BlockSpec((total, tile), lambda p, _: (0, which * pairs + first + p))

    part = pl.BlockSpec((total, tile), lambda p, _: (0, p))
    return steps.launch(
        "attention_backward",
        functools.partial(backward_kernel, step=step),
        [length, qkv, qkv, qkv, context, context_grad, log_totals, strips],
        [
            columns(0),
            columns(1),
            columns(2),
            columns(0, start - held),
            columns(0),
            pl.BlockSpec((1, 2, total), lambda p, _: (start - held + p, 0, 0)),
            pl.BlockSpec((2, tile, strip_width), lambda p, _: (start + p, 0, 0)),
        ],
        [part, part, part, pl.BlockSpec((2, tile, strip_width), lambda p, _: (p, 0, 0))],
        [((total, tile), low)] * 3 + [((2, tile, strip_width), wide)],
        scratch=[pltpu.VMEM((total, tile), wide)] * 2,
        memory=32,
        stored=(3,),
        estimate=(1e10, 6 << 20),
    )


def gelu_and_slope(values):
    distance = jnp.abs(values) * math.sqrt(0.5)
    ratio = 1.0 / (1.0 + 0.3275911 * distance)
    density = jnp.exp(-distance * distance)
    poly = 1.061405429 * ratio - 1.453152027
    poly = poly * ratio + 1.421413741
    poly = poly * ratio - 0.284496736
    poly = poly * ratio + 0.254829592
    tail = (0.5 * ratio) * poly * density
    cumulative = jnp.where(values >= 0, 1.0 - tail, tail)
    slope = cumulative + values * density * (1.0 / math.sqrt(2.0 * math.pi))
    return values * cumulative, slope


def beside(refs):
    return jnp.concatenate([ref[...] for ref in refs], axis=1)


def pinned(array):
    return pltpu.with_memory_space_constraint(array, pltpu.HBM)


def start_copies(index_ref, pieces, target, semaphores, columns=None):
    copies = []
    for number, piece in enumerate(pieces):
        for side in (0, 1):
            entry = 2 * number + side
            rows = piece.shape[-2]
            where = pl.ds(pl.multiple_of(index_ref[entry] * rows, rows), rows)
            if columns is not None:
                source, place = piece.at[side, :, columns], target.at[where, :]
            else:
                source, place = piece.at[side], target.at[:, where, :]
            copies.append(pltpu.make_async_copy(source, place, semaphores.at[entry]))
    for copy in copies:
        copy.start()
    return copies


def transposed_rows(order_ref, source_ref, target_ref, columns, chips, ordered):
    share = source_ref.shape[1] // chips
    for block in range(chips):
        if ordered:
            first = pl.multiple_of(order_ref[block] * share, share)
            part = source_ref[:, pl.ds(first, share)]
        else:
            part = source_ref[:, block * share : (block + 1) * share]
        target_ref[block * share : (block + 1) * share, columns] = part.T.astype(low)


def send_kernel(odd_ref, block_ref, first_ref, second_ref):
    @pl.when(pl.program_id(0) == 0)
    def _():
        first_ref[...] = block_ref[0]

    @pl.when(pl.program_id(0) == 1)
    def _():
        second_ref[...] = block_ref[0]


def send_blocks(steps, odd, blocks):
    shape = blocks.shape[1:]
    out = pl.BlockSpec(shape, lambda i, _: (0, 0))
    return steps.launch(
        "send_blocks",
        send_kernel,
        [odd, pinned(blocks)],
        [pl.BlockSpec((1,) + shape, lambda i, odd_ref: ((odd_ref[0] + i) % 2, 0, 0))],
        [out, out],
        [(shape, low)] * 2,
        grid=(2,),
        memory=8,
        estimate=(0, 2 << 20),
    )


def scaled(block, gain):
    return (gain * block.astype(wide)).astype(low)


def column_copies(core, weights, targets, semaphores, first=0, parts=1, part=0):
    copies = []
    for number, (weight, target) in enumerate(zip(weights, targets)):
        width = weight.shape[1] // (2 * parts)
        columns = pl.ds(pl.multiple_of((parts * core + part) * width, width), width)
        copies.append(
            pltpu.make_async_copy(weight.at[:, columns], target, semaphores.at[first + number])
        )
    return copies


def run_copies(copies):
    for copy in copies:
        copy.start()
    for copy in copies:
        copy.wait()


def side_kernel(core_ref, *refs):
    attention, feed = refs[:4], refs[4:6]
    gain_ref, out_ref, semaphores = refs[6:]
    core = 1 - core_ref[0]
    inner = attention[0].shape[1] // 2
    hidden = feed[0].shape[1] // 4
    targets = [out_ref.at[:, n * inner : (n + 1) * inner] for n in range(4)]
    copies = column_copies(core, attention, targets, semaphores)
    first = 4 * inner
    for part in (0, 1):
        start = first + 2 * part * hidden
        targets = [out_ref.at[:, start + n * hidden : start + (n + 1) * hidden] for n in (0, 1)]
        copies += column_copies(core, feed, targets, semaphores, 4 + 2 * part, 2, part)
    run_copies(copies)
    out_ref[:, : 3 * inner] = scaled(out_ref[:, : 3 * inner], gain_ref[:, :1])
    for part in (0, 1):
        columns = slice(first + 2 * part * hidden, first + (2 * part + 1) * hidden)
        out_ref[:, columns] = scaled(out_ref[:, columns], gain_ref[:, 1:])


def pair_kernel(first_ref, second_ref, out_ref):
    out_ref[0] = first_ref[...]
    out_ref[1] = second_ref[...]


def pair(steps, first, second):
    rows, width = first.shape
    step = rows // 2
    block = pl.BlockSpec((step, width), lambda i: (i, 0))
    return steps.launch(
        "pair",
        pair_kernel,
        [first, second],
        [block] * 2,
        [pl.BlockSpec((2, step, width), lambda i: (0, i, 0))],
        [((2, rows, width), low)],
        grid=(2,),
        prefetch=0,
        memory=8,
    )[0]


def other_side(steps, core, attention, feed, gains):
    rows = attention[0].shape[0]
    columns = sum(weight.shape[1] for weight in attention + feed) // 2
    return steps.launch(
        "other_side",
        side_kernel,
        [core, *map(pinned, (*attention, *feed)), gains],
        [in_hbm] * 6 + [in_vmem],
        [in_vmem],
        [((rows, columns), low)],
        scratch=[pltpu.SemaphoreType.DMA((8,))],
        memory=8,
    )[0]


def attention_shard_kernel(core_ref, *refs):
    attention = refs[:4]
    gain_ref, arrived_ref, out_ref, semaphores = refs[4:]
    inner = attention[0].shape[1] // 2
    targets = [out_ref.at[0, :, n * inner : (n + 1) * inner] for n in range(4)]
    copies = column_copies(core_ref[0], attention, targets, semaphores)
    source = arrived_ref.at[:, : 4 * inner]
    copies.append(pltpu.make_async_copy(source, out_ref.at[1], semaphores.at[4]))
    run_copies(copies)
    out_ref[0, :, : 3 * inner] = scaled(out_ref[0, :, : 3 * inner], gain_ref[:, :1])


def attention_shard(steps, core, weights, gains, arrived):
    rows = weights[0].shape[0]
    columns = sum(weight.shape[1] for weight in weights) // 2
    return steps.launch(
        "attention_shard",
        attention_shard_kernel,
        [core, *map(pinned, weights), gains, arrived],
        [in_hbm] * 4 + [in_vmem, anywhere],
        [in_vmem],
        [((2, rows, columns), low)],
        scratch=[pltpu.SemaphoreType.DMA((5,))],
        memory=8,
    )[0]


def hidden_shard_kernel(core_ref, *refs, part):
    feed = refs[:2]
    gain_ref, arrived_ref, out_ref, semaphores = refs[2:]
    hidden = out_ref.shape[3]
    targets = [out_ref.at[0, number] for number in (0, 1)]
    copies = column_copies(core_ref[0], feed, targets, semaphores, 0, 2, part)
    for number in (0, 1):
        start = 2 * hidden * (1 + part) + number * hidden
        source = arrived_ref.at[:, start : start + hidden]
        copies.append(
            pltpu.make_async_copy(source, out_ref.at[1, number], semaphores.at[2 + number])
        )
    run_copies(copies)
    out_ref[0, 0] = scaled(out_ref[0, 0], gain_ref[:, 1:])


def hidden_shard(steps, core, part, weights, gains, arrived):
    rows, columns = weights[0].shape
    return steps.launch(
        "hidden_shard",
        functools.partial(hidden_shard_kernel, part=part),
        [core, *map(pinned, weights), gains, arrived],
        [in_hbm] * 2 + [in_vmem, anywhere],
        [in_vmem],
        [((2, 2, rows, columns // 4), low)],
        scratch=[pltpu.SemaphoreType.DMA((4,))],
        memory=8,
    )[0]


def token_kernel(place_ref, *refs, normed, chips, ordered):
    halves = refs[:2]
    plain_ref, first_ref, first_t_ref, semaphores = refs[-4:]
    total = plain_ref.shape[0]
    step = total // 4
    copies = []
    for number in range(4):
        where = pl.ds(pl.multiple_of(place_ref[number] * step, step), step)
        source = halves[number // 2].at[number % 2]
        copies.append(
            pltpu.make_async_copy(source, plain_ref.at[where, :], semaphores.at[number])
        )
    for copy in copies:
        copy.start()
    for copy in copies:
        copy.wait()
    for block in range(4):
        rows = slice(block * step, (block + 1) * step)
        values = plain_ref[rows, :].astype(wide)
        if normed:
            values = normalize(values)[0]
        else:
            position = block * step + lax.broadcasted_iota(jnp.int32, values.shape, 0)
            values = jnp.where(position < place_ref[4], values, 0.0)
        first_ref[rows, :] = values.astype(low)
        transposed_rows(
            place_ref.at[pl.ds(5, chips)],
            first_ref.at[rows, :],
            first_t_ref,
            rows,
            chips,
            ordered,
        )


def token_rows_of(steps, places, pieces, normed, chips, ordered):
    total, width = 4 * pieces[0].shape[1], pieces[0].shape[2]
    return steps.launch(
        "token_rows" if normed else "cotangent_rows",
        functools.partial(token_kernel, normed=normed, chips=chips, ordered=ordered),
        [places, *pieces],
        [anywhere] * 2,
        [in_vmem] * 3,
        [((total, width), low), ((total, width), low), ((width, total), low)],
        scratch=[pltpu.SemaphoreType.DMA((4,))],
        memory=24,
        estimate=(0, 10 << 20),
    )


def rows_product_kernel(place_ref, *refs, factors, count, columns, across):
    rows = refs[:factors]
    pieces = refs[factors : factors + count]
    out_ref, weight, semaphores = refs[factors + count :]

    @pl.when(pl.program_id(0) == 0)
    def _():
        for copy in start_copies(place_ref, pieces, weight, semaphores, columns):
            copy.wait()

    operand = beside(rows)
    out_ref[...] = dot(operand, weight[...], 1, 1 if across else 0).astype(low)


def rows_product(steps, places, rows, pieces, first, last, across, name, step=256):
    total, depth = rows[0].shape
    count = len(pieces)
    whole = (2 * count * pieces[0].shape[1], last - first)
    width = whole[0] if across else whole[1]
    return steps.launch(
        name,
        functools.partial(
            rows_product_kernel,
            factors=len(rows),
            count=count,
            columns=pl.ds(first, last - first),
            across=across,
        ),
        [places, *rows, *pieces],
        [pl.BlockSpec((step, depth), lambda i, _: (i, 0))] * len(rows) + [anywhere] * count,
        [pl.BlockSpec((step, width), lambda i, _: (i, 0))],
        [((total, width), low)],
        grid=(total // step,),
        scratch=[pltpu.VMEM(whole, low), pltpu.SemaphoreType.DMA((2 * count,))],
        estimate=(2 * total * whole[0] * whole[1], 8 << 20),
    )[0]


def second_norm_kernel(
    order_ref, token_ref, mine_ref, other_ref, hidden_ref, normed_ref, normed_t_ref, *, chips, ordered
):
    attended = mine_ref[...].astype(wide) + other_ref[...].astype(wide)
    hidden = token_ref[...].astype(wide) + attended
    hidden_ref[...] = hidden
    normed_ref[...] = normalize(hidden)[0].astype(low)
    transposed_rows(order_ref, normed_ref, normed_t_ref, slice(None), chips, ordered)


def second_norm(steps, order, tokens, mine, other, chips, ordered, step=256):
    total, width = tokens.shape
    block = pl.BlockSpec((step, width), lambda i, _: (i, 0))
    return steps.launch(
        "second_norm",
        functools.partial(second_norm_kernel, chips=chips, ordered=ordered),
        [order, tokens, mine, other],
        [block] * 3,
        [block, block, pl.BlockSpec((width, step), lambda i, _: (0, i))],
        [((total, width), wide), ((total, width), low), ((width, total), low)],
        grid=(total // step,),
        estimate=(0, 14 << 20),
    )


def feed_forward_kernel(
    place_ref, normed_ref, normed_t_ref, grad_ref, grad_t_ref, *refs, count, first
):
    pieces = refs[:count]
    refs = refs[count:]
    if first:
        mixed_sum, normed_sum, keep_ref, send_ref, weight, semaphores = refs
        before = ()
    else:
        before = refs[:2]
        own_ref, other_ref, normed_grad_ref, keep_ref, send_ref = refs[2:7]
        weight, semaphores, mixed_sum, normed_sum = refs[7:]
    index = pl.program_id(0)
    step = keep_ref.shape[2]
    half = keep_ref.shape[1]
    carried = [
        pltpu.make_async_copy(source, target, semaphores.at[2 * count + number])
        for number, (source, target) in enumerate(zip(before, (mixed_sum, normed_sum)))
    ]

    @pl.when(index == 0)
    def _():
        copies = start_copies(place_ref, pieces, weight, semaphores)
        for copy in carried:
            copy.start()
        for copy in copies:
            copy.wait()

    columns = pl.ds(pl.multiple_of(index * step, step), step)
    expand = weight[0, :, columns]
    contract = weight[1, :, columns]
    pre_act = dot(normed_ref[...], expand, 1, 0)
    act_grad = dot(grad_ref[...], contract, 1, 0).astype(low).astype(wide)
    activated, slope = gelu_and_slope(pre_act)
    activated = activated.astype(low)
    pre_grad = (act_grad * slope).astype(low)
    for part, (rows_ref, values) in enumerate(
        ((normed_t_ref, pre_grad), (grad_t_ref, activated))
    ):
        keep_ref[part] = dot(rows_ref[:half, :], values, 1, 0).astype(low)
        send_ref[part] = dot(rows_ref[half:, :], values, 1, 0).astype(low)
    mixed = dot(activated, contract, 1, 1)
    normed_grad = dot(pre_grad, expand, 1, 1)
    if first:

        @pl.when(index == 0)
        def _():
            mixed_sum[...] = mixed
            normed_sum[...] = normed_grad

        @pl.when(index > 0)
        def _():
            mixed_sum[...] += mixed
            normed_sum[...] += normed_grad

    else:

        @pl.when(index == 0)
        def _():
            for copy in carried:
                copy.wait()

        mixed_sum[...] += mixed
        normed_sum[...] += normed_grad

        @pl.when(index == pl.num_programs(0) - 1)
        def _():
            rows = own_ref.shape[0]
            core = place_ref[2 * count]
            own = pl.multiple_of(core * rows, rows)
            away = pl.multiple_of((1 - core) * rows, rows)
            own_ref[...] = mixed_sum[pl.ds(own, rows), :].astype(low)
            other_ref[...] = mixed_sum[pl.ds(away, rows), :].astype(low)
            normed_grad_ref[...] = normed_sum[...].astype(low)


def feed_forward(steps, places, normed, normed_t, grad, grad_t, pieces, before=None, step=512):
    rows, width = normed.shape
    count = len(pieces)
    hidden = pieces[0].shape[3]
    first = before is None

    def fixed(shape):
        return pl.BlockSpec(shape, lambda i, _: (0,) * len(shape), pipeline_mode=pl.Buffered(1))

    whole = fixed((rows, width))
    scratch = [
        pltpu.VMEM((2, width, hidden), low),
        pltpu.SemaphoreType.DMA((2 * count + 2,)),
    ]
    if first:
        before = ()
        out_specs = [whole, whole]
        out_shape = [((rows, width), wide)] * 2
    else:
        part = fixed((rows // 2, width))
        out_specs = [part, part, whole]
        out_shape = [((rows // 2, width), low)] * 2 + [((rows, width), low)]
        scratch += [pltpu.VMEM((rows, width), wide)] * 2
    return steps.launch(
        "feed_forward",
        functools.partial(feed_forward_kernel, count=count, first=first),
        [places, normed, normed_t, grad, grad_t, *pieces, *before],
        [whole, fixed((width, rows))] * 2 + [anywhere] * (count + len(before)),
        out_specs + [pl.BlockSpec((2, width // 2, step), lambda i, _: (0, 0, i))] * 2,
        out_shape + [((2, width // 2, hidden), low)] * 2,
        grid=(hidden // step,),
        scratch=scratch,
        memory=58,
        stored=(0, 1) if first else (),
        estimate=(20 * rows * width * hidden, 40 << 20),
    )


def hidden_back_kernel(
    place_ref, mine_ref, other_ref, hidden_ref, grad_ref, *refs, count, columns, chips, ordered
):
    pieces = refs[:count]
    hidden_grad_ref, low_ref, low_t_ref, context_grad_ref, weight, semaphores = refs[count:]

    @pl.when(pl.program_id(0) == 0)
    def _():
        for copy in start_copies(place_ref, pieces, weight, semaphores, columns):
            copy.wait()

    upstream = mine_ref[...].astype(wide) + other_ref[...].astype(wide)
    hidden = hidden_ref[...]
    scale = normalize(hidden)[1]
    hidden_grad = grad_ref[...].astype(wide) + normalize_back(hidden, scale, upstream)
    hidden_grad_ref[...] = hidden_grad
    low_ref[...] = hidden_grad.astype(low)
    context_grad_ref[...] = dot(low_ref[...], weight[...], 1, 0).astype(low)
    order_ref = place_ref.at[pl.ds(2 * count + 1, chips)]
    transposed_rows(order_ref, low_ref, low_t_ref, slice(None), chips, ordered)


def hidden_back(
    steps, places, mine, other, hidden, grad, pieces, first, last, chips, ordered, step=256
):
    total, width = hidden.shape
    count = len(pieces)
    inner = last - first
    block = pl.BlockSpec((step, width), lambda i, _: (i, 0))
    return steps.launch(
        "hidden_back",
        functools.partial(
            hidden_back_kernel,
            count=count,
            columns=pl.ds(first, inner),
            chips=chips,
            ordered=ordered,
        ),
        [places, mine, other, hidden, grad, *pieces],
        [block] * 4 + [anywhere] * count,
        [
            block,
            block,
            pl.BlockSpec((width, step), lambda i, _: (0, i)),
            pl.BlockSpec((step, inner), lambda i, _: (i, 0)),
        ],
        [((total, width), wide), ((total, width), low), ((width, total), low), ((total, inner), low)],
        grid=(total // step,),
        scratch=[pltpu.VMEM((width, inner), low), pltpu.SemaphoreType.DMA((2 * count,))],
        estimate=(4 * total * width * inner, 24 << 20),
    )


def terms_kernel(*refs, contexts):
    grad_t_ref, normed_t_ref = refs[:2]
    factors = refs[2:-2]
    for number, target in enumerate(refs[-2:]):

        @pl.when(pl.program_id(0) == number)
        def _():
            first = 0
            if contexts:
                part = dot(grad_t_ref[...], beside(factors[:contexts]), 1, 0)
                first = part.shape[1]
                target[:, :first] = part.astype(low)
            part = dot(normed_t_ref[...], beside(factors[contexts:]), 1, 0)
            target[:, first:] = part.astype(low)


def attention_terms(steps, grad_t, normed_t, contexts, grads):
    width, total = normed_t.shape
    factors = list(contexts) + list(grads)
    columns = sum(factor.shape[1] for factor in factors)
    block = pl.BlockSpec((width // 2, total), lambda i: (i, 0))
    fixed = pl.BlockSpec((width // 2, columns), lambda i: (0, 0))
    return steps.launch(
        "attention_terms",
        functools.partial(terms_kernel, contexts=len(contexts)),
        [grad_t, normed_t, *factors],
        [block, block]
        + [
            pl.BlockSpec(factor.shape, lambda i: (0, 0), pipeline_mode=pl.Buffered(1))
            for factor in factors
        ],
        [fixed, fixed],
        [((width // 2, columns), low)] * 2,
        grid=(2,),
        prefetch=0,
        estimate=(2 * total * width * columns, 10 << 20),
    )


def sum_kernel(*refs):
    total = refs[0][...].astype(wide)
    for ref in refs[1:-1]:
        total += ref[...].astype(wide)
    refs[-1][...] = total.astype(low)


def row_sums(steps, parts):
    first = parts[0]
    rows = first[0].shape[-2] // (1 if first[1] is None else 2)
    shape = first[0].shape[:-2] + (rows, first[0].shape[-1])
    count = 4
    block = shape[:-2] + (rows // count, shape[-1])
    leading = (0,) * (len(shape) - 2)

    def spec(offset):
        return pl.BlockSpec(block, lambda i: leading + (i + offset, 0))

    return steps.launch(
        "row_sums",
        sum_kernel,
        [part for part, _ in parts],
        [spec(count if which else 0) for _, which in parts],
        [spec(0)],
        [(shape, low)],
        grid=(count,),
        prefetch=0,
        memory=12,
        estimate=(0, 4 << 20),
    )[0]


def input_product_kernel(place_ref, *refs, count, factors):
    grads = refs[:factors]
    pieces = refs[factors : factors + count]
    own_ref, other_ref, weight, semaphores = refs[factors + count :]
    index = pl.program_id(0)

    @pl.when(index == 0)
    def _():
        columns = pl.ds(0, weight.shape[1])
        for copy in start_copies(place_ref, pieces, weight, semaphores, columns):
            copy.wait()

    ordered = [ref for block in range(3) for ref in grads[block::3]]
    product = dot(beside(ordered), weight[...], 1, 1)

    @pl.when(index < 2)
    def _():
        other_ref[...] = product.astype(low)

    @pl.when(index >= 2)
    def _():
        own_ref[...] = product


def input_product(steps, places, grads, pieces):
    total = grads[0].shape[0]
    count = len(pieces)
    inner = sum(grad.shape[1] for grad in grads)
    width = 2 * count * pieces[0].shape[1]
    step = total // 4

    def rows(i, place_ref):
        core = place_ref[2 * count]
        return (jnp.where(i < 2, 2 * (1 - core) + i, 2 * core + i - 2), 0)

    return steps.launch(
        "input_product",
        functools.partial(input_product_kernel, count=count, factors=len(grads)),
        [places, *grads, *pieces],
        [pl.BlockSpec((step, grad.shape[1]), rows) for grad in grads] + [anywhere] * count,
        [
            pl.BlockSpec((step, width), lambda i, _: (jnp.maximum(i - 2, 0), 0)),
            pl.BlockSpec((step, width), lambda i, _: (jnp.minimum(i, 1), 0)),
        ],
        [((total // 2, width), wide), ((total // 2, width), low)],
        grid=(4,),
        scratch=[pltpu.VMEM((width, inner), low), pltpu.SemaphoreType.DMA((2 * count,))],
        memory=24,
        estimate=(2 * total * width * inner, 14 << 20),
    )


def finish_kernel(
    place_ref, own_ref, other_ref, base_ref, token_ref, first_ref, second_ref, *, back
):
    index = pl.program_id(0)
    summed = own_ref[...].astype(wide) + other_ref[...].astype(wide)
    if back:
        tokens = token_ref[...].astype(wide)
        values = base_ref[...] + normalize_back(tokens, normalize(tokens)[1], summed)
    else:
        row = (2 * place_ref[0] + index) * summed.shape[0]
        position = row + lax.broadcasted_iota(jnp.int32, summed.shape, 0)
        values = jnp.where(position < place_ref[2], base_ref[...] + summed, 0.0)
    values = values.astype(low)

    @pl.when(index == place_ref[1])
    def _():
        first_ref[...] = values

    @pl.when(index != place_ref[1])
    def _():
        second_ref[...] = values


def finish_half(steps, core, odd, length, own, other, base, tokens, back):
    rows, width = own.shape
    step = rows // 2
    half = pl.BlockSpec((step, width), lambda i, _: (i, 0))
    whole = pl.BlockSpec((step, width), lambda i, place_ref: (2 * place_ref[0] + i, 0))
    quarter = pl.BlockSpec((step, width), lambda i, _: (0, 0))
    return steps.launch(
        "input_gradient_rows" if back else "result_rows",
        functools.partial(finish_kernel, back=back),
        [jnp.stack([core, odd, length]).astype(jnp.int32), own, other, base, tokens],
        [half, half, whole, whole],
        [quarter, quarter],
        [((step, width), low)] * 2,
        grid=(2,),
        memory=12,
        estimate=(0, 6 << 20),
    )


def pick_kernel(slot_ref, *refs, count):
    pieces = refs[:count]
    own_ref, other_ref, semaphores = refs[count:]
    for row in range(4):
        target = (own_ref if row < 2 else other_ref).at[row % 2]
        for number in range(2 * count):

            @pl.when(slot_ref[row] == slot_ref[4 + number])
            def _():
                source = pieces[number // 2].at[number % 2]
                copy = pltpu.make_async_copy(source, target, semaphores.at[row])
                copy.start()
                copy.wait()


def pick_slots(steps, slots, pieces):
    count = len(pieces)
    return steps.launch(
        "pick_slots",
        functools.partial(pick_kernel, count=count),
        [slots, *pieces],
        [anywhere] * count,
        [in_vmem] * 2,
        [(pieces[0].shape, low)] * 2,
        scratch=[pltpu.SemaphoreType.DMA((4,))],
        memory=8,
        estimate=(0, 4 << 20),
    )


def normalize(values):
    scaled = lax.rsqrt(jnp.mean(values * values, axis=-1, keepdims=True) + epsilon)
    return (values * scaled, scaled)


def normalize_back(values, scaled, upstream):
    unit_rows = values * scaled
    return scaled * (upstream - unit_rows * jnp.mean(upstream * unit_rows, axis=-1, keepdims=True))


class Links:
    def __init__(self, buckets):
        self.buckets = buckets
        self.shards = lax.axis_size("fsdp")
        self.depth = lax.axis_size("ctx")
        self.shard = lax.axis_index("fsdp")
        self.level = lax.axis_index("ctx")
        self.chips = self.shards // 2
        self.chip = self.shard // 2
        self.core = self.shard % 2
        self.groups = [list(range(core, self.shards, 2)) for core in (0, 1)]
        self.square = self.chips == 4

    def sibling(self, array):
        return lax.ppermute(array, "fsdp", [(i, i ^ 1) for i in range(self.shards)])

    def across(self, array, bit):
        return lax.ppermute(array, "fsdp", [(i, i ^ (2 * bit)) for i in range(self.shards)])

    def in_order(self, mine, other):
        return jnp.concatenate(
            [jnp.where(self.core == 0, mine, other), jnp.where(self.core == 0, other, mine)], axis=0
        )

    def turn(self, array, second):
        pairs = [(i, i ^ (2 if (i % 2 == 0) != second else 4)) for i in range(self.shards)]
        return lax.ppermute(array, "fsdp", pairs)

    def order(self):
        if not self.square:
            return list(range(self.chips))
        return [self.chip, self.chip ^ (1 + self.core), self.chip ^ (2 - self.core), self.chip ^ 3]

    def gather(self, shard):
        if not self.square:
            whole = lax.all_gather(shard, "fsdp", axis=0, axis_index_groups=self.groups)
            return [whole[chip] for chip in range(self.chips)]
        first = self.turn(shard, False)
        second = self.turn(shard, True)
        return [shard, first, second, self.turn(first, True)]

    def weight_places(self):
        return [2 * chip + side for chip in self.order() for side in (self.core, 1 - self.core)]

    def scatter(self, keep, send):
        dim = keep.ndim - 2
        if not self.square:
            summed = lax.psum_scatter(
                jnp.concatenate([keep, send], axis=dim),
                "fsdp",
                scatter_dimension=dim,
                tiled=True,
                axis_index_groups=self.groups,
            )
            return keep, summed.astype(low)
        return keep, self.turn(send, True)

    def scatter_near(self, steps, terms):
        keep, arrived = terms
        if not self.square:
            return keep, arrived, None
        near = row_sums(steps, [(keep, True), (arrived, True)])
        return keep, arrived, self.turn(near, False)

    def scatter_own(self, steps, terms):
        keep, arrived, last = terms
        total = arrived
        if self.square:
            total = row_sums(steps, [(keep, False), (arrived, False), (last, None)])
        return total, lax.ppermute(total, "ctx", [(0, 1), (3, 2)])

    def small_hops(self, small):
        hops = []
        bit = 1
        while bit < self.chips:
            hops.append(("fsdp", [(i, i ^ (2 * bit)) for i in range(self.shards)]))
            bit *= 2
        bit = 1
        while bit < self.depth:
            hops.append(("ctx", [(i, i ^ bit) for i in range(self.depth)]))
            bit *= 2
        for axis, pairs in hops:
            other = lax.ppermute(small, axis, pairs)
            lane = lax.broadcasted_iota(jnp.int32, small.shape, 1)
            small = jnp.where(lane < self.buckets, small + other, jnp.maximum(small, other))
            yield small

    def level_across(self, steps, terms):
        joined = row_sums(steps, [(part, None) for part in terms])
        return joined, lax.ppermute(joined, "ctx", [(1, 2), (2, 1)])

    def level_out(self, steps, terms):
        total = row_sums(steps, [(part, None) for part in terms])
        outward = lax.ppermute(total, "ctx", [(1, 0), (2, 3)])
        inner = (self.level == 1) | (self.level == 2)
        return self.exchange_rows(jnp.where(inner, total, outward))

    def exchange_rows(self, rows):
        dim = rows.ndim - 2
        half = rows.shape[dim] // 2
        mine = lax.dynamic_slice_in_dim(rows, self.core * half, half, dim)
        other = self.sibling(lax.dynamic_slice_in_dim(rows, (1 - self.core) * half, half, dim))
        return jnp.where(self.core == 0, mine, other), jnp.where(self.core == 0, other, mine)

    def trade(self, array, outward, swapped):
        pairs = []
        for level in range(self.depth):
            for shard in range(self.shards):
                chip, core = divmod(shard, 2)
                side, odd = divmod(level, 2)
                slot = odd if not swapped else 1 - odd
                held = level * self.shards + shard
                worked = (2 * core + slot) * self.shards + 2 * chip + side
                pairs.append((held, worked) if outward else (worked, held))
        return lax.ppermute(array, ("ctx", "fsdp"), pairs)

    def to_slot(self, sends):
        return self.trade(sends[0], True, False), self.trade(sends[1], True, True)

    def both_halves(self, steps, trades):
        half = pair(steps, *trades)
        return half, self.sibling(half)

    def quarter_places(self):
        odd = self.level % 2
        near, far = 2 * self.core, 2 * (1 - self.core)
        return [near + odd, near + 1 - odd, far + odd, far + 1 - odd]

    def from_slot(self, quarters):
        return self.trade(quarters[0], False, False), self.trade(quarters[1], False, True)

    def received(self, trades):
        first, second = trades
        flip = self.level % 2 == 0
        return jnp.stack([jnp.where(flip, first, second), jnp.where(flip, second, first)])


def local(
    tokens,
    cotangent,
    sequence_lengths,
    slot_sequence,
    offset_bucket,
    first_gain,
    second_gain,
    query_weight,
    key_weight,
    value_weight,
    output_weight,
    expand_weight,
    contract_weight,
    bias_table,
    clip_limit,
):
    links = Links(bias_table.shape[0])
    core = links.core
    held_count, local_length, model_width = tokens.shape
    total_length = local_length * links.depth
    bucket_count, head_count = bias_table.shape
    inner_width = query_weight.shape[1]
    head_size = inner_width // head_count
    own_heads = head_count // 2
    own_inner = inner_width // 2
    slot_count = slot_sequence.shape[0]
    assert held_count == 2 and links.depth == 4

    slots = jnp.arange(slot_count)
    slot = links.chip * (2 * held_count) + links.level
    sequence = jnp.sum(jnp.where(slots == slot, slot_sequence, 0))
    length = jnp.sum(jnp.where(slots == sequence, sequence_lengths, 0)).astype(jnp.int32)
    odd = links.level % 2

    def numbers(*values):
        return jnp.stack([jnp.asarray(value, jnp.int32) for value in values])

    core_line = numbers(core)
    first_column = first_gain.astype(wide)[:, None]
    second_column = second_gain.astype(wide)[:, None]
    gains = jnp.concatenate([first_column, second_column], axis=1)
    attention_weights = (query_weight, key_weight, value_weight, output_weight)
    feed_weights = (expand_weight, contract_weight)
    steps = Steps()
    odd_line = odd.reshape(1)
    chips, square = links.chips, links.square
    order = links.order()
    places = numbers(*links.weight_places(), core, *order)
    order_line = numbers(*order)
    slot_places = numbers(*links.quarter_places(), length, *order)
    length_line = length.reshape(1)

    line_width = 2 * total_length
    falling = jnp.concatenate([jnp.flip(offset_bucket), jnp.full((1,), -1, jnp.int32)])
    matching = falling[:, None] == jnp.arange(bucket_count)[None, :]
    own_table = lax.dynamic_slice_in_dim(bias_table, core * own_heads, own_heads, 1)
    lines = dot(own_table, matching.astype(low), 0, 1)

    token_trades = links.to_slot(send_blocks(steps, odd_line, tokens))
    arrived = links.sibling(other_side(steps, core_line, attention_weights, feed_weights, gains))
    attention_pieces = links.gather(
        attention_shard(steps, core_line, attention_weights, gains, arrived)
    )
    strips = bias_strips(steps, lines.reshape(own_heads, 1, line_width))
    cotangent_sends = send_blocks(steps, odd_line, cotangent)
    late_shard = hidden_shard(steps, core_line, 1, feed_weights, gains, arrived)
    token_halves = links.both_halves(steps, token_trades)
    steps.wait(*attention_pieces[1:3])
    early_shard = hidden_shard(steps, core_line, 0, feed_weights, gains, arrived)
    cotangent_trades = links.to_slot(cotangent_sends)
    early_pieces = links.gather(early_shard)
    token_low, normed_one, normed_one_t = token_rows_of(
        steps, slot_places, token_halves, True, chips, square
    )
    qkv_width = 3 * own_inner
    qkv = rows_product(
        steps, places, [normed_one], attention_pieces, 0, qkv_width, False, "qkv_product"
    )
    pairs = own_inner // tile
    half_pairs = pairs // 2
    forward = functools.partial(attention_forward, steps, length_line, qkv, strips)
    first_context, first_totals, first_tops = forward(0, half_pairs)
    cotangent_halves = links.both_halves(steps, cotangent_trades)
    steps.wait(*early_pieces[1:3])
    last_context, last_totals, last_tops = forward(half_pairs, half_pairs)
    contexts = [first_context, last_context]
    output_columns = (qkv_width, qkv_width + own_inner)
    attended = rows_product(
        steps, places, contexts, attention_pieces, *output_columns, True, "attended_product"
    )
    attended_other = links.sibling(attended)
    _, out_low, out_low_t = token_rows_of(
        steps, slot_places, cotangent_halves, False, chips, square
    )
    late_pieces = links.gather(late_shard)
    hidden_one, normed_two, normed_two_t = second_norm(
        steps, order_line, token_low, attended, attended_other, chips, square
    )
    operands = (normed_two, normed_two_t, out_low, out_low_t)
    steps.wait(late_pieces[1])
    mixed_sum, normed_sum, *early_terms = feed_forward(steps, places, *operands, early_pieces)
    early = links.scatter(*early_terms)
    mixed_own, mixed_away, normed_two_part, *late_terms = feed_forward(
        steps, places, *operands, late_pieces, (mixed_sum, normed_sum)
    )
    normed_two_other = links.sibling(normed_two_part)
    mixed_other = links.sibling(mixed_away)
    late = links.scatter(*late_terms)
    early = links.scatter_near(steps, early)
    hidden_grad, attended_grad, attended_grad_t, context_grad = hidden_back(
        steps,
        places,
        normed_two_part,
        normed_two_other,
        hidden_one,
        out_low,
        attention_pieces,
        *output_columns,
        chips,
        square,
    )
    result_quarters = finish_half(
        steps, core, odd, length, mixed_own, mixed_other, hidden_one, token_low, False
    )
    result_trades = links.from_slot(result_quarters)

    def backward(pair):
        half = pair // half_pairs
        return attention_backward(
            steps,
            length_line,
            qkv,
            contexts[half],
            context_grad,
            (first_totals, last_totals)[half],
            strips,
            pair,
            half * half_pairs,
        )

    *grads_a, strips_a = backward(0)
    *grads_b, strips_b = backward(1)
    early = links.scatter_own(steps, early)
    late = links.scatter_near(steps, late)
    first = links.scatter(
        *attention_terms(steps, attended_grad_t, normed_one_t, contexts, grads_a + grads_b)
    )
    *grads_c, strips_c = backward(2)
    late = links.scatter_own(steps, late)
    *grads_d, strips_d = backward(3)
    early = links.level_across(steps, early)
    first = links.scatter_near(steps, first)
    last = links.scatter(
        *attention_terms(steps, attended_grad_t, normed_one_t, (), grads_c + grads_d)
    )
    own_part, away_part = input_product(
        steps, places, grads_a + grads_b + grads_c + grads_d, attention_pieces
    )
    away_other = links.sibling(away_part)
    first = links.scatter_own(steps, first)
    late = links.level_across(steps, late)
    last = links.scatter_near(steps, last)
    early_left, early_right = links.level_out(steps, early)
    input_quarters = finish_half(
        steps, core, odd, length, own_part, away_other, hidden_grad, token_low, True
    )
    last = links.scatter_own(steps, last)
    first = links.level_across(steps, first)
    result_pieces = links.gather(links.received(result_trades))
    late_left, late_right = links.level_out(steps, late)
    input_trades = links.from_slot(input_quarters)
    last = links.level_across(steps, last)
    first_left, first_right = links.level_out(steps, first)
    diagonals = jnp.concatenate(
        [diagonal_sums(steps, part) for part in (strips_a, strips_b, strips_c, strips_d)], axis=0
    ).reshape(own_heads, line_width)
    table_grad = lax.dot_general(
        diagonals,
        matching.astype(wide),
        (((1,), (0,)), ((), ())),
        precision=lax.Precision.HIGHEST,
        preferred_element_type=wide,
    )
    tops = jnp.concatenate([first_tops, last_tops], axis=0).reshape(own_heads, tile)
    small = jnp.concatenate([table_grad, tops[:, : tile - bucket_count]], axis=1)
    for small in links.small_hops(small):
        pass
    last_left, last_right = links.level_out(steps, last)
    input_gradient = links.received(input_trades).astype(wide)

    def slot_of(wanted):
        return jnp.sum(jnp.where(slot_sequence == wanted, slots, 0))

    own_slots = [slot_of(links.shard * held_count + row) for row in range(held_count)]
    other_slots = [slot_of((links.shard ^ 1) * held_count + row) for row in range(held_count)]
    piece_slots = [
        (2 * chip + core) * held_count + row
        for chip in order
        for row in range(held_count)
    ]
    picked, picked_other = pick_slots(
        steps,
        numbers(*own_slots, *other_slots, *piece_slots),
        result_pieces,
    )
    from_other = links.sibling(picked_other)
    output = jnp.stack(
        [
            jnp.where((s // held_count) % 2 == core, picked[row], from_other[row])
            for row, s in enumerate(own_slots)
        ]
    )

    def side_by_side(*parts):
        return jnp.concatenate(parts, axis=1).astype(wide)

    raw_two = side_by_side(early_left[0], late_left[0], early_right[0], late_right[0])
    contract_weight_gradient = side_by_side(
        early_left[1], late_left[1], early_right[1], late_right[1]
    )

    output_weight_gradient = side_by_side(first_left[:, :own_inner], first_right[:, :own_inner])

    def inner_columns(block):
        pieces = []
        for first_side, last_side in ((first_left, last_left), (first_right, last_right)):
            for start, side in ((own_inner, first_side), (0, last_side)):
                for pair in range(half_pairs):
                    first = start + (3 * pair + block) * tile
                    pieces.append(side[:, first : first + tile])
        return side_by_side(*pieces)

    raw_query, raw_key, raw_value = (inner_columns(block) for block in range(3))
    first_gain_gradient = jnp.sum(
        query_weight.astype(wide) * raw_query
        + key_weight.astype(wide) * raw_key
        + value_weight.astype(wide) * raw_value,
        axis=1,
    )
    second_gain_gradient = jnp.sum(expand_weight.astype(wide) * raw_two, axis=1)
    query_weight_gradient = first_column * raw_query
    key_weight_gradient = first_column * raw_key
    value_weight_gradient = first_column * raw_value
    expand_weight_gradient = second_column * raw_two

    small = links.in_order(small, links.sibling(small))
    table_rows = bucket_count // links.shards
    bias_table_gradient = lax.dynamic_slice_in_dim(
        small[:, :bucket_count].T, links.shard * table_rows, table_rows, 0
    )
    largest = small[:, bucket_count]
    shrink = clip_limit / jnp.maximum(clip_limit, largest)
    column_scale = jnp.repeat(jnp.sqrt(shrink), head_size)
    new_query_weight = query_weight.astype(wide) * column_scale[None, :]
    new_key_weight = key_weight.astype(wide) * column_scale[None, :]
    return (
        output,
        input_gradient,
        first_gain_gradient,
        second_gain_gradient,
        query_weight_gradient,
        key_weight_gradient,
        value_weight_gradient,
        output_weight_gradient,
        expand_weight_gradient,
        contract_weight_gradient,
        bias_table_gradient,
        largest,
        new_query_weight,
        new_key_weight,
    )


def solution(mesh):
    return jax.shard_map(
        local,
        mesh=mesh,
        in_specs=(
            P("fsdp", "ctx", None),
            P("fsdp", "ctx", None),
            P(),
            P(),
            P(),
            P("fsdp"),
            P("fsdp"),
            P("fsdp", None),
            P("fsdp", None),
            P("fsdp", None),
            P("fsdp", None),
            P("fsdp", None),
            P("fsdp", None),
            P(),
            P(),
        ),
        out_specs=(
            P("fsdp", "ctx", None),
            P("fsdp", "ctx", None),
            P("fsdp"),
            P("fsdp"),
            P("fsdp", None),
            P("fsdp", None),
            P("fsdp", None),
            P("fsdp", None),
            P("fsdp", None),
            P("fsdp", None),
            P("fsdp", None),
            P(),
            P("fsdp", None),
            P("fsdp", None),
        ),
        check_vma=False,
    )
```

time: 682 us -> 488 us (0.72); the launches traced: 671 us -> 484 us
  Pallas kernels: 107 us -> 207 us
  local copies, waits for them, and re-layouts: 123 us -> 46.6 us
  other arithmetic: 91.1 us -> 20.4 us
  waiting for transfers between devices: 143 us -> 84.4 us
  starting transfers between devices: 169 us -> 116 us
  matrix products: 25.5 us -> 1.22 us
    pallas_call x5 -> x49, Pallas kernels: 107 us -> 207 us  [launch(): pl.pallas_call(run, grid_spec=pltpu.PrefetchScalarGridSpec(num_scalar_pre...]
    ppermute x64 -> x36, starting transfers between devices: 132 us -> 64.5 us  [the longest x20 23.9 us: turn(): return lax.ppermute(array, 'fsdp', pairs)]
    ppermute x64 -> x36, waiting for transfers between devices: 137 us -> 78.5 us  [the longest x20 29.7 us: turn(): return lax.ppermute(array, 'fsdp', pairs)]
    dot_general x7 -> x1, matrix products: 24.9 us -> 0.64 us  [dot(): lax.dot_general(left, right, (((left_dim,), (right_dim,)), ((), ())), pre...]
    ppermute x8, starting transfers between devices: 19.2 us -> 41 us  [trade(): return lax.ppermute(array, ('ctx', 'fsdp'), pairs)]
    convert_element_type x15 -> x4, other arithmetic: 19.8 us -> 5.09 us  [the longest x2 2.37 us: side_by_side(): return jnp.concatenate(parts, axis=1).astype(wide)]
    dynamic_slice x18 -> x4, local copies, waits for them, and re-layouts: 15.5 us -> 0.93 us  [exchange_rows(): lax.dynamic_slice_in_dim(rows, (1 - self.core) * half, half, dim)]
    dynamic_update_slice x26 -> x0, local copies, waits for them, and re-layouts: 14.1 us -> none  [put(): return lax.dynamic_update_slice_in_dim(array, part[None], index, 0)]
  transfers between devices with their start and end apart: 85 -> 57, of which waited for: 29 -> 12; matrix products, arithmetic and copies ran while one was open for 31% -> 5% of each run, Pallas kernels for 10% -> 38%
where the time goes in v3:
time: 488 us; the launch traced here: 484 us
  Pallas kernels  207 us (42%)
  starting transfers between devices  116 us (24%)
  waiting for transfers between devices  84.4 us (17%)
  local copies, waits for them, and re-layouts  46.6 us (10%)
  other arithmetic  20.4 us (4%)
  between operations  7.87 us (2%)
    pallas_call x49, Pallas kernels, launch(): pl.pallas_call(run, grid_spec=pltpu.PrefetchScalarGridSpec(num_scalar_pre...  207 us
    ppermute x8, starting transfers between devices, trade(): return lax.ppermute(array, ('ctx', 'fsdp'), pairs)  41 us
    unnamed x200, local copies, waits for them, and re-layouts  39.7 us
    ppermute x20, waiting for transfers between devices, turn(): return lax.ppermute(array, 'fsdp', pairs)  29.7 us
    ppermute x4, waiting for transfers between devices, level_out(): outward = lax.ppermute(total, 'ctx', [(1, 0), (2, 3)])  24.8 us
    ppermute x4, waiting for transfers between devices, small_hops(): other = lax.ppermute(small, axis, pairs)  23.9 us
    ppermute x20, starting transfers between devices, turn(): return lax.ppermute(array, 'fsdp', pairs)  23.9 us
    ppermute x4, starting transfers between devices, scatter_own(): return (total, lax.ppermute(total, 'ctx', [(0, 1), (3, 2)]))  20.5 us
  transfers between devices with their start and end apart: 57, of which 12 were waited for; matrix products, arithmetic and copies ran while one was open for 5% of the time, Pallas kernels for 38%

profile of v3, /device:TPU:0, one launch (start us, length us, event | category | flops | bytes accessed | tf_op | source)
XLA Modules:
  0.0 483.5 jit_solution(16328606791515979660)
XLA Ops:
  2.1 2.2 send_blocks.2
  4.3 1.7 other_side.1
  6.6 3.0 collective-permute-done.2.refs_6_.refs_4_
  9.6 2.2 attention_shard.1
  11.9 2.9 collective-permute-start.4
  14.8 1.7 collective-permute-start
  20.6 5.7 %bias_strips.1 = (f32[8,128,2048]{2,1,0:T(8,128)}, f32[8,128]{1,0:T(8,128)S(1)}) custom-call(f32[8,1,2048]{2,1,0:T(1,128)S(1)} %reshape.43.refs_0_, f32[8,128]{1,0:T(8,128)S(1)} %get-tuple-element.154.refs_1_), custom_call_target="tpu_custom_call" | custom-call | bytes 8388608 | tf_op jit(solution)/shard_map/bias_strips/pallas_call | solution.py:53
  31.6 2.0 pair.2
  33.5 6.4 %collective-permute-start.3 = (bf16[2,256,1024]{2,1,0:T(8,128)(2,1)}, bf16[2,256,1024]{2,1,0:T(8,128)(2,1)}, u32[]{:S(2)}, u32[]{:S(2)}) collective-permute-start(bf16[2,256,1024]{2,1,0:T(8,128)(2,1)} %get-tuple-element.158.refs_1_), channel_id=1, source_target_pairs={{0,1},{1,0},{2,3},{3,2},{4,5},{5,4},{6,7},{7,6},{8,9},{9,8},{10,11... | collective-permute-start | bytes 3145736 | tf_op jit(solution)/shard_map/ppermute | solution.py:1035
  44.2 1.8 collective-permute-start.7
  46.1 6.5 %collective-permute-start.8 = (bf16[256,1024]{1,0:T(8,128)(2,1)}, bf16[256,1024]{1,0:T(8,128)(2,1)S(1)}, u32[]{:S(2)}, u32[]{:S(2)}) collective-permute-start(bf16[256,1024]{1,0:T(8,128)(2,1)} %copy-done.60), channel_id=1, source_target_pairs={{0,8},{1,24},{2,10},{3,26},{4,12},{5,28},{6,14},{7,30},{8,0},{9,16... | collective-permute-start | bytes 1572872 | tf_op jit(solution)/shard_map/ppermute | solution.py:1135
  55.7 3.6 token_rows.1
  60.6 6.5 %qkv_product.1 = (bf16[1024,1536]{1,0:T(8,128)(2,1)S(1)}, f32[8,128]{1,0:T(8,128)S(1)}) custom-call(s32[13]{0:T(128)S(1)} %stack.175.refs_0_, bf16[1024,1024]{1,0:T(8,128)(2,1)S(1)} %get-tuple-element.163.refs_1_, bf16[2,128,2048]{2,1,0:T(8,128)(2,1)} %get-tuple-element.160.refs_2_.refs_3_.refs_5_.refs_13_, ...), custom_call_target="tpu_custom_call" | custom-call | flops 3221225472 | bytes 8388608 | tf_op jit(solution)/shard_map/qkv_product/pallas_call | solution.py:53
  67.2 10.8 %attention_forward.2 = (bf16[1024,256]{1,0:T(8,128)(2,1)S(1)}, f32[2,2,1024]{2,1,0:T(2,128)S(1)}, f32[2,2,128]{2,1,0:T(2,128)S(1)}, f32[8,128]{1,0:T(8,128)S(1)}) custom-call(s32[1]{0:T(128)} %bitcast.14.refs_0_, bf16[1024,1536]{1,0:T(8,128)(2,1)S(1)} %get-tuple-element.165.refs_1_.refs_2_.refs_3_, ...), custom_call_target="tpu_custom_call" | custom-call | flops 12000000000 | bytes 6291456 | tf_op jit(solution)/shard_map/attention_forward/pallas_call | solution.py:53
  79.9 10.8 %attention_forward.3 = (bf16[1024,256]{1,0:T(8,128)(2,1)S(1)}, f32[2,2,1024]{2,1,0:T(2,128)S(1)}, f32[2,2,128]{2,1,0:T(2,128)S(1)}, f32[8,128]{1,0:T(8,128)S(1)}) custom-call(s32[1]{0:T(128)} %bitcast.14.refs_0_, bf16[1024,1536]{1,0:T(8,128)(2,1)S(1)} %get-tuple-element.165.refs_1_.refs_2_.refs_3_, ...), custom_call_target="tpu_custom_call" | custom-call | flops 12000000000 | bytes 6291456 | tf_op jit(solution)/shard_map/attention_forward/pallas_call | solution.py:53
  90.8 3.8 attended_product.1
  98.8 21.4 %collective-permute-done.13.refs_10_.refs_6_ = bf16[2,2,128,1024]{3,2,1,0:T(8,128)(2,1)} collective-permute-done((bf16[2,2,128,1024]{3,2,1,0:T(8,128)(2,1)S(1)}, bf16[2,2,128,1024]{3,2,1,0:T(8,128)(2,1)}, u32[]{:S(2)}, u32[]{:S(2)}) %collective-permute-start.13) | collective-permute-done | bytes 1048608 | tf_op jit(solution)/shard_map/ppermute | solution.py:1047
  120.3 2.2 collective-permute-start.15
  122.5 3.2 cotangent_rows.1
  128.3 3.0 second_norm.1
  131.3 2.0 copy-done.2
  137.0 27.2 %feed_forward.2 = (f32[1024,1024]{1,0:T(8,128)}, f32[1024,1024]{1,0:T(8,128)}, bf16[2,512,1024]{2,1,0:T(8,128)(2,1)}, bf16[2,512,1024]{2,1,0:T(8,128)(2,1)}, f32[8,128]{1,0:T(8,128)}) custom-call(s32[13]{0:T(128)} %copy-done.36, bf16[1024,1024]{1,0:T(8,128)(2,1)} %copy-done.49, bf16[1024,1024]{1,0:T(8,128)(2,1)} %copy-done.50, ...), custom_call_target="tpu_custom_call" | custom-call | flops 21474836480 | bytes 41943040 | tf_op jit(solution)/shard_map/feed_forward/pallas_call | solution.py:53
  164.3 27.0 %feed_forward.3 = (bf16[512,1024]{1,0:T(8,128)(2,1)}, bf16[512,1024]{1,0:T(8,128)(2,1)}, bf16[1024,1024]{1,0:T(8,128)(2,1)}, bf16[2,512,1024]{2,1,0:T(8,128)(2,1...) custom-call(s32[13]{0:T(128)} %copy-done.36, bf16[1024,1024]{1,0:T(8,128)(2,1)} %copy-done.49, ...), custom_call_target="tpu_custom_call" | custom-call | flops 21474836480 | bytes 41943040 | tf_op jit(solution)/shard_map/feed_forward/pallas_call | solution.py:53
  191.9 2.0 collective-permute-start.25
  195.4 2.6 row_sums.16
  201.6 6.6 %hidden_back.1 = (f32[1024,1024]{1,0:T(8,128)S(1)}, bf16[1024,1024]{1,0:T(8,128)(2,1)}, bf16[1024,1024]{1,0:T(8,128)(2,1)S(1)}, bf16[1024,512]{1,0:T(8,128)(2,1)S(1)}, f32[8,128]{1,0:T(8,128)S(1)}) custom-call(s32[13]{0:T(128)S(1)} %copy-done.37, bf16[1024,1024]{1,0:T(8,128)(2,1)S(1)} %copy-done.14, bf16[1024,1024]{1,0:T(8,128)(2,1)S(1)} %collective-permute-done.18.refs_2_, ...), custom_call_target="tpu_custom_call" | custom-call | flops 2147483648 | bytes 25165824 | tf_op jit(solution)/shard_map/hidden_back/pallas_call | solution.py:53
  208.3 2.4 result_rows.1
  210.8 2.2 copy-done.64
  213.0 3.4 copy-done.41
  216.4 9.6 %attention_backward.4 = (bf16[1024,128]{1,0:T(8,128)(2,1)S(1)}, bf16[1024,128]{1,0:T(8,128)(2,1)S(1)}, bf16[1024,128]{1,0:T(8,128)(2,1)S(1)}, f32[2,128,2048]{2,1,0:T(8,128)}, f32[8,128]{1,0:T(8,128)S(1)}) custom-call(s32[1]{0:T(128)} %bitcast.14.refs_0_, bf16[1024,1536]{1,0:T(8,128)(2,1)S(1)} %copy-done.64, bf16[1024,1536]{1,0:T(8,128)(2,1)S(1)} %copy-done.64, ...), custom_call_target="tpu_custom_call" | custom-call | flops 10000000000 | bytes 6291456 | tf_op jit(solution)/shard_map/attention_backward/pallas_call | solution.py:53
  226.0 9.6 %attention_backward.5 = (bf16[1024,128]{1,0:T(8,128)(2,1)S(1)}, bf16[1024,128]{1,0:T(8,128)(2,1)S(1)}, bf16[1024,128]{1,0:T(8,128)(2,1)S(1)}, f32[2,128,2048]{2,1,0:T(8,128)}, f32[8,128]{1,0:T(8,128)S(1)}) custom-call(s32[1]{0:T(128)} %bitcast.14.refs_0_, bf16[1024,1536]{1,0:T(8,128)(2,1)S(1)} %copy-done.64, bf16[1024,1536]{1,0:T(8,128)(2,1)S(1)} %copy-done.64, ...), custom_call_target="tpu_custom_call" | custom-call | flops 10000000000 | bytes 6291456 | tf_op jit(solution)/shard_map/attention_backward/pallas_call | solution.py:53
  235.5 2.7 row_sums.17
  240.5 4.2 attention_terms.2
  246.1 4.4 collective-permute-start.29
  250.6 3.4 copy-done.42
  254.0 9.5 %attention_backward.6 = (bf16[1024,128]{1,0:T(8,128)(2,1)S(1)}, bf16[1024,128]{1,0:T(8,128)(2,1)S(1)}, bf16[1024,128]{1,0:T(8,128)(2,1)S(1)}, f32[2,128,2048]{2,1,0:T(8,128)}, f32[8,128]{1,0:T(8,128)S(1)}) custom-call(s32[1]{0:T(128)} %bitcast.14.refs_0_, bf16[1024,1536]{1,0:T(8,128)(2,1)S(1)} %copy-done.65, bf16[1024,1536]{1,0:T(8,128)(2,1)S(1)} %copy-done.65, ...), custom_call_target="tpu_custom_call" | custom-call | flops 10000000000 | bytes 6291456 | tf_op jit(solution)/shard_map/attention_backward/pallas_call | solution.py:53
  264.3 2.0 collective-permute-start.31
  266.3 3.4 copy-done.43
  269.7 9.6 %attention_backward.7 = (bf16[1024,128]{1,0:T(8,128)(2,1)S(1)}, bf16[1024,128]{1,0:T(8,128)(2,1)S(1)}, bf16[1024,128]{1,0:T(8,128)(2,1)S(1)}, f32[2,128,2048]{2,1,0:T(8,128)}, f32[8,128]{1,0:T(8,128)S(1)}) custom-call(s32[1]{0:T(128)} %bitcast.14.refs_0_, bf16[1024,1536]{1,0:T(8,128)(2,1)S(1)} %copy-done.65, bf16[1024,1536]{1,0:T(8,128)(2,1)S(1)} %copy-done.65, ...), custom_call_target="tpu_custom_call" | custom-call | flops 10000000000 | bytes 6291456 | tf_op jit(solution)/shard_map/attention_backward/pallas_call | solution.py:53
  281.2 2.0 attention_terms.3
  283.3 1.7 collective-permute-start.30
  285.6 6.7 %input_product.1 = (f32[512,1024]{1,0:T(8,128)S(1)}, bf16[512,1024]{1,0:T(8,128)(2,1)S(1)}, f32[8,128]{1,0:T(8,128)S(1)}) custom-call(s32[13]{0:T(128)S(1)} %copy-done.37, bf16[1024,128]{1,0:T(8,128)(2,1)S(1)} %get-tuple-element.206.refs_4_.refs_1_, bf16[1024,128]{1,0:T(8,128)(2,1)S(1)} %copy-done.67, bf16[1024,128]{1,0:T(8,128)(2,1)S(1)} %copy-done.69, ...), custom_call_target="tpu_custom_call" | custom-call | flops 3221225472 | bytes 14680064 | tf_op jit(solution)/shard_map/input_product/pallas_call | solution.py:53
  293.6 6.7 %collective-permute-done.32.refs_2_ = bf16[256,1280]{1,0:T(8,128)(2,1)S(1)} collective-permute-done((bf16[256,1280]{1,0:T(8,128)(2,1)S(1)}, bf16[256,1280]{1,0:T(8,128)(2,1)S(1)}, u32[]{:S(2)}, u32[]{:S(2)}) %collective-permute-start.32) | collective-permute-done | bytes 655392 | tf_op jit(solution)/shard_map/ppermute | solution.py:1047
  301.8 6.1 %collective-permute-start.38 = (bf16[256,1280]{1,0:T(8,128)(2,1)}, bf16[256,1280]{1,0:T(8,128)(2,1)}, u32[]{:S(2)}, u32[]{:S(2)}) collective-permute-start(bf16[256,1280]{1,0:T(8,128)(2,1)} %get-tuple-element.253.refs_0_), channel_id=1, source_target_pairs={{0,8},{24,16},{1,9},{25,17},{2,10},{26,18},{3,11},{27,19},{4,12},{... | collective-permute-start | bytes 1966088 | tf_op jit(solution)/shard_map/ppermute | solution.py:1090
  307.9 5.4 %collective-permute-start.20 = (bf16[256,1024]{1,0:T(8,128)(2,1)}, bf16[256,1024]{1,0:T(8,128)(2,1)}, u32[]{:S(2)}, u32[]{:S(2)}) collective-permute-start(bf16[256,1024]{1,0:T(8,128)(2,1)} %get-tuple-element.198), channel_id=1, source_target_pairs={{0,0},{16,1},{2,2},{18,3},{4,4},{20,5},{6,6},{22,7},{8,8},{24,9},{... | collective-permute-start | bytes 1572872 | tf_op jit(solution)/shard_map/ppermute | solution.py:1135
  313.3 1.8 row_sums.23
  317.8 1.7 collective-permute-start.37
  323.6 2.2 copy-done.7
  325.8 1.7 input_gradient_rows.1
  329.2 2.3 row_sums.27
  335.6 8.0 %collective-permute-start.36 = (bf16[256,768]{1,0:T(8,128)(2,1)}, bf16[256,768]{1,0:T(8,128)(2,1)}, u32[]{:S(2)}, u32[]{:S(2)}) collective-permute-start(bf16[256,768]{1,0:T(8,128)(2,1)} %get-tuple-element.251.refs_0_), channel_id=1, source_target_pairs={{0,8},{24,16},{1,9},{25,17},{2,10},{26,18},{3,11},{27,19},{4,12},{... | collective-permute-start | bytes 1179656 | tf_op jit(solution)/shard_map/ppermute | solution.py:1090
  346.1 5.4 %collective-permute-start.42 = (bf16[256,1024]{1,0:T(8,128)(2,1)}, bf16[256,1024]{1,0:T(8,128)(2,1)}, u32[]{:S(2)}, u32[]{:S(2)}) collective-permute-start(bf16[256,1024]{1,0:T(8,128)(2,1)} %copy-done.59), channel_id=1, source_target_pairs={{0,0},{16,1},{2,2},{18,3},{4,4},{20,5},{6,6},{22,7},{8,8},{24,9},{... | collective-permute-start | bytes 1572872 | tf_op jit(solution)/shard_map/ppermute | solution.py:1135
  351.5 18.7 %collective-permute-start.43 = (bf16[256,1024]{1,0:T(8,128)(2,1)}, bf16[256,1024]{1,0:T(8,128)(2,1)}, u32[]{:S(2)}, u32[]{:S(2)}) collective-permute-start(bf16[256,1024]{1,0:T(8,128)(2,1)} %copy-done.58), channel_id=1, source_target_pairs={{8,0},{24,1},{10,2},{26,3},{12,4},{28,5},{14,6},{30,7},{0,8},{16,9... | collective-permute-start | bytes 1572872 | tf_op jit(solution)/shard_map/ppermute | solution.py:1135
  370.1 3.8 row_sums.28
  373.9 2.2 row_sums.29
  386.8 2.7 stack.158.refs_0_
  395.1 20.7 %collective-permute-done.53 = f32[8,128]{1,0:T(8,128)S(1)} collective-permute-done((f32[8,128]{1,0:T(8,128)S(1)}, f32[8,128]{1,0:T(8,128)S(1)}, u32[]{:S(2)}, u32[]{:S(2)}) %collective-permute-start.53) | collective-permute-done | bytes 4128 | tf_op jit(solution)/shard_map/ppermute | solution.py:1103
  415.8 5.2 %collective-permute-start.54 = (f32[8,128]{1,0:T(8,128)S(1)}, f32[8,128]{1,0:T(8,128)S(1)}, u32[]{:S(2)}, u32[]{:S(2)}) collective-permute-start(f32[8,128]{1,0:T(8,128)S(1)} %maximum_select_fusion.2), channel_id=1, source_target_pairs={{0,8},{8,0},{16,24},{24,16},{1,9},{9,1},{17,25},{25,17},{2,10},{10... | collective-permute-start | bytes 12296 | tf_op jit(solution)/shard_map/ppermute | solution.py:1103
  425.2 3.1 collective-permute-start.55
  428.5 3.3 collective-permute-done.55
  437.9 1.9 row_sums.31
  445.6 24.8 %collective-permute-done.46 = bf16[256,768]{1,0:T(8,128)(2,1)S(1)} collective-permute-done((bf16[256,768]{1,0:T(8,128)(2,1)S(1)}, bf16[256,768]{1,0:T(8,128)(2,1)S(1)}, u32[]{:S(2)}, u32[]{:S(2)}) %collective-permute-start.46) | collective-permute-done | bytes 393248 | tf_op jit(solution)/shard_map/ppermute | solution.py:1114
  474.6 2.3 convert_multiply_fusion.6
  480.9 2.4 convert_multiply_fusion
  (359 shorter events, 97.6 us)
Async XLA Ops:
  6.1 3.6 collective-permute-start.2
  11.9 28.1 %collective-permute-start.4 = (bf16[2,128,2048]{2,1,0:T(8,128)(2,1)}, bf16[2,128,2048]{2,1,0:T(8,128)(2,1)S(1)}, u32[]{:S(2)}, u32[]{:S(2)}) collective-permute-start(bf16[2,128,2048]{2,1,0:T(8,128)(2,1)} %get-tuple-element.160.refs_2_.refs_3_.refs_5_.refs_13_), channel_id=1, source_target_pairs={{0,2},{1,5},{2,0},{3,7},{4,6},{5,1},{6,4},{7,3},{8,10},{9,13},{10,... | collective-permute-start | bytes 3145736 | tf_op jit(solution)/shard_map/ppermute | solution.py:1047
  14.8 16.6 %collective-permute-start = (bf16[256,1024]{1,0:T(8,128)(2,1)}, bf16[256,1024]{1,0:T(8,128)(2,1)S(1)}, u32[]{:S(2)}, u32[]{:S(2)}) collective-permute-start(bf16[256,1024]{1,0:T(8,128)(2,1)} %get-tuple-element.149), channel_id=1, source_target_pairs={{0,0},{1,16},{2,2},{3,18},{4,4},{5,20},{6,6},{7,22},{8,8},{9,24},{... | collective-permute-start | bytes 1572872 | tf_op jit(solution)/shard_map/ppermute | solution.py:1135
  16.5 15.1 %collective-permute-start.1 = (bf16[256,1024]{1,0:T(8,128)(2,1)}, bf16[256,1024]{1,0:T(8,128)(2,1)}, u32[]{:S(2)}, u32[]{:S(2)}) collective-permute-start(bf16[256,1024]{1,0:T(8,128)(2,1)} %get-tuple-element.150), channel_id=1, source_target_pairs={{0,8},{1,24},{2,10},{3,26},{4,12},{5,28},{6,14},{7,30},{8,0},{9,16... | collective-permute-start | bytes 1572872 | tf_op jit(solution)/shard_map/ppermute | solution.py:1135
  19.0 33.6 %collective-permute-start.5 = (bf16[2,128,2048]{2,1,0:T(8,128)(2,1)}, bf16[2,128,2048]{2,1,0:T(8,128)(2,1)}, u32[]{:S(2)}, u32[]{:S(2)}) collective-permute-start(bf16[2,128,2048]{2,1,0:T(8,128)(2,1)} %get-tuple-element.160.refs_2_.refs_3_.refs_5_.refs_13_), channel_id=1, source_target_pairs={{0,4},{1,3},{2,6},{3,1},{4,0},{5,7},{6,2},{7,5},{8,12},{9,11},{10,... | collective-permute-start | bytes 3145736 | tf_op jit(solution)/shard_map/ppermute | solution.py:1047
  33.5 21.0 %collective-permute-start.3 = (bf16[2,256,1024]{2,1,0:T(8,128)(2,1)}, bf16[2,256,1024]{2,1,0:T(8,128)(2,1)}, u32[]{:S(2)}, u32[]{:S(2)}) collective-permute-start(bf16[2,256,1024]{2,1,0:T(8,128)(2,1)} %get-tuple-element.158.refs_1_), channel_id=1, source_target_pairs={{0,1},{1,0},{2,3},{3,2},{4,5},{5,4},{6,7},{7,6},{8,9},{9,8},{10,11... | collective-permute-start | bytes 3145736 | tf_op jit(solution)/shard_map/ppermute | solution.py:1035
  40.0 20.6 %collective-permute-start.6 = (bf16[2,128,2048]{2,1,0:T(8,128)(2,1)S(1)}, bf16[2,128,2048]{2,1,0:T(8,128)(2,1)}, u32[]{:S(2)}, u32[]{:S(2)}) collective-permute-start(bf16[2,128,2048]{2,1,0:T(8,128)(2,1)S(1)} %collective-permute-done.4.refs_6_.refs_3_.refs_4_.refs_14_), channel_id=1, source_target_pairs={{0,4},{1,3},{2,6},{3,1},{4,0},{5,7},{6,2},{7,5},{8,12},{9,11},{10,... | collective-permute-start | bytes 3145736 | tf_op jit(solution)/shard_map/ppermute | solution.py:1047
  44.2 46.5 %copy-start.36 = (s32[13]{0:T(128)}, s32[13]{0:T(128)S(1)}, u32[]{:S(2)}) copy-start(s32[13]{0:T(128)S(1)} %stack.175.refs_0_) | copy-start | bytes 160
  44.2 33.8 %collective-permute-start.7 = (bf16[256,1024]{1,0:T(8,128)(2,1)}, bf16[256,1024]{1,0:T(8,128)(2,1)S(1)}, u32[]{:S(2)}, u32[]{:S(2)}) collective-permute-start(bf16[256,1024]{1,0:T(8,128)(2,1)} %copy-done.61), channel_id=1, source_target_pairs={{0,0},{1,16},{2,2},{3,18},{4,4},{5,20},{6,6},{7,22},{8,8},{9,24},{... | collective-permute-start | bytes 1572872 | tf_op jit(solution)/shard_map/ppermute | solution.py:1135
  46.1 32.0 %collective-permute-start.8 = (bf16[256,1024]{1,0:T(8,128)(2,1)}, bf16[256,1024]{1,0:T(8,128)(2,1)S(1)}, u32[]{:S(2)}, u32[]{:S(2)}) collective-permute-start(bf16[256,1024]{1,0:T(8,128)(2,1)} %copy-done.60), channel_id=1, source_target_pairs={{0,8},{1,24},{2,10},{3,26},{4,12},{5,28},{6,14},{7,30},{8,0},{9,16... | collective-permute-start | bytes 1572872 | tf_op jit(solution)/shard_map/ppermute | solution.py:1135
  53.9 24.5 %collective-permute-start.9 = (bf16[2,2,128,1024]{3,2,1,0:T(8,128)(2,1)S(1)}, bf16[2,2,128,1024]{3,2,1,0:T(8,128)(2,1)S(1)}, u32[]{:S(2)}, u32[]{:S(2)}) collective-permute-start(bf16[2,2,128,1024]{3,2,1,0:T(8,128)(2,1)S(1)} %get-tuple-element.173.refs_5_), channel_id=1, source_target_pairs={{0,2},{1,5},{2,0},{3,7},{4,6},{5,1},{6,4},{7,3},{8,10},{9,13},{10,... | collective-permute-start | bytes 3145736 | tf_op jit(solution)/shard_map/ppermute | solution.py:1047
  54.5 25.3 %collective-permute-start.10 = (bf16[2,2,128,1024]{3,2,1,0:T(8,128)(2,1)S(1)}, bf16[2,2,128,1024]{3,2,1,0:T(8,128)(2,1)S(1)}, u32[]{:S(2)}, u32[]{:S(2)}) collective-permute-start(bf16[2,2,128,1024]{3,2,1,0:T(8,128)(2,1)S(1)} %get-tuple-element.173.refs_5_), channel_id=1, source_target_pairs={{0,4},{1,3},{2,6},{3,1},{4,0},{5,7},{6,2},{7,5},{8,12},{9,11},{10,... | collective-permute-start | bytes 3145736 | tf_op jit(solution)/shard_map/ppermute | solution.py:1047
  94.6 33.7 %collective-permute-start.11 = (bf16[1024,1024]{1,0:T(8,128)(2,1)S(1)}, bf16[1024,1024]{1,0:T(8,128)(2,1)S(1)}, u32[]{:S(2)}, u32[]{:S(2)}) collective-permute-start(bf16[1024,1024]{1,0:T(8,128)(2,1)S(1)} %get-tuple-element.176.refs_2_), channel_id=1, source_target_pairs={{0,1},{1,0},{2,3},{3,2},{4,5},{5,4},{6,7},{7,6},{8,9},{9,8},{10,11... | collective-permute-start | bytes 6291464 | tf_op jit(solution)/shard_map/ppermute | solution.py:1035
  95.2 25.1 %collective-permute-start.13 = (bf16[2,2,128,1024]{3,2,1,0:T(8,128)(2,1)S(1)}, bf16[2,2,128,1024]{3,2,1,0:T(8,128)(2,1)}, u32[]{:S(2)}, u32[]{:S(2)}) collective-permute-start(bf16[2,2,128,1024]{3,2,1,0:T(8,128)(2,1)S(1)} %copy-done.52), channel_id=1, source_target_pairs={{0,2},{1,5},{2,0},{3,7},{4,6},{5,1},{6,4},{7,3},{8,10},{9,13},{10,... | collective-permute-start | bytes 3145736 | tf_op jit(solution)/shard_map/ppermute | solution.py:1047
  96.7 25.7 %collective-permute-start.12 = (bf16[2,256,1024]{2,1,0:T(8,128)(2,1)S(1)}, bf16[2,256,1024]{2,1,0:T(8,128)(2,1)S(1)}, u32[]{:S(2)}, u32[]{:S(2)}) collective-permute-start(bf16[2,256,1024]{2,1,0:T(8,128)(2,1)S(1)} %get-tuple-element.177.refs_1_), channel_id=1, source_target_pairs={{0,1},{1,0},{2,3},{3,2},{4,5},{5,4},{6,7},{7,6},{8,9},{9,8},{10,11... | collective-permute-start | bytes 3145736 | tf_op jit(solution)/shard_map/ppermute | solution.py:1035
  96.7 39.2 %collective-permute-start.16 = (bf16[2,2,128,1024]{3,2,1,0:T(8,128)(2,1)S(1)}, bf16[2,2,128,1024]{3,2,1,0:T(8,128)(2,1)S(1)}, u32[]{:S(2)}, u32[]{:S(2)}) collective-permute-start(bf16[2,2,128,1024]{3,2,1,0:T(8,128)(2,1)S(1)} %collective-permute-done.9.refs_6_), channel_id=1, source_target_pairs={{0,4},{1,3},{2,6},{3,1},{4,0},{5,7},{6,2},{7,5},{8,12},{9,11},{10,... | collective-permute-start | bytes 3145736 | tf_op jit(solution)/shard_map/ppermute | solution.py:1047
  97.3 67.0 %collective-permute-start.14 = (bf16[2,2,128,1024]{3,2,1,0:T(8,128)(2,1)S(1)}, bf16[2,2,128,1024]{3,2,1,0:T(8,128)(2,1)}, u32[]{:S(2)}, u32[]{:S(2)}) collective-permute-start(bf16[2,2,128,1024]{3,2,1,0:T(8,128)(2,1)S(1)} %copy-done.52), channel_id=1, source_target_pairs={{0,4},{1,3},{2,6},{3,1},{4,0},{5,7},{6,2},{7,5},{8,12},{9,11},{10,... | collective-permute-start | bytes 3145736 | tf_op jit(solution)/shard_map/ppermute | solution.py:1047
  120.3 44.0 %collective-permute-start.15 = (bf16[2,2,128,1024]{3,2,1,0:T(8,128)(2,1)}, bf16[2,2,128,1024]{3,2,1,0:T(8,128)(2,1)}, u32[]{:S(2)}, u32[]{:S(2)}) collective-permute-start(bf16[2,2,128,1024]{3,2,1,0:T(8,128)(2,1)} %collective-permute-done.13.refs_10_.refs_6_), channel_id=1, source_target_pairs={{0,4},{1,3},{2,6},{3,1},{4,0},{5,7},{6,2},{7,5},{8,12},{9,11},{10,... | collective-permute-start | bytes 3145736 | tf_op jit(solution)/shard_map/ppermute | solution.py:1047
  164.2 30.5 %collective-permute-start.19 = (bf16[2,512,1024]{2,1,0:T(8,128)(2,1)}, bf16[2,512,1024]{2,1,0:T(8,128)(2,1)}, u32[]{:S(2)}, u32[]{:S(2)}) collective-permute-start(bf16[2,512,1024]{2,1,0:T(8,128)(2,1)} %get-tuple-element.194), channel_id=1, source_target_pairs={{0,4},{1,3},{2,6},{3,1},{4,0},{5,7},{6,2},{7,5},{8,12},{9,11},{10,... | collective-permute-start | bytes 6291464 | tf_op jit(solution)/shard_map/ppermute | solution.py:1047
  164.3 30.4 %copy-start.5 = (bf16[2,512,1024]{2,1,0:T(8,128)(2,1)S(1)}, bf16[2,512,1024]{2,1,0:T(8,128)(2,1)}, u32[]{:S(2)}) copy-start(bf16[2,512,1024]{2,1,0:T(8,128)(2,1)} %get-tuple-element.193.refs_0_) | copy-start | bytes 6291460
  191.3 7.1 %collective-permute-start.18 = (bf16[1024,1024]{1,0:T(8,128)(2,1)}, bf16[1024,1024]{1,0:T(8,128)(2,1)S(1)}, u32[]{:S(2)}, u32[]{:S(2)}) collective-permute-start(bf16[1024,1024]{1,0:T(8,128)(2,1)} %get-tuple-element.192.refs_1_), channel_id=1, source_target_pairs={{0,1},{1,0},{2,3},{3,2},{4,5},{5,4},{6,7},{7,6},{8,9},{9,8},{10,11... | collective-permute-start | bytes 6291464 | tf_op jit(solution)/shard_map/ppermute | solution.py:1035
  191.4 16.8 %collective-permute-start.17 = (bf16[512,1024]{1,0:T(8,128)(2,1)}, bf16[512,1024]{1,0:T(8,128)(2,1)S(1)}, u32[]{:S(2)}, u32[]{:S(2)}) collective-permute-start(bf16[512,1024]{1,0:T(8,128)(2,1)} %get-tuple-element.190), channel_id=1, source_target_pairs={{0,1},{1,0},{2,3},{3,2},{4,5},{5,4},{6,7},{7,6},{8,9},{9,8},{10,11... | collective-permute-start | bytes 3145736 | tf_op jit(solution)/shard_map/ppermute | solution.py:1035
  191.9 46.3 %collective-permute-start.25 = (bf16[2,512,1024]{2,1,0:T(8,128)(2,1)}, bf16[2,512,1024]{2,1,0:T(8,128)(2,1)S(1)}, u32[]{:S(2)}, u32[]{:S(2)}) collective-permute-start(bf16[2,512,1024]{2,1,0:T(8,128)(2,1)} %get-tuple-element.214), channel_id=1, source_target_pairs={{0,4},{1,3},{2,6},{3,1},{4,0},{5,7},{6,2},{7,5},{8,12},{9,11},{10,... | collective-permute-start | bytes 6291464 | tf_op jit(solution)/shard_map/ppermute | solution.py:1047
  197.9 37.6 %collective-permute-start.26 = (bf16[2,256,1024]{2,1,0:T(8,128)(2,1)S(1)}, bf16[2,256,1024]{2,1,0:T(8,128)(2,1)S(1)}, u32[]{:S(2)}, u32[]{:S(2)}) collective-permute-start(bf16[2,256,1024]{2,1,0:T(8,128)(2,1)S(1)} %get-tuple-element.215), channel_id=1, source_target_pairs={{0,2},{1,5},{2,0},{3,7},{4,6},{5,1},{6,4},{7,3},{8,10},{9,13},{10,... | collective-permute-start | bytes 3145736 | tf_op jit(solution)/shard_map/ppermute | solution.py:1047
  208.2 32.3 %copy-start.46 = (bf16[1024,1024]{1,0:T(8,128)(2,1)}, bf16[1024,1024]{1,0:T(8,128)(2,1)S(1)}, u32[]{:S(2)}) copy-start(bf16[1024,1024]{1,0:T(8,128)(2,1)S(1)} %get-tuple-element.200.refs_0_) | copy-start | bytes 6291460
  238.8 24.7 %collective-permute-start.27 = (bf16[2,256,1024]{2,1,0:T(8,128)(2,1)S(1)}, bf16[2,256,1024]{2,1,0:T(8,128)(2,1)S(1)}, u32[]{:S(2)}, u32[]{:S(2)}) collective-permute-start(bf16[2,256,1024]{2,1,0:T(8,128)(2,1)S(1)} %get-tuple-element.223), channel_id=1, source_target_pairs={{0,2},{1,5},{2,0},{3,7},{4,6},{5,1},{6,4},{7,3},{8,10},{9,13},{10,... | collective-permute-start | bytes 3145736 | tf_op jit(solution)/shard_map/ppermute | solution.py:1047
  244.7 35.9 %collective-permute-start.28 = (bf16[512,1280]{1,0:T(8,128)(2,1)}, bf16[512,1280]{1,0:T(8,128)(2,1)S(1)}, u32[]{:S(2)}, u32[]{:S(2)}) collective-permute-start(bf16[512,1280]{1,0:T(8,128)(2,1)} %get-tuple-element.230), channel_id=1, source_target_pairs={{0,4},{1,3},{2,6},{3,1},{4,0},{5,7},{6,2},{7,5},{8,12},{9,11},{10,... | collective-permute-start | bytes 3932168 | tf_op jit(solution)/shard_map/ppermute | solution.py:1047
  246.1 33.1 %collective-permute-start.29 = (bf16[2,256,1024]{2,1,0:T(8,128)(2,1)S(1)}, bf16[2,256,1024]{2,1,0:T(8,128)(2,1)S(1)}, u32[]{:S(2)}, u32[]{:S(2)}) collective-permute-start(bf16[2,256,1024]{2,1,0:T(8,128)(2,1)S(1)} %get-tuple-element.231.refs_0_), channel_id=1, source_target_pairs={{0,8},{24,16},{1,9},{25,17},{2,10},{26,18},{3,11},{27,19},{4,12},{... | collective-permute-start | bytes 3145736 | tf_op jit(solution)/shard_map/ppermute | solution.py:1090
  264.3 43.6 %collective-permute-start.31 = (bf16[2,256,1024]{2,1,0:T(8,128)(2,1)S(1)}, bf16[2,256,1024]{2,1,0:T(8,128)(2,1)S(1)}, u32[]{:S(2)}, u32[]{:S(2)}) collective-permute-start(bf16[2,256,1024]{2,1,0:T(8,128)(2,1)S(1)} %get-tuple-element.237.refs_0_), channel_id=1, source_target_pairs={{0,8},{24,16},{1,9},{25,17},{2,10},{26,18},{3,11},{27,19},{4,12},{... | collective-permute-start | bytes 3145736 | tf_op jit(solution)/shard_map/ppermute | solution.py:1090
  279.8 36.7 %collective-permute-start.35 = (bf16[2,256,1024]{2,1,0:T(8,128)(2,1)S(1)}, bf16[2,256,1024]{2,1,0:T(8,128)(2,1)S(1)}, u32[]{:S(2)}, u32[]{:S(2)}) collective-permute-start(bf16[2,256,1024]{2,1,0:T(8,128)(2,1)S(1)} %get-tuple-element.247.refs_0_), channel_id=1, source_target_pairs={{8,16},{16,8},{9,17},{17,9},{10,18},{18,10},{11,19},{19,11},{12,20... | collective-permute-start | bytes 3145736 | tf_op jit(solution)/shard_map/ppermute | solution.py:1110
  283.2 31.8 %copy-start.8 = (bf16[512,768]{1,0:T(8,128)(2,1)}, bf16[512,768]{1,0:T(8,128)(2,1)S(1)}, u32[]{:S(2)}) copy-start(bf16[512,768]{1,0:T(8,128)(2,1)S(1)} %get-tuple-element.235.refs_0_) | copy-start | bytes 2359300
  283.3 30.0 %collective-permute-start.30 = (bf16[512,768]{1,0:T(8,128)(2,1)S(1)}, bf16[512,768]{1,0:T(8,128)(2,1)S(1)}, u32[]{:S(2)}, u32[]{:S(2)}) collective-permute-start(bf16[512,768]{1,0:T(8,128)(2,1)S(1)} %get-tuple-element.236), channel_id=1, source_target_pairs={{0,4},{1,3},{2,6},{3,1},{4,0},{5,7},{6,2},{7,5},{8,12},{9,11},{10,... | collective-permute-start | bytes 2359304 | tf_op jit(solution)/shard_map/ppermute | solution.py:1047
  285.0 15.3 %collective-permute-start.32 = (bf16[256,1280]{1,0:T(8,128)(2,1)S(1)}, bf16[256,1280]{1,0:T(8,128)(2,1)S(1)}, u32[]{:S(2)}, u32[]{:S(2)}) collective-permute-start(bf16[256,1280]{1,0:T(8,128)(2,1)S(1)} %get-tuple-element.238), channel_id=1, source_target_pairs={{0,2},{1,5},{2,0},{3,7},{4,6},{5,1},{6,4},{7,3},{8,10},{9,13},{10,... | collective-permute-start | bytes 1966088 | tf_op jit(solution)/shard_map/ppermute | solution.py:1047
  293.6 24.3 %collective-permute-start.34 = (bf16[512,1024]{1,0:T(8,128)(2,1)S(1)}, bf16[512,1024]{1,0:T(8,128)(2,1)S(1)}, u32[]{:S(2)}, u32[]{:S(2)}) collective-permute-start(bf16[512,1024]{1,0:T(8,128)(2,1)S(1)} %get-tuple-element.245), channel_id=1, source_target_pairs={{0,1},{1,0},{2,3},{3,2},{4,5},{5,4},{6,7},{7,6},{8,9},{9,8},{10,11... | collective-permute-start | bytes 3145736 | tf_op jit(solution)/shard_map/ppermute | solution.py:1035
  301.8 27.4 %collective-permute-start.38 = (bf16[256,1280]{1,0:T(8,128)(2,1)}, bf16[256,1280]{1,0:T(8,128)(2,1)}, u32[]{:S(2)}, u32[]{:S(2)}) collective-permute-start(bf16[256,1280]{1,0:T(8,128)(2,1)} %get-tuple-element.253.refs_0_), channel_id=1, source_target_pairs={{0,8},{24,16},{1,9},{25,17},{2,10},{26,18},{3,11},{27,19},{4,12},{... | collective-permute-start | bytes 1966088 | tf_op jit(solution)/shard_map/ppermute | solution.py:1090
  307.9 24.4 %collective-permute-start.20 = (bf16[256,1024]{1,0:T(8,128)(2,1)}, bf16[256,1024]{1,0:T(8,128)(2,1)}, u32[]{:S(2)}, u32[]{:S(2)}) collective-permute-start(bf16[256,1024]{1,0:T(8,128)(2,1)} %get-tuple-element.198), channel_id=1, source_target_pairs={{0,0},{16,1},{2,2},{18,3},{4,4},{20,5},{6,6},{22,7},{8,8},{24,9},{... | collective-permute-start | bytes 1572872 | tf_op jit(solution)/shard_map/ppermute | solution.py:1135
  313.2 20.5 %collective-permute-start.21 = (bf16[256,1024]{1,0:T(8,128)(2,1)}, bf16[256,1024]{1,0:T(8,128)(2,1)}, u32[]{:S(2)}, u32[]{:S(2)}) collective-permute-start(bf16[256,1024]{1,0:T(8,128)(2,1)} %get-tuple-element.199), channel_id=1, source_target_pairs={{8,0},{24,1},{10,2},{26,3},{12,4},{28,5},{14,6},{30,7},{0,8},{16,9... | collective-permute-start | bytes 1572872 | tf_op jit(solution)/shard_map/ppermute | solution.py:1135
  317.5 10.1 %collective-permute-start.33 = (bf16[256,768]{1,0:T(8,128)(2,1)}, bf16[256,768]{1,0:T(8,128)(2,1)S(1)}, u32[]{:S(2)}, u32[]{:S(2)}) collective-permute-start(bf16[256,768]{1,0:T(8,128)(2,1)} %get-tuple-element.243), channel_id=1, source_target_pairs={{0,2},{1,5},{2,0},{3,7},{4,6},{5,1},{6,4},{7,3},{8,10},{9,13},{10,... | collective-permute-start | bytes 1179656 | tf_op jit(solution)/shard_map/ppermute | solution.py:1047
  317.8 33.6 %collective-permute-start.37 = (bf16[2,256,1024]{2,1,0:T(8,128)(2,1)}, bf16[2,256,1024]{2,1,0:T(8,128)(2,1)}, u32[]{:S(2)}, u32[]{:S(2)}) collective-permute-start(bf16[2,256,1024]{2,1,0:T(8,128)(2,1)} %get-tuple-element.252.refs_0_), channel_id=1, source_target_pairs={{8,16},{16,8},{9,17},{17,9},{10,18},{18,10},{11,19},{19,11},{12,20... | collective-permute-start | bytes 3145736 | tf_op jit(solution)/shard_map/ppermute | solution.py:1110
  331.5 44.6 %collective-permute-start.40 = (bf16[256,1280]{1,0:T(8,128)(2,1)S(1)}, bf16[256,1280]{1,0:T(8,128)(2,1)S(1)}, u32[]{:S(2)}, u32[]{:S(2)}) collective-permute-start(bf16[256,1280]{1,0:T(8,128)(2,1)S(1)} %get-tuple-element.262.refs_0_), channel_id=1, source_target_pairs={{8,16},{16,8},{9,17},{17,9},{10,18},{18,10},{11,19},{19,11},{12,20... | collective-permute-start | bytes 1966088 | tf_op jit(solution)/shard_map/ppermute | solution.py:1110
  335.2 55.3 %collective-permute-start.22 = (bf16[2,256,1024]{2,1,0:T(8,128)(2,1)S(1)}, bf16[2,256,1024]{2,1,0:T(8,128)(2,1)S(1)}, u32[]{:S(2)}, u32[]{:S(2)}) collective-permute-start(bf16[2,256,1024]{2,1,0:T(8,128)(2,1)S(1)} %pad_maximum_fusion.refs_1_), channel_id=1, source_target_pairs={{0,2},{1,5},{2,0},{3,7},{4,6},{5,1},{6,4},{7,3},{8,10},{9,13},{10,... | collective-permute-start | bytes 3145736 | tf_op jit(solution)/shard_map/ppermute | solution.py:1047
  335.6 38.4 %collective-permute-start.36 = (bf16[256,768]{1,0:T(8,128)(2,1)}, bf16[256,768]{1,0:T(8,128)(2,1)}, u32[]{:S(2)}, u32[]{:S(2)}) collective-permute-start(bf16[256,768]{1,0:T(8,128)(2,1)} %get-tuple-element.251.refs_0_), channel_id=1, source_target_pairs={{0,8},{24,16},{1,9},{25,17},{2,10},{26,18},{3,11},{27,19},{4,12},{... | collective-permute-start | bytes 1179656 | tf_op jit(solution)/shard_map/ppermute | solution.py:1090
  346.1 47.0 %collective-permute-start.42 = (bf16[256,1024]{1,0:T(8,128)(2,1)}, bf16[256,1024]{1,0:T(8,128)(2,1)}, u32[]{:S(2)}, u32[]{:S(2)}) collective-permute-start(bf16[256,1024]{1,0:T(8,128)(2,1)} %copy-done.59), channel_id=1, source_target_pairs={{0,0},{16,1},{2,2},{18,3},{4,4},{20,5},{6,6},{22,7},{8,8},{24,9},{... | collective-permute-start | bytes 1572872 | tf_op jit(solution)/shard_map/ppermute | solution.py:1135
  351.5 42.4 %collective-permute-start.43 = (bf16[256,1024]{1,0:T(8,128)(2,1)}, bf16[256,1024]{1,0:T(8,128)(2,1)}, u32[]{:S(2)}, u32[]{:S(2)}) collective-permute-start(bf16[256,1024]{1,0:T(8,128)(2,1)} %copy-done.58), channel_id=1, source_target_pairs={{8,0},{24,1},{10,2},{26,3},{12,4},{28,5},{14,6},{30,7},{0,8},{16,9... | collective-permute-start | bytes 1572872 | tf_op jit(solution)/shard_map/ppermute | solution.py:1135
  383.0 8.7 %collective-permute-start.52 = (f32[8,128]{1,0:T(8,128)S(1)}, f32[8,128]{1,0:T(8,128)S(1)}, u32[]{:S(2)}, u32[]{:S(2)}) collective-permute-start(f32[8,128]{1,0:T(8,128)S(1)} %pad_maximum_fusion.6), channel_id=1, source_target_pairs={{0,2},{1,3},{2,0},{3,1},{4,6},{5,7},{6,4},{7,5},{8,10},{9,11},{10,... | collective-permute-start | bytes 12296 | tf_op jit(solution)/shard_map/ppermute | solution.py:1103
  389.6 50.3 %collective-permute-start.23 = (bf16[2,256,1024]{2,1,0:T(8,128)(2,1)S(1)}, bf16[2,256,1024]{2,1,0:T(8,128)(2,1)S(1)}, u32[]{:S(2)}, u32[]{:S(2)}) collective-permute-start(bf16[2,256,1024]{2,1,0:T(8,128)(2,1)S(1)} %pad_maximum_fusion.refs_1_), channel_id=1, source_target_pairs={{0,4},{1,3},{2,6},{3,1},{4,0},{5,7},{6,2},{7,5},{8,12},{9,11},{10,... | collective-permute-start | bytes 3145736 | tf_op jit(solution)/shard_map/ppermute | solution.py:1047
  390.4 49.4 %collective-permute-start.24 = (bf16[2,256,1024]{2,1,0:T(8,128)(2,1)S(1)}, bf16[2,256,1024]{2,1,0:T(8,128)(2,1)}, u32[]{:S(2)}, u32[]{:S(2)}) collective-permute-start(bf16[2,256,1024]{2,1,0:T(8,128)(2,1)S(1)} %collective-permute-done.22.refs_2_), channel_id=1, source_target_pairs={{0,4},{1,3},{2,6},{3,1},{4,0},{5,7},{6,2},{7,5},{8,12},{9,11},{10,... | collective-permute-start | bytes 3145736 | tf_op jit(solution)/shard_map/ppermute | solution.py:1047
  391.7 33.5 %collective-permute-start.48 = (bf16[2,256,1024]{2,1,0:T(8,128)(2,1)}, bf16[2,256,1024]{2,1,0:T(8,128)(2,1)S(1)}, u32[]{:S(2)}, u32[]{:S(2)}) collective-permute-start(bf16[2,256,1024]{2,1,0:T(8,128)(2,1)} %copy-done.21), channel_id=1, source_target_pairs={{8,0},{16,24},{9,1},{17,25},{10,2},{18,26},{11,3},{19,27},{12,4},{... | collective-permute-start | bytes 3145736 | tf_op jit(solution)/shard_map/ppermute | solution.py:1114
  393.0 22.7 %collective-permute-start.53 = (f32[8,128]{1,0:T(8,128)S(1)}, f32[8,128]{1,0:T(8,128)S(1)}, u32[]{:S(2)}, u32[]{:S(2)}) collective-permute-start(f32[8,128]{1,0:T(8,128)S(1)} %maximum_select_fusion.3), channel_id=1, source_target_pairs={{0,4},{1,5},{2,6},{3,7},{4,0},{5,1},{6,2},{7,3},{8,12},{9,13},{10,... | collective-permute-start | bytes 12296 | tf_op jit(solution)/shard_map/ppermute | solution.py:1103
  395.1 27.4 %copy-start.35 = (bf16[256,768]{1,0:T(8,128)(2,1)S(1)}, bf16[256,768]{1,0:T(8,128)(2,1)}, u32[]{:S(2)}) copy-start(bf16[256,768]{1,0:T(8,128)(2,1)} %copy-done.34) | copy-start | bytes 1179652
  395.1 33.2 %copy-start.22 = (bf16[2,256,1024]{2,1,0:T(8,128)(2,1)S(1)}, bf16[2,256,1024]{2,1,0:T(8,128)(2,1)}, u32[]{:S(2)}) copy-start(bf16[2,256,1024]{2,1,0:T(8,128)(2,1)} %copy-done.21) | copy-start | bytes 3145732
  415.8 8.1 %collective-permute-start.54 = (f32[8,128]{1,0:T(8,128)S(1)}, f32[8,128]{1,0:T(8,128)S(1)}, u32[]{:S(2)}, u32[]{:S(2)}) collective-permute-start(f32[8,128]{1,0:T(8,128)S(1)} %maximum_select_fusion.2), channel_id=1, source_target_pairs={{0,8},{8,0},{16,24},{24,16},{1,9},{9,1},{17,25},{25,17},{2,10},{10... | collective-permute-start | bytes 12296 | tf_op jit(solution)/shard_map/ppermute | solution.py:1103
  422.5 14.1 %collective-permute-start.39 = (bf16[256,768]{1,0:T(8,128)(2,1)S(1)}, bf16[256,768]{1,0:T(8,128)(2,1)}, u32[]{:S(2)}, u32[]{:S(2)}) collective-permute-start(bf16[256,768]{1,0:T(8,128)(2,1)S(1)} %copy-done.35), channel_id=1, source_target_pairs={{8,16},{16,8},{9,17},{17,9},{10,18},{18,10},{11,19},{19,11},{12,20... | collective-permute-start | bytes 1179656 | tf_op jit(solution)/shard_map/ppermute | solution.py:1110
  423.9 48.2 %collective-permute-start.50 = (bf16[2,256,1024]{2,1,0:T(8,128)(2,1)}, bf16[2,256,1024]{2,1,0:T(8,128)(2,1)}, u32[]{:S(2)}, u32[]{:S(2)}) collective-permute-start(bf16[2,256,1024]{2,1,0:T(8,128)(2,1)} %get-tuple-element.277), channel_id=1, source_target_pairs={{8,0},{16,24},{9,1},{17,25},{10,2},{18,26},{11,3},{19,27},{12,4},{... | collective-permute-start | bytes 3145736 | tf_op jit(solution)/shard_map/ppermute | solution.py:1114
  425.2 6.5 %collective-permute-start.55 = (f32[8,128]{1,0:T(8,128)S(1)}, f32[8,128]{1,0:T(8,128)S(1)}, u32[]{:S(2)}, u32[]{:S(2)}) collective-permute-start(f32[8,128]{1,0:T(8,128)S(1)} %maximum_select_fusion.1), channel_id=1, source_target_pairs={{0,16},{8,24},{16,0},{24,8},{1,17},{9,25},{17,1},{25,9},{2,18},{10... | collective-permute-start | bytes 12296 | tf_op jit(solution)/shard_map/ppermute | solution.py:1103
  431.8 1.2 collective-permute-start.56
  432.9 11.4 %collective-permute-start.49 = (bf16[2,128,1024]{2,1,0:T(8,128)(2,1)}, bf16[2,128,1024]{2,1,0:T(8,128)(2,1)}, u32[]{:S(2)}, u32[]{:S(2)}) collective-permute-start(bf16[2,128,1024]{2,1,0:T(8,128)(2,1)} %constant_dynamic-slice_fusion.1), channel_id=1, source_target_pairs={{0,1},{1,0},{2,3},{3,2},{4,5},{5,4},{6,7},{7,6},{8,9},{9,8},{10,11... | collective-permute-start | bytes 1572872 | tf_op jit(solution)/shard_map/ppermute | solution.py:1035
  436.6 34.0 %collective-permute-start.44 = (bf16[256,1280]{1,0:T(8,128)(2,1)}, bf16[256,1280]{1,0:T(8,128)(2,1)S(1)}, u32[]{:S(2)}, u32[]{:S(2)}) collective-permute-start(bf16[256,1280]{1,0:T(8,128)(2,1)} %copy-done.28), channel_id=1, source_target_pairs={{8,0},{16,24},{9,1},{17,25},{10,2},{18,26},{11,3},{19,27},{12,4},{... | collective-permute-start | bytes 1966088 | tf_op jit(solution)/shard_map/ppermute | solution.py:1114
  441.4 36.4 %collective-permute-start.41 = (bf16[2,256,1024]{2,1,0:T(8,128)(2,1)S(1)}, bf16[2,256,1024]{2,1,0:T(8,128)(2,1)S(1)}, u32[]{:S(2)}, u32[]{:S(2)}) collective-permute-start(bf16[2,256,1024]{2,1,0:T(8,128)(2,1)S(1)} %get-tuple-element.271), channel_id=1, source_target_pairs={{0,1},{1,0},{2,3},{3,2},{4,5},{5,4},{6,7},{7,6},{8,9},{9,8},{10,11... | collective-permute-start | bytes 3145736 | tf_op jit(solution)/shard_map/ppermute | solution.py:1035
  442.8 27.7 %collective-permute-start.46 = (bf16[256,768]{1,0:T(8,128)(2,1)S(1)}, bf16[256,768]{1,0:T(8,128)(2,1)S(1)}, u32[]{:S(2)}, u32[]{:S(2)}) collective-permute-start(bf16[256,768]{1,0:T(8,128)(2,1)S(1)} %get-tuple-element.275), channel_id=1, source_target_pairs={{8,0},{16,24},{9,1},{17,25},{10,2},{18,26},{11,3},{19,27},{12,4},{... | collective-permute-start | bytes 1179656 | tf_op jit(solution)/shard_map/ppermute | solution.py:1114
  445.6 25.1 %copy-start.29 = (bf16[256,1280]{1,0:T(8,128)(2,1)S(1)}, bf16[256,1280]{1,0:T(8,128)(2,1)}, u32[]{:S(2)}) copy-start(bf16[256,1280]{1,0:T(8,128)(2,1)} %copy-done.28) | copy-start | bytes 1966084
  470.5 1.5 collective-permute-start.47
  470.7 3.1 collective-permute-start.45
  473.6 5.3 %collective-permute-start.51 = (bf16[2,128,1024]{2,1,0:T(8,128)(2,1)S(1)}, bf16[2,128,1024]{2,1,0:T(8,128)(2,1)S(1)}, u32[]{:S(2)}, u32[]{:S(2)}) collective-permute-start(bf16[2,128,1024]{2,1,0:T(8,128)(2,1)S(1)} %constant_dynamic-slice_fusion), channel_id=1, source_target_pairs={{0,1},{1,0},{2,3},{3,2},{4,5},{5,4},{6,7},{7,6},{8,9},{9,8},{10,11... | collective-permute-start | bytes 1572872 | tf_op jit(solution)/shard_map/ppermute | solution.py:1035
  (88 other events, 421.6 us)

commit v4 on v3

--- a/solution.py
+++ b/solution.py
@@ -17,6 +17,10 @@
 anywhere = pl.BlockSpec(memory_space=pl.ANY)
 in_vmem = pl.BlockSpec(memory_space=pltpu.VMEM)
 in_hbm = pl.BlockSpec(memory_space=pltpu.HBM)
+
+
+def pinned(array):
+    return pltpu.with_memory_space_constraint(array, pltpu.HBM)
 
 
 class Steps:
@@ -208,7 +212,7 @@
     return steps.launch(
         "attention_forward",
         functools.partial(forward_kernel, step=step),
-        [length, qkv, qkv, qkv, strips],
+        [length, qkv, qkv, qkv, pinned(strips)],
         [columns(which) for which in range(3)]
         + [pl.BlockSpec((2, tile, strip_width), lambda p, _: (start + p, 0, 0))],
         [
@@ -302,7 +306,7 @@
     return steps.launch(
         "attention_backward",
         functools.partial(backward_kernel, step=step),
-        [length, qkv, qkv, qkv, context, context_grad, log_totals, strips],
+        [length, qkv, qkv, qkv, context, context_grad, log_totals, pinned(strips)],
         [
             columns(0),
             columns(1),
@@ -337,10 +341,6 @@
 
 def beside(refs):
     return jnp.concatenate([ref[...] for ref in refs], axis=1)
-
-
-def pinned(array):
-    return pltpu.with_memory_space_constraint(array, pltpu.HBM)
 
 
 def start_copies(index_ref, pieces, target, semaphores, columns=None):
@@ -437,6 +437,25 @@
     for part in (0, 1):
         columns = slice(first + 2 * part * hidden, first + (2 * part + 1) * hidden)
         out_ref[:, columns] = scaled(out_ref[:, columns], gain_ref[:, 1:])
+
+
+def relay_kernel(source_ref, target_ref):
+    target_ref[...] = source_ref[...]
+
+
+def relay(steps, array):
+    block = pl.BlockSpec((1,) + array.shape[1:], lambda i: (i,) + (0,) * (array.ndim - 1))
+    return steps.launch(
+        "relay",
+        relay_kernel,
+        [array],
+        [block],
+        [block],
+        [(array.shape, low)],
+        grid=(array.shape[0],),
+        prefetch=0,
+        memory=8,
+    )[0]
 
 
 def pair_kernel(first_ref, second_ref, out_ref):
@@ -579,6 +598,7 @@
         [((total, width), low), ((total, width), low), ((width, total), low)],
         scratch=[pltpu.SemaphoreType.DMA((4,))],
         memory=24,
+        stored=() if normed else (1, 2),
         estimate=(0, 10 << 20),
     )
 
@@ -642,6 +662,7 @@
         [block, block, pl.BlockSpec((width, step), lambda i, _: (0, i))],
         [((total, width), wide), ((total, width), low), ((width, total), low)],
         grid=(total // step,),
+        stored=(0, 1, 2),
         estimate=(0, 14 << 20),
     )
 
@@ -722,7 +743,7 @@
             normed_grad_ref[...] = normed_sum[...].astype(low)
 
 
-def feed_forward(steps, places, normed, normed_t, grad, grad_t, pieces, before=None, step=512):
+def feed_forward(steps, places, normed, normed_t, grad, grad_t, pieces, before=None, step=1024):
     rows, width = normed.shape
     count = len(pieces)
     hidden = pieces[0].shape[3]
@@ -748,7 +769,7 @@
     return steps.launch(
         "feed_forward",
         functools.partial(feed_forward_kernel, count=count, first=first),
-        [places, normed, normed_t, grad, grad_t, *pieces, *before],
+        [places, *map(pinned, (normed, normed_t, grad, grad_t)), *pieces, *before],
         [whole, fixed((width, rows))] * 2 + [anywhere] * (count + len(before)),
         out_specs + [pl.BlockSpec((2, width // 2, step), lambda i, _: (0, 0, i))] * 2,
         out_shape + [((2, width // 2, hidden), low)] * 2,
@@ -798,7 +819,7 @@
             chips=chips,
             ordered=ordered,
         ),
-        [places, mine, other, hidden, grad, *pieces],
+        [places, mine, other, pinned(hidden), pinned(grad), *pieces],
         [block] * 4 + [anywhere] * count,
         [
             block,
@@ -1051,13 +1072,18 @@
             return list(range(self.chips))
         return [self.chip, self.chip ^ (1 + self.core), self.chip ^ (2 - self.core), self.chip ^ 3]
 
-    def gather(self, shard):
+    def gather_first(self, shard):
         if not self.square:
             whole = lax.all_gather(shard, "fsdp", axis=0, axis_index_groups=self.groups)
             return [whole[chip] for chip in range(self.chips)]
-        first = self.turn(shard, False)
-        second = self.turn(shard, True)
-        return [shard, first, second, self.turn(first, True)]
+        return [shard, self.turn(shard, False), self.turn(shard, True)]
+
+    def gather_last(self, pieces, arrived):
+        return [*pieces, self.turn(arrived, True)] if self.square else pieces
+
+    def gather(self, shard):
+        pieces = self.gather_first(shard)
+        return self.gather_last(pieces, pieces[1])
 
     def weight_places(self):
         return [2 * chip + side for chip in self.order() for side in (self.core, 1 - self.core)]
@@ -1111,7 +1137,10 @@
 
     def level_out(self, steps, terms):
         total = row_sums(steps, [(part, None) for part in terms])
-        outward = lax.ppermute(total, "ctx", [(1, 0), (2, 3)])
+        return total, lax.ppermute(total, "ctx", [(1, 0), (2, 3)])
+
+    def level_done(self, terms):
+        total, outward = terms
         inner = (self.level == 1) | (self.level == 2)
         return self.exchange_rows(jnp.where(inner, total, outward))
 
@@ -1250,12 +1279,12 @@
     _, out_low, out_low_t = token_rows_of(
         steps, slot_places, cotangent_halves, False, chips, square
     )
-    late_pieces = links.gather(late_shard)
+    late_pieces = links.gather_first(late_shard)
     hidden_one, normed_two, normed_two_t = second_norm(
         steps, order_line, token_low, attended, attended_other, chips, square
     )
     operands = (normed_two, normed_two_t, out_low, out_low_t)
-    steps.wait(late_pieces[1])
+    late_pieces = links.gather_last(late_pieces, relay(steps, late_pieces[1]))
     mixed_sum, normed_sum, *early_terms = feed_forward(steps, places, *operands, early_pieces)
     early = links.scatter(*early_terms)
     mixed_own, mixed_away, normed_two_part, *late_terms = feed_forward(
@@ -1298,6 +1327,7 @@
 
     *grads_a, strips_a = backward(0)
     *grads_b, strips_b = backward(1)
+    steps.wait(*result_trades)
     early = links.scatter_own(steps, early)
     late = links.scatter_near(steps, late)
     first = links.scatter(
@@ -1318,17 +1348,20 @@
     first = links.scatter_own(steps, first)
     late = links.level_across(steps, late)
     last = links.scatter_near(steps, last)
-    early_left, early_right = links.level_out(steps, early)
+    early = links.level_out(steps, early)
+    last = links.scatter_own(steps, last)
+    first = links.level_across(steps, first)
     input_quarters = finish_half(
         steps, core, odd, length, own_part, away_other, hidden_grad, token_low, True
     )
-    last = links.scatter_own(steps, last)
-    first = links.level_across(steps, first)
+    input_trades = links.from_slot(input_quarters)
+    steps.wait(early[1])
+    late = links.level_out(steps, late)
+    last = links.level_across(steps, last)
     result_pieces = links.gather(links.received(result_trades))
-    late_left, late_right = links.level_out(steps, late)
-    input_trades = links.from_slot(input_quarters)
-    last = links.level_across(steps, last)
-    first_left, first_right = links.level_out(steps, first)
+    first = links.level_out(steps, first)
+    early_left, early_right = links.level_done(early)
+    steps.wait(late[1], *input_trades)
     diagonals = jnp.concatenate(
         [diagonal_sums(steps, part) for part in (strips_a, strips_b, strips_c, strips_d)], axis=0
     ).reshape(own_heads, line_width)
@@ -1343,7 +1376,10 @@
     small = jnp.concatenate([table_grad, tops[:, : tile - bucket_count]], axis=1)
     for small in links.small_hops(small):
         pass
-    last_left, last_right = links.level_out(steps, last)
+    last = links.level_out(steps, last)
+    late_left, late_right = links.level_done(late)
+    first_left, first_right = links.level_done(first)
+    last_left, last_right = links.level_done(last)
     input_gradient = links.received(input_trades).astype(wide)
 
     def slot_of(wanted):

time: 488 us -> 424 us (0.87)
  local copies, waits for them, and re-layouts: 46.6 us -> 22.4 us
  waiting for transfers between devices: 84.4 us -> 60.3 us
  starting transfers between devices: 116 us -> 97.1 us
    unnamed x200 -> x156, local copies, waits for them, and re-layouts: 39.7 us -> 16 us
    ppermute x8, starting transfers between devices: 41 us -> 18.7 us  [trade(): return lax.ppermute(array, ('ctx', 'fsdp'), pairs)]
    ppermute x4, waiting for transfers between devices: 23.9 us -> 3.28 us  [small_hops(): other = lax.ppermute(small, axis, pairs)]
    ppermute x20, waiting for transfers between devices: 29.7 us -> 12.1 us  [turn(): return lax.ppermute(array, 'fsdp', pairs)]
    ppermute x13, starting transfers between devices: 10.5 us -> 17.9 us  [sibling(): return lax.ppermute(array, 'fsdp', [(i, i ^ 1) for i in range(self.shards)])]
    ppermute x4, waiting for transfers between devices: 24.8 us -> 30.7 us  [level_out(): return (total, lax.ppermute(total, 'ctx', [(1, 0), (2, 3)]))]
    pallas_call x49 -> x50, Pallas kernels: 207 us -> 209 us  [launch(): pl.pallas_call(run, grid_spec=pltpu.PrefetchScalarGridSpec(num_scalar_pre...]
  transfers between devices with their start and end apart: 57 -> 57, of which waited for: 12 -> 13; matrix products, arithmetic and copies ran while one was open for 5% -> 6% of each run, Pallas kernels for 38% -> 44%
where the time goes in v4:
time: 424 us; the launch traced here: 419 us
  Pallas kernels  209 us (49%)
  starting transfers between devices  97.1 us (23%)
  waiting for transfers between devices  60.3 us (14%)
  local copies, waits for them, and re-layouts  22.4 us (5%)
  other arithmetic  21.4 us (5%)
  between operations  7.65 us (2%)
    pallas_call x50, Pallas kernels, launch(): pl.pallas_call(run, grid_spec=pltpu.PrefetchScalarGridSpec(num_scalar_pre...  209 us
    ppermute x4, waiting for transfers between devices, level_out(): return (total, lax.ppermute(total, 'ctx', [(1, 0), (2, 3)]))  30.7 us
    ppermute x20, starting transfers between devices, turn(): return lax.ppermute(array, 'fsdp', pairs)  23.8 us
    ppermute x4, starting transfers between devices, scatter_own(): return (total, lax.ppermute(total, 'ctx', [(0, 1), (3, 2)]))  21.4 us
    ppermute x8, starting transfers between devices, trade(): return lax.ppermute(array, ('ctx', 'fsdp'), pairs)  18.7 us
    ppermute x13, starting transfers between devices, sibling(): return lax.ppermute(array, 'fsdp', [(i, i ^ 1) for i in range(self.shards)])  17.9 us
    unnamed x156, local copies, waits for them, and re-layouts  16 us
    ppermute x20, waiting for transfers between devices, turn(): return lax.ppermute(array, 'fsdp', pairs)  12.1 us
  transfers between devices with their start and end apart: 57, of which 13 were waited for; matrix products, arithmetic and copies ran while one was open for 6% of the time, Pallas kernels for 44%

profile of v4, /device:TPU:0, one launch (start us, length us, event | category | flops | bytes accessed | tf_op | source)
XLA Modules:
  0.0 418.9 jit_solution(6561704648977521592)
XLA Ops:
  2.1 2.2 send_blocks.2
  4.3 1.7 other_side.1
  6.6 3.0 collective-permute-done.2.refs_6_.refs_4_
  9.6 2.2 attention_shard.1
  11.9 2.9 collective-permute-start.4
  14.8 5.4 %collective-permute-start = (bf16[256,1024]{1,0:T(8,128)(2,1)}, bf16[256,1024]{1,0:T(8,128)(2,1)}, u32[]{:S(2)}, u32[]{:S(2)}) collective-permute-start(bf16[256,1024]{1,0:T(8,128)(2,1)} %get-tuple-element.151), channel_id=1, source_target_pairs={{0,0},{1,16},{2,2},{3,18},{4,4},{5,20},{6,6},{7,22},{8,8},{9,24},{... | collective-permute-start | bytes 1572872 | tf_op jit(solution)/shard_map/ppermute | solution.py:1164
  20.1 1.6 collective-permute-start.1
  23.3 1.6 collective-permute-start.5
  24.8 5.7 %bias_strips.1 = (f32[8,128,2048]{2,1,0:T(8,128)}, f32[8,128]{1,0:T(8,128)S(1)}) custom-call(f32[8,1,2048]{2,1,0:T(1,128)S(1)} %reshape.43.refs_0_, f32[8,128]{1,0:T(8,128)S(1)} %get-tuple-element.156.refs_1_), custom_call_target="tpu_custom_call" | custom-call | bytes 8388608 | tf_op jit(solution)/shard_map/bias_strips/pallas_call | solution.py:57
  35.6 4.2 collective-permute-done.1.refs_1_
  39.8 2.0 pair.2
  41.8 1.6 collective-permute-start.6
  46.3 2.0 collective-permute-start.7
  48.2 4.4 %collective-permute-start.8 = (bf16[256,1024]{1,0:T(8,128)(2,1)}, bf16[256,1024]{1,0:T(8,128)(2,1)S(1)}, u32[]{:S(2)}, u32[]{:S(2)}) collective-permute-start(bf16[256,1024]{1,0:T(8,128)(2,1)} %copy-done.42), channel_id=1, source_target_pairs={{0,8},{1,24},{2,10},{3,26},{4,12},{5,28},{6,14},{7,30},{8,0},{9,16... | collective-permute-start | bytes 1572872 | tf_op jit(solution)/shard_map/ppermute | solution.py:1164
  55.6 3.6 token_rows.1
  60.5 6.2 %qkv_product.1 = (bf16[1024,1536]{1,0:T(8,128)(2,1)S(1)}, f32[8,128]{1,0:T(8,128)S(1)}) custom-call(s32[13]{0:T(128)S(1)} %stack.175.refs_0_, bf16[1024,1024]{1,0:T(8,128)(2,1)S(1)} %get-tuple-element.165.refs_1_, bf16[2,128,2048]{2,1,0:T(8,128)(2,1)} %get-tuple-element.162.refs_2_.refs_3_.refs_5_.refs_13_, ...), custom_call_target="tpu_custom_call" | custom-call | flops 3221225472 | bytes 8388608 | tf_op jit(solution)/shard_map/qkv_product/pallas_call | solution.py:57
  66.7 12.5 %attention_forward.2 = (bf16[1024,256]{1,0:T(8,128)(2,1)S(1)}, f32[2,2,1024]{2,1,0:T(2,128)S(1)}, f32[2,2,128]{2,1,0:T(2,128)S(1)}, f32[8,128]{1,0:T(8,128)S(1)}) custom-call(s32[1]{0:T(128)} %bitcast.14.refs_0_, bf16[1024,1536]{1,0:T(8,128)(2,1)S(1)} %get-tuple-element.167.refs_1_.refs_2_.refs_3_, ...), custom_call_target="tpu_custom_call" | custom-call | flops 12000000000 | bytes 6291456 | tf_op jit(solution)/shard_map/attention_forward/pallas_call | solution.py:57
  79.8 12.2 %attention_forward.3 = (bf16[1024,256]{1,0:T(8,128)(2,1)S(1)}, f32[2,2,1024]{2,1,0:T(2,128)S(1)}, f32[2,2,128]{2,1,0:T(2,128)S(1)}, f32[8,128]{1,0:T(8,128)S(1)}) custom-call(s32[1]{0:T(128)} %bitcast.14.refs_0_, bf16[1024,1536]{1,0:T(8,128)(2,1)S(1)} %get-tuple-element.167.refs_1_.refs_2_.refs_3_, ...), custom_call_target="tpu_custom_call" | custom-call | flops 12000000000 | bytes 6291456 | tf_op jit(solution)/shard_map/attention_forward/pallas_call | solution.py:57
  92.1 3.8 attended_product.1
  95.9 1.9 collective-permute-start.11
  100.7 2.5 collective-permute-done.12.refs_2_
  103.2 4.4 %cotangent_rows.1 = (bf16[1024,1024]{1,0:T(8,128)(2,1)}, bf16[1024,1024]{1,0:T(8,128)(2,1)}, bf16[1024,1024]{1,0:T(8,128)(2,1)}, f32[8,128]{1,0:T(8,128)S(1)}) custom-call(s32[9]{0:T(128)S(1)} %stack.181.refs_0_, bf16[2,256,1024]{2,1,0:T(8,128)(2,1)S(1)} %get-tuple-element.179.refs_1_, bf16[2,256,1024]{2,1,0:T(8,128)(2,1)S(1)} %collective-permute-done.12.refs_2_, ...), custom_call_target="tpu_custom_call" | custom-call | bytes 10485760 | tf_op jit(solution)/shard_map/cotangent_rows/pallas_call | solution.py:57
  107.5 4.8 %second_norm.1 = (f32[1024,1024]{1,0:T(8,128)}, bf16[1024,1024]{1,0:T(8,128)(2,1)}, bf16[1024,1024]{1,0:T(8,128)(2,1)}, f32[8,128]{1,0:T(8,128)S(1)}) custom-call(s32[4]{0:T(128)S(1)} %pad_add_fusion.2.refs_0_, bf16[1024,1024]{1,0:T(8,128)(2,1)S(1)} %get-tuple-element.164.refs_1_.refs_4_, bf16[1024,1024]{1,0:T(8,128)(2,1)S(1)} %get-tuple-element.178.refs_2_, ...), custom_call_target="tpu_custom_call" | custom-call | bytes 14680064 | tf_op jit(solution)/shard_map/second_norm/pallas_call | solution.py:57
  112.3 11.7 %collective-permute-done.13.refs_0_.refs_6_ = bf16[2,2,128,1024]{3,2,1,0:T(8,128)(2,1)S(1)} collective-permute-done((bf16[2,2,128,1024]{3,2,1,0:T(8,128)(2,1)S(1)}, bf16[2,2,128,1024]{3,2,1,0:T(8,128)(2,1)S(1)}, u32[]{:S(2)}, u32[]{:S(2)}) %collective-permute-start.13) | collective-permute-done | bytes 1048608 | tf_op jit(solution)/shard_map/ppermute | solution.py:1068
  126.8 23.4 %feed_forward.2 = (f32[1024,1024]{1,0:T(8,128)}, f32[1024,1024]{1,0:T(8,128)}, bf16[2,512,1024]{2,1,0:T(8,128)(2,1)}, bf16[2,512,1024]{2,1,0:T(8,128)(2,1)}, f32[8,128]{1,0:T(8,128)}) custom-call(s32[13]{0:T(128)} %copy-done.28, bf16[1024,1024]{1,0:T(8,128)(2,1)} %get-tuple-element.182.refs_1_, bf16[1024,1024]{1,0:T(8,128)(2,1)} %get-tuple-element.183.refs_2_, ...), custom_call_target="tpu_custom_call" | custom-call | flops 21474836480 | bytes 41943040 | tf_op jit(solution)/shard_map/feed_forward/pallas_call | solution.py:57
  150.2 1.9 collective-permute-start.19
  152.1 24.5 %feed_forward.3 = (bf16[512,1024]{1,0:T(8,128)(2,1)}, bf16[512,1024]{1,0:T(8,128)(2,1)}, bf16[1024,1024]{1,0:T(8,128)(2,1)}, bf16[2,512,1024]{2,1,0:T(8,128)(2,1...) custom-call(s32[13]{0:T(128)} %copy-done.28, bf16[1024,1024]{1,0:T(8,128)(2,1)} %get-tuple-element.182.refs_1_, ...), custom_call_target="tpu_custom_call" | custom-call | flops 21474836480 | bytes 41943040 | tf_op jit(solution)/shard_map/feed_forward/pallas_call | solution.py:57
  178.9 2.4 row_sums.16
  181.4 2.0 collective-permute-start.26
  183.4 8.8 %hidden_back.1 = (f32[1024,1024]{1,0:T(8,128)S(1)}, bf16[1024,1024]{1,0:T(8,128)(2,1)}, bf16[1024,1024]{1,0:T(8,128)(2,1)S(1)}, bf16[1024,512]{1,0:T(8,128)(2,1)S(1)}, f32[8,128]{1,0:T(8,128)S(1)}) custom-call(s32[13]{0:T(128)S(1)} %copy-done.29, bf16[1024,1024]{1,0:T(8,128)(2,1)S(1)} %copy-done.11, bf16[1024,1024]{1,0:T(8,128)(2,1)S(1)} %collective-permute-done.18.refs_2_, ...), custom_call_target="tpu_custom_call" | custom-call | flops 2147483648 | bytes 25165824 | tf_op jit(solution)/shard_map/hidden_back/pallas_call | solution.py:57
  195.2 2.2 collective-permute-start.21
  197.4 11.1 %attention_backward.4 = (bf16[1024,128]{1,0:T(8,128)(2,1)S(1)}, bf16[1024,128]{1,0:T(8,128)(2,1)S(1)}, bf16[1024,128]{1,0:T(8,128)(2,1)S(1)}, f32[2,128,2048]{2,1,0:T(8,128)}, f32[8,128]{1,0:T(8,128)S(1)}) custom-call(s32[1]{0:T(128)} %bitcast.14.refs_0_, bf16[1024,1536]{1,0:T(8,128)(2,1)S(1)} %copy-done.47, bf16[1024,1536]{1,0:T(8,128)(2,1)S(1)} %copy-done.47, ...), custom_call_target="tpu_custom_call" | custom-call | flops 10000000000 | bytes 6291456 | tf_op jit(solution)/shard_map/attention_backward/pallas_call | solution.py:57
  208.4 11.1 %attention_backward.5 = (bf16[1024,128]{1,0:T(8,128)(2,1)S(1)}, bf16[1024,128]{1,0:T(8,128)(2,1)S(1)}, bf16[1024,128]{1,0:T(8,128)(2,1)S(1)}, f32[2,128,2048]{2,1,0:T(8,128)}, f32[8,128]{1,0:T(8,128)S(1)}) custom-call(s32[1]{0:T(128)} %bitcast.14.refs_0_, bf16[1024,1536]{1,0:T(8,128)(2,1)S(1)} %copy-done.47, bf16[1024,1536]{1,0:T(8,128)(2,1)S(1)} %copy-done.47, ...), custom_call_target="tpu_custom_call" | custom-call | flops 10000000000 | bytes 6291456 | tf_op jit(solution)/shard_map/attention_backward/pallas_call | solution.py:57
  219.6 2.9 row_sums.17
  224.5 3.1 attention_terms.2
  228.5 2.5 collective-permute-start.29
  231.0 11.4 %attention_backward.6 = (bf16[1024,128]{1,0:T(8,128)(2,1)S(1)}, bf16[1024,128]{1,0:T(8,128)(2,1)S(1)}, bf16[1024,128]{1,0:T(8,128)(2,1)S(1)}, f32[2,128,2048]{2,1,0:T(8,128)}, f32[8,128]{1,0:T(8,128)S(1)}) custom-call(s32[1]{0:T(128)} %bitcast.14.refs_0_, bf16[1024,1536]{1,0:T(8,128)(2,1)S(1)} %copy-done.47, bf16[1024,1536]{1,0:T(8,128)(2,1)S(1)} %copy-done.47, ...), custom_call_target="tpu_custom_call" | custom-call | flops 10000000000 | bytes 6291456 | tf_op jit(solution)/shard_map/attention_backward/pallas_call | solution.py:57
  244.6 11.1 %attention_backward.7 = (bf16[1024,128]{1,0:T(8,128)(2,1)S(1)}, bf16[1024,128]{1,0:T(8,128)(2,1)S(1)}, bf16[1024,128]{1,0:T(8,128)(2,1)S(1)}, f32[2,128,2048]{2,1,0:T(8,128)}, f32[8,128]{1,0:T(8,128)S(1)}) custom-call(s32[1]{0:T(128)} %bitcast.14.refs_0_, bf16[1024,1536]{1,0:T(8,128)(2,1)S(1)} %copy-done.47, bf16[1024,1536]{1,0:T(8,128)(2,1)S(1)} %copy-done.47, ...), custom_call_target="tpu_custom_call" | custom-call | flops 10000000000 | bytes 6291456 | tf_op jit(solution)/shard_map/attention_backward/pallas_call | solution.py:57
  257.2 2.0 attention_terms.3
  261.6 7.5 %input_product.1 = (f32[512,1024]{1,0:T(8,128)S(1)}, bf16[512,1024]{1,0:T(8,128)(2,1)}, f32[8,128]{1,0:T(8,128)S(1)}) custom-call(s32[13]{0:T(128)S(1)} %copy-done.29, bf16[1024,128]{1,0:T(8,128)(2,1)S(1)} %get-tuple-element.210.refs_4_.refs_1_, bf16[1024,128]{1,0:T(8,128)(2,1)S(1)} %get-tuple-element.211.refs_5_.refs_2_, ...), custom_call_target="tpu_custom_call" | custom-call | flops 3221225472 | bytes 14680064 | tf_op jit(solution)/shard_map/input_product/pallas_call | solution.py:57
  270.5 10.9 %collective-permute-start.37 = (bf16[512,1024]{1,0:T(8,128)(2,1)}, bf16[512,1024]{1,0:T(8,128)(2,1)}, u32[]{:S(2)}, u32[]{:S(2)}) collective-permute-start(bf16[512,1024]{1,0:T(8,128)(2,1)} %get-tuple-element.254), channel_id=1, source_target_pairs={{0,1},{1,0},{2,3},{3,2},{4,5},{5,4},{6,7},{7,6},{8,9},{9,8},{10,11... | collective-permute-start | bytes 3145736 | tf_op jit(solution)/shard_map/ppermute | solution.py:1056
  283.0 1.7 row_sums.23
  284.7 1.8 collective-permute-start.36
  287.4 1.8 row_sums.25
  291.0 13.2 %collective-permute-start.38 = (bf16[256,1280]{1,0:T(8,128)(2,1)}, bf16[256,1280]{1,0:T(8,128)(2,1)}, u32[]{:S(2)}, u32[]{:S(2)}) collective-permute-start(bf16[256,1280]{1,0:T(8,128)(2,1)} %get-tuple-element.256.refs_0_), channel_id=1, source_target_pairs={{0,8},{24,16},{1,9},{25,17},{2,10},{26,18},{3,11},{27,19},{4,12},{... | collective-permute-start | bytes 1966088 | tf_op jit(solution)/shard_map/ppermute | solution.py:1116
  304.3 2.1 collective-permute-start.22
  311.6 2.6 stack.158.refs_0_
  316.7 1.6 collective-permute-done.38.refs_1_
  318.3 4.4 %collective-permute-start.35 = (bf16[256,768]{1,0:T(8,128)(2,1)S(1)}, bf16[256,768]{1,0:T(8,128)(2,1)S(1)}, u32[]{:S(2)}, u32[]{:S(2)}) collective-permute-start(bf16[256,768]{1,0:T(8,128)(2,1)S(1)} %get-tuple-element.251.refs_0_), channel_id=1, source_target_pairs={{0,8},{24,16},{1,9},{25,17},{2,10},{26,18},{3,11},{27,19},{4,12},{... | collective-permute-start | bytes 1179656 | tf_op jit(solution)/shard_map/ppermute | solution.py:1116
  322.7 2.3 row_sums.27
  325.8 2.2 copy-done.6
  327.9 2.8 input_gradient_rows.1
  331.4 1.7 collective-permute-start.44
  333.1 2.4 row_sums.28
  338.3 2.1 collective-permute-start.50
  342.1 2.4 collective-permute-done.44.refs_4_
  349.8 25.3 %collective-permute-done.42.refs_2_ = bf16[2,256,1024]{2,1,0:T(8,128)(2,1)S(1)} collective-permute-done((bf16[2,256,1024]{2,1,0:T(8,128)(2,1)S(1)}, bf16[2,256,1024]{2,1,0:T(8,128)(2,1)S(1)}, u32[]{:S(2)}, u32[]{:S(2)}) %collective-permute-start.42) | collective-permute-done | bytes 1048608 | tf_op jit(solution)/shard_map/ppermute | solution.py:1140
  383.3 1.7 collective-permute-done.52
  385.7 3.5 collective-permute-done.46
  391.2 1.9 pick_slots.1
  394.5 4.3 %collective-permute-start.55 = (f32[8,128]{1,0:T(8,128)S(1)}, f32[8,128]{1,0:T(8,128)S(1)}, u32[]{:S(2)}, u32[]{:S(2)}) collective-permute-start(f32[8,128]{1,0:T(8,128)S(1)} %maximum_select_fusion.1), channel_id=1, source_target_pairs={{0,16},{8,24},{16,0},{24,8},{1,17},{9,25},{17,1},{25,9},{2,18},{10... | collective-permute-start | bytes 12296 | tf_op jit(solution)/shard_map/ppermute | solution.py:1129
  404.9 1.9 collective-permute-done.48
  411.1 2.4 convert_multiply_fusion
  413.9 2.3 convert_multiply_fusion.6
  (315 shorter events, 80.3 us)
Async XLA Ops:
  0.6 21.9 %copy-start = (bf16[32,16]{0,1:T(8,128)(2,1)S(1)}, bf16[32,16]{0,1:T(8,128)(2,1)}, u32[]{:S(2)}) copy-start(bf16[32,16]{0,1:T(8,128)(2,1)} %param.28) | copy-start | bytes 3076
  6.0 15.7 %copy-start.63 = (s32[2047]{0:T(1024)S(1)}, s32[2047]{0:T(1024)}, u32[]{:S(2)}) copy-start(s32[2047]{0:T(1024)} %param.19) | copy-start | bytes 24568
  6.1 3.6 collective-permute-start.2
  11.9 29.9 %collective-permute-start.4 = (bf16[2,128,2048]{2,1,0:T(8,128)(2,1)}, bf16[2,128,2048]{2,1,0:T(8,128)(2,1)S(1)}, u32[]{:S(2)}, u32[]{:S(2)}) collective-permute-start(bf16[2,128,2048]{2,1,0:T(8,128)(2,1)} %get-tuple-element.162.refs_2_.refs_3_.refs_5_.refs_13_), channel_id=1, source_target_pairs={{0,2},{1,5},{2,0},{3,7},{4,6},{5,1},{6,4},{7,3},{8,10},{9,13},{10,... | collective-permute-start | bytes 3145736 | tf_op jit(solution)/shard_map/ppermute | solution.py:1068
  14.8 20.8 %collective-permute-start = (bf16[256,1024]{1,0:T(8,128)(2,1)}, bf16[256,1024]{1,0:T(8,128)(2,1)}, u32[]{:S(2)}, u32[]{:S(2)}) collective-permute-start(bf16[256,1024]{1,0:T(8,128)(2,1)} %get-tuple-element.151), channel_id=1, source_target_pairs={{0,0},{1,16},{2,2},{3,18},{4,4},{5,20},{6,6},{7,22},{8,8},{9,24},{... | collective-permute-start | bytes 1572872 | tf_op jit(solution)/shard_map/ppermute | solution.py:1164
  20.1 19.6 %collective-permute-start.1 = (bf16[256,1024]{1,0:T(8,128)(2,1)}, bf16[256,1024]{1,0:T(8,128)(2,1)}, u32[]{:S(2)}, u32[]{:S(2)}) collective-permute-start(bf16[256,1024]{1,0:T(8,128)(2,1)} %get-tuple-element.152), channel_id=1, source_target_pairs={{0,8},{1,24},{2,10},{3,26},{4,12},{5,28},{6,14},{7,30},{8,0},{9,16... | collective-permute-start | bytes 1572872 | tf_op jit(solution)/shard_map/ppermute | solution.py:1164
  23.3 29.4 %collective-permute-start.5 = (bf16[2,128,2048]{2,1,0:T(8,128)(2,1)}, bf16[2,128,2048]{2,1,0:T(8,128)(2,1)}, u32[]{:S(2)}, u32[]{:S(2)}) collective-permute-start(bf16[2,128,2048]{2,1,0:T(8,128)(2,1)} %get-tuple-element.162.refs_2_.refs_3_.refs_5_.refs_13_), channel_id=1, source_target_pairs={{0,4},{1,3},{2,6},{3,1},{4,0},{5,7},{6,2},{7,5},{8,12},{9,11},{10,... | collective-permute-start | bytes 3145736 | tf_op jit(solution)/shard_map/ppermute | solution.py:1068
  41.8 12.7 %collective-permute-start.3 = (bf16[2,256,1024]{2,1,0:T(8,128)(2,1)}, bf16[2,256,1024]{2,1,0:T(8,128)(2,1)}, u32[]{:S(2)}, u32[]{:S(2)}) collective-permute-start(bf16[2,256,1024]{2,1,0:T(8,128)(2,1)} %get-tuple-element.160.refs_1_), channel_id=1, source_target_pairs={{0,1},{1,0},{2,3},{3,2},{4,5},{5,4},{6,7},{7,6},{8,9},{9,8},{10,11... | collective-permute-start | bytes 3145736 | tf_op jit(solution)/shard_map/ppermute | solution.py:1056
  41.8 18.7 %collective-permute-start.6 = (bf16[2,128,2048]{2,1,0:T(8,128)(2,1)S(1)}, bf16[2,128,2048]{2,1,0:T(8,128)(2,1)}, u32[]{:S(2)}, u32[]{:S(2)}) collective-permute-start(bf16[2,128,2048]{2,1,0:T(8,128)(2,1)S(1)} %collective-permute-done.4.refs_6_.refs_3_.refs_4_.refs_14_), channel_id=1, source_target_pairs={{0,4},{1,3},{2,6},{3,1},{4,0},{5,7},{6,2},{7,5},{8,12},{9,11},{10,... | collective-permute-start | bytes 3145736 | tf_op jit(solution)/shard_map/ppermute | solution.py:1068
  46.2 45.8 %copy-start.28 = (s32[13]{0:T(128)}, s32[13]{0:T(128)S(1)}, u32[]{:S(2)}) copy-start(s32[13]{0:T(128)S(1)} %stack.175.refs_0_) | copy-start | bytes 160
  46.3 33.0 %collective-permute-start.7 = (bf16[256,1024]{1,0:T(8,128)(2,1)}, bf16[256,1024]{1,0:T(8,128)(2,1)S(1)}, u32[]{:S(2)}, u32[]{:S(2)}) collective-permute-start(bf16[256,1024]{1,0:T(8,128)(2,1)} %copy-done.43), channel_id=1, source_target_pairs={{0,0},{1,16},{2,2},{3,18},{4,4},{5,20},{6,6},{7,22},{8,8},{9,24},{... | collective-permute-start | bytes 1572872 | tf_op jit(solution)/shard_map/ppermute | solution.py:1164
  48.2 31.0 %collective-permute-start.8 = (bf16[256,1024]{1,0:T(8,128)(2,1)}, bf16[256,1024]{1,0:T(8,128)(2,1)S(1)}, u32[]{:S(2)}, u32[]{:S(2)}) collective-permute-start(bf16[256,1024]{1,0:T(8,128)(2,1)} %copy-done.42), channel_id=1, source_target_pairs={{0,8},{1,24},{2,10},{3,26},{4,12},{5,28},{6,14},{7,30},{8,0},{9,16... | collective-permute-start | bytes 1572872 | tf_op jit(solution)/shard_map/ppermute | solution.py:1164
  53.9 25.6 %collective-permute-start.9 = (bf16[2,2,128,1024]{3,2,1,0:T(8,128)(2,1)S(1)}, bf16[2,2,128,1024]{3,2,1,0:T(8,128)(2,1)S(1)}, u32[]{:S(2)}, u32[]{:S(2)}) collective-permute-start(bf16[2,2,128,1024]{3,2,1,0:T(8,128)(2,1)S(1)} %get-tuple-element.175.refs_5_), channel_id=1, source_target_pairs={{0,2},{1,5},{2,0},{3,7},{4,6},{5,1},{6,4},{7,3},{8,10},{9,13},{10,... | collective-permute-start | bytes 3145736 | tf_op jit(solution)/shard_map/ppermute | solution.py:1068
  54.5 25.3 %collective-permute-start.10 = (bf16[2,2,128,1024]{3,2,1,0:T(8,128)(2,1)S(1)}, bf16[2,2,128,1024]{3,2,1,0:T(8,128)(2,1)S(1)}, u32[]{:S(2)}, u32[]{:S(2)}) collective-permute-start(bf16[2,2,128,1024]{3,2,1,0:T(8,128)(2,1)S(1)} %get-tuple-element.175.refs_5_), channel_id=1, source_target_pairs={{0,4},{1,3},{2,6},{3,1},{4,0},{5,7},{6,2},{7,5},{8,12},{9,11},{10,... | collective-permute-start | bytes 3145736 | tf_op jit(solution)/shard_map/ppermute | solution.py:1068
  79.5 19.1 %copy-start.40 = (bf16[2,2,128,1024]{3,2,1,0:T(8,128)(2,1)}, bf16[2,2,128,1024]{3,2,1,0:T(8,128)(2,1)S(1)}, u32[]{:S(2)}) copy-start(bf16[2,2,128,1024]{3,2,1,0:T(8,128)(2,1)S(1)} %collective-permute-done.9.refs_6_) | copy-start | bytes 3145732
  95.9 11.6 %collective-permute-start.11 = (bf16[1024,1024]{1,0:T(8,128)(2,1)S(1)}, bf16[1024,1024]{1,0:T(8,128)(2,1)S(1)}, u32[]{:S(2)}, u32[]{:S(2)}) collective-permute-start(bf16[1024,1024]{1,0:T(8,128)(2,1)S(1)} %get-tuple-element.178.refs_2_), channel_id=1, source_target_pairs={{0,1},{1,0},{2,3},{3,2},{4,5},{5,4},{6,7},{7,6},{8,9},{9,8},{10,11... | collective-permute-start | bytes 6291464 | tf_op jit(solution)/shard_map/ppermute | solution.py:1056
  97.9 5.3 %collective-permute-start.12 = (bf16[2,256,1024]{2,1,0:T(8,128)(2,1)S(1)}, bf16[2,256,1024]{2,1,0:T(8,128)(2,1)S(1)}, u32[]{:S(2)}, u32[]{:S(2)}) collective-permute-start(bf16[2,256,1024]{2,1,0:T(8,128)(2,1)S(1)} %get-tuple-element.179.refs_1_), channel_id=1, source_target_pairs={{0,1},{1,0},{2,3},{3,2},{4,5},{5,4},{6,7},{7,6},{8,9},{9,8},{10,11... | collective-permute-start | bytes 3145736 | tf_op jit(solution)/shard_map/ppermute | solution.py:1056
  98.0 26.0 %collective-permute-start.13 = (bf16[2,2,128,1024]{3,2,1,0:T(8,128)(2,1)S(1)}, bf16[2,2,128,1024]{3,2,1,0:T(8,128)(2,1)S(1)}, u32[]{:S(2)}, u32[]{:S(2)}) collective-permute-start(bf16[2,2,128,1024]{3,2,1,0:T(8,128)(2,1)S(1)} %copy-done.38), channel_id=1, source_target_pairs={{0,2},{1,5},{2,0},{3,7},{4,6},{5,1},{6,4},{7,3},{8,10},{9,13},{10,... | collective-permute-start | bytes 3145736 | tf_op jit(solution)/shard_map/ppermute | solution.py:1068
  98.6 27.2 %collective-permute-start.16 = (bf16[2,2,128,1024]{3,2,1,0:T(8,128)(2,1)S(1)}, bf16[2,2,128,1024]{3,2,1,0:T(8,128)(2,1)S(1)}, u32[]{:S(2)}, u32[]{:S(2)}) collective-permute-start(bf16[2,2,128,1024]{3,2,1,0:T(8,128)(2,1)S(1)} %collective-permute-done.9.refs_6_), channel_id=1, source_target_pairs={{0,4},{1,3},{2,6},{3,1},{4,0},{5,7},{6,2},{7,5},{8,12},{9,11},{10,... | collective-permute-start | bytes 3145736 | tf_op jit(solution)/shard_map/ppermute | solution.py:1068
  100.2 51.9 %collective-permute-start.14 = (bf16[2,2,128,1024]{3,2,1,0:T(8,128)(2,1)S(1)}, bf16[2,2,128,1024]{3,2,1,0:T(8,128)(2,1)}, u32[]{:S(2)}, u32[]{:S(2)}) collective-permute-start(bf16[2,2,128,1024]{3,2,1,0:T(8,128)(2,1)S(1)} %copy-done.38), channel_id=1, source_target_pairs={{0,4},{1,3},{2,6},{3,1},{4,0},{5,7},{6,2},{7,5},{8,12},{9,11},{10,... | collective-permute-start | bytes 3145736 | tf_op jit(solution)/shard_map/ppermute | solution.py:1068
  125.6 26.5 %collective-permute-start.15 = (bf16[2,2,128,1024]{3,2,1,0:T(8,128)(2,1)S(1)}, bf16[2,2,128,1024]{3,2,1,0:T(8,128)(2,1)}, u32[]{:S(2)}, u32[]{:S(2)}) collective-permute-start(bf16[2,2,128,1024]{3,2,1,0:T(8,128)(2,1)S(1)} %get-tuple-element.188), channel_id=1, source_target_pairs={{0,4},{1,3},{2,6},{3,1},{4,0},{5,7},{6,2},{7,5},{8,12},{9,11},{10,... | collective-permute-start | bytes 3145736 | tf_op jit(solution)/shard_map/ppermute | solution.py:1068
  150.2 28.1 %collective-permute-start.19 = (bf16[2,512,1024]{2,1,0:T(8,128)(2,1)}, bf16[2,512,1024]{2,1,0:T(8,128)(2,1)}, u32[]{:S(2)}, u32[]{:S(2)}) collective-permute-start(bf16[2,512,1024]{2,1,0:T(8,128)(2,1)} %get-tuple-element.198), channel_id=1, source_target_pairs={{0,4},{1,3},{2,6},{3,1},{4,0},{5,7},{6,2},{7,5},{8,12},{9,11},{10,... | collective-permute-start | bytes 6291464 | tf_op jit(solution)/shard_map/ppermute | solution.py:1068
  152.1 26.2 %copy-start.4 = (bf16[2,512,1024]{2,1,0:T(8,128)(2,1)S(1)}, bf16[2,512,1024]{2,1,0:T(8,128)(2,1)}, u32[]{:S(2)}) copy-start(bf16[2,512,1024]{2,1,0:T(8,128)(2,1)} %get-tuple-element.197.refs_0_) | copy-start | bytes 6291460
  176.6 6.8 %collective-permute-start.18 = (bf16[1024,1024]{1,0:T(8,128)(2,1)}, bf16[1024,1024]{1,0:T(8,128)(2,1)S(1)}, u32[]{:S(2)}, u32[]{:S(2)}) collective-permute-start(bf16[1024,1024]{1,0:T(8,128)(2,1)} %get-tuple-element.196.refs_1_), channel_id=1, source_target_pairs={{0,1},{1,0},{2,3},{3,2},{4,5},{5,4},{6,7},{7,6},{8,9},{9,8},{10,11... | collective-permute-start | bytes 6291464 | tf_op jit(solution)/shard_map/ppermute | solution.py:1056
  176.8 15.4 %collective-permute-start.17 = (bf16[512,1024]{1,0:T(8,128)(2,1)}, bf16[512,1024]{1,0:T(8,128)(2,1)S(1)}, u32[]{:S(2)}, u32[]{:S(2)}) collective-permute-start(bf16[512,1024]{1,0:T(8,128)(2,1)} %get-tuple-element.194), channel_id=1, source_target_pairs={{0,1},{1,0},{2,3},{3,2},{4,5},{5,4},{6,7},{7,6},{8,9},{9,8},{10,11... | collective-permute-start | bytes 3145736 | tf_op jit(solution)/shard_map/ppermute | solution.py:1056
  177.3 45.1 %collective-permute-start.25 = (bf16[2,512,1024]{2,1,0:T(8,128)(2,1)}, bf16[2,512,1024]{2,1,0:T(8,128)(2,1)S(1)}, u32[]{:S(2)}, u32[]{:S(2)}) collective-permute-start(bf16[2,512,1024]{2,1,0:T(8,128)(2,1)} %get-tuple-element.218), channel_id=1, source_target_pairs={{0,4},{1,3},{2,6},{3,1},{4,0},{5,7},{6,2},{7,5},{8,12},{9,11},{10,... | collective-permute-start | bytes 6291464 | tf_op jit(solution)/shard_map/ppermute | solution.py:1068
  181.4 38.1 %collective-permute-start.26 = (bf16[2,256,1024]{2,1,0:T(8,128)(2,1)S(1)}, bf16[2,256,1024]{2,1,0:T(8,128)(2,1)S(1)}, u32[]{:S(2)}, u32[]{:S(2)}) collective-permute-start(bf16[2,256,1024]{2,1,0:T(8,128)(2,1)S(1)} %get-tuple-element.219), channel_id=1, source_target_pairs={{0,2},{1,5},{2,0},{3,7},{4,6},{5,1},{6,4},{7,3},{8,10},{9,13},{10,... | collective-permute-start | bytes 3145736 | tf_op jit(solution)/shard_map/ppermute | solution.py:1068
  194.3 25.2 %collective-permute-start.20 = (bf16[256,1024]{1,0:T(8,128)(2,1)S(1)}, bf16[256,1024]{1,0:T(8,128)(2,1)S(1)}, u32[]{:S(2)}, u32[]{:S(2)}) collective-permute-start(bf16[256,1024]{1,0:T(8,128)(2,1)S(1)} %get-tuple-element.202), channel_id=1, source_target_pairs={{0,0},{16,1},{2,2},{18,3},{4,4},{20,5},{6,6},{22,7},{8,8},{24,9},{... | collective-permute-start | bytes 1572872 | tf_op jit(solution)/shard_map/ppermute | solution.py:1164
  195.2 24.4 %collective-permute-start.21 = (bf16[256,1024]{1,0:T(8,128)(2,1)S(1)}, bf16[256,1024]{1,0:T(8,128)(2,1)S(1)}, u32[]{:S(2)}, u32[]{:S(2)}) collective-permute-start(bf16[256,1024]{1,0:T(8,128)(2,1)S(1)} %get-tuple-element.203), channel_id=1, source_target_pairs={{8,0},{24,1},{10,2},{26,3},{12,4},{28,5},{14,6},{30,7},{0,8},{16,9... | collective-permute-start | bytes 1572872 | tf_op jit(solution)/shard_map/ppermute | solution.py:1164
  223.1 19.4 %collective-permute-start.27 = (bf16[2,256,1024]{2,1,0:T(8,128)(2,1)S(1)}, bf16[2,256,1024]{2,1,0:T(8,128)(2,1)S(1)}, u32[]{:S(2)}, u32[]{:S(2)}) collective-permute-start(bf16[2,256,1024]{2,1,0:T(8,128)(2,1)S(1)} %get-tuple-element.227), channel_id=1, source_target_pairs={{0,2},{1,5},{2,0},{3,7},{4,6},{5,1},{6,4},{7,3},{8,10},{9,13},{10,... | collective-permute-start | bytes 3145736 | tf_op jit(solution)/shard_map/ppermute | solution.py:1068
  227.6 29.3 %collective-permute-start.28 = (bf16[512,1280]{1,0:T(8,128)(2,1)S(1)}, bf16[512,1280]{1,0:T(8,128)(2,1)S(1)}, u32[]{:S(2)}, u32[]{:S(2)}) collective-permute-start(bf16[512,1280]{1,0:T(8,128)(2,1)S(1)} %get-tuple-element.234), channel_id=1, source_target_pairs={{0,4},{1,3},{2,6},{3,1},{4,0},{5,7},{6,2},{7,5},{8,12},{9,11},{10,... | collective-permute-start | bytes 3932168 | tf_op jit(solution)/shard_map/ppermute | solution.py:1068
  228.5 27.1 %collective-permute-start.29 = (bf16[2,256,1024]{2,1,0:T(8,128)(2,1)S(1)}, bf16[2,256,1024]{2,1,0:T(8,128)(2,1)S(1)}, u32[]{:S(2)}, u32[]{:S(2)}) collective-permute-start(bf16[2,256,1024]{2,1,0:T(8,128)(2,1)S(1)} %get-tuple-element.235.refs_0_), channel_id=1, source_target_pairs={{0,8},{24,16},{1,9},{25,17},{2,10},{26,18},{3,11},{27,19},{4,12},{... | collective-permute-start | bytes 3145736 | tf_op jit(solution)/shard_map/ppermute | solution.py:1116
  243.2 39.7 %collective-permute-start.31 = (bf16[2,256,1024]{2,1,0:T(8,128)(2,1)S(1)}, bf16[2,256,1024]{2,1,0:T(8,128)(2,1)S(1)}, u32[]{:S(2)}, u32[]{:S(2)}) collective-permute-start(bf16[2,256,1024]{2,1,0:T(8,128)(2,1)S(1)} %get-tuple-element.241.refs_0_), channel_id=1, source_target_pairs={{0,8},{24,16},{1,9},{25,17},{2,10},{26,18},{3,11},{27,19},{4,12},{... | collective-permute-start | bytes 3145736 | tf_op jit(solution)/shard_map/ppermute | solution.py:1116
  256.2 31.2 %collective-permute-start.34 = (bf16[2,256,1024]{2,1,0:T(8,128)(2,1)S(1)}, bf16[2,256,1024]{2,1,0:T(8,128)(2,1)S(1)}, u32[]{:S(2)}, u32[]{:S(2)}) collective-permute-start(bf16[2,256,1024]{2,1,0:T(8,128)(2,1)S(1)} %get-tuple-element.248.refs_0_), channel_id=1, source_target_pairs={{8,16},{16,8},{9,17},{17,9},{10,18},{18,10},{11,19},{19,11},{12,20... | collective-permute-start | bytes 3145736 | tf_op jit(solution)/shard_map/ppermute | solution.py:1136
  259.2 27.3 %copy-start.7 = (bf16[512,768]{1,0:T(8,128)(2,1)}, bf16[512,768]{1,0:T(8,128)(2,1)S(1)}, u32[]{:S(2)}) copy-start(bf16[512,768]{1,0:T(8,128)(2,1)S(1)} %get-tuple-element.239.refs_0_) | copy-start | bytes 2359300
  259.2 27.2 %collective-permute-start.30 = (bf16[512,768]{1,0:T(8,128)(2,1)S(1)}, bf16[512,768]{1,0:T(8,128)(2,1)S(1)}, u32[]{:S(2)}, u32[]{:S(2)}) collective-permute-start(bf16[512,768]{1,0:T(8,128)(2,1)S(1)} %get-tuple-element.240), channel_id=1, source_target_pairs={{0,4},{1,3},{2,6},{3,1},{4,0},{5,7},{6,2},{7,5},{8,12},{9,11},{10,... | collective-permute-start | bytes 2359304 | tf_op jit(solution)/shard_map/ppermute | solution.py:1068
  260.5 20.9 %collective-permute-start.32 = (bf16[256,1280]{1,0:T(8,128)(2,1)S(1)}, bf16[256,1280]{1,0:T(8,128)(2,1)S(1)}, u32[]{:S(2)}, u32[]{:S(2)}) collective-permute-start(bf16[256,1280]{1,0:T(8,128)(2,1)S(1)} %get-tuple-element.242), channel_id=1, source_target_pairs={{0,2},{1,5},{2,0},{3,7},{4,6},{5,1},{6,4},{7,3},{8,10},{9,13},{10,... | collective-permute-start | bytes 1966088 | tf_op jit(solution)/shard_map/ppermute | solution.py:1068
  270.5 54.5 %collective-permute-start.37 = (bf16[512,1024]{1,0:T(8,128)(2,1)}, bf16[512,1024]{1,0:T(8,128)(2,1)}, u32[]{:S(2)}, u32[]{:S(2)}) collective-permute-start(bf16[512,1024]{1,0:T(8,128)(2,1)} %get-tuple-element.254), channel_id=1, source_target_pairs={{0,1},{1,0},{2,3},{3,2},{4,5},{5,4},{6,7},{7,6},{8,9},{9,8},{10,11... | collective-permute-start | bytes 3145736 | tf_op jit(solution)/shard_map/ppermute | solution.py:1056
  284.7 46.0 %collective-permute-start.36 = (bf16[2,256,1024]{2,1,0:T(8,128)(2,1)}, bf16[2,256,1024]{2,1,0:T(8,128)(2,1)}, u32[]{:S(2)}, u32[]{:S(2)}) collective-permute-start(bf16[2,256,1024]{2,1,0:T(8,128)(2,1)} %get-tuple-element.252.refs_0_), channel_id=1, source_target_pairs={{8,16},{16,8},{9,17},{17,9},{10,18},{18,10},{11,19},{19,11},{12,20... | collective-permute-start | bytes 3145736 | tf_op jit(solution)/shard_map/ppermute | solution.py:1136
  289.1 42.3 %collective-permute-start.39 = (bf16[2,256,1024]{2,1,0:T(8,128)(2,1)}, bf16[2,256,1024]{2,1,0:T(8,128)(2,1)}, u32[]{:S(2)}, u32[]{:S(2)}) collective-permute-start(bf16[2,256,1024]{2,1,0:T(8,128)(2,1)} %get-tuple-element.260), channel_id=1, source_target_pairs={{8,0},{16,24},{9,1},{17,25},{10,2},{18,26},{11,3},{19,27},{12,4},{... | collective-permute-start | bytes 3145736 | tf_op jit(solution)/shard_map/ppermute | solution.py:1140
  290.4 13.8 %collective-permute-start.33 = (bf16[256,768]{1,0:T(8,128)(2,1)}, bf16[256,768]{1,0:T(8,128)(2,1)S(1)}, u32[]{:S(2)}, u32[]{:S(2)}) collective-permute-start(bf16[256,768]{1,0:T(8,128)(2,1)} %copy-done.44), channel_id=1, source_target_pairs={{0,2},{1,5},{2,0},{3,7},{4,6},{5,1},{6,4},{7,3},{8,10},{9,13},{10,... | collective-permute-start | bytes 1179656 | tf_op jit(solution)/shard_map/ppermute | solution.py:1068
  291.0 27.3 %collective-permute-start.38 = (bf16[256,1280]{1,0:T(8,128)(2,1)}, bf16[256,1280]{1,0:T(8,128)(2,1)}, u32[]{:S(2)}, u32[]{:S(2)}) collective-permute-start(bf16[256,1280]{1,0:T(8,128)(2,1)} %get-tuple-element.256.refs_0_), channel_id=1, source_target_pairs={{0,8},{24,16},{1,9},{25,17},{2,10},{26,18},{3,11},{27,19},{4,12},{... | collective-permute-start | bytes 1966088 | tf_op jit(solution)/shard_map/ppermute | solution.py:1116
  304.3 32.7 %collective-permute-start.22 = (bf16[2,256,1024]{2,1,0:T(8,128)(2,1)S(1)}, bf16[2,256,1024]{2,1,0:T(8,128)(2,1)}, u32[]{:S(2)}, u32[]{:S(2)}) collective-permute-start(bf16[2,256,1024]{2,1,0:T(8,128)(2,1)S(1)} %pad_maximum_fusion.refs_1_), channel_id=1, source_target_pairs={{0,2},{1,5},{2,0},{3,7},{4,6},{5,1},{6,4},{7,3},{8,10},{9,13},{10,... | collective-permute-start | bytes 3145736 | tf_op jit(solution)/shard_map/ppermute | solution.py:1068
  318.3 20.0 %collective-permute-start.35 = (bf16[256,768]{1,0:T(8,128)(2,1)S(1)}, bf16[256,768]{1,0:T(8,128)(2,1)S(1)}, u32[]{:S(2)}, u32[]{:S(2)}) collective-permute-start(bf16[256,768]{1,0:T(8,128)(2,1)S(1)} %get-tuple-element.251.refs_0_), channel_id=1, source_target_pairs={{0,8},{24,16},{1,9},{25,17},{2,10},{26,18},{3,11},{27,19},{4,12},{... | collective-permute-start | bytes 1179656 | tf_op jit(solution)/shard_map/ppermute | solution.py:1116
  325.0 21.4 %collective-permute-start.41 = (bf16[256,1280]{1,0:T(8,128)(2,1)S(1)}, bf16[256,1280]{1,0:T(8,128)(2,1)S(1)}, u32[]{:S(2)}, u32[]{:S(2)}) collective-permute-start(bf16[256,1280]{1,0:T(8,128)(2,1)S(1)} %get-tuple-element.267.refs_0_), channel_id=1, source_target_pairs={{8,16},{16,8},{9,17},{17,9},{10,18},{18,10},{11,19},{19,11},{12,20... | collective-permute-start | bytes 1966088 | tf_op jit(solution)/shard_map/ppermute | solution.py:1136
  330.7 9.9 %collective-permute-start.43 = (bf16[256,1024]{1,0:T(8,128)(2,1)S(1)}, bf16[256,1024]{1,0:T(8,128)(2,1)S(1)}, u32[]{:S(2)}, u32[]{:S(2)}) collective-permute-start(bf16[256,1024]{1,0:T(8,128)(2,1)S(1)} %get-tuple-element.271), channel_id=1, source_target_pairs={{0,0},{16,1},{2,2},{18,3},{4,4},{20,5},{6,6},{22,7},{8,8},{24,9},{... | collective-permute-start | bytes 1572872 | tf_op jit(solution)/shard_map/ppermute | solution.py:1164
  331.4 13.1 %collective-permute-start.44 = (bf16[256,1024]{1,0:T(8,128)(2,1)S(1)}, bf16[256,1024]{1,0:T(8,128)(2,1)S(1)}, u32[]{:S(2)}, u32[]{:S(2)}) collective-permute-start(bf16[256,1024]{1,0:T(8,128)(2,1)S(1)} %get-tuple-element.272), channel_id=1, source_target_pairs={{8,0},{24,1},{10,2},{26,3},{12,4},{28,5},{14,6},{30,7},{0,8},{16,9... | collective-permute-start | bytes 1572872 | tf_op jit(solution)/shard_map/ppermute | solution.py:1164
  337.0 38.1 %collective-permute-start.42 = (bf16[2,256,1024]{2,1,0:T(8,128)(2,1)S(1)}, bf16[2,256,1024]{2,1,0:T(8,128)(2,1)S(1)}, u32[]{:S(2)}, u32[]{:S(2)}) collective-permute-start(bf16[2,256,1024]{2,1,0:T(8,128)(2,1)S(1)} %get-tuple-element.270), channel_id=1, source_target_pairs={{8,0},{16,24},{9,1},{17,25},{10,2},{18,26},{11,3},{19,27},{12,4},{... | collective-permute-start | bytes 3145736 | tf_op jit(solution)/shard_map/ppermute | solution.py:1140
  338.3 9.0 %collective-permute-start.50 = (bf16[2,128,1024]{2,1,0:T(8,128)(2,1)S(1)}, bf16[2,128,1024]{2,1,0:T(8,128)(2,1)S(1)}, u32[]{:S(2)}, u32[]{:S(2)}) collective-permute-start(bf16[2,128,1024]{2,1,0:T(8,128)(2,1)S(1)} %constant_dynamic-slice_fusion.1), channel_id=1, source_target_pairs={{0,1},{1,0},{2,3},{3,2},{4,5},{5,4},{6,7},{7,6},{8,9},{9,8},{10,11... | collective-permute-start | bytes 1572872 | tf_op jit(solution)/shard_map/ppermute | solution.py:1056
  340.6 50.6 %collective-permute-start.23 = (bf16[2,256,1024]{2,1,0:T(8,128)(2,1)S(1)}, bf16[2,256,1024]{2,1,0:T(8,128)(2,1)S(1)}, u32[]{:S(2)}, u32[]{:S(2)}) collective-permute-start(bf16[2,256,1024]{2,1,0:T(8,128)(2,1)S(1)} %pad_maximum_fusion.refs_1_), channel_id=1, source_target_pairs={{0,4},{1,3},{2,6},{3,1},{4,0},{5,7},{6,2},{7,5},{8,12},{9,11},{10,... | collective-permute-start | bytes 3145736 | tf_op jit(solution)/shard_map/ppermute | solution.py:1068
  344.5 46.7 %collective-permute-start.24 = (bf16[2,256,1024]{2,1,0:T(8,128)(2,1)}, bf16[2,256,1024]{2,1,0:T(8,128)(2,1)S(1)}, u32[]{:S(2)}, u32[]{:S(2)}) collective-permute-start(bf16[2,256,1024]{2,1,0:T(8,128)(2,1)} %collective-permute-done.22.refs_2_), channel_id=1, source_target_pairs={{0,4},{1,3},{2,6},{3,1},{4,0},{5,7},{6,2},{7,5},{8,12},{9,11},{10,... | collective-permute-start | bytes 3145736 | tf_op jit(solution)/shard_map/ppermute | solution.py:1068
  346.4 44.7 %collective-permute-start.40 = (bf16[256,768]{1,0:T(8,128)(2,1)S(1)}, bf16[256,768]{1,0:T(8,128)(2,1)S(1)}, u32[]{:S(2)}, u32[]{:S(2)}) collective-permute-start(bf16[256,768]{1,0:T(8,128)(2,1)S(1)} %get-tuple-element.262.refs_0_), channel_id=1, source_target_pairs={{8,16},{16,8},{9,17},{17,9},{10,18},{18,10},{11,19},{19,11},{12,20... | collective-permute-start | bytes 1179656 | tf_op jit(solution)/shard_map/ppermute | solution.py:1136
  347.1 28.1 %copy-start.12 = (f32[2,128,2048]{2,1,0:T(8,128)S(1)}, f32[2,128,2048]{2,1,0:T(8,128)}, u32[]{:S(2)}) copy-start(f32[2,128,2048]{2,1,0:T(8,128)} %get-tuple-element.266.refs_0_) | copy-start | bytes 6291460
  347.3 41.8 %collective-permute-start.46 = (bf16[256,1280]{1,0:T(8,128)(2,1)S(1)}, bf16[256,1280]{1,0:T(8,128)(2,1)S(1)}, u32[]{:S(2)}, u32[]{:S(2)}) collective-permute-start(bf16[256,1280]{1,0:T(8,128)(2,1)S(1)} %get-tuple-element.280), channel_id=1, source_target_pairs={{8,0},{16,24},{9,1},{17,25},{10,2},{18,26},{11,3},{19,27},{12,4},{... | collective-permute-start | bytes 1966088 | tf_op jit(solution)/shard_map/ppermute | solution.py:1140
  381.4 3.6 collective-permute-start.52
  385.1 4.2 %collective-permute-start.53 = (f32[8,128]{1,0:T(8,128)S(1)}, f32[8,128]{1,0:T(8,128)S(1)}, u32[]{:S(2)}, u32[]{:S(2)}) collective-permute-start(f32[8,128]{1,0:T(8,128)S(1)} %maximum_select_fusion.3), channel_id=1, source_target_pairs={{0,4},{1,5},{2,6},{3,7},{4,0},{5,1},{6,2},{7,3},{8,12},{9,13},{10,... | collective-permute-start | bytes 12296 | tf_op jit(solution)/shard_map/ppermute | solution.py:1129
  389.3 5.2 %collective-permute-start.54 = (f32[8,128]{1,0:T(8,128)S(1)}, f32[8,128]{1,0:T(8,128)S(1)}, u32[]{:S(2)}, u32[]{:S(2)}) collective-permute-start(f32[8,128]{1,0:T(8,128)S(1)} %maximum_select_fusion.2), channel_id=1, source_target_pairs={{0,8},{8,0},{16,24},{24,16},{1,9},{9,1},{17,25},{25,17},{2,10},{10... | collective-permute-start | bytes 12296 | tf_op jit(solution)/shard_map/ppermute | solution.py:1129
  390.2 12.6 %collective-permute-start.47 = (bf16[128,1280]{1,0:T(8,128)(2,1)}, bf16[128,1280]{1,0:T(8,128)(2,1)}, u32[]{:S(2)}, u32[]{:S(2)}) collective-permute-start(bf16[128,1280]{1,0:T(8,128)(2,1)} %constant_dynamic-slice_fusion.3), channel_id=1, source_target_pairs={{0,1},{1,0},{2,3},{3,2},{4,5},{5,4},{6,7},{7,6},{8,9},{9,8},{10,11... | collective-permute-start | bytes 983048 | tf_op jit(solution)/shard_map/ppermute | solution.py:1056
  393.1 23.1 %collective-permute-start.45 = (bf16[2,256,1024]{2,1,0:T(8,128)(2,1)}, bf16[2,256,1024]{2,1,0:T(8,128)(2,1)}, u32[]{:S(2)}, u32[]{:S(2)}) collective-permute-start(bf16[2,256,1024]{2,1,0:T(8,128)(2,1)} %get-tuple-element.279), channel_id=1, source_target_pairs={{0,1},{1,0},{2,3},{3,2},{4,5},{5,4},{6,7},{7,6},{8,9},{9,8},{10,11... | collective-permute-start | bytes 3145736 | tf_op jit(solution)/shard_map/ppermute | solution.py:1056
  393.2 13.6 %collective-permute-start.48 = (bf16[256,768]{1,0:T(8,128)(2,1)S(1)}, bf16[256,768]{1,0:T(8,128)(2,1)}, u32[]{:S(2)}, u32[]{:S(2)}) collective-permute-start(bf16[256,768]{1,0:T(8,128)(2,1)S(1)} %get-tuple-element.281), channel_id=1, source_target_pairs={{8,0},{16,24},{9,1},{17,25},{10,2},{18,26},{11,3},{19,27},{12,4},{... | collective-permute-start | bytes 1179656 | tf_op jit(solution)/shard_map/ppermute | solution.py:1140
  394.5 6.0 %collective-permute-start.55 = (f32[8,128]{1,0:T(8,128)S(1)}, f32[8,128]{1,0:T(8,128)S(1)}, u32[]{:S(2)}, u32[]{:S(2)}) collective-permute-start(f32[8,128]{1,0:T(8,128)S(1)} %maximum_select_fusion.1), channel_id=1, source_target_pairs={{0,16},{8,24},{16,0},{24,8},{1,17},{9,25},{17,1},{25,9},{2,18},{10... | collective-permute-start | bytes 12296 | tf_op jit(solution)/shard_map/ppermute | solution.py:1129
  400.5 1.2 collective-permute-start.56
  400.5 7.4 %collective-permute-start.51 = (bf16[2,128,1024]{2,1,0:T(8,128)(2,1)S(1)}, bf16[2,128,1024]{2,1,0:T(8,128)(2,1)}, u32[]{:S(2)}, u32[]{:S(2)}) collective-permute-start(bf16[2,128,1024]{2,1,0:T(8,128)(2,1)S(1)} %constant_dynamic-slice_fusion), channel_id=1, source_target_pairs={{0,1},{1,0},{2,3},{3,2},{4,5},{5,4},{6,7},{7,6},{8,9},{9,8},{10,11... | collective-permute-start | bytes 1572872 | tf_op jit(solution)/shard_map/ppermute | solution.py:1056
  407.9 5.6 %collective-permute-start.49 = (bf16[128,768]{1,0:T(8,128)(2,1)S(1)}, bf16[128,768]{1,0:T(8,128)(2,1)S(1)}, u32[]{:S(2)}, u32[]{:S(2)}) collective-permute-start(bf16[128,768]{1,0:T(8,128)(2,1)S(1)} %constant_dynamic-slice_fusion.2), channel_id=1, source_target_pairs={{0,1},{1,0},{2,3},{3,2},{4,5},{5,4},{6,7},{7,6},{8,9},{9,8},{10,11... | collective-permute-start | bytes 589832 | tf_op jit(solution)/shard_map/ppermute | solution.py:1056
  (66 other events, 263.0 us)

commit v5 on v4

--- a/solution.py
+++ b/solution.py
@@ -212,7 +212,7 @@
     return steps.launch(
         "attention_forward",
         functools.partial(forward_kernel, step=step),
-        [length, qkv, qkv, qkv, pinned(strips)],
+        [length, qkv, qkv, qkv, strips],
         [columns(which) for which in range(3)]
         + [pl.BlockSpec((2, tile, strip_width), lambda p, _: (start + p, 0, 0))],
         [
@@ -439,23 +439,24 @@
         out_ref[:, columns] = scaled(out_ref[:, columns], gain_ref[:, 1:])
 
 
-def relay_kernel(source_ref, target_ref):
-    target_ref[...] = source_ref[...]
-
-
-def relay(steps, array):
-    block = pl.BlockSpec((1,) + array.shape[1:], lambda i: (i,) + (0,) * (array.ndim - 1))
+def relay_kernel(first_ref, second_ref, first_out_ref, second_out_ref):
+    first_out_ref[...] = first_ref[...]
+    second_out_ref[...] = second_ref[...]
+
+
+def relay(steps, first, second):
+    block = pl.BlockSpec((1,) + first.shape[1:], lambda i: (i,) + (0,) * (first.ndim - 1))
     return steps.launch(
         "relay",
         relay_kernel,
-        [array],
-        [block],
-        [block],
-        [(array.shape, low)],
-        grid=(array.shape[0],),
+        [first, second],
+        [block, block],
+        [block, block],
+        [(first.shape, low)] * 2,
+        grid=(first.shape[0],),
         prefetch=0,
         memory=8,
-    )[0]
+    )
 
 
 def pair_kernel(first_ref, second_ref, out_ref):
@@ -513,7 +514,7 @@
     return steps.launch(
         "attention_shard",
         attention_shard_kernel,
-        [core, *map(pinned, weights), gains, arrived],
+        [core, *map(pinned, weights), gains, pinned(arrived)],
         [in_hbm] * 4 + [in_vmem, anywhere],
         [in_vmem],
         [((2, rows, columns), low)],
@@ -543,7 +544,7 @@
     return steps.launch(
         "hidden_shard",
         functools.partial(hidden_shard_kernel, part=part),
-        [core, *map(pinned, weights), gains, arrived],
+        [core, *map(pinned, weights), gains, pinned(arrived)],
         [in_hbm] * 2 + [in_vmem, anywhere],
         [in_vmem],
         [((2, 2, rows, columns // 4), low)],
@@ -592,7 +593,7 @@
     return steps.launch(
         "token_rows" if normed else "cotangent_rows",
         functools.partial(token_kernel, normed=normed, chips=chips, ordered=ordered),
-        [places, *pieces],
+        [places, *map(pinned, pieces)],
         [anywhere] * 2,
         [in_vmem] * 3,
         [((total, width), low), ((total, width), low), ((width, total), low)],
@@ -989,7 +990,7 @@
     return steps.launch(
         "input_gradient_rows" if back else "result_rows",
         functools.partial(finish_kernel, back=back),
-        [jnp.stack([core, odd, length]).astype(jnp.int32), own, other, base, tokens],
+        [jnp.stack([core, odd, length]).astype(jnp.int32), pinned(own), other, base, tokens],
         [half, half, whole, whole],
         [quarter, quarter],
         [((step, width), low)] * 2,
@@ -1072,18 +1073,21 @@
             return list(range(self.chips))
         return [self.chip, self.chip ^ (1 + self.core), self.chip ^ (2 - self.core), self.chip ^ 3]
 
-    def gather_first(self, shard):
+    def gather_whole(self, shard):
+        whole = lax.all_gather(shard, "fsdp", axis=0, axis_index_groups=self.groups)
+        return [whole[chip] for chip in range(self.chips)]
+
+    def gather(self, shard):
         if not self.square:
-            whole = lax.all_gather(shard, "fsdp", axis=0, axis_index_groups=self.groups)
-            return [whole[chip] for chip in range(self.chips)]
-        return [shard, self.turn(shard, False), self.turn(shard, True)]
-
-    def gather_last(self, pieces, arrived):
-        return [*pieces, self.turn(arrived, True)] if self.square else pieces
-
-    def gather(self, shard):
-        pieces = self.gather_first(shard)
-        return self.gather_last(pieces, pieces[1])
+            return self.gather_whole(shard)
+        first = self.turn(shard, False)
+        return [shard, first, self.turn(shard, True), self.turn(first, True)]
+
+    def gather_slowly(self, steps, shard, first):
+        if not self.square:
+            return self.gather_whole(shard)
+        arrived, own = relay(steps, first, shard)
+        return [shard, first, self.turn(own, True), self.turn(arrived, True)]
 
     def weight_places(self):
         return [2 * chip + side for chip in self.order() for side in (self.core, 1 - self.core)]
@@ -1243,22 +1247,21 @@
     own_table = lax.dynamic_slice_in_dim(bias_table, core * own_heads, own_heads, 1)
     lines = dot(own_table, matching.astype(low), 0, 1)
 
+    arrived = links.sibling(other_side(steps, core_line, attention_weights, feed_weights, gains))
     token_trades = links.to_slot(send_blocks(steps, odd_line, tokens))
-    arrived = links.sibling(other_side(steps, core_line, attention_weights, feed_weights, gains))
     attention_pieces = links.gather(
         attention_shard(steps, core_line, attention_weights, gains, arrived)
     )
     strips = bias_strips(steps, lines.reshape(own_heads, 1, line_width))
-    cotangent_sends = send_blocks(steps, odd_line, cotangent)
     late_shard = hidden_shard(steps, core_line, 1, feed_weights, gains, arrived)
+    steps.wait(*attention_pieces[1:3])
     token_halves = links.both_halves(steps, token_trades)
-    steps.wait(*attention_pieces[1:3])
-    early_shard = hidden_shard(steps, core_line, 0, feed_weights, gains, arrived)
-    cotangent_trades = links.to_slot(cotangent_sends)
-    early_pieces = links.gather(early_shard)
     token_low, normed_one, normed_one_t = token_rows_of(
         steps, slot_places, token_halves, True, chips, square
     )
+    early_shard = hidden_shard(steps, core_line, 0, feed_weights, gains, arrived)
+    early_pieces = links.gather(early_shard)
+    cotangent_trades = links.to_slot(send_blocks(steps, odd_line, cotangent))
     qkv_width = 3 * own_inner
     qkv = rows_product(
         steps, places, [normed_one], attention_pieces, 0, qkv_width, False, "qkv_product"
@@ -1271,20 +1274,21 @@
     steps.wait(*early_pieces[1:3])
     last_context, last_totals, last_tops = forward(half_pairs, half_pairs)
     contexts = [first_context, last_context]
+    steps.wait(early_pieces[-1])
     output_columns = (qkv_width, qkv_width + own_inner)
     attended = rows_product(
         steps, places, contexts, attention_pieces, *output_columns, True, "attended_product"
     )
     attended_other = links.sibling(attended)
+    late_first = links.turn(late_shard, False)
     _, out_low, out_low_t = token_rows_of(
         steps, slot_places, cotangent_halves, False, chips, square
     )
-    late_pieces = links.gather_first(late_shard)
     hidden_one, normed_two, normed_two_t = second_norm(
         steps, order_line, token_low, attended, attended_other, chips, square
     )
+    late_pieces = links.gather_slowly(steps, late_shard, late_first)
     operands = (normed_two, normed_two_t, out_low, out_low_t)
-    late_pieces = links.gather_last(late_pieces, relay(steps, late_pieces[1]))
     mixed_sum, normed_sum, *early_terms = feed_forward(steps, places, *operands, early_pieces)
     early = links.scatter(*early_terms)
     mixed_own, mixed_away, normed_two_part, *late_terms = feed_forward(

time: 424 us -> 420 us (level)
    ppermute x20, waiting for transfers between devices: 12.1 us -> 3.79 us  [turn(): return lax.ppermute(array, 'fsdp', pairs)]
    unnamed x156 -> x154, local copies, waits for them, and re-layouts: 16 us -> 14.4 us
  transfers between devices with their start and end apart: 57 -> 57, of which waited for: 13 -> 13; matrix products, arithmetic and copies ran while one was open for 6% -> 6% of each run, Pallas kernels for 44% -> 48%
where the time goes in v5:
time: 420 us; the launch traced here: 415 us
  Pallas kernels  213 us (51%)
  starting transfers between devices  94.5 us (22%)
  waiting for transfers between devices  56.5 us (13%)
  other arithmetic  21.3 us (5%)
  local copies, waits for them, and re-layouts  20.9 us (5%)
  between operations  7.46 us (2%)
    pallas_call x50, Pallas kernels, launch(): pl.pallas_call(run, grid_spec=pltpu.PrefetchScalarGridSpec(num_scalar_pre...  213 us
    ppermute x4, waiting for transfers between devices, level_out(): return (total, lax.ppermute(total, 'ctx', [(1, 0), (2, 3)]))  31.5 us
    ppermute x20, starting transfers between devices, turn(): return lax.ppermute(array, 'fsdp', pairs)  23.6 us
    ppermute x4, starting transfers between devices, scatter_own(): return (total, lax.ppermute(total, 'ctx', [(0, 1), (3, 2)]))  23.3 us
    ppermute x8, starting transfers between devices, trade(): return lax.ppermute(array, ('ctx', 'fsdp'), pairs)  21 us
    ppermute x13, starting transfers between devices, sibling(): return lax.ppermute(array, 'fsdp', [(i, i ^ 1) for i in range(self.shards)])  15.1 us
    unnamed x154, local copies, waits for them, and re-layouts  14.4 us
    ppermute x8, waiting for transfers between devices, trade(): return lax.ppermute(array, ('ctx', 'fsdp'), pairs)  10.1 us
  transfers between devices with their start and end apart: 57, of which 13 were waited for; matrix products, arithmetic and copies ran while one was open for 6% of the time, Pallas kernels for 48%

profile of v5, /device:TPU:0, one launch (start us, length us, event | category | flops | bytes accessed | tf_op | source)
XLA Modules:
  0.0 414.8 jit_solution(15566445295006757277)
XLA Ops:
  2.1 1.7 other_side.1
  4.3 2.2 send_blocks.2
  7.5 2.4 attention_shard.1
  10.0 2.9 collective-permute-start.3
  12.9 1.5 collective-permute-start.4
  14.4 5.4 %collective-permute-start = (bf16[256,1024]{1,0:T(8,128)(2,1)}, bf16[256,1024]{1,0:T(8,128)(2,1)}, u32[]{:S(2)}, u32[]{:S(2)}) collective-permute-start(bf16[256,1024]{1,0:T(8,128)(2,1)} %get-tuple-element.153), channel_id=1, source_target_pairs={{0,0},{1,16},{2,2},{3,18},{4,4},{5,20},{6,6},{7,22},{8,8},{9,24},{... | collective-permute-start | bytes 1572872 | tf_op jit(solution)/shard_map/ppermute | solution.py:1168
  19.8 1.6 collective-permute-start.1
  22.9 5.7 %bias_strips.1 = (f32[8,128,2048]{2,1,0:T(8,128)}, f32[8,128]{1,0:T(8,128)S(1)}) custom-call(f32[8,1,2048]{2,1,0:T(1,128)S(1)} %reshape.43.refs_0_, f32[8,128]{1,0:T(8,128)S(1)} %get-tuple-element.157.refs_1_), custom_call_target="tpu_custom_call" | custom-call | bytes 8388608 | tf_op jit(solution)/shard_map/bias_strips/pallas_call | solution.py:57
  30.9 8.5 %collective-permute-done.1.refs_1_ = bf16[256,1024]{1,0:T(8,128)(2,1)} collective-permute-done((bf16[256,1024]{1,0:T(8,128)(2,1)}, bf16[256,1024]{1,0:T(8,128)(2,1)}, u32[]{:S(2)}, u32[]{:S(2)}) %collective-permute-start.1) | collective-permute-done | bytes 524320 | tf_op jit(solution)/shard_map/ppermute | solution.py:1168
  39.4 1.7 pair.2
  44.6 3.6 token_rows.1
  48.3 2.1 hidden_shard.3
  50.6 1.9 collective-permute-start.10
  54.8 4.4 %collective-permute-start.8 = (bf16[256,1024]{1,0:T(8,128)(2,1)S(1)}, bf16[256,1024]{1,0:T(8,128)(2,1)S(1)}, u32[]{:S(2)}, u32[]{:S(2)}) collective-permute-start(bf16[256,1024]{1,0:T(8,128)(2,1)S(1)} %get-tuple-element.173), channel_id=1, source_target_pairs={{0,8},{1,24},{2,10},{3,26},{4,12},{5,28},{6,14},{7,30},{8,0},{9,16... | collective-permute-start | bytes 1572872 | tf_op jit(solution)/shard_map/ppermute | solution.py:1168
  59.2 6.3 %qkv_product.1 = (bf16[1024,1536]{1,0:T(8,128)(2,1)S(1)}, f32[8,128]{1,0:T(8,128)S(1)}) custom-call(s32[13]{0:T(128)S(1)} %stack.175.refs_0_, bf16[1024,1024]{1,0:T(8,128)(2,1)S(1)} %get-tuple-element.164.refs_1_, bf16[2,128,2048]{2,1,0:T(8,128)(2,1)} %get-tuple-element.160.refs_2_.refs_3_.refs_5_.refs_13_, ...), custom_call_target="tpu_custom_call" | custom-call | flops 3221225472 | bytes 8388608 | tf_op jit(solution)/shard_map/qkv_product/pallas_call | solution.py:57
  65.5 10.8 %attention_forward.2 = (bf16[1024,256]{1,0:T(8,128)(2,1)S(1)}, f32[2,2,1024]{2,1,0:T(2,128)S(1)}, f32[2,2,128]{2,1,0:T(2,128)S(1)}, f32[8,128]{1,0:T(8,128)S(1)}) custom-call(s32[1]{0:T(128)} %bitcast.14.refs_0_, bf16[1024,1536]{1,0:T(8,128)(2,1)S(1)} %get-tuple-element.168.refs_1_.refs_2_.refs_3_, ...), custom_call_target="tpu_custom_call" | custom-call | flops 12000000000 | bytes 6291456 | tf_op jit(solution)/shard_map/attention_forward/pallas_call | solution.py:57
  76.6 1.6 collective-permute-start.11
  78.5 10.8 %attention_forward.3 = (bf16[1024,256]{1,0:T(8,128)(2,1)S(1)}, f32[2,2,1024]{2,1,0:T(2,128)S(1)}, f32[2,2,128]{2,1,0:T(2,128)S(1)}, f32[8,128]{1,0:T(8,128)S(1)}) custom-call(s32[1]{0:T(128)} %bitcast.14.refs_0_, bf16[1024,1536]{1,0:T(8,128)(2,1)S(1)} %get-tuple-element.168.refs_1_.refs_2_.refs_3_, ...), custom_call_target="tpu_custom_call" | custom-call | flops 12000000000 | bytes 6291456 | tf_op jit(solution)/shard_map/attention_forward/pallas_call | solution.py:57
  89.4 2.1 collective-permute-done.11.refs_8_
  91.5 3.8 attended_product.1
  95.3 2.3 collective-permute-start.12
  99.1 3.8 collective-permute-done.13.refs_2_
  103.9 5.7 %cotangent_rows.1 = (bf16[1024,1024]{1,0:T(8,128)(2,1)}, bf16[1024,1024]{1,0:T(8,128)(2,1)}, bf16[1024,1024]{1,0:T(8,128)(2,1)}, f32[8,128]{1,0:T(8,128)S(1)}) custom-call(s32[9]{0:T(128)S(1)} %stack.181.refs_0_, bf16[2,256,1024]{2,1,0:T(8,128)(2,1)} %copy-done.25, bf16[2,256,1024]{2,1,0:T(8,128)(2,1)} %copy-done.55, f32[8,128]{1,0:T(8,128)S(1)} %get-tuple-element.181.refs_3_), custom_call_target="tpu_custom_call" | custom-call | bytes 10485760 | tf_op jit(solution)/shard_map/cotangent_rows/pallas_call | solution.py:57
  109.6 4.8 %second_norm.1 = (f32[1024,1024]{1,0:T(8,128)}, bf16[1024,1024]{1,0:T(8,128)(2,1)}, bf16[1024,1024]{1,0:T(8,128)(2,1)}, f32[8,128]{1,0:T(8,128)S(1)}) custom-call(s32[4]{0:T(128)S(1)} %pad_add_fusion.2.refs_0_, bf16[1024,1024]{1,0:T(8,128)(2,1)S(1)} %get-tuple-element.163.refs_1_.refs_4_, bf16[1024,1024]{1,0:T(8,128)(2,1)S(1)} %get-tuple-element.179.refs_2_, ...), custom_call_target="tpu_custom_call" | custom-call | bytes 14680064 | tf_op jit(solution)/shard_map/second_norm/pallas_call | solution.py:57
  114.4 2.0 relay.1
  118.5 23.4 %feed_forward.2 = (f32[1024,1024]{1,0:T(8,128)}, f32[1024,1024]{1,0:T(8,128)}, bf16[2,512,1024]{2,1,0:T(8,128)(2,1)}, bf16[2,512,1024]{2,1,0:T(8,128)(2,1)}, f32[8,128]{1,0:T(8,128)}) custom-call(s32[13]{0:T(128)} %copy-done.34, bf16[1024,1024]{1,0:T(8,128)(2,1)} %get-tuple-element.183.refs_1_, bf16[1024,1024]{1,0:T(8,128)(2,1)} %get-tuple-element.184.refs_2_, ...), custom_call_target="tpu_custom_call" | custom-call | flops 21474836480 | bytes 41943040 | tf_op jit(solution)/shard_map/feed_forward/pallas_call | solution.py:57
  144.2 24.5 %feed_forward.3 = (bf16[512,1024]{1,0:T(8,128)(2,1)}, bf16[512,1024]{1,0:T(8,128)(2,1)}, bf16[1024,1024]{1,0:T(8,128)(2,1)}, bf16[2,512,1024]{2,1,0:T(8,128)(2,1...) custom-call(s32[13]{0:T(128)} %copy-done.34, bf16[1024,1024]{1,0:T(8,128)(2,1)} %get-tuple-element.183.refs_1_, ...), custom_call_target="tpu_custom_call" | custom-call | flops 21474836480 | bytes 41943040 | tf_op jit(solution)/shard_map/feed_forward/pallas_call | solution.py:57
  170.8 1.6 copy-done.6
  173.1 2.4 row_sums.16
  176.9 8.4 %hidden_back.1 = (f32[1024,1024]{1,0:T(8,128)S(1)}, bf16[1024,1024]{1,0:T(8,128)(2,1)}, bf16[1024,1024]{1,0:T(8,128)(2,1)S(1)}, bf16[1024,512]{1,0:T(8,128)(2,1)S(1)}, f32[8,128]{1,0:T(8,128)S(1)}) custom-call(s32[13]{0:T(128)S(1)} %copy-done.35, bf16[1024,1024]{1,0:T(8,128)(2,1)S(1)} %copy-done.14, bf16[1024,1024]{1,0:T(8,128)(2,1)S(1)} %collective-permute-done.18.refs_2_, ...), custom_call_target="tpu_custom_call" | custom-call | flops 2147483648 | bytes 25165824 | tf_op jit(solution)/shard_map/hidden_back/pallas_call | solution.py:57
  185.4 4.3 %result_rows.1 = (bf16[256,1024]{1,0:T(8,128)(2,1)S(1)}, bf16[256,1024]{1,0:T(8,128)(2,1)S(1)}, f32[8,128]{1,0:T(8,128)S(1)}) custom-call(s32[3]{0:T(128)S(1)} %pad_add_fusion.1.refs_0_, bf16[512,1024]{1,0:T(8,128)(2,1)} %get-tuple-element.195.refs_1_, bf16[512,1024]{1,0:T(8,128)(2,1)S(1)} %collective-permute-done.17.refs_2_, f32[1024,1024]{1,0:T(8,128)S(1)} %copy-done.2, ...), custom_call_target="tpu_custom_call" | custom-call | bytes 6291456 | tf_op jit(solution)/shard_map/result_rows/pallas_call | solution.py:57
  190.4 6.4 %collective-permute-start.21 = (bf16[256,1024]{1,0:T(8,128)(2,1)S(1)}, bf16[256,1024]{1,0:T(8,128)(2,1)S(1)}, u32[]{:S(2)}, u32[]{:S(2)}) collective-permute-start(bf16[256,1024]{1,0:T(8,128)(2,1)S(1)} %get-tuple-element.205), channel_id=1, source_target_pairs={{8,0},{24,1},{10,2},{26,3},{12,4},{28,5},{14,6},{30,7},{0,8},{16,9... | collective-permute-start | bytes 1572872 | tf_op jit(solution)/shard_map/ppermute | solution.py:1168
  196.8 11.0 %attention_backward.4 = (bf16[1024,128]{1,0:T(8,128)(2,1)S(1)}, bf16[1024,128]{1,0:T(8,128)(2,1)S(1)}, bf16[1024,128]{1,0:T(8,128)(2,1)S(1)}, f32[2,128,2048]{2,1,0:T(8,128)}, f32[8,128]{1,0:T(8,128)S(1)}) custom-call(s32[1]{0:T(128)} %bitcast.14.refs_0_, bf16[1024,1536]{1,0:T(8,128)(2,1)S(1)} %copy-done.49, bf16[1024,1536]{1,0:T(8,128)(2,1)S(1)} %copy-done.49, ...), custom_call_target="tpu_custom_call" | custom-call | flops 10000000000 | bytes 6291456 | tf_op jit(solution)/shard_map/attention_backward/pallas_call | solution.py:57
  207.8 11.2 %attention_backward.5 = (bf16[1024,128]{1,0:T(8,128)(2,1)S(1)}, bf16[1024,128]{1,0:T(8,128)(2,1)S(1)}, bf16[1024,128]{1,0:T(8,128)(2,1)S(1)}, f32[2,128,2048]{2,1,0:T(8,128)}, f32[8,128]{1,0:T(8,128)S(1)}) custom-call(s32[1]{0:T(128)} %bitcast.14.refs_0_, bf16[1024,1536]{1,0:T(8,128)(2,1)S(1)} %copy-done.49, bf16[1024,1536]{1,0:T(8,128)(2,1)S(1)} %copy-done.49, ...), custom_call_target="tpu_custom_call" | custom-call | flops 10000000000 | bytes 6291456 | tf_op jit(solution)/shard_map/attention_backward/pallas_call | solution.py:57
  219.1 2.8 row_sums.17
  223.7 3.1 attention_terms.2
  227.7 2.0 collective-permute-start.29
  229.7 11.4 %attention_backward.6 = (bf16[1024,128]{1,0:T(8,128)(2,1)S(1)}, bf16[1024,128]{1,0:T(8,128)(2,1)S(1)}, bf16[1024,128]{1,0:T(8,128)(2,1)S(1)}, f32[2,128,2048]{2,1,0:T(8,128)}, f32[8,128]{1,0:T(8,128)S(1)}) custom-call(s32[1]{0:T(128)} %bitcast.14.refs_0_, bf16[1024,1536]{1,0:T(8,128)(2,1)S(1)} %copy-done.49, bf16[1024,1536]{1,0:T(8,128)(2,1)S(1)} %copy-done.49, ...), custom_call_target="tpu_custom_call" | custom-call | flops 10000000000 | bytes 6291456 | tf_op jit(solution)/shard_map/attention_backward/pallas_call | solution.py:57
  244.5 11.1 %attention_backward.7 = (bf16[1024,128]{1,0:T(8,128)(2,1)S(1)}, bf16[1024,128]{1,0:T(8,128)(2,1)S(1)}, bf16[1024,128]{1,0:T(8,128)(2,1)S(1)}, f32[2,128,2048]{2,1,0:T(8,128)}, f32[8,128]{1,0:T(8,128)S(1)}) custom-call(s32[1]{0:T(128)} %bitcast.14.refs_0_, bf16[1024,1536]{1,0:T(8,128)(2,1)S(1)} %copy-done.49, bf16[1024,1536]{1,0:T(8,128)(2,1)S(1)} %copy-done.49, ...), custom_call_target="tpu_custom_call" | custom-call | flops 10000000000 | bytes 6291456 | tf_op jit(solution)/shard_map/attention_backward/pallas_call | solution.py:57
  257.1 2.0 attention_terms.3
  260.8 7.3 %input_product.1 = (f32[512,1024]{1,0:T(8,128)S(1)}, bf16[512,1024]{1,0:T(8,128)(2,1)}, f32[8,128]{1,0:T(8,128)S(1)}) custom-call(s32[13]{0:T(128)S(1)} %copy-done.35, bf16[1024,128]{1,0:T(8,128)(2,1)S(1)} %get-tuple-element.212.refs_4_.refs_1_, bf16[1024,128]{1,0:T(8,128)(2,1)S(1)} %get-tuple-element.213.refs_5_.refs_2_, ...), custom_call_target="tpu_custom_call" | custom-call | flops 3221225472 | bytes 14680064 | tf_op jit(solution)/shard_map/input_product/pallas_call | solution.py:57
  269.4 6.7 %collective-permute-start.37 = (bf16[512,1024]{1,0:T(8,128)(2,1)}, bf16[512,1024]{1,0:T(8,128)(2,1)}, u32[]{:S(2)}, u32[]{:S(2)}) collective-permute-start(bf16[512,1024]{1,0:T(8,128)(2,1)} %get-tuple-element.256), channel_id=1, source_target_pairs={{0,1},{1,0},{2,3},{3,2},{4,5},{5,4},{6,7},{7,6},{8,9},{9,8},{10,11... | collective-permute-start | bytes 3145736 | tf_op jit(solution)/shard_map/ppermute | solution.py:1057
  276.1 1.5 row_sums.22
  277.7 1.7 row_sums.23
  279.4 1.8 collective-permute-start.36
  282.1 1.8 row_sums.25
  286.6 14.4 %collective-permute-start.38 = (bf16[256,1280]{1,0:T(8,128)(2,1)}, bf16[256,1280]{1,0:T(8,128)(2,1)}, u32[]{:S(2)}, u32[]{:S(2)}) collective-permute-start(bf16[256,1280]{1,0:T(8,128)(2,1)} %get-tuple-element.258.refs_0_), channel_id=1, source_target_pairs={{0,8},{24,16},{1,9},{25,17},{2,10},{26,18},{3,11},{27,19},{4,12},{... | collective-permute-start | bytes 1966088 | tf_op jit(solution)/shard_map/ppermute | solution.py:1120
  307.5 2.6 stack.158.refs_0_
  312.6 5.6 %collective-permute-start.35 = (bf16[256,768]{1,0:T(8,128)(2,1)S(1)}, bf16[256,768]{1,0:T(8,128)(2,1)S(1)}, u32[]{:S(2)}, u32[]{:S(2)}) collective-permute-start(bf16[256,768]{1,0:T(8,128)(2,1)S(1)} %get-tuple-element.253.refs_0_), channel_id=1, source_target_pairs={{0,8},{24,16},{1,9},{25,17},{2,10},{26,18},{3,11},{27,19},{4,12},{... | collective-permute-start | bytes 1179656 | tf_op jit(solution)/shard_map/ppermute | solution.py:1120
  318.2 2.3 row_sums.27
  321.2 2.2 copy-done.9
  323.4 3.1 input_gradient_rows.1
  328.1 2.4 row_sums.28
  333.3 2.6 collective-permute-start.50
  337.1 1.6 collective-permute-done.44.refs_4_
  344.5 25.0 %collective-permute-done.42.refs_2_ = bf16[2,256,1024]{2,1,0:T(8,128)(2,1)S(1)} collective-permute-done((bf16[2,256,1024]{2,1,0:T(8,128)(2,1)S(1)}, bf16[2,256,1024]{2,1,0:T(8,128)(2,1)S(1)}, u32[]{:S(2)}, u32[]{:S(2)}) %collective-permute-start.42) | collective-permute-done | bytes 1048608 | tf_op jit(solution)/shard_map/ppermute | solution.py:1144
  377.9 1.5 collective-permute-done.52
  380.4 3.2 collective-permute-done.46
  386.2 2.8 pick_slots.1
  390.7 4.4 %collective-permute-done.55 = f32[8,128]{1,0:T(8,128)S(1)} collective-permute-done((f32[8,128]{1,0:T(8,128)S(1)}, f32[8,128]{1,0:T(8,128)S(1)}, u32[]{:S(2)}, u32[]{:S(2)}) %collective-permute-start.55) | collective-permute-done | bytes 4128 | tf_op jit(solution)/shard_map/ppermute | solution.py:1133
  399.5 3.2 collective-permute-done.48
  405.5 1.5 maximum_convert_fusion.1
  407.1 2.4 convert_multiply_fusion
  409.8 2.3 convert_multiply_fusion.6
  (314 shorter events, 78.4 us)
Async XLA Ops:
  0.6 21.6 %copy-start = (bf16[32,16]{0,1:T(8,128)(2,1)S(1)}, bf16[32,16]{0,1:T(8,128)(2,1)}, u32[]{:S(2)}) copy-start(bf16[32,16]{0,1:T(8,128)(2,1)} %param.28) | copy-start | bytes 3076
  3.8 17.6 %copy-start.60 = (s32[2047]{0:T(1024)S(1)}, s32[2047]{0:T(1024)}, u32[]{:S(2)}) copy-start(s32[2047]{0:T(1024)} %param.19) | copy-start | bytes 24568
  3.8 3.7 collective-permute-start.2
  10.0 29.4 %collective-permute-start.3 = (bf16[2,128,2048]{2,1,0:T(8,128)(2,1)}, bf16[2,128,2048]{2,1,0:T(8,128)(2,1)S(1)}, u32[]{:S(2)}, u32[]{:S(2)}) collective-permute-start(bf16[2,128,2048]{2,1,0:T(8,128)(2,1)} %get-tuple-element.160.refs_2_.refs_3_.refs_5_.refs_13_), channel_id=1, source_target_pairs={{0,2},{1,5},{2,0},{3,7},{4,6},{5,1},{6,4},{7,3},{8,10},{9,13},{10,... | collective-permute-start | bytes 3145736 | tf_op jit(solution)/shard_map/ppermute | solution.py:1069
  12.9 26.5 %collective-permute-start.4 = (bf16[2,128,2048]{2,1,0:T(8,128)(2,1)}, bf16[2,128,2048]{2,1,0:T(8,128)(2,1)S(1)}, u32[]{:S(2)}, u32[]{:S(2)}) collective-permute-start(bf16[2,128,2048]{2,1,0:T(8,128)(2,1)} %get-tuple-element.160.refs_2_.refs_3_.refs_5_.refs_13_), channel_id=1, source_target_pairs={{0,4},{1,3},{2,6},{3,1},{4,0},{5,7},{6,2},{7,5},{8,12},{9,11},{10,... | collective-permute-start | bytes 3145736 | tf_op jit(solution)/shard_map/ppermute | solution.py:1069
  14.4 16.5 %collective-permute-start = (bf16[256,1024]{1,0:T(8,128)(2,1)}, bf16[256,1024]{1,0:T(8,128)(2,1)}, u32[]{:S(2)}, u32[]{:S(2)}) collective-permute-start(bf16[256,1024]{1,0:T(8,128)(2,1)} %get-tuple-element.153), channel_id=1, source_target_pairs={{0,0},{1,16},{2,2},{3,18},{4,4},{5,20},{6,6},{7,22},{8,8},{9,24},{... | collective-permute-start | bytes 1572872 | tf_op jit(solution)/shard_map/ppermute | solution.py:1168
  19.8 19.6 %collective-permute-start.1 = (bf16[256,1024]{1,0:T(8,128)(2,1)}, bf16[256,1024]{1,0:T(8,128)(2,1)}, u32[]{:S(2)}, u32[]{:S(2)}) collective-permute-start(bf16[256,1024]{1,0:T(8,128)(2,1)} %get-tuple-element.154), channel_id=1, source_target_pairs={{0,8},{1,24},{2,10},{3,26},{4,12},{5,28},{6,14},{7,30},{8,0},{9,16... | collective-permute-start | bytes 1572872 | tf_op jit(solution)/shard_map/ppermute | solution.py:1168
  41.1 3.5 collective-permute-start.5
  41.2 18.0 %collective-permute-start.6 = (bf16[2,128,2048]{2,1,0:T(8,128)(2,1)S(1)}, bf16[2,128,2048]{2,1,0:T(8,128)(2,1)}, u32[]{:S(2)}, u32[]{:S(2)}) collective-permute-start(bf16[2,128,2048]{2,1,0:T(8,128)(2,1)S(1)} %collective-permute-done.3.refs_3_.refs_4_.refs_6_.refs_14_), channel_id=1, source_target_pairs={{0,4},{1,3},{2,6},{3,1},{4,0},{5,7},{6,2},{7,5},{8,12},{9,11},{10,... | collective-permute-start | bytes 3145736 | tf_op jit(solution)/shard_map/ppermute | solution.py:1069
  44.6 46.9 %copy-start.34 = (s32[13]{0:T(128)}, s32[13]{0:T(128)S(1)}, u32[]{:S(2)}) copy-start(s32[13]{0:T(128)S(1)} %stack.175.refs_0_) | copy-start | bytes 160
  48.2 17.3 %slice-start = ((s8[8388608]{0:T(1024)(128)(4,1)}), s8[4194304]{0:T(1024)(128)(4,1)S(1)}, s32[]{:S(2)}) async-start(s8[8388608]{0:T(1024)(128)(4,1)} %bitcast.67), calls=%async_computation | async-start | bytes 8388608
  50.4 26.2 %collective-permute-start.9 = (bf16[2,2,128,1024]{3,2,1,0:T(8,128)(2,1)S(1)}, bf16[2,2,128,1024]{3,2,1,0:T(8,128)(2,1)S(1)}, u32[]{:S(2)}, u32[]{:S(2)}) collective-permute-start(bf16[2,2,128,1024]{3,2,1,0:T(8,128)(2,1)S(1)} %get-tuple-element.176.refs_5_), channel_id=1, source_target_pairs={{0,2},{1,5},{2,0},{3,7},{4,6},{5,1},{6,4},{7,3},{8,10},{9,13},{10,... | collective-permute-start | bytes 3145736 | tf_op jit(solution)/shard_map/ppermute | solution.py:1069
  50.6 27.9 %collective-permute-start.10 = (bf16[2,2,128,1024]{3,2,1,0:T(8,128)(2,1)S(1)}, bf16[2,2,128,1024]{3,2,1,0:T(8,128)(2,1)S(1)}, u32[]{:S(2)}, u32[]{:S(2)}) collective-permute-start(bf16[2,2,128,1024]{3,2,1,0:T(8,128)(2,1)S(1)} %get-tuple-element.176.refs_5_), channel_id=1, source_target_pairs={{0,4},{1,3},{2,6},{3,1},{4,0},{5,7},{6,2},{7,5},{8,12},{9,11},{10,... | collective-permute-start | bytes 3145736 | tf_op jit(solution)/shard_map/ppermute | solution.py:1069
  53.8 22.5 %collective-permute-start.7 = (bf16[256,1024]{1,0:T(8,128)(2,1)S(1)}, bf16[256,1024]{1,0:T(8,128)(2,1)S(1)}, u32[]{:S(2)}, u32[]{:S(2)}) collective-permute-start(bf16[256,1024]{1,0:T(8,128)(2,1)S(1)} %get-tuple-element.172), channel_id=1, source_target_pairs={{0,0},{1,16},{2,2},{3,18},{4,4},{5,20},{6,6},{7,22},{8,8},{9,24},{... | collective-permute-start | bytes 1572872 | tf_op jit(solution)/shard_map/ppermute | solution.py:1168
  54.8 21.5 %collective-permute-start.8 = (bf16[256,1024]{1,0:T(8,128)(2,1)S(1)}, bf16[256,1024]{1,0:T(8,128)(2,1)S(1)}, u32[]{:S(2)}, u32[]{:S(2)}) collective-permute-start(bf16[256,1024]{1,0:T(8,128)(2,1)S(1)} %get-tuple-element.173), channel_id=1, source_target_pairs={{0,8},{1,24},{2,10},{3,26},{4,12},{5,28},{6,14},{7,30},{8,0},{9,16... | collective-permute-start | bytes 1572872 | tf_op jit(solution)/shard_map/ppermute | solution.py:1168
  76.5 21.1 %copy-start.25 = (bf16[2,256,1024]{2,1,0:T(8,128)(2,1)}, bf16[2,256,1024]{2,1,0:T(8,128)(2,1)S(1)}, u32[]{:S(2)}) copy-start(bf16[2,256,1024]{2,1,0:T(8,128)(2,1)S(1)} %get-tuple-element.180.refs_1_) | copy-start | bytes 3145732
  76.6 14.9 %collective-permute-start.11 = (bf16[2,2,128,1024]{3,2,1,0:T(8,128)(2,1)S(1)}, bf16[2,2,128,1024]{3,2,1,0:T(8,128)(2,1)S(1)}, u32[]{:S(2)}, u32[]{:S(2)}) collective-permute-start(bf16[2,2,128,1024]{3,2,1,0:T(8,128)(2,1)S(1)} %collective-permute-done.9.refs_6_), channel_id=1, source_target_pairs={{0,4},{1,3},{2,6},{3,1},{4,0},{5,7},{6,2},{7,5},{8,12},{9,11},{10,... | collective-permute-start | bytes 3145736 | tf_op jit(solution)/shard_map/ppermute | solution.py:1069
  95.3 14.3 %collective-permute-start.12 = (bf16[1024,1024]{1,0:T(8,128)(2,1)S(1)}, bf16[1024,1024]{1,0:T(8,128)(2,1)S(1)}, u32[]{:S(2)}, u32[]{:S(2)}) collective-permute-start(bf16[1024,1024]{1,0:T(8,128)(2,1)S(1)} %get-tuple-element.179.refs_2_), channel_id=1, source_target_pairs={{0,1},{1,0},{2,3},{3,2},{4,5},{5,4},{6,7},{7,6},{8,9},{9,8},{10,11... | collective-permute-start | bytes 6291464 | tf_op jit(solution)/shard_map/ppermute | solution.py:1057
  97.6 5.3 %collective-permute-start.13 = (bf16[2,256,1024]{2,1,0:T(8,128)(2,1)S(1)}, bf16[2,256,1024]{2,1,0:T(8,128)(2,1)S(1)}, u32[]{:S(2)}, u32[]{:S(2)}) collective-permute-start(bf16[2,256,1024]{2,1,0:T(8,128)(2,1)S(1)} %get-tuple-element.180.refs_1_), channel_id=1, source_target_pairs={{0,1},{1,0},{2,3},{3,2},{4,5},{5,4},{6,7},{7,6},{8,9},{9,8},{10,11... | collective-permute-start | bytes 3145736 | tf_op jit(solution)/shard_map/ppermute | solution.py:1057
  97.7 16.7 %collective-permute-start.14 = (bf16[2,2,128,1024]{3,2,1,0:T(8,128)(2,1)S(1)}, bf16[2,2,128,1024]{3,2,1,0:T(8,128)(2,1)S(1)}, u32[]{:S(2)}, u32[]{:S(2)}) collective-permute-start(bf16[2,2,128,1024]{3,2,1,0:T(8,128)(2,1)S(1)} %copy-done.27), channel_id=1, source_target_pairs={{0,2},{1,5},{2,0},{3,7},{4,6},{5,1},{6,4},{7,3},{8,10},{9,13},{10,... | collective-permute-start | bytes 3145736 | tf_op jit(solution)/shard_map/ppermute | solution.py:1069
  116.4 26.8 %collective-permute-start.15 = (bf16[2,2,128,1024]{3,2,1,0:T(8,128)(2,1)}, bf16[2,2,128,1024]{3,2,1,0:T(8,128)(2,1)S(1)}, u32[]{:S(2)}, u32[]{:S(2)}) collective-permute-start(bf16[2,2,128,1024]{3,2,1,0:T(8,128)(2,1)} %get-tuple-element.189), channel_id=1, source_target_pairs={{0,4},{1,3},{2,6},{3,1},{4,0},{5,7},{6,2},{7,5},{8,12},{9,11},{10,... | collective-permute-start | bytes 3145736 | tf_op jit(solution)/shard_map/ppermute | solution.py:1069
  117.7 25.5 %collective-permute-start.16 = (bf16[2,2,128,1024]{3,2,1,0:T(8,128)(2,1)}, bf16[2,2,128,1024]{3,2,1,0:T(8,128)(2,1)}, u32[]{:S(2)}, u32[]{:S(2)}) collective-permute-start(bf16[2,2,128,1024]{3,2,1,0:T(8,128)(2,1)} %get-tuple-element.190), channel_id=1, source_target_pairs={{0,4},{1,3},{2,6},{3,1},{4,0},{5,7},{6,2},{7,5},{8,12},{9,11},{10,... | collective-permute-start | bytes 3145736 | tf_op jit(solution)/shard_map/ppermute | solution.py:1069
  141.9 28.9 %collective-permute-start.19 = (bf16[2,512,1024]{2,1,0:T(8,128)(2,1)}, bf16[2,512,1024]{2,1,0:T(8,128)(2,1)}, u32[]{:S(2)}, u32[]{:S(2)}) collective-permute-start(bf16[2,512,1024]{2,1,0:T(8,128)(2,1)} %get-tuple-element.200), channel_id=1, source_target_pairs={{0,4},{1,3},{2,6},{3,1},{4,0},{5,7},{6,2},{7,5},{8,12},{9,11},{10,... | collective-permute-start | bytes 6291464 | tf_op jit(solution)/shard_map/ppermute | solution.py:1069
  168.7 8.2 %collective-permute-start.18 = (bf16[1024,1024]{1,0:T(8,128)(2,1)}, bf16[1024,1024]{1,0:T(8,128)(2,1)S(1)}, u32[]{:S(2)}, u32[]{:S(2)}) collective-permute-start(bf16[1024,1024]{1,0:T(8,128)(2,1)} %get-tuple-element.198.refs_1_), channel_id=1, source_target_pairs={{0,1},{1,0},{2,3},{3,2},{4,5},{5,4},{6,7},{7,6},{8,9},{9,8},{10,11... | collective-permute-start | bytes 6291464 | tf_op jit(solution)/shard_map/ppermute | solution.py:1057
  168.8 16.6 %collective-permute-start.17 = (bf16[512,1024]{1,0:T(8,128)(2,1)}, bf16[512,1024]{1,0:T(8,128)(2,1)S(1)}, u32[]{:S(2)}, u32[]{:S(2)}) collective-permute-start(bf16[512,1024]{1,0:T(8,128)(2,1)} %get-tuple-element.196), channel_id=1, source_target_pairs={{0,1},{1,0},{2,3},{3,2},{4,5},{5,4},{6,7},{7,6},{8,9},{9,8},{10,11... | collective-permute-start | bytes 3145736 | tf_op jit(solution)/shard_map/ppermute | solution.py:1057
  169.3 52.6 %collective-permute-start.25 = (bf16[2,512,1024]{2,1,0:T(8,128)(2,1)}, bf16[2,512,1024]{2,1,0:T(8,128)(2,1)S(1)}, u32[]{:S(2)}, u32[]{:S(2)}) collective-permute-start(bf16[2,512,1024]{2,1,0:T(8,128)(2,1)} %get-tuple-element.220), channel_id=1, source_target_pairs={{0,4},{1,3},{2,6},{3,1},{4,0},{5,7},{6,2},{7,5},{8,12},{9,11},{10,... | collective-permute-start | bytes 6291464 | tf_op jit(solution)/shard_map/ppermute | solution.py:1069
  175.5 43.5 %collective-permute-start.26 = (bf16[2,256,1024]{2,1,0:T(8,128)(2,1)S(1)}, bf16[2,256,1024]{2,1,0:T(8,128)(2,1)S(1)}, u32[]{:S(2)}, u32[]{:S(2)}) collective-permute-start(bf16[2,256,1024]{2,1,0:T(8,128)(2,1)S(1)} %get-tuple-element.221), channel_id=1, source_target_pairs={{0,2},{1,5},{2,0},{3,7},{4,6},{5,1},{6,4},{7,3},{8,10},{9,13},{10,... | collective-permute-start | bytes 3145736 | tf_op jit(solution)/shard_map/ppermute | solution.py:1069
  189.7 29.3 %collective-permute-start.20 = (bf16[256,1024]{1,0:T(8,128)(2,1)S(1)}, bf16[256,1024]{1,0:T(8,128)(2,1)S(1)}, u32[]{:S(2)}, u32[]{:S(2)}) collective-permute-start(bf16[256,1024]{1,0:T(8,128)(2,1)S(1)} %get-tuple-element.204), channel_id=1, source_target_pairs={{0,0},{16,1},{2,2},{18,3},{4,4},{20,5},{6,6},{22,7},{8,8},{24,9},{... | collective-permute-start | bytes 1572872 | tf_op jit(solution)/shard_map/ppermute | solution.py:1168
  190.4 28.6 %collective-permute-start.21 = (bf16[256,1024]{1,0:T(8,128)(2,1)S(1)}, bf16[256,1024]{1,0:T(8,128)(2,1)S(1)}, u32[]{:S(2)}, u32[]{:S(2)}) collective-permute-start(bf16[256,1024]{1,0:T(8,128)(2,1)S(1)} %get-tuple-element.205), channel_id=1, source_target_pairs={{8,0},{24,1},{10,2},{26,3},{12,4},{28,5},{14,6},{30,7},{0,8},{16,9... | collective-permute-start | bytes 1572872 | tf_op jit(solution)/shard_map/ppermute | solution.py:1168
  222.5 19.9 %collective-permute-start.27 = (bf16[2,256,1024]{2,1,0:T(8,128)(2,1)S(1)}, bf16[2,256,1024]{2,1,0:T(8,128)(2,1)S(1)}, u32[]{:S(2)}, u32[]{:S(2)}) collective-permute-start(bf16[2,256,1024]{2,1,0:T(8,128)(2,1)S(1)} %get-tuple-element.229), channel_id=1, source_target_pairs={{0,2},{1,5},{2,0},{3,7},{4,6},{5,1},{6,4},{7,3},{8,10},{9,13},{10,... | collective-permute-start | bytes 3145736 | tf_op jit(solution)/shard_map/ppermute | solution.py:1069
  226.8 30.0 %collective-permute-start.28 = (bf16[512,1280]{1,0:T(8,128)(2,1)S(1)}, bf16[512,1280]{1,0:T(8,128)(2,1)S(1)}, u32[]{:S(2)}, u32[]{:S(2)}) collective-permute-start(bf16[512,1280]{1,0:T(8,128)(2,1)S(1)} %get-tuple-element.236), channel_id=1, source_target_pairs={{0,4},{1,3},{2,6},{3,1},{4,0},{5,7},{6,2},{7,5},{8,12},{9,11},{10,... | collective-permute-start | bytes 3932168 | tf_op jit(solution)/shard_map/ppermute | solution.py:1069
  227.7 27.9 %collective-permute-start.29 = (bf16[2,256,1024]{2,1,0:T(8,128)(2,1)S(1)}, bf16[2,256,1024]{2,1,0:T(8,128)(2,1)S(1)}, u32[]{:S(2)}, u32[]{:S(2)}) collective-permute-start(bf16[2,256,1024]{2,1,0:T(8,128)(2,1)S(1)} %get-tuple-element.237.refs_0_), channel_id=1, source_target_pairs={{0,8},{24,16},{1,9},{25,17},{2,10},{26,18},{3,11},{27,19},{4,12},{... | collective-permute-start | bytes 3145736 | tf_op jit(solution)/shard_map/ppermute | solution.py:1120
  243.1 34.6 %collective-permute-start.31 = (bf16[2,256,1024]{2,1,0:T(8,128)(2,1)S(1)}, bf16[2,256,1024]{2,1,0:T(8,128)(2,1)S(1)}, u32[]{:S(2)}, u32[]{:S(2)}) collective-permute-start(bf16[2,256,1024]{2,1,0:T(8,128)(2,1)S(1)} %get-tuple-element.243.refs_0_), channel_id=1, source_target_pairs={{0,8},{24,16},{1,9},{25,17},{2,10},{26,18},{3,11},{27,19},{4,12},{... | collective-permute-start | bytes 3145736 | tf_op jit(solution)/shard_map/ppermute | solution.py:1120
  256.1 26.0 %collective-permute-start.34 = (bf16[2,256,1024]{2,1,0:T(8,128)(2,1)S(1)}, bf16[2,256,1024]{2,1,0:T(8,128)(2,1)S(1)}, u32[]{:S(2)}, u32[]{:S(2)}) collective-permute-start(bf16[2,256,1024]{2,1,0:T(8,128)(2,1)S(1)} %get-tuple-element.250.refs_0_), channel_id=1, source_target_pairs={{8,16},{16,8},{9,17},{17,9},{10,18},{18,10},{11,19},{19,11},{12,20... | collective-permute-start | bytes 3145736 | tf_op jit(solution)/shard_map/ppermute | solution.py:1140
  259.1 22.1 %copy-start.10 = (bf16[512,768]{1,0:T(8,128)(2,1)}, bf16[512,768]{1,0:T(8,128)(2,1)S(1)}, u32[]{:S(2)}) copy-start(bf16[512,768]{1,0:T(8,128)(2,1)S(1)} %get-tuple-element.241.refs_0_) | copy-start | bytes 2359300
  259.1 22.1 %collective-permute-start.30 = (bf16[512,768]{1,0:T(8,128)(2,1)S(1)}, bf16[512,768]{1,0:T(8,128)(2,1)S(1)}, u32[]{:S(2)}, u32[]{:S(2)}) collective-permute-start(bf16[512,768]{1,0:T(8,128)(2,1)S(1)} %get-tuple-element.242), channel_id=1, source_target_pairs={{0,4},{1,3},{2,6},{3,1},{4,0},{5,7},{6,2},{7,5},{8,12},{9,11},{10,... | collective-permute-start | bytes 2359304 | tf_op jit(solution)/shard_map/ppermute | solution.py:1069
  260.0 16.1 %collective-permute-start.32 = (bf16[256,1280]{1,0:T(8,128)(2,1)S(1)}, bf16[256,1280]{1,0:T(8,128)(2,1)S(1)}, u32[]{:S(2)}, u32[]{:S(2)}) collective-permute-start(bf16[256,1280]{1,0:T(8,128)(2,1)S(1)} %get-tuple-element.244), channel_id=1, source_target_pairs={{0,2},{1,5},{2,0},{3,7},{4,6},{5,1},{6,4},{7,3},{8,10},{9,13},{10,... | collective-permute-start | bytes 1966088 | tf_op jit(solution)/shard_map/ppermute | solution.py:1069
  269.4 51.1 %collective-permute-start.37 = (bf16[512,1024]{1,0:T(8,128)(2,1)}, bf16[512,1024]{1,0:T(8,128)(2,1)}, u32[]{:S(2)}, u32[]{:S(2)}) collective-permute-start(bf16[512,1024]{1,0:T(8,128)(2,1)} %get-tuple-element.256), channel_id=1, source_target_pairs={{0,1},{1,0},{2,3},{3,2},{4,5},{5,4},{6,7},{7,6},{8,9},{9,8},{10,11... | collective-permute-start | bytes 3145736 | tf_op jit(solution)/shard_map/ppermute | solution.py:1057
  279.4 47.0 %collective-permute-start.36 = (bf16[2,256,1024]{2,1,0:T(8,128)(2,1)}, bf16[2,256,1024]{2,1,0:T(8,128)(2,1)}, u32[]{:S(2)}, u32[]{:S(2)}) collective-permute-start(bf16[2,256,1024]{2,1,0:T(8,128)(2,1)} %get-tuple-element.254.refs_0_), channel_id=1, source_target_pairs={{8,16},{16,8},{9,17},{17,9},{10,18},{18,10},{11,19},{19,11},{12,20... | collective-permute-start | bytes 3145736 | tf_op jit(solution)/shard_map/ppermute | solution.py:1140
  283.9 43.3 %collective-permute-start.39 = (bf16[2,256,1024]{2,1,0:T(8,128)(2,1)}, bf16[2,256,1024]{2,1,0:T(8,128)(2,1)}, u32[]{:S(2)}, u32[]{:S(2)}) collective-permute-start(bf16[2,256,1024]{2,1,0:T(8,128)(2,1)} %get-tuple-element.262), channel_id=1, source_target_pairs={{8,0},{16,24},{9,1},{17,25},{10,2},{18,26},{11,3},{19,27},{12,4},{... | collective-permute-start | bytes 3145736 | tf_op jit(solution)/shard_map/ppermute | solution.py:1144
  285.2 15.8 %collective-permute-start.33 = (bf16[256,768]{1,0:T(8,128)(2,1)}, bf16[256,768]{1,0:T(8,128)(2,1)S(1)}, u32[]{:S(2)}, u32[]{:S(2)}) collective-permute-start(bf16[256,768]{1,0:T(8,128)(2,1)} %copy-done.46), channel_id=1, source_target_pairs={{0,2},{1,5},{2,0},{3,7},{4,6},{5,1},{6,4},{7,3},{8,10},{9,13},{10,... | collective-permute-start | bytes 1179656 | tf_op jit(solution)/shard_map/ppermute | solution.py:1069
  286.6 26.0 %collective-permute-start.38 = (bf16[256,1280]{1,0:T(8,128)(2,1)}, bf16[256,1280]{1,0:T(8,128)(2,1)}, u32[]{:S(2)}, u32[]{:S(2)}) collective-permute-start(bf16[256,1280]{1,0:T(8,128)(2,1)} %get-tuple-element.258.refs_0_), channel_id=1, source_target_pairs={{0,8},{24,16},{1,9},{25,17},{2,10},{26,18},{3,11},{27,19},{4,12},{... | collective-permute-start | bytes 1966088 | tf_op jit(solution)/shard_map/ppermute | solution.py:1120
  301.0 31.0 %collective-permute-start.22 = (bf16[2,256,1024]{2,1,0:T(8,128)(2,1)S(1)}, bf16[2,256,1024]{2,1,0:T(8,128)(2,1)}, u32[]{:S(2)}, u32[]{:S(2)}) collective-permute-start(bf16[2,256,1024]{2,1,0:T(8,128)(2,1)S(1)} %pad_maximum_fusion.refs_1_), channel_id=1, source_target_pairs={{0,2},{1,5},{2,0},{3,7},{4,6},{5,1},{6,4},{7,3},{8,10},{9,13},{10,... | collective-permute-start | bytes 3145736 | tf_op jit(solution)/shard_map/ppermute | solution.py:1069
  312.6 20.7 %collective-permute-start.35 = (bf16[256,768]{1,0:T(8,128)(2,1)S(1)}, bf16[256,768]{1,0:T(8,128)(2,1)S(1)}, u32[]{:S(2)}, u32[]{:S(2)}) collective-permute-start(bf16[256,768]{1,0:T(8,128)(2,1)S(1)} %get-tuple-element.253.refs_0_), channel_id=1, source_target_pairs={{0,8},{24,16},{1,9},{25,17},{2,10},{26,18},{3,11},{27,19},{4,12},{... | collective-permute-start | bytes 1179656 | tf_op jit(solution)/shard_map/ppermute | solution.py:1120
  320.5 20.6 %collective-permute-start.41 = (bf16[256,1280]{1,0:T(8,128)(2,1)S(1)}, bf16[256,1280]{1,0:T(8,128)(2,1)S(1)}, u32[]{:S(2)}, u32[]{:S(2)}) collective-permute-start(bf16[256,1280]{1,0:T(8,128)(2,1)S(1)} %get-tuple-element.269.refs_0_), channel_id=1, source_target_pairs={{8,16},{16,8},{9,17},{17,9},{10,18},{18,10},{11,19},{19,11},{12,20... | collective-permute-start | bytes 1966088 | tf_op jit(solution)/shard_map/ppermute | solution.py:1140
  326.5 9.6 %collective-permute-start.43 = (bf16[256,1024]{1,0:T(8,128)(2,1)S(1)}, bf16[256,1024]{1,0:T(8,128)(2,1)S(1)}, u32[]{:S(2)}, u32[]{:S(2)}) collective-permute-start(bf16[256,1024]{1,0:T(8,128)(2,1)S(1)} %get-tuple-element.273), channel_id=1, source_target_pairs={{0,0},{16,1},{2,2},{18,3},{4,4},{20,5},{6,6},{22,7},{8,8},{24,9},{... | collective-permute-start | bytes 1572872 | tf_op jit(solution)/shard_map/ppermute | solution.py:1168
  327.2 11.5 %collective-permute-start.44 = (bf16[256,1024]{1,0:T(8,128)(2,1)S(1)}, bf16[256,1024]{1,0:T(8,128)(2,1)S(1)}, u32[]{:S(2)}, u32[]{:S(2)}) collective-permute-start(bf16[256,1024]{1,0:T(8,128)(2,1)S(1)} %get-tuple-element.274), channel_id=1, source_target_pairs={{8,0},{24,1},{10,2},{26,3},{12,4},{28,5},{14,6},{30,7},{0,8},{16,9... | collective-permute-start | bytes 1572872 | tf_op jit(solution)/shard_map/ppermute | solution.py:1168
  332.0 37.5 %collective-permute-start.42 = (bf16[2,256,1024]{2,1,0:T(8,128)(2,1)S(1)}, bf16[2,256,1024]{2,1,0:T(8,128)(2,1)S(1)}, u32[]{:S(2)}, u32[]{:S(2)}) collective-permute-start(bf16[2,256,1024]{2,1,0:T(8,128)(2,1)S(1)} %get-tuple-element.272), channel_id=1, source_target_pairs={{8,0},{16,24},{9,1},{17,25},{10,2},{18,26},{11,3},{19,27},{12,4},{... | collective-permute-start | bytes 3145736 | tf_op jit(solution)/shard_map/ppermute | solution.py:1144
  333.3 8.7 %collective-permute-start.50 = (bf16[2,128,1024]{2,1,0:T(8,128)(2,1)S(1)}, bf16[2,128,1024]{2,1,0:T(8,128)(2,1)S(1)}, u32[]{:S(2)}, u32[]{:S(2)}) collective-permute-start(bf16[2,128,1024]{2,1,0:T(8,128)(2,1)S(1)} %constant_dynamic-slice_fusion.1), channel_id=1, source_target_pairs={{0,1},{1,0},{2,3},{3,2},{4,5},{5,4},{6,7},{7,6},{8,9},{9,8},{10,11... | collective-permute-start | bytes 1572872 | tf_op jit(solution)/shard_map/ppermute | solution.py:1057
  336.1 50.1 %collective-permute-start.23 = (bf16[2,256,1024]{2,1,0:T(8,128)(2,1)S(1)}, bf16[2,256,1024]{2,1,0:T(8,128)(2,1)S(1)}, u32[]{:S(2)}, u32[]{:S(2)}) collective-permute-start(bf16[2,256,1024]{2,1,0:T(8,128)(2,1)S(1)} %pad_maximum_fusion.refs_1_), channel_id=1, source_target_pairs={{0,4},{1,3},{2,6},{3,1},{4,0},{5,7},{6,2},{7,5},{8,12},{9,11},{10,... | collective-permute-start | bytes 3145736 | tf_op jit(solution)/shard_map/ppermute | solution.py:1069
  338.7 47.6 %collective-permute-start.24 = (bf16[2,256,1024]{2,1,0:T(8,128)(2,1)}, bf16[2,256,1024]{2,1,0:T(8,128)(2,1)S(1)}, u32[]{:S(2)}, u32[]{:S(2)}) collective-permute-start(bf16[2,256,1024]{2,1,0:T(8,128)(2,1)} %collective-permute-done.22.refs_2_), channel_id=1, source_target_pairs={{0,4},{1,3},{2,6},{3,1},{4,0},{5,7},{6,2},{7,5},{8,12},{9,11},{10,... | collective-permute-start | bytes 3145736 | tf_op jit(solution)/shard_map/ppermute | solution.py:1069
  341.1 45.0 %collective-permute-start.40 = (bf16[256,768]{1,0:T(8,128)(2,1)S(1)}, bf16[256,768]{1,0:T(8,128)(2,1)S(1)}, u32[]{:S(2)}, u32[]{:S(2)}) collective-permute-start(bf16[256,768]{1,0:T(8,128)(2,1)S(1)} %get-tuple-element.264.refs_0_), channel_id=1, source_target_pairs={{8,16},{16,8},{9,17},{17,9},{10,18},{18,10},{11,19},{19,11},{12,20... | collective-permute-start | bytes 1179656 | tf_op jit(solution)/shard_map/ppermute | solution.py:1140
  341.8 27.8 %copy-start.15 = (f32[2,128,2048]{2,1,0:T(8,128)S(1)}, f32[2,128,2048]{2,1,0:T(8,128)}, u32[]{:S(2)}) copy-start(f32[2,128,2048]{2,1,0:T(8,128)} %get-tuple-element.268.refs_0_) | copy-start | bytes 6291460
  342.0 41.6 %collective-permute-start.46 = (bf16[256,1280]{1,0:T(8,128)(2,1)S(1)}, bf16[256,1280]{1,0:T(8,128)(2,1)S(1)}, u32[]{:S(2)}, u32[]{:S(2)}) collective-permute-start(bf16[256,1280]{1,0:T(8,128)(2,1)S(1)} %get-tuple-element.282), channel_id=1, source_target_pairs={{8,0},{16,24},{9,1},{17,25},{10,2},{18,26},{11,3},{19,27},{12,4},{... | collective-permute-start | bytes 1966088 | tf_op jit(solution)/shard_map/ppermute | solution.py:1144
  375.8 3.6 collective-permute-start.52
  379.5 4.2 %collective-permute-start.53 = (f32[8,128]{1,0:T(8,128)S(1)}, f32[8,128]{1,0:T(8,128)S(1)}, u32[]{:S(2)}, u32[]{:S(2)}) collective-permute-start(f32[8,128]{1,0:T(8,128)S(1)} %maximum_select_fusion.3), channel_id=1, source_target_pairs={{0,4},{1,5},{2,6},{3,7},{4,0},{5,1},{6,2},{7,3},{8,12},{9,13},{10,... | collective-permute-start | bytes 12296 | tf_op jit(solution)/shard_map/ppermute | solution.py:1133
  383.7 6.8 %collective-permute-start.54 = (f32[8,128]{1,0:T(8,128)S(1)}, f32[8,128]{1,0:T(8,128)S(1)}, u32[]{:S(2)}, u32[]{:S(2)}) collective-permute-start(f32[8,128]{1,0:T(8,128)S(1)} %maximum_select_fusion.2), channel_id=1, source_target_pairs={{0,8},{8,0},{16,24},{24,16},{1,9},{9,1},{17,25},{25,17},{2,10},{10... | collective-permute-start | bytes 12296 | tf_op jit(solution)/shard_map/ppermute | solution.py:1133
  384.6 12.8 %collective-permute-start.47 = (bf16[128,1280]{1,0:T(8,128)(2,1)}, bf16[128,1280]{1,0:T(8,128)(2,1)}, u32[]{:S(2)}, u32[]{:S(2)}) collective-permute-start(bf16[128,1280]{1,0:T(8,128)(2,1)} %constant_dynamic-slice_fusion.3), channel_id=1, source_target_pairs={{0,1},{1,0},{2,3},{3,2},{4,5},{5,4},{6,7},{7,6},{8,9},{9,8},{10,11... | collective-permute-start | bytes 983048 | tf_op jit(solution)/shard_map/ppermute | solution.py:1057
  389.1 23.1 %collective-permute-start.45 = (bf16[2,256,1024]{2,1,0:T(8,128)(2,1)}, bf16[2,256,1024]{2,1,0:T(8,128)(2,1)}, u32[]{:S(2)}, u32[]{:S(2)}) collective-permute-start(bf16[2,256,1024]{2,1,0:T(8,128)(2,1)} %get-tuple-element.281), channel_id=1, source_target_pairs={{0,1},{1,0},{2,3},{3,2},{4,5},{5,4},{6,7},{7,6},{8,9},{9,8},{10,11... | collective-permute-start | bytes 3145736 | tf_op jit(solution)/shard_map/ppermute | solution.py:1057
  389.2 13.6 %collective-permute-start.48 = (bf16[256,768]{1,0:T(8,128)(2,1)S(1)}, bf16[256,768]{1,0:T(8,128)(2,1)}, u32[]{:S(2)}, u32[]{:S(2)}) collective-permute-start(bf16[256,768]{1,0:T(8,128)(2,1)S(1)} %get-tuple-element.283), channel_id=1, source_target_pairs={{8,0},{16,24},{9,1},{17,25},{10,2},{18,26},{11,3},{19,27},{12,4},{... | collective-permute-start | bytes 1179656 | tf_op jit(solution)/shard_map/ppermute | solution.py:1144
  390.5 4.6 %collective-permute-start.55 = (f32[8,128]{1,0:T(8,128)S(1)}, f32[8,128]{1,0:T(8,128)S(1)}, u32[]{:S(2)}, u32[]{:S(2)}) collective-permute-start(f32[8,128]{1,0:T(8,128)S(1)} %maximum_select_fusion.1), channel_id=1, source_target_pairs={{0,16},{8,24},{16,0},{24,8},{1,17},{9,25},{17,1},{25,9},{2,18},{10... | collective-permute-start | bytes 12296 | tf_op jit(solution)/shard_map/ppermute | solution.py:1133
  395.1 1.2 collective-permute-start.56
  395.1 8.8 %collective-permute-start.51 = (bf16[2,128,1024]{2,1,0:T(8,128)(2,1)S(1)}, bf16[2,128,1024]{2,1,0:T(8,128)(2,1)}, u32[]{:S(2)}, u32[]{:S(2)}) collective-permute-start(bf16[2,128,1024]{2,1,0:T(8,128)(2,1)S(1)} %constant_dynamic-slice_fusion), channel_id=1, source_target_pairs={{0,1},{1,0},{2,3},{3,2},{4,5},{5,4},{6,7},{7,6},{8,9},{9,8},{10,11... | collective-permute-start | bytes 1572872 | tf_op jit(solution)/shard_map/ppermute | solution.py:1057
  403.9 5.6 %collective-permute-start.49 = (bf16[128,768]{1,0:T(8,128)(2,1)S(1)}, bf16[128,768]{1,0:T(8,128)(2,1)S(1)}, u32[]{:S(2)}, u32[]{:S(2)}) collective-permute-start(bf16[128,768]{1,0:T(8,128)(2,1)S(1)} %constant_dynamic-slice_fusion.2), channel_id=1, source_target_pairs={{0,1},{1,0},{2,3},{3,2},{4,5},{5,4},{6,7},{7,6},{8,9},{9,8},{10,11... | collective-permute-start | bytes 589832 | tf_op jit(solution)/shard_map/ppermute | solution.py:1057
  (65 other events, 306.2 us)

commit v6 on v5

--- a/solution.py
+++ b/solution.py
@@ -593,7 +593,7 @@
     return steps.launch(
         "token_rows" if normed else "cotangent_rows",
         functools.partial(token_kernel, normed=normed, chips=chips, ordered=ordered),
-        [places, *map(pinned, pieces)],
+        [places, *(map(pinned, pieces) if normed else pieces)],
         [anywhere] * 2,
         [in_vmem] * 3,
         [((total, width), low), ((total, width), low), ((width, total), low)],
@@ -990,7 +990,13 @@
     return steps.launch(
         "input_gradient_rows" if back else "result_rows",
         functools.partial(finish_kernel, back=back),
-        [jnp.stack([core, odd, length]).astype(jnp.int32), pinned(own), other, base, tokens],
+        [
+            jnp.stack([core, odd, length]).astype(jnp.int32),
+            pinned(own) if back else own,
+            other,
+            pinned(base) if back else base,
+            tokens,
+        ],
         [half, half, whole, whole],
         [quarter, quarter],
         [((step, width), low)] * 2,

time: 420 us -> 414 us (0.986)
  Pallas kernels: 213 us -> 208 us
    pallas_call x50, Pallas kernels: 213 us -> 208 us  [launch(): pl.pallas_call(run, grid_spec=pltpu.PrefetchScalarGridSpec(num_scalar_pre...]
    unnamed x154 -> x150, local copies, waits for them, and re-layouts: 14.4 us -> 11.9 us
  transfers between devices with their start and end apart: 57 -> 57, of which waited for: 13 -> 15; matrix products, arithmetic and copies ran while one was open for 6% -> 6% of each run, Pallas kernels for 48% -> 48%
where the time goes in v6:
time: 414 us; the launch traced here: 408 us
  Pallas kernels  208 us (50%)
  starting transfers between devices  95 us (23%)
  waiting for transfers between devices  56.5 us (14%)
  other arithmetic  21.3 us (5%)
  local copies, waits for them, and re-layouts  18.3 us (4%)
  between operations  7.4 us (2%)
    pallas_call x50, Pallas kernels, launch(): pl.pallas_call(run, grid_spec=pltpu.PrefetchScalarGridSpec(num_scalar_pre...  208 us
    ppermute x4, waiting for transfers between devices, level_out(): return (total, lax.ppermute(total, 'ctx', [(1, 0), (2, 3)]))  31.4 us
    ppermute x4, starting transfers between devices, scatter_own(): return (total, lax.ppermute(total, 'ctx', [(0, 1), (3, 2)]))  24.7 us
    ppermute x20, starting transfers between devices, turn(): return lax.ppermute(array, 'fsdp', pairs)  23.5 us
    ppermute x8, starting transfers between devices, trade(): return lax.ppermute(array, ('ctx', 'fsdp'), pairs)  21.2 us
    ppermute x13, starting transfers between devices, sibling(): return lax.ppermute(array, 'fsdp', [(i, i ^ 1) for i in range(self.shards)])  14.1 us
    unnamed x150, local copies, waits for them, and re-layouts  11.9 us
    ppermute x8, waiting for transfers between devices, trade(): return lax.ppermute(array, ('ctx', 'fsdp'), pairs)  10.1 us
  transfers between devices with their start and end apart: 57, of which 15 were waited for; matrix products, arithmetic and copies ran while one was open for 6% of the time, Pallas kernels for 48%

profile of v6, /device:TPU:0, one launch (start us, length us, event | category | flops | bytes accessed | tf_op | source)
XLA Modules:
  0.0 408.0 jit_solution(15388641772219622004)
XLA Ops:
  2.1 1.7 other_side.1
  4.3 2.2 send_blocks.2
  7.5 2.4 attention_shard.1
  10.0 2.9 collective-permute-start.3
  12.9 1.5 collective-permute-start.4
  14.4 5.4 %collective-permute-start = (bf16[256,1024]{1,0:T(8,128)(2,1)}, bf16[256,1024]{1,0:T(8,128)(2,1)}, u32[]{:S(2)}, u32[]{:S(2)}) collective-permute-start(bf16[256,1024]{1,0:T(8,128)(2,1)} %get-tuple-element.153), channel_id=1, source_target_pairs={{0,0},{1,16},{2,2},{3,18},{4,4},{5,20},{6,6},{7,22},{8,8},{9,24},{... | collective-permute-start | bytes 1572872 | tf_op jit(solution)/shard_map/ppermute | solution.py:1174
  19.8 1.6 collective-permute-start.1
  22.9 5.7 %bias_strips.1 = (f32[8,128,2048]{2,1,0:T(8,128)}, f32[8,128]{1,0:T(8,128)S(1)}) custom-call(f32[8,1,2048]{2,1,0:T(1,128)S(1)} %reshape.43.refs_0_, f32[8,128]{1,0:T(8,128)S(1)} %get-tuple-element.157.refs_1_), custom_call_target="tpu_custom_call" | custom-call | bytes 8388608 | tf_op jit(solution)/shard_map/bias_strips/pallas_call | solution.py:57
  31.0 8.5 %collective-permute-done.1.refs_1_ = bf16[256,1024]{1,0:T(8,128)(2,1)} collective-permute-done((bf16[256,1024]{1,0:T(8,128)(2,1)}, bf16[256,1024]{1,0:T(8,128)(2,1)}, u32[]{:S(2)}, u32[]{:S(2)}) %collective-permute-start.1) | collective-permute-done | bytes 524320 | tf_op jit(solution)/shard_map/ppermute | solution.py:1174
  39.4 1.7 pair.2
  44.6 3.6 token_rows.1
  48.2 2.1 hidden_shard.3
  50.6 1.9 collective-permute-start.10
  54.8 4.4 %collective-permute-start.8 = (bf16[256,1024]{1,0:T(8,128)(2,1)S(1)}, bf16[256,1024]{1,0:T(8,128)(2,1)S(1)}, u32[]{:S(2)}, u32[]{:S(2)}) collective-permute-start(bf16[256,1024]{1,0:T(8,128)(2,1)S(1)} %get-tuple-element.173), channel_id=1, source_target_pairs={{0,8},{1,24},{2,10},{3,26},{4,12},{5,28},{6,14},{7,30},{8,0},{9,16... | collective-permute-start | bytes 1572872 | tf_op jit(solution)/shard_map/ppermute | solution.py:1174
  59.2 6.3 %qkv_product.1 = (bf16[1024,1536]{1,0:T(8,128)(2,1)S(1)}, f32[8,128]{1,0:T(8,128)S(1)}) custom-call(s32[13]{0:T(128)S(1)} %stack.175.refs_0_, bf16[1024,1024]{1,0:T(8,128)(2,1)S(1)} %get-tuple-element.164.refs_1_, bf16[2,128,2048]{2,1,0:T(8,128)(2,1)} %get-tuple-element.160.refs_2_.refs_3_.refs_5_.refs_13_, ...), custom_call_target="tpu_custom_call" | custom-call | flops 3221225472 | bytes 8388608 | tf_op jit(solution)/shard_map/qkv_product/pallas_call | solution.py:57
  65.5 10.7 %attention_forward.2 = (bf16[1024,256]{1,0:T(8,128)(2,1)S(1)}, f32[2,2,1024]{2,1,0:T(2,128)S(1)}, f32[2,2,128]{2,1,0:T(2,128)S(1)}, f32[8,128]{1,0:T(8,128)S(1)}) custom-call(s32[1]{0:T(128)} %bitcast.14.refs_0_, bf16[1024,1536]{1,0:T(8,128)(2,1)S(1)} %get-tuple-element.168.refs_1_.refs_2_.refs_3_, ...), custom_call_target="tpu_custom_call" | custom-call | flops 12000000000 | bytes 6291456 | tf_op jit(solution)/shard_map/attention_forward/pallas_call | solution.py:57
  76.5 1.6 collective-permute-start.11
  78.5 10.7 %attention_forward.3 = (bf16[1024,256]{1,0:T(8,128)(2,1)S(1)}, f32[2,2,1024]{2,1,0:T(2,128)S(1)}, f32[2,2,128]{2,1,0:T(2,128)S(1)}, f32[8,128]{1,0:T(8,128)S(1)}) custom-call(s32[1]{0:T(128)} %bitcast.14.refs_0_, bf16[1024,1536]{1,0:T(8,128)(2,1)S(1)} %get-tuple-element.168.refs_1_.refs_2_.refs_3_, ...), custom_call_target="tpu_custom_call" | custom-call | flops 12000000000 | bytes 6291456 | tf_op jit(solution)/shard_map/attention_forward/pallas_call | solution.py:57
  89.3 2.0 collective-permute-done.11.refs_8_
  91.3 3.8 attended_product.1
  95.2 2.4 collective-permute-start.12
  99.0 3.8 collective-permute-done.13.refs_2_
  102.8 4.4 %cotangent_rows.1 = (bf16[1024,1024]{1,0:T(8,128)(2,1)}, bf16[1024,1024]{1,0:T(8,128)(2,1)}, bf16[1024,1024]{1,0:T(8,128)(2,1)}, f32[8,128]{1,0:T(8,128)S(1)}) custom-call(s32[9]{0:T(128)S(1)} %stack.181.refs_0_, bf16[2,256,1024]{2,1,0:T(8,128)(2,1)S(1)} %get-tuple-element.180.refs_1_, bf16[2,256,1024]{2,1,0:T(8,128)(2,1)S(1)} %collective-permute-done.13.refs_2_, ...), custom_call_target="tpu_custom_call" | custom-call | bytes 10485760 | tf_op jit(solution)/shard_map/cotangent_rows/pallas_call | solution.py:57
  107.2 4.8 %second_norm.1 = (f32[1024,1024]{1,0:T(8,128)}, bf16[1024,1024]{1,0:T(8,128)(2,1)}, bf16[1024,1024]{1,0:T(8,128)(2,1)}, f32[8,128]{1,0:T(8,128)S(1)}) custom-call(s32[4]{0:T(128)S(1)} %pad_add_fusion.2.refs_0_, bf16[1024,1024]{1,0:T(8,128)(2,1)S(1)} %get-tuple-element.163.refs_1_.refs_4_, bf16[1024,1024]{1,0:T(8,128)(2,1)S(1)} %get-tuple-element.179.refs_2_, ...), custom_call_target="tpu_custom_call" | custom-call | bytes 14680064 | tf_op jit(solution)/shard_map/second_norm/pallas_call | solution.py:57
  112.4 2.0 relay.1
  116.5 23.4 %feed_forward.2 = (f32[1024,1024]{1,0:T(8,128)}, f32[1024,1024]{1,0:T(8,128)}, bf16[2,512,1024]{2,1,0:T(8,128)(2,1)}, bf16[2,512,1024]{2,1,0:T(8,128)(2,1)}, f32[8,128]{1,0:T(8,128)}) custom-call(s32[13]{0:T(128)} %copy-done.33, bf16[1024,1024]{1,0:T(8,128)(2,1)} %get-tuple-element.183.refs_1_, bf16[1024,1024]{1,0:T(8,128)(2,1)} %get-tuple-element.184.refs_2_, ...), custom_call_target="tpu_custom_call" | custom-call | flops 21474836480 | bytes 41943040 | tf_op jit(solution)/shard_map/feed_forward/pallas_call | solution.py:57
  142.2 24.5 %feed_forward.3 = (bf16[512,1024]{1,0:T(8,128)(2,1)}, bf16[512,1024]{1,0:T(8,128)(2,1)}, bf16[1024,1024]{1,0:T(8,128)(2,1)}, bf16[2,512,1024]{2,1,0:T(8,128)(2,1...) custom-call(s32[13]{0:T(128)} %copy-done.33, bf16[1024,1024]{1,0:T(8,128)(2,1)} %get-tuple-element.183.refs_1_, ...), custom_call_target="tpu_custom_call" | custom-call | flops 21474836480 | bytes 41943040 | tf_op jit(solution)/shard_map/feed_forward/pallas_call | solution.py:57
  168.7 1.6 copy-done.6
  171.0 2.4 row_sums.16
  174.8 8.7 %hidden_back.1 = (f32[1024,1024]{1,0:T(8,128)S(1)}, bf16[1024,1024]{1,0:T(8,128)(2,1)}, bf16[1024,1024]{1,0:T(8,128)(2,1)S(1)}, bf16[1024,512]{1,0:T(8,128)(2,1)S(1)}, f32[8,128]{1,0:T(8,128)S(1)}) custom-call(s32[13]{0:T(128)S(1)} %copy-done.34, bf16[1024,1024]{1,0:T(8,128)(2,1)S(1)} %copy-done.13, bf16[1024,1024]{1,0:T(8,128)(2,1)S(1)} %collective-permute-done.18.refs_2_, ...), custom_call_target="tpu_custom_call" | custom-call | flops 2147483648 | bytes 25165824 | tf_op jit(solution)/shard_map/hidden_back/pallas_call | solution.py:57
  183.6 1.5 result_rows.1
  186.5 6.5 %collective-permute-start.21 = (bf16[256,1024]{1,0:T(8,128)(2,1)S(1)}, bf16[256,1024]{1,0:T(8,128)(2,1)S(1)}, u32[]{:S(2)}, u32[]{:S(2)}) collective-permute-start(bf16[256,1024]{1,0:T(8,128)(2,1)S(1)} %get-tuple-element.205), channel_id=1, source_target_pairs={{8,0},{24,1},{10,2},{26,3},{12,4},{28,5},{14,6},{30,7},{0,8},{16,9... | collective-permute-start | bytes 1572872 | tf_op jit(solution)/shard_map/ppermute | solution.py:1174
  192.9 11.0 %attention_backward.4 = (bf16[1024,128]{1,0:T(8,128)(2,1)S(1)}, bf16[1024,128]{1,0:T(8,128)(2,1)S(1)}, bf16[1024,128]{1,0:T(8,128)(2,1)S(1)}, f32[2,128,2048]{2,1,0:T(8,128)}, f32[8,128]{1,0:T(8,128)S(1)}) custom-call(s32[1]{0:T(128)} %bitcast.14.refs_0_, bf16[1024,1536]{1,0:T(8,128)(2,1)S(1)} %copy-done.48, bf16[1024,1536]{1,0:T(8,128)(2,1)S(1)} %copy-done.48, ...), custom_call_target="tpu_custom_call" | custom-call | flops 10000000000 | bytes 6291456 | tf_op jit(solution)/shard_map/attention_backward/pallas_call | solution.py:57
  203.9 11.1 %attention_backward.5 = (bf16[1024,128]{1,0:T(8,128)(2,1)S(1)}, bf16[1024,128]{1,0:T(8,128)(2,1)S(1)}, bf16[1024,128]{1,0:T(8,128)(2,1)S(1)}, f32[2,128,2048]{2,1,0:T(8,128)}, f32[8,128]{1,0:T(8,128)S(1)}) custom-call(s32[1]{0:T(128)} %bitcast.14.refs_0_, bf16[1024,1536]{1,0:T(8,128)(2,1)S(1)} %copy-done.48, bf16[1024,1536]{1,0:T(8,128)(2,1)S(1)} %copy-done.48, ...), custom_call_target="tpu_custom_call" | custom-call | flops 10000000000 | bytes 6291456 | tf_op jit(solution)/shard_map/attention_backward/pallas_call | solution.py:57
  215.1 2.8 row_sums.17
  219.7 3.1 attention_terms.2
  223.7 2.5 collective-permute-start.29
  226.2 11.4 %attention_backward.6 = (bf16[1024,128]{1,0:T(8,128)(2,1)S(1)}, bf16[1024,128]{1,0:T(8,128)(2,1)S(1)}, bf16[1024,128]{1,0:T(8,128)(2,1)S(1)}, f32[2,128,2048]{2,1,0:T(8,128)}, f32[8,128]{1,0:T(8,128)S(1)}) custom-call(s32[1]{0:T(128)} %bitcast.14.refs_0_, bf16[1024,1536]{1,0:T(8,128)(2,1)S(1)} %copy-done.48, bf16[1024,1536]{1,0:T(8,128)(2,1)S(1)} %copy-done.48, ...), custom_call_target="tpu_custom_call" | custom-call | flops 10000000000 | bytes 6291456 | tf_op jit(solution)/shard_map/attention_backward/pallas_call | solution.py:57
  239.1 2.2 collective-permute-start.31
  241.3 11.0 %attention_backward.7 = (bf16[1024,128]{1,0:T(8,128)(2,1)S(1)}, bf16[1024,128]{1,0:T(8,128)(2,1)S(1)}, bf16[1024,128]{1,0:T(8,128)(2,1)S(1)}, f32[2,128,2048]{2,1,0:T(8,128)}, f32[8,128]{1,0:T(8,128)S(1)}) custom-call(s32[1]{0:T(128)} %bitcast.14.refs_0_, bf16[1024,1536]{1,0:T(8,128)(2,1)S(1)} %copy-done.48, bf16[1024,1536]{1,0:T(8,128)(2,1)S(1)} %copy-done.48, ...), custom_call_target="tpu_custom_call" | custom-call | flops 10000000000 | bytes 6291456 | tf_op jit(solution)/shard_map/attention_backward/pallas_call | solution.py:57
  253.9 2.0 attention_terms.3
  257.6 7.3 %input_product.1 = (f32[512,1024]{1,0:T(8,128)S(1)}, bf16[512,1024]{1,0:T(8,128)(2,1)}, f32[8,128]{1,0:T(8,128)S(1)}) custom-call(s32[13]{0:T(128)S(1)} %copy-done.34, bf16[1024,128]{1,0:T(8,128)(2,1)S(1)} %get-tuple-element.212.refs_4_.refs_1_, bf16[1024,128]{1,0:T(8,128)(2,1)S(1)} %get-tuple-element.213.refs_5_.refs_2_, ...), custom_call_target="tpu_custom_call" | custom-call | flops 3221225472 | bytes 14680064 | tf_op jit(solution)/shard_map/input_product/pallas_call | solution.py:57
  266.2 5.7 %collective-permute-start.37 = (bf16[512,1024]{1,0:T(8,128)(2,1)}, bf16[512,1024]{1,0:T(8,128)(2,1)}, u32[]{:S(2)}, u32[]{:S(2)}) collective-permute-start(bf16[512,1024]{1,0:T(8,128)(2,1)} %get-tuple-element.256), channel_id=1, source_target_pairs={{0,1},{1,0},{2,3},{3,2},{4,5},{5,4},{6,7},{7,6},{8,9},{9,8},{10,11... | collective-permute-start | bytes 3145736 | tf_op jit(solution)/shard_map/ppermute | solution.py:1063
  271.9 1.5 row_sums.22
  273.5 1.7 row_sums.23
  275.2 1.8 collective-permute-start.36
  277.9 1.8 row_sums.25
  282.3 14.4 %collective-permute-start.38 = (bf16[256,1280]{1,0:T(8,128)(2,1)}, bf16[256,1280]{1,0:T(8,128)(2,1)}, u32[]{:S(2)}, u32[]{:S(2)}) collective-permute-start(bf16[256,1280]{1,0:T(8,128)(2,1)} %get-tuple-element.258.refs_0_), channel_id=1, source_target_pairs={{0,8},{24,16},{1,9},{25,17},{2,10},{26,18},{3,11},{27,19},{4,12},{... | collective-permute-start | bytes 1966088 | tf_op jit(solution)/shard_map/ppermute | solution.py:1126
  303.2 2.6 stack.158.refs_0_
  308.4 5.6 %collective-permute-start.35 = (bf16[256,768]{1,0:T(8,128)(2,1)S(1)}, bf16[256,768]{1,0:T(8,128)(2,1)S(1)}, u32[]{:S(2)}, u32[]{:S(2)}) collective-permute-start(bf16[256,768]{1,0:T(8,128)(2,1)S(1)} %get-tuple-element.253.refs_0_), channel_id=1, source_target_pairs={{0,8},{24,16},{1,9},{25,17},{2,10},{26,18},{3,11},{27,19},{4,12},{... | collective-permute-start | bytes 1179656 | tf_op jit(solution)/shard_map/ppermute | solution.py:1126
  313.9 2.3 row_sums.27
  317.0 3.6 input_gradient_rows.1
  322.3 2.4 row_sums.28
  327.5 2.6 collective-permute-start.50
  331.2 1.6 collective-permute-done.44.refs_4_
  338.7 25.0 %collective-permute-done.42.refs_2_ = bf16[2,256,1024]{2,1,0:T(8,128)(2,1)S(1)} collective-permute-done((bf16[2,256,1024]{2,1,0:T(8,128)(2,1)S(1)}, bf16[2,256,1024]{2,1,0:T(8,128)(2,1)S(1)}, u32[]{:S(2)}, u32[]{:S(2)}) %collective-permute-start.42) | collective-permute-done | bytes 1048608 | tf_op jit(solution)/shard_map/ppermute | solution.py:1150
  372.1 1.5 collective-permute-done.52
  374.5 3.2 collective-permute-done.46
  380.4 1.8 pick_slots.1
  383.9 4.4 %collective-permute-done.55 = f32[8,128]{1,0:T(8,128)S(1)} collective-permute-done((f32[8,128]{1,0:T(8,128)S(1)}, f32[8,128]{1,0:T(8,128)S(1)}, u32[]{:S(2)}, u32[]{:S(2)}) %collective-permute-start.55) | collective-permute-done | bytes 4128 | tf_op jit(solution)/shard_map/ppermute | solution.py:1139
  392.7 3.2 collective-permute-done.48
  398.6 1.5 maximum_convert_fusion.1
  400.2 2.4 convert_multiply_fusion
  403.0 2.3 convert_multiply_fusion.6
  (310 shorter events, 76.6 us)
Async XLA Ops:
  0.6 21.6 %copy-start = (bf16[32,16]{0,1:T(8,128)(2,1)S(1)}, bf16[32,16]{0,1:T(8,128)(2,1)}, u32[]{:S(2)}) copy-start(bf16[32,16]{0,1:T(8,128)(2,1)} %param.28) | copy-start | bytes 3076
  3.8 17.6 %copy-start.58 = (s32[2047]{0:T(1024)S(1)}, s32[2047]{0:T(1024)}, u32[]{:S(2)}) copy-start(s32[2047]{0:T(1024)} %param.19) | copy-start | bytes 24568
  3.8 3.7 collective-permute-start.2
  10.0 29.5 %collective-permute-start.3 = (bf16[2,128,2048]{2,1,0:T(8,128)(2,1)}, bf16[2,128,2048]{2,1,0:T(8,128)(2,1)S(1)}, u32[]{:S(2)}, u32[]{:S(2)}) collective-permute-start(bf16[2,128,2048]{2,1,0:T(8,128)(2,1)} %get-tuple-element.160.refs_2_.refs_3_.refs_5_.refs_13_), channel_id=1, source_target_pairs={{0,2},{1,5},{2,0},{3,7},{4,6},{5,1},{6,4},{7,3},{8,10},{9,13},{10,... | collective-permute-start | bytes 3145736 | tf_op jit(solution)/shard_map/ppermute | solution.py:1075
  12.9 26.5 %collective-permute-start.4 = (bf16[2,128,2048]{2,1,0:T(8,128)(2,1)}, bf16[2,128,2048]{2,1,0:T(8,128)(2,1)S(1)}, u32[]{:S(2)}, u32[]{:S(2)}) collective-permute-start(bf16[2,128,2048]{2,1,0:T(8,128)(2,1)} %get-tuple-element.160.refs_2_.refs_3_.refs_5_.refs_13_), channel_id=1, source_target_pairs={{0,4},{1,3},{2,6},{3,1},{4,0},{5,7},{6,2},{7,5},{8,12},{9,11},{10,... | collective-permute-start | bytes 3145736 | tf_op jit(solution)/shard_map/ppermute | solution.py:1075
  14.4 16.5 %collective-permute-start = (bf16[256,1024]{1,0:T(8,128)(2,1)}, bf16[256,1024]{1,0:T(8,128)(2,1)}, u32[]{:S(2)}, u32[]{:S(2)}) collective-permute-start(bf16[256,1024]{1,0:T(8,128)(2,1)} %get-tuple-element.153), channel_id=1, source_target_pairs={{0,0},{1,16},{2,2},{3,18},{4,4},{5,20},{6,6},{7,22},{8,8},{9,24},{... | collective-permute-start | bytes 1572872 | tf_op jit(solution)/shard_map/ppermute | solution.py:1174
  19.8 19.6 %collective-permute-start.1 = (bf16[256,1024]{1,0:T(8,128)(2,1)}, bf16[256,1024]{1,0:T(8,128)(2,1)}, u32[]{:S(2)}, u32[]{:S(2)}) collective-permute-start(bf16[256,1024]{1,0:T(8,128)(2,1)} %get-tuple-element.154), channel_id=1, source_target_pairs={{0,8},{1,24},{2,10},{3,26},{4,12},{5,28},{6,14},{7,30},{8,0},{9,16... | collective-permute-start | bytes 1572872 | tf_op jit(solution)/shard_map/ppermute | solution.py:1174
  41.1 3.4 collective-permute-start.5
  41.2 18.0 %collective-permute-start.6 = (bf16[2,128,2048]{2,1,0:T(8,128)(2,1)S(1)}, bf16[2,128,2048]{2,1,0:T(8,128)(2,1)}, u32[]{:S(2)}, u32[]{:S(2)}) collective-permute-start(bf16[2,128,2048]{2,1,0:T(8,128)(2,1)S(1)} %collective-permute-done.3.refs_3_.refs_4_.refs_6_.refs_14_), channel_id=1, source_target_pairs={{0,4},{1,3},{2,6},{3,1},{4,0},{5,7},{6,2},{7,5},{8,12},{9,11},{10,... | collective-permute-start | bytes 3145736 | tf_op jit(solution)/shard_map/ppermute | solution.py:1075
  44.5 46.8 %copy-start.33 = (s32[13]{0:T(128)}, s32[13]{0:T(128)S(1)}, u32[]{:S(2)}) copy-start(s32[13]{0:T(128)S(1)} %stack.175.refs_0_) | copy-start | bytes 160
  48.2 17.3 %slice-start = ((s8[8388608]{0:T(1024)(128)(4,1)}), s8[4194304]{0:T(1024)(128)(4,1)S(1)}, s32[]{:S(2)}) async-start(s8[8388608]{0:T(1024)(128)(4,1)} %bitcast.67), calls=%async_computation | async-start | bytes 8388608
  50.4 26.2 %collective-permute-start.9 = (bf16[2,2,128,1024]{3,2,1,0:T(8,128)(2,1)S(1)}, bf16[2,2,128,1024]{3,2,1,0:T(8,128)(2,1)S(1)}, u32[]{:S(2)}, u32[]{:S(2)}) collective-permute-start(bf16[2,2,128,1024]{3,2,1,0:T(8,128)(2,1)S(1)} %get-tuple-element.176.refs_5_), channel_id=1, source_target_pairs={{0,2},{1,5},{2,0},{3,7},{4,6},{5,1},{6,4},{7,3},{8,10},{9,13},{10,... | collective-permute-start | bytes 3145736 | tf_op jit(solution)/shard_map/ppermute | solution.py:1075
  50.6 28.0 %collective-permute-start.10 = (bf16[2,2,128,1024]{3,2,1,0:T(8,128)(2,1)S(1)}, bf16[2,2,128,1024]{3,2,1,0:T(8,128)(2,1)S(1)}, u32[]{:S(2)}, u32[]{:S(2)}) collective-permute-start(bf16[2,2,128,1024]{3,2,1,0:T(8,128)(2,1)S(1)} %get-tuple-element.176.refs_5_), channel_id=1, source_target_pairs={{0,4},{1,3},{2,6},{3,1},{4,0},{5,7},{6,2},{7,5},{8,12},{9,11},{10,... | collective-permute-start | bytes 3145736 | tf_op jit(solution)/shard_map/ppermute | solution.py:1075
  53.8 22.5 %collective-permute-start.7 = (bf16[256,1024]{1,0:T(8,128)(2,1)S(1)}, bf16[256,1024]{1,0:T(8,128)(2,1)S(1)}, u32[]{:S(2)}, u32[]{:S(2)}) collective-permute-start(bf16[256,1024]{1,0:T(8,128)(2,1)S(1)} %get-tuple-element.172), channel_id=1, source_target_pairs={{0,0},{1,16},{2,2},{3,18},{4,4},{5,20},{6,6},{7,22},{8,8},{9,24},{... | collective-permute-start | bytes 1572872 | tf_op jit(solution)/shard_map/ppermute | solution.py:1174
  54.8 21.5 %collective-permute-start.8 = (bf16[256,1024]{1,0:T(8,128)(2,1)S(1)}, bf16[256,1024]{1,0:T(8,128)(2,1)S(1)}, u32[]{:S(2)}, u32[]{:S(2)}) collective-permute-start(bf16[256,1024]{1,0:T(8,128)(2,1)S(1)} %get-tuple-element.173), channel_id=1, source_target_pairs={{0,8},{1,24},{2,10},{3,26},{4,12},{5,28},{6,14},{7,30},{8,0},{9,16... | collective-permute-start | bytes 1572872 | tf_op jit(solution)/shard_map/ppermute | solution.py:1174
  76.2 15.1 %copy-start.31 = (bf16[1024,256]{1,0:T(8,128)(2,1)}, bf16[1024,256]{1,0:T(8,128)(2,1)S(1)}, u32[]{:S(2)}) copy-start(bf16[1024,256]{1,0:T(8,128)(2,1)S(1)} %get-tuple-element.171.refs_1_.refs_4_.refs_2_) | copy-start | bytes 1572868
  76.5 14.8 %collective-permute-start.11 = (bf16[2,2,128,1024]{3,2,1,0:T(8,128)(2,1)S(1)}, bf16[2,2,128,1024]{3,2,1,0:T(8,128)(2,1)S(1)}, u32[]{:S(2)}, u32[]{:S(2)}) collective-permute-start(bf16[2,2,128,1024]{3,2,1,0:T(8,128)(2,1)S(1)} %collective-permute-done.9.refs_6_), channel_id=1, source_target_pairs={{0,4},{1,3},{2,6},{3,1},{4,0},{5,7},{6,2},{7,5},{8,12},{9,11},{10,... | collective-permute-start | bytes 3145736 | tf_op jit(solution)/shard_map/ppermute | solution.py:1075
  95.2 12.0 %collective-permute-start.12 = (bf16[1024,1024]{1,0:T(8,128)(2,1)S(1)}, bf16[1024,1024]{1,0:T(8,128)(2,1)S(1)}, u32[]{:S(2)}, u32[]{:S(2)}) collective-permute-start(bf16[1024,1024]{1,0:T(8,128)(2,1)S(1)} %get-tuple-element.179.refs_2_), channel_id=1, source_target_pairs={{0,1},{1,0},{2,3},{3,2},{4,5},{5,4},{6,7},{7,6},{8,9},{9,8},{10,11... | collective-permute-start | bytes 6291464 | tf_op jit(solution)/shard_map/ppermute | solution.py:1063
  97.6 5.3 %collective-permute-start.13 = (bf16[2,256,1024]{2,1,0:T(8,128)(2,1)S(1)}, bf16[2,256,1024]{2,1,0:T(8,128)(2,1)S(1)}, u32[]{:S(2)}, u32[]{:S(2)}) collective-permute-start(bf16[2,256,1024]{2,1,0:T(8,128)(2,1)S(1)} %get-tuple-element.180.refs_1_), channel_id=1, source_target_pairs={{0,1},{1,0},{2,3},{3,2},{4,5},{5,4},{6,7},{7,6},{8,9},{9,8},{10,11... | collective-permute-start | bytes 3145736 | tf_op jit(solution)/shard_map/ppermute | solution.py:1063
  97.6 14.8 %collective-permute-start.14 = (bf16[2,2,128,1024]{3,2,1,0:T(8,128)(2,1)S(1)}, bf16[2,2,128,1024]{3,2,1,0:T(8,128)(2,1)S(1)}, u32[]{:S(2)}, u32[]{:S(2)}) collective-permute-start(bf16[2,2,128,1024]{3,2,1,0:T(8,128)(2,1)S(1)} %copy-done.25), channel_id=1, source_target_pairs={{0,2},{1,5},{2,0},{3,7},{4,6},{5,1},{6,4},{7,3},{8,10},{9,13},{10,... | collective-permute-start | bytes 3145736 | tf_op jit(solution)/shard_map/ppermute | solution.py:1075
  114.4 26.7 %collective-permute-start.15 = (bf16[2,2,128,1024]{3,2,1,0:T(8,128)(2,1)}, bf16[2,2,128,1024]{3,2,1,0:T(8,128)(2,1)S(1)}, u32[]{:S(2)}, u32[]{:S(2)}) collective-permute-start(bf16[2,2,128,1024]{3,2,1,0:T(8,128)(2,1)} %get-tuple-element.189), channel_id=1, source_target_pairs={{0,4},{1,3},{2,6},{3,1},{4,0},{5,7},{6,2},{7,5},{8,12},{9,11},{10,... | collective-permute-start | bytes 3145736 | tf_op jit(solution)/shard_map/ppermute | solution.py:1075
  115.7 25.5 %collective-permute-start.16 = (bf16[2,2,128,1024]{3,2,1,0:T(8,128)(2,1)}, bf16[2,2,128,1024]{3,2,1,0:T(8,128)(2,1)}, u32[]{:S(2)}, u32[]{:S(2)}) collective-permute-start(bf16[2,2,128,1024]{3,2,1,0:T(8,128)(2,1)} %get-tuple-element.190), channel_id=1, source_target_pairs={{0,4},{1,3},{2,6},{3,1},{4,0},{5,7},{6,2},{7,5},{8,12},{9,11},{10,... | collective-permute-start | bytes 3145736 | tf_op jit(solution)/shard_map/ppermute | solution.py:1075
  139.9 28.8 %collective-permute-start.19 = (bf16[2,512,1024]{2,1,0:T(8,128)(2,1)}, bf16[2,512,1024]{2,1,0:T(8,128)(2,1)}, u32[]{:S(2)}, u32[]{:S(2)}) collective-permute-start(bf16[2,512,1024]{2,1,0:T(8,128)(2,1)} %get-tuple-element.200), channel_id=1, source_target_pairs={{0,4},{1,3},{2,6},{3,1},{4,0},{5,7},{6,2},{7,5},{8,12},{9,11},{10,... | collective-permute-start | bytes 6291464 | tf_op jit(solution)/shard_map/ppermute | solution.py:1075
  166.7 8.1 %collective-permute-start.18 = (bf16[1024,1024]{1,0:T(8,128)(2,1)}, bf16[1024,1024]{1,0:T(8,128)(2,1)S(1)}, u32[]{:S(2)}, u32[]{:S(2)}) collective-permute-start(bf16[1024,1024]{1,0:T(8,128)(2,1)} %get-tuple-element.198.refs_1_), channel_id=1, source_target_pairs={{0,1},{1,0},{2,3},{3,2},{4,5},{5,4},{6,7},{7,6},{8,9},{9,8},{10,11... | collective-permute-start | bytes 6291464 | tf_op jit(solution)/shard_map/ppermute | solution.py:1063
  166.7 16.8 %collective-permute-start.17 = (bf16[512,1024]{1,0:T(8,128)(2,1)}, bf16[512,1024]{1,0:T(8,128)(2,1)S(1)}, u32[]{:S(2)}, u32[]{:S(2)}) collective-permute-start(bf16[512,1024]{1,0:T(8,128)(2,1)} %get-tuple-element.196), channel_id=1, source_target_pairs={{0,1},{1,0},{2,3},{3,2},{4,5},{5,4},{6,7},{7,6},{8,9},{9,8},{10,11... | collective-permute-start | bytes 3145736 | tf_op jit(solution)/shard_map/ppermute | solution.py:1063
  167.2 50.6 %collective-permute-start.25 = (bf16[2,512,1024]{2,1,0:T(8,128)(2,1)}, bf16[2,512,1024]{2,1,0:T(8,128)(2,1)S(1)}, u32[]{:S(2)}, u32[]{:S(2)}) collective-permute-start(bf16[2,512,1024]{2,1,0:T(8,128)(2,1)} %get-tuple-element.220), channel_id=1, source_target_pairs={{0,4},{1,3},{2,6},{3,1},{4,0},{5,7},{6,2},{7,5},{8,12},{9,11},{10,... | collective-permute-start | bytes 6291464 | tf_op jit(solution)/shard_map/ppermute | solution.py:1075
  173.4 41.6 %collective-permute-start.26 = (bf16[2,256,1024]{2,1,0:T(8,128)(2,1)S(1)}, bf16[2,256,1024]{2,1,0:T(8,128)(2,1)S(1)}, u32[]{:S(2)}, u32[]{:S(2)}) collective-permute-start(bf16[2,256,1024]{2,1,0:T(8,128)(2,1)S(1)} %get-tuple-element.221), channel_id=1, source_target_pairs={{0,2},{1,5},{2,0},{3,7},{4,6},{5,1},{6,4},{7,3},{8,10},{9,13},{10,... | collective-permute-start | bytes 3145736 | tf_op jit(solution)/shard_map/ppermute | solution.py:1075
  185.6 29.4 %collective-permute-start.20 = (bf16[256,1024]{1,0:T(8,128)(2,1)S(1)}, bf16[256,1024]{1,0:T(8,128)(2,1)S(1)}, u32[]{:S(2)}, u32[]{:S(2)}) collective-permute-start(bf16[256,1024]{1,0:T(8,128)(2,1)S(1)} %get-tuple-element.204), channel_id=1, source_target_pairs={{0,0},{16,1},{2,2},{18,3},{4,4},{20,5},{6,6},{22,7},{8,8},{24,9},{... | collective-permute-start | bytes 1572872 | tf_op jit(solution)/shard_map/ppermute | solution.py:1174
  186.5 28.6 %collective-permute-start.21 = (bf16[256,1024]{1,0:T(8,128)(2,1)S(1)}, bf16[256,1024]{1,0:T(8,128)(2,1)S(1)}, u32[]{:S(2)}, u32[]{:S(2)}) collective-permute-start(bf16[256,1024]{1,0:T(8,128)(2,1)S(1)} %get-tuple-element.205), channel_id=1, source_target_pairs={{8,0},{24,1},{10,2},{26,3},{12,4},{28,5},{14,6},{30,7},{0,8},{16,9... | collective-permute-start | bytes 1572872 | tf_op jit(solution)/shard_map/ppermute | solution.py:1174
  218.5 19.9 %collective-permute-start.27 = (bf16[2,256,1024]{2,1,0:T(8,128)(2,1)S(1)}, bf16[2,256,1024]{2,1,0:T(8,128)(2,1)S(1)}, u32[]{:S(2)}, u32[]{:S(2)}) collective-permute-start(bf16[2,256,1024]{2,1,0:T(8,128)(2,1)S(1)} %get-tuple-element.229), channel_id=1, source_target_pairs={{0,2},{1,5},{2,0},{3,7},{4,6},{5,1},{6,4},{7,3},{8,10},{9,13},{10,... | collective-permute-start | bytes 3145736 | tf_op jit(solution)/shard_map/ppermute | solution.py:1075
  222.8 30.8 %collective-permute-start.28 = (bf16[512,1280]{1,0:T(8,128)(2,1)S(1)}, bf16[512,1280]{1,0:T(8,128)(2,1)S(1)}, u32[]{:S(2)}, u32[]{:S(2)}) collective-permute-start(bf16[512,1280]{1,0:T(8,128)(2,1)S(1)} %get-tuple-element.236), channel_id=1, source_target_pairs={{0,4},{1,3},{2,6},{3,1},{4,0},{5,7},{6,2},{7,5},{8,12},{9,11},{10,... | collective-permute-start | bytes 3932168 | tf_op jit(solution)/shard_map/ppermute | solution.py:1075
  223.7 28.7 %collective-permute-start.29 = (bf16[2,256,1024]{2,1,0:T(8,128)(2,1)S(1)}, bf16[2,256,1024]{2,1,0:T(8,128)(2,1)S(1)}, u32[]{:S(2)}, u32[]{:S(2)}) collective-permute-start(bf16[2,256,1024]{2,1,0:T(8,128)(2,1)S(1)} %get-tuple-element.237.refs_0_), channel_id=1, source_target_pairs={{0,8},{24,16},{1,9},{25,17},{2,10},{26,18},{3,11},{27,19},{4,12},{... | collective-permute-start | bytes 3145736 | tf_op jit(solution)/shard_map/ppermute | solution.py:1126
  239.1 34.4 %collective-permute-start.31 = (bf16[2,256,1024]{2,1,0:T(8,128)(2,1)S(1)}, bf16[2,256,1024]{2,1,0:T(8,128)(2,1)S(1)}, u32[]{:S(2)}, u32[]{:S(2)}) collective-permute-start(bf16[2,256,1024]{2,1,0:T(8,128)(2,1)S(1)} %get-tuple-element.243.refs_0_), channel_id=1, source_target_pairs={{0,8},{24,16},{1,9},{25,17},{2,10},{26,18},{3,11},{27,19},{4,12},{... | collective-permute-start | bytes 3145736 | tf_op jit(solution)/shard_map/ppermute | solution.py:1126
  252.9 25.0 %collective-permute-start.34 = (bf16[2,256,1024]{2,1,0:T(8,128)(2,1)S(1)}, bf16[2,256,1024]{2,1,0:T(8,128)(2,1)S(1)}, u32[]{:S(2)}, u32[]{:S(2)}) collective-permute-start(bf16[2,256,1024]{2,1,0:T(8,128)(2,1)S(1)} %get-tuple-element.250.refs_0_), channel_id=1, source_target_pairs={{8,16},{16,8},{9,17},{17,9},{10,18},{18,10},{11,19},{19,11},{12,20... | collective-permute-start | bytes 3145736 | tf_op jit(solution)/shard_map/ppermute | solution.py:1146
  255.9 21.1 %copy-start.9 = (bf16[512,768]{1,0:T(8,128)(2,1)}, bf16[512,768]{1,0:T(8,128)(2,1)S(1)}, u32[]{:S(2)}) copy-start(bf16[512,768]{1,0:T(8,128)(2,1)S(1)} %get-tuple-element.241.refs_0_) | copy-start | bytes 2359300
  255.9 21.1 %collective-permute-start.30 = (bf16[512,768]{1,0:T(8,128)(2,1)S(1)}, bf16[512,768]{1,0:T(8,128)(2,1)S(1)}, u32[]{:S(2)}, u32[]{:S(2)}) collective-permute-start(bf16[512,768]{1,0:T(8,128)(2,1)S(1)} %get-tuple-element.242), channel_id=1, source_target_pairs={{0,4},{1,3},{2,6},{3,1},{4,0},{5,7},{6,2},{7,5},{8,12},{9,11},{10,... | collective-permute-start | bytes 2359304 | tf_op jit(solution)/shard_map/ppermute | solution.py:1075
  256.8 15.1 %collective-permute-start.32 = (bf16[256,1280]{1,0:T(8,128)(2,1)S(1)}, bf16[256,1280]{1,0:T(8,128)(2,1)S(1)}, u32[]{:S(2)}, u32[]{:S(2)}) collective-permute-start(bf16[256,1280]{1,0:T(8,128)(2,1)S(1)} %get-tuple-element.244), channel_id=1, source_target_pairs={{0,2},{1,5},{2,0},{3,7},{4,6},{5,1},{6,4},{7,3},{8,10},{9,13},{10,... | collective-permute-start | bytes 1966088 | tf_op jit(solution)/shard_map/ppermute | solution.py:1075
  266.2 50.0 %collective-permute-start.37 = (bf16[512,1024]{1,0:T(8,128)(2,1)}, bf16[512,1024]{1,0:T(8,128)(2,1)}, u32[]{:S(2)}, u32[]{:S(2)}) collective-permute-start(bf16[512,1024]{1,0:T(8,128)(2,1)} %get-tuple-element.256), channel_id=1, source_target_pairs={{0,1},{1,0},{2,3},{3,2},{4,5},{5,4},{6,7},{7,6},{8,9},{9,8},{10,11... | collective-permute-start | bytes 3145736 | tf_op jit(solution)/shard_map/ppermute | solution.py:1063
  275.2 45.4 %collective-permute-start.36 = (bf16[2,256,1024]{2,1,0:T(8,128)(2,1)}, bf16[2,256,1024]{2,1,0:T(8,128)(2,1)}, u32[]{:S(2)}, u32[]{:S(2)}) collective-permute-start(bf16[2,256,1024]{2,1,0:T(8,128)(2,1)} %get-tuple-element.254.refs_0_), channel_id=1, source_target_pairs={{8,16},{16,8},{9,17},{17,9},{10,18},{18,10},{11,19},{19,11},{12,20... | collective-permute-start | bytes 3145736 | tf_op jit(solution)/shard_map/ppermute | solution.py:1146
  279.7 41.6 %collective-permute-start.39 = (bf16[2,256,1024]{2,1,0:T(8,128)(2,1)}, bf16[2,256,1024]{2,1,0:T(8,128)(2,1)}, u32[]{:S(2)}, u32[]{:S(2)}) collective-permute-start(bf16[2,256,1024]{2,1,0:T(8,128)(2,1)} %get-tuple-element.262), channel_id=1, source_target_pairs={{8,0},{16,24},{9,1},{17,25},{10,2},{18,26},{11,3},{19,27},{12,4},{... | collective-permute-start | bytes 3145736 | tf_op jit(solution)/shard_map/ppermute | solution.py:1150
  281.0 15.8 %collective-permute-start.33 = (bf16[256,768]{1,0:T(8,128)(2,1)}, bf16[256,768]{1,0:T(8,128)(2,1)S(1)}, u32[]{:S(2)}, u32[]{:S(2)}) collective-permute-start(bf16[256,768]{1,0:T(8,128)(2,1)} %copy-done.45), channel_id=1, source_target_pairs={{0,2},{1,5},{2,0},{3,7},{4,6},{5,1},{6,4},{7,3},{8,10},{9,13},{10,... | collective-permute-start | bytes 1179656 | tf_op jit(solution)/shard_map/ppermute | solution.py:1075
  282.3 26.0 %collective-permute-start.38 = (bf16[256,1280]{1,0:T(8,128)(2,1)}, bf16[256,1280]{1,0:T(8,128)(2,1)}, u32[]{:S(2)}, u32[]{:S(2)}) collective-permute-start(bf16[256,1280]{1,0:T(8,128)(2,1)} %get-tuple-element.258.refs_0_), channel_id=1, source_target_pairs={{0,8},{24,16},{1,9},{25,17},{2,10},{26,18},{3,11},{27,19},{4,12},{... | collective-permute-start | bytes 1966088 | tf_op jit(solution)/shard_map/ppermute | solution.py:1126
  296.8 29.3 %collective-permute-start.22 = (bf16[2,256,1024]{2,1,0:T(8,128)(2,1)S(1)}, bf16[2,256,1024]{2,1,0:T(8,128)(2,1)}, u32[]{:S(2)}, u32[]{:S(2)}) collective-permute-start(bf16[2,256,1024]{2,1,0:T(8,128)(2,1)S(1)} %pad_maximum_fusion.refs_1_), channel_id=1, source_target_pairs={{0,2},{1,5},{2,0},{3,7},{4,6},{5,1},{6,4},{7,3},{8,10},{9,13},{10,... | collective-permute-start | bytes 3145736 | tf_op jit(solution)/shard_map/ppermute | solution.py:1075
  308.4 19.1 %collective-permute-start.35 = (bf16[256,768]{1,0:T(8,128)(2,1)S(1)}, bf16[256,768]{1,0:T(8,128)(2,1)S(1)}, u32[]{:S(2)}, u32[]{:S(2)}) collective-permute-start(bf16[256,768]{1,0:T(8,128)(2,1)S(1)} %get-tuple-element.253.refs_0_), channel_id=1, source_target_pairs={{0,8},{24,16},{1,9},{25,17},{2,10},{26,18},{3,11},{27,19},{4,12},{... | collective-permute-start | bytes 1179656 | tf_op jit(solution)/shard_map/ppermute | solution.py:1126
  316.3 19.0 %collective-permute-start.41 = (bf16[256,1280]{1,0:T(8,128)(2,1)S(1)}, bf16[256,1280]{1,0:T(8,128)(2,1)S(1)}, u32[]{:S(2)}, u32[]{:S(2)}) collective-permute-start(bf16[256,1280]{1,0:T(8,128)(2,1)S(1)} %get-tuple-element.269.refs_0_), channel_id=1, source_target_pairs={{8,16},{16,8},{9,17},{17,9},{10,18},{18,10},{11,19},{19,11},{12,20... | collective-permute-start | bytes 1966088 | tf_op jit(solution)/shard_map/ppermute | solution.py:1146
  320.6 9.6 %collective-permute-start.43 = (bf16[256,1024]{1,0:T(8,128)(2,1)S(1)}, bf16[256,1024]{1,0:T(8,128)(2,1)S(1)}, u32[]{:S(2)}, u32[]{:S(2)}) collective-permute-start(bf16[256,1024]{1,0:T(8,128)(2,1)S(1)} %get-tuple-element.273), channel_id=1, source_target_pairs={{0,0},{16,1},{2,2},{18,3},{4,4},{20,5},{6,6},{22,7},{8,8},{24,9},{... | collective-permute-start | bytes 1572872 | tf_op jit(solution)/shard_map/ppermute | solution.py:1174
  321.3 11.5 %collective-permute-start.44 = (bf16[256,1024]{1,0:T(8,128)(2,1)S(1)}, bf16[256,1024]{1,0:T(8,128)(2,1)S(1)}, u32[]{:S(2)}, u32[]{:S(2)}) collective-permute-start(bf16[256,1024]{1,0:T(8,128)(2,1)S(1)} %get-tuple-element.274), channel_id=1, source_target_pairs={{8,0},{24,1},{10,2},{26,3},{12,4},{28,5},{14,6},{30,7},{0,8},{16,9... | collective-permute-start | bytes 1572872 | tf_op jit(solution)/shard_map/ppermute | solution.py:1174
  326.1 37.5 %collective-permute-start.42 = (bf16[2,256,1024]{2,1,0:T(8,128)(2,1)S(1)}, bf16[2,256,1024]{2,1,0:T(8,128)(2,1)S(1)}, u32[]{:S(2)}, u32[]{:S(2)}) collective-permute-start(bf16[2,256,1024]{2,1,0:T(8,128)(2,1)S(1)} %get-tuple-element.272), channel_id=1, source_target_pairs={{8,0},{16,24},{9,1},{17,25},{10,2},{18,26},{11,3},{19,27},{12,4},{... | collective-permute-start | bytes 3145736 | tf_op jit(solution)/shard_map/ppermute | solution.py:1150
  327.5 8.7 %collective-permute-start.50 = (bf16[2,128,1024]{2,1,0:T(8,128)(2,1)S(1)}, bf16[2,128,1024]{2,1,0:T(8,128)(2,1)S(1)}, u32[]{:S(2)}, u32[]{:S(2)}) collective-permute-start(bf16[2,128,1024]{2,1,0:T(8,128)(2,1)S(1)} %constant_dynamic-slice_fusion.1), channel_id=1, source_target_pairs={{0,1},{1,0},{2,3},{3,2},{4,5},{5,4},{6,7},{7,6},{8,9},{9,8},{10,11... | collective-permute-start | bytes 1572872 | tf_op jit(solution)/shard_map/ppermute | solution.py:1063
  330.2 50.1 %collective-permute-start.23 = (bf16[2,256,1024]{2,1,0:T(8,128)(2,1)S(1)}, bf16[2,256,1024]{2,1,0:T(8,128)(2,1)S(1)}, u32[]{:S(2)}, u32[]{:S(2)}) collective-permute-start(bf16[2,256,1024]{2,1,0:T(8,128)(2,1)S(1)} %pad_maximum_fusion.refs_1_), channel_id=1, source_target_pairs={{0,4},{1,3},{2,6},{3,1},{4,0},{5,7},{6,2},{7,5},{8,12},{9,11},{10,... | collective-permute-start | bytes 3145736 | tf_op jit(solution)/shard_map/ppermute | solution.py:1075
  332.8 47.5 %collective-permute-start.24 = (bf16[2,256,1024]{2,1,0:T(8,128)(2,1)}, bf16[2,256,1024]{2,1,0:T(8,128)(2,1)S(1)}, u32[]{:S(2)}, u32[]{:S(2)}) collective-permute-start(bf16[2,256,1024]{2,1,0:T(8,128)(2,1)} %collective-permute-done.22.refs_2_), channel_id=1, source_target_pairs={{0,4},{1,3},{2,6},{3,1},{4,0},{5,7},{6,2},{7,5},{8,12},{9,11},{10,... | collective-permute-start | bytes 3145736 | tf_op jit(solution)/shard_map/ppermute | solution.py:1075
  335.2 45.0 %collective-permute-start.40 = (bf16[256,768]{1,0:T(8,128)(2,1)S(1)}, bf16[256,768]{1,0:T(8,128)(2,1)S(1)}, u32[]{:S(2)}, u32[]{:S(2)}) collective-permute-start(bf16[256,768]{1,0:T(8,128)(2,1)S(1)} %get-tuple-element.264.refs_0_), channel_id=1, source_target_pairs={{8,16},{16,8},{9,17},{17,9},{10,18},{18,10},{11,19},{19,11},{12,20... | collective-permute-start | bytes 1179656 | tf_op jit(solution)/shard_map/ppermute | solution.py:1146
  335.9 27.8 %copy-start.14 = (f32[2,128,2048]{2,1,0:T(8,128)S(1)}, f32[2,128,2048]{2,1,0:T(8,128)}, u32[]{:S(2)}) copy-start(f32[2,128,2048]{2,1,0:T(8,128)} %get-tuple-element.268.refs_0_) | copy-start | bytes 6291460
  336.2 41.5 %collective-permute-start.46 = (bf16[256,1280]{1,0:T(8,128)(2,1)S(1)}, bf16[256,1280]{1,0:T(8,128)(2,1)S(1)}, u32[]{:S(2)}, u32[]{:S(2)}) collective-permute-start(bf16[256,1280]{1,0:T(8,128)(2,1)S(1)} %get-tuple-element.282), channel_id=1, source_target_pairs={{8,0},{16,24},{9,1},{17,25},{10,2},{18,26},{11,3},{19,27},{12,4},{... | collective-permute-start | bytes 1966088 | tf_op jit(solution)/shard_map/ppermute | solution.py:1150
  369.9 3.6 collective-permute-start.52
  373.6 4.2 %collective-permute-start.53 = (f32[8,128]{1,0:T(8,128)S(1)}, f32[8,128]{1,0:T(8,128)S(1)}, u32[]{:S(2)}, u32[]{:S(2)}) collective-permute-start(f32[8,128]{1,0:T(8,128)S(1)} %maximum_select_fusion.3), channel_id=1, source_target_pairs={{0,4},{1,5},{2,6},{3,7},{4,0},{5,1},{6,2},{7,3},{8,12},{9,13},{10,... | collective-permute-start | bytes 12296 | tf_op jit(solution)/shard_map/ppermute | solution.py:1139
  377.8 5.8 %collective-permute-start.54 = (f32[8,128]{1,0:T(8,128)S(1)}, f32[8,128]{1,0:T(8,128)S(1)}, u32[]{:S(2)}, u32[]{:S(2)}) collective-permute-start(f32[8,128]{1,0:T(8,128)S(1)} %maximum_select_fusion.2), channel_id=1, source_target_pairs={{0,8},{8,0},{16,24},{24,16},{1,9},{9,1},{17,25},{25,17},{2,10},{10... | collective-permute-start | bytes 12296 | tf_op jit(solution)/shard_map/ppermute | solution.py:1139
  378.7 11.8 %collective-permute-start.47 = (bf16[128,1280]{1,0:T(8,128)(2,1)}, bf16[128,1280]{1,0:T(8,128)(2,1)}, u32[]{:S(2)}, u32[]{:S(2)}) collective-permute-start(bf16[128,1280]{1,0:T(8,128)(2,1)} %constant_dynamic-slice_fusion.3), channel_id=1, source_target_pairs={{0,1},{1,0},{2,3},{3,2},{4,5},{5,4},{6,7},{7,6},{8,9},{9,8},{10,11... | collective-permute-start | bytes 983048 | tf_op jit(solution)/shard_map/ppermute | solution.py:1063
  382.2 23.1 %collective-permute-start.45 = (bf16[2,256,1024]{2,1,0:T(8,128)(2,1)}, bf16[2,256,1024]{2,1,0:T(8,128)(2,1)}, u32[]{:S(2)}, u32[]{:S(2)}) collective-permute-start(bf16[2,256,1024]{2,1,0:T(8,128)(2,1)} %get-tuple-element.281), channel_id=1, source_target_pairs={{0,1},{1,0},{2,3},{3,2},{4,5},{5,4},{6,7},{7,6},{8,9},{9,8},{10,11... | collective-permute-start | bytes 3145736 | tf_op jit(solution)/shard_map/ppermute | solution.py:1063
  382.3 13.5 %collective-permute-start.48 = (bf16[256,768]{1,0:T(8,128)(2,1)S(1)}, bf16[256,768]{1,0:T(8,128)(2,1)}, u32[]{:S(2)}, u32[]{:S(2)}) collective-permute-start(bf16[256,768]{1,0:T(8,128)(2,1)S(1)} %get-tuple-element.283), channel_id=1, source_target_pairs={{8,0},{16,24},{9,1},{17,25},{10,2},{18,26},{11,3},{19,27},{12,4},{... | collective-permute-start | bytes 1179656 | tf_op jit(solution)/shard_map/ppermute | solution.py:1150
  383.7 4.6 %collective-permute-start.55 = (f32[8,128]{1,0:T(8,128)S(1)}, f32[8,128]{1,0:T(8,128)S(1)}, u32[]{:S(2)}, u32[]{:S(2)}) collective-permute-start(f32[8,128]{1,0:T(8,128)S(1)} %maximum_select_fusion.1), channel_id=1, source_target_pairs={{0,16},{8,24},{16,0},{24,8},{1,17},{9,25},{17,1},{25,9},{2,18},{10... | collective-permute-start | bytes 12296 | tf_op jit(solution)/shard_map/ppermute | solution.py:1139
  388.3 1.2 collective-permute-start.56
  388.3 8.8 %collective-permute-start.51 = (bf16[2,128,1024]{2,1,0:T(8,128)(2,1)S(1)}, bf16[2,128,1024]{2,1,0:T(8,128)(2,1)}, u32[]{:S(2)}, u32[]{:S(2)}) collective-permute-start(bf16[2,128,1024]{2,1,0:T(8,128)(2,1)S(1)} %constant_dynamic-slice_fusion), channel_id=1, source_target_pairs={{0,1},{1,0},{2,3},{3,2},{4,5},{5,4},{6,7},{7,6},{8,9},{9,8},{10,11... | collective-permute-start | bytes 1572872 | tf_op jit(solution)/shard_map/ppermute | solution.py:1063
  397.0 5.6 %collective-permute-start.49 = (bf16[128,768]{1,0:T(8,128)(2,1)S(1)}, bf16[128,768]{1,0:T(8,128)(2,1)S(1)}, u32[]{:S(2)}, u32[]{:S(2)}) collective-permute-start(bf16[128,768]{1,0:T(8,128)(2,1)S(1)} %constant_dynamic-slice_fusion.2), channel_id=1, source_target_pairs={{0,1},{1,0},{2,3},{3,2},{4,5},{5,4},{6,7},{7,6},{8,9},{9,8},{10,11... | collective-permute-start | bytes 589832 | tf_op jit(solution)/shard_map/ppermute | solution.py:1063
  (63 other events, 289.1 us)

commit v7 on v6

--- a/solution.py
+++ b/solution.py
@@ -885,7 +885,7 @@
     first = parts[0]
     rows = first[0].shape[-2] // (1 if first[1] is None else 2)
     shape = first[0].shape[:-2] + (rows, first[0].shape[-1])
-    count = 4
+    count = 2
     block = shape[:-2] + (rows // count, shape[-1])
     leading = (0,) * (len(shape) - 2)
 

time: 414 us -> 409 us (0.988)
  Pallas kernels: 208 us -> 203 us
    pallas_call x50, Pallas kernels: 208 us -> 203 us  [launch(): pl.pallas_call(run, grid_spec=pltpu.PrefetchScalarGridSpec(num_scalar_pre...]
  transfers between devices with their start and end apart: 57 -> 57, of which waited for: 15 -> 15; matrix products, arithmetic and copies ran while one was open for 6% -> 6% of each run, Pallas kernels for 48% -> 47%
where the time goes in v7:
time: 409 us; the launch traced here: 403 us
  Pallas kernels  203 us (50%)
  starting transfers between devices  95 us (23%)
  waiting for transfers between devices  56.4 us (14%)
  other arithmetic  21.3 us (5%)
  local copies, waits for them, and re-layouts  18.7 us (5%)
  between operations  7.38 us (2%)
    pallas_call x50, Pallas kernels, launch(): pl.pallas_call(run, grid_spec=pltpu.PrefetchScalarGridSpec(num_scalar_pre...  203 us
    ppermute x4, waiting for transfers between devices, level_out(): return (total, lax.ppermute(total, 'ctx', [(1, 0), (2, 3)]))  30.8 us
    ppermute x4, starting transfers between devices, scatter_own(): return (total, lax.ppermute(total, 'ctx', [(0, 1), (3, 2)]))  24.8 us
    ppermute x20, starting transfers between devices, turn(): return lax.ppermute(array, 'fsdp', pairs)  23.4 us
    ppermute x8, starting transfers between devices, trade(): return lax.ppermute(array, ('ctx', 'fsdp'), pairs)  21.2 us
    ppermute x13, starting transfers between devices, sibling(): return lax.ppermute(array, 'fsdp', [(i, i ^ 1) for i in range(self.shards)])  14.1 us
    unnamed x150, local copies, waits for them, and re-layouts  12.3 us
    ppermute x8, waiting for transfers between devices, trade(): return lax.ppermute(array, ('ctx', 'fsdp'), pairs)  10.6 us
  transfers between devices with their start and end apart: 57, of which 15 were waited for; matrix products, arithmetic and copies ran while one was open for 6% of the time, Pallas kernels for 47%

profile of v7, /device:TPU:0, one launch (start us, length us, event | category | flops | bytes accessed | tf_op | source)
XLA Modules:
  0.0 403.1 jit_solution(15935170389956780848)
XLA Ops:
  2.1 1.7 other_side.1
  4.3 2.2 send_blocks.2
  7.5 2.4 attention_shard.1
  10.0 2.9 collective-permute-start.3
  12.9 1.5 collective-permute-start.4
  14.4 5.4 %collective-permute-start = (bf16[256,1024]{1,0:T(8,128)(2,1)}, bf16[256,1024]{1,0:T(8,128)(2,1)}, u32[]{:S(2)}, u32[]{:S(2)}) collective-permute-start(bf16[256,1024]{1,0:T(8,128)(2,1)} %get-tuple-element.153), channel_id=1, source_target_pairs={{0,0},{1,16},{2,2},{3,18},{4,4},{5,20},{6,6},{7,22},{8,8},{9,24},{... | collective-permute-start | bytes 1572872 | tf_op jit(solution)/shard_map/ppermute | solution.py:1174
  19.8 1.6 collective-permute-start.1
  22.9 5.7 %bias_strips.1 = (f32[8,128,2048]{2,1,0:T(8,128)}, f32[8,128]{1,0:T(8,128)S(1)}) custom-call(f32[8,1,2048]{2,1,0:T(1,128)S(1)} %reshape.43.refs_0_, f32[8,128]{1,0:T(8,128)S(1)} %get-tuple-element.157.refs_1_), custom_call_target="tpu_custom_call" | custom-call | bytes 8388608 | tf_op jit(solution)/shard_map/bias_strips/pallas_call | solution.py:57
  31.0 8.5 %collective-permute-done.1.refs_1_ = bf16[256,1024]{1,0:T(8,128)(2,1)} collective-permute-done((bf16[256,1024]{1,0:T(8,128)(2,1)}, bf16[256,1024]{1,0:T(8,128)(2,1)}, u32[]{:S(2)}, u32[]{:S(2)}) %collective-permute-start.1) | collective-permute-done | bytes 524320 | tf_op jit(solution)/shard_map/ppermute | solution.py:1174
  39.4 1.7 pair.2
  44.6 3.6 token_rows.1
  48.2 2.1 hidden_shard.3
  50.6 1.9 collective-permute-start.10
  54.8 4.4 %collective-permute-start.8 = (bf16[256,1024]{1,0:T(8,128)(2,1)S(1)}, bf16[256,1024]{1,0:T(8,128)(2,1)S(1)}, u32[]{:S(2)}, u32[]{:S(2)}) collective-permute-start(bf16[256,1024]{1,0:T(8,128)(2,1)S(1)} %get-tuple-element.173), channel_id=1, source_target_pairs={{0,8},{1,24},{2,10},{3,26},{4,12},{5,28},{6,14},{7,30},{8,0},{9,16... | collective-permute-start | bytes 1572872 | tf_op jit(solution)/shard_map/ppermute | solution.py:1174
  59.2 6.3 %qkv_product.1 = (bf16[1024,1536]{1,0:T(8,128)(2,1)S(1)}, f32[8,128]{1,0:T(8,128)S(1)}) custom-call(s32[13]{0:T(128)S(1)} %stack.175.refs_0_, bf16[1024,1024]{1,0:T(8,128)(2,1)S(1)} %get-tuple-element.164.refs_1_, bf16[2,128,2048]{2,1,0:T(8,128)(2,1)} %get-tuple-element.160.refs_2_.refs_3_.refs_5_.refs_13_, ...), custom_call_target="tpu_custom_call" | custom-call | flops 3221225472 | bytes 8388608 | tf_op jit(solution)/shard_map/qkv_product/pallas_call | solution.py:57
  65.5 10.7 %attention_forward.2 = (bf16[1024,256]{1,0:T(8,128)(2,1)S(1)}, f32[2,2,1024]{2,1,0:T(2,128)S(1)}, f32[2,2,128]{2,1,0:T(2,128)S(1)}, f32[8,128]{1,0:T(8,128)S(1)}) custom-call(s32[1]{0:T(128)} %bitcast.14.refs_0_, bf16[1024,1536]{1,0:T(8,128)(2,1)S(1)} %get-tuple-element.168.refs_1_.refs_2_.refs_3_, ...), custom_call_target="tpu_custom_call" | custom-call | flops 12000000000 | bytes 6291456 | tf_op jit(solution)/shard_map/attention_forward/pallas_call | solution.py:57
  76.5 1.6 collective-permute-start.11
  78.5 10.7 %attention_forward.3 = (bf16[1024,256]{1,0:T(8,128)(2,1)S(1)}, f32[2,2,1024]{2,1,0:T(2,128)S(1)}, f32[2,2,128]{2,1,0:T(2,128)S(1)}, f32[8,128]{1,0:T(8,128)S(1)}) custom-call(s32[1]{0:T(128)} %bitcast.14.refs_0_, bf16[1024,1536]{1,0:T(8,128)(2,1)S(1)} %get-tuple-element.168.refs_1_.refs_2_.refs_3_, ...), custom_call_target="tpu_custom_call" | custom-call | flops 12000000000 | bytes 6291456 | tf_op jit(solution)/shard_map/attention_forward/pallas_call | solution.py:57
  89.3 2.0 collective-permute-done.11.refs_8_
  91.3 3.8 attended_product.1
  95.2 2.4 collective-permute-start.12
  99.0 3.8 collective-permute-done.13.refs_2_
  102.8 4.4 %cotangent_rows.1 = (bf16[1024,1024]{1,0:T(8,128)(2,1)}, bf16[1024,1024]{1,0:T(8,128)(2,1)}, bf16[1024,1024]{1,0:T(8,128)(2,1)}, f32[8,128]{1,0:T(8,128)S(1)}) custom-call(s32[9]{0:T(128)S(1)} %stack.181.refs_0_, bf16[2,256,1024]{2,1,0:T(8,128)(2,1)S(1)} %get-tuple-element.180.refs_1_, bf16[2,256,1024]{2,1,0:T(8,128)(2,1)S(1)} %collective-permute-done.13.refs_2_, ...), custom_call_target="tpu_custom_call" | custom-call | bytes 10485760 | tf_op jit(solution)/shard_map/cotangent_rows/pallas_call | solution.py:57
  107.2 4.8 %second_norm.1 = (f32[1024,1024]{1,0:T(8,128)}, bf16[1024,1024]{1,0:T(8,128)(2,1)}, bf16[1024,1024]{1,0:T(8,128)(2,1)}, f32[8,128]{1,0:T(8,128)S(1)}) custom-call(s32[4]{0:T(128)S(1)} %pad_add_fusion.2.refs_0_, bf16[1024,1024]{1,0:T(8,128)(2,1)S(1)} %get-tuple-element.163.refs_1_.refs_4_, bf16[1024,1024]{1,0:T(8,128)(2,1)S(1)} %get-tuple-element.179.refs_2_, ...), custom_call_target="tpu_custom_call" | custom-call | bytes 14680064 | tf_op jit(solution)/shard_map/second_norm/pallas_call | solution.py:57
  112.4 2.0 relay.1
  116.5 23.4 %feed_forward.2 = (f32[1024,1024]{1,0:T(8,128)}, f32[1024,1024]{1,0:T(8,128)}, bf16[2,512,1024]{2,1,0:T(8,128)(2,1)}, bf16[2,512,1024]{2,1,0:T(8,128)(2,1)}, f32[8,128]{1,0:T(8,128)}) custom-call(s32[13]{0:T(128)} %copy-done.33, bf16[1024,1024]{1,0:T(8,128)(2,1)} %get-tuple-element.183.refs_1_, bf16[1024,1024]{1,0:T(8,128)(2,1)} %get-tuple-element.184.refs_2_, ...), custom_call_target="tpu_custom_call" | custom-call | flops 21474836480 | bytes 41943040 | tf_op jit(solution)/shard_map/feed_forward/pallas_call | solution.py:57
  142.2 24.5 %feed_forward.3 = (bf16[512,1024]{1,0:T(8,128)(2,1)}, bf16[512,1024]{1,0:T(8,128)(2,1)}, bf16[1024,1024]{1,0:T(8,128)(2,1)}, bf16[2,512,1024]{2,1,0:T(8,128)(2,1...) custom-call(s32[13]{0:T(128)} %copy-done.33, bf16[1024,1024]{1,0:T(8,128)(2,1)} %get-tuple-element.183.refs_1_, ...), custom_call_target="tpu_custom_call" | custom-call | flops 21474836480 | bytes 41943040 | tf_op jit(solution)/shard_map/feed_forward/pallas_call | solution.py:57
  168.7 1.6 copy-done.6
  171.0 1.6 row_sums.16
  173.9 8.7 %hidden_back.1 = (f32[1024,1024]{1,0:T(8,128)S(1)}, bf16[1024,1024]{1,0:T(8,128)(2,1)}, bf16[1024,1024]{1,0:T(8,128)(2,1)S(1)}, bf16[1024,512]{1,0:T(8,128)(2,1)S(1)}, f32[8,128]{1,0:T(8,128)S(1)}) custom-call(s32[13]{0:T(128)S(1)} %copy-done.34, bf16[1024,1024]{1,0:T(8,128)(2,1)S(1)} %copy-done.13, bf16[1024,1024]{1,0:T(8,128)(2,1)S(1)} %collective-permute-done.18.refs_2_, ...), custom_call_target="tpu_custom_call" | custom-call | flops 2147483648 | bytes 25165824 | tf_op jit(solution)/shard_map/hidden_back/pallas_call | solution.py:57
  182.7 1.5 result_rows.1
  185.6 6.5 %collective-permute-start.21 = (bf16[256,1024]{1,0:T(8,128)(2,1)S(1)}, bf16[256,1024]{1,0:T(8,128)(2,1)S(1)}, u32[]{:S(2)}, u32[]{:S(2)}) collective-permute-start(bf16[256,1024]{1,0:T(8,128)(2,1)S(1)} %get-tuple-element.205), channel_id=1, source_target_pairs={{8,0},{24,1},{10,2},{26,3},{12,4},{28,5},{14,6},{30,7},{0,8},{16,9... | collective-permute-start | bytes 1572872 | tf_op jit(solution)/shard_map/ppermute | solution.py:1174
  192.1 11.0 %attention_backward.4 = (bf16[1024,128]{1,0:T(8,128)(2,1)S(1)}, bf16[1024,128]{1,0:T(8,128)(2,1)S(1)}, bf16[1024,128]{1,0:T(8,128)(2,1)S(1)}, f32[2,128,2048]{2,1,0:T(8,128)}, f32[8,128]{1,0:T(8,128)S(1)}) custom-call(s32[1]{0:T(128)} %bitcast.14.refs_0_, bf16[1024,1536]{1,0:T(8,128)(2,1)S(1)} %copy-done.48, bf16[1024,1536]{1,0:T(8,128)(2,1)S(1)} %copy-done.48, ...), custom_call_target="tpu_custom_call" | custom-call | flops 10000000000 | bytes 6291456 | tf_op jit(solution)/shard_map/attention_backward/pallas_call | solution.py:57
  203.1 11.1 %attention_backward.5 = (bf16[1024,128]{1,0:T(8,128)(2,1)S(1)}, bf16[1024,128]{1,0:T(8,128)(2,1)S(1)}, bf16[1024,128]{1,0:T(8,128)(2,1)S(1)}, f32[2,128,2048]{2,1,0:T(8,128)}, f32[8,128]{1,0:T(8,128)S(1)}) custom-call(s32[1]{0:T(128)} %bitcast.14.refs_0_, bf16[1024,1536]{1,0:T(8,128)(2,1)S(1)} %copy-done.48, bf16[1024,1536]{1,0:T(8,128)(2,1)S(1)} %copy-done.48, ...), custom_call_target="tpu_custom_call" | custom-call | flops 10000000000 | bytes 6291456 | tf_op jit(solution)/shard_map/attention_backward/pallas_call | solution.py:57
  214.2 2.0 row_sums.17
  218.3 3.1 attention_terms.2
  222.3 2.5 collective-permute-start.29
  224.8 11.4 %attention_backward.6 = (bf16[1024,128]{1,0:T(8,128)(2,1)S(1)}, bf16[1024,128]{1,0:T(8,128)(2,1)S(1)}, bf16[1024,128]{1,0:T(8,128)(2,1)S(1)}, f32[2,128,2048]{2,1,0:T(8,128)}, f32[8,128]{1,0:T(8,128)S(1)}) custom-call(s32[1]{0:T(128)} %bitcast.14.refs_0_, bf16[1024,1536]{1,0:T(8,128)(2,1)S(1)} %copy-done.48, bf16[1024,1536]{1,0:T(8,128)(2,1)S(1)} %copy-done.48, ...), custom_call_target="tpu_custom_call" | custom-call | flops 10000000000 | bytes 6291456 | tf_op jit(solution)/shard_map/attention_backward/pallas_call | solution.py:57
  237.6 2.2 collective-permute-start.31
  239.8 11.0 %attention_backward.7 = (bf16[1024,128]{1,0:T(8,128)(2,1)S(1)}, bf16[1024,128]{1,0:T(8,128)(2,1)S(1)}, bf16[1024,128]{1,0:T(8,128)(2,1)S(1)}, f32[2,128,2048]{2,1,0:T(8,128)}, f32[8,128]{1,0:T(8,128)S(1)}) custom-call(s32[1]{0:T(128)} %bitcast.14.refs_0_, bf16[1024,1536]{1,0:T(8,128)(2,1)S(1)} %copy-done.48, bf16[1024,1536]{1,0:T(8,128)(2,1)S(1)} %copy-done.48, ...), custom_call_target="tpu_custom_call" | custom-call | flops 10000000000 | bytes 6291456 | tf_op jit(solution)/shard_map/attention_backward/pallas_call | solution.py:57
  252.3 2.0 attention_terms.3
  256.0 7.3 %input_product.1 = (f32[512,1024]{1,0:T(8,128)S(1)}, bf16[512,1024]{1,0:T(8,128)(2,1)}, f32[8,128]{1,0:T(8,128)S(1)}) custom-call(s32[13]{0:T(128)S(1)} %copy-done.34, bf16[1024,128]{1,0:T(8,128)(2,1)S(1)} %get-tuple-element.212.refs_4_.refs_1_, bf16[1024,128]{1,0:T(8,128)(2,1)S(1)} %get-tuple-element.213.refs_5_.refs_2_, ...), custom_call_target="tpu_custom_call" | custom-call | flops 3221225472 | bytes 14680064 | tf_op jit(solution)/shard_map/input_product/pallas_call | solution.py:57
  264.6 5.8 %collective-permute-start.37 = (bf16[512,1024]{1,0:T(8,128)(2,1)}, bf16[512,1024]{1,0:T(8,128)(2,1)}, u32[]{:S(2)}, u32[]{:S(2)}) collective-permute-start(bf16[512,1024]{1,0:T(8,128)(2,1)} %get-tuple-element.256), channel_id=1, source_target_pairs={{0,1},{1,0},{2,3},{3,2},{4,5},{5,4},{6,7},{7,6},{8,9},{9,8},{10,11... | collective-permute-start | bytes 3145736 | tf_op jit(solution)/shard_map/ppermute | solution.py:1063
  272.6 1.8 collective-permute-start.36
  279.1 14.4 %collective-permute-start.38 = (bf16[256,1280]{1,0:T(8,128)(2,1)}, bf16[256,1280]{1,0:T(8,128)(2,1)}, u32[]{:S(2)}, u32[]{:S(2)}) collective-permute-start(bf16[256,1280]{1,0:T(8,128)(2,1)} %get-tuple-element.258.refs_0_), channel_id=1, source_target_pairs={{0,8},{24,16},{1,9},{25,17},{2,10},{26,18},{3,11},{27,19},{4,12},{... | collective-permute-start | bytes 1966088 | tf_op jit(solution)/shard_map/ppermute | solution.py:1126
  300.1 2.6 stack.158.refs_0_
  305.2 5.6 %collective-permute-start.35 = (bf16[256,768]{1,0:T(8,128)(2,1)S(1)}, bf16[256,768]{1,0:T(8,128)(2,1)S(1)}, u32[]{:S(2)}, u32[]{:S(2)}) collective-permute-start(bf16[256,768]{1,0:T(8,128)(2,1)S(1)} %get-tuple-element.253.refs_0_), channel_id=1, source_target_pairs={{0,8},{24,16},{1,9},{25,17},{2,10},{26,18},{3,11},{27,19},{4,12},{... | collective-permute-start | bytes 1179656 | tf_op jit(solution)/shard_map/ppermute | solution.py:1126
  312.9 3.6 input_gradient_rows.1
  318.2 1.7 row_sums.28
  322.6 2.6 collective-permute-start.50
  326.6 2.2 collective-permute-done.44.refs_4_
  329.7 1.5 maximum_convert_fusion
  332.1 1.4 collective-permute-start.46
  334.6 24.2 %collective-permute-done.42.refs_2_ = bf16[2,256,1024]{2,1,0:T(8,128)(2,1)S(1)} collective-permute-done((bf16[2,256,1024]{2,1,0:T(8,128)(2,1)S(1)}, bf16[2,256,1024]{2,1,0:T(8,128)(2,1)S(1)}, u32[]{:S(2)}, u32[]{:S(2)}) %collective-permute-start.42) | collective-permute-done | bytes 1048608 | tf_op jit(solution)/shard_map/ppermute | solution.py:1150
  367.1 1.5 collective-permute-done.52
  369.6 3.3 collective-permute-done.46
  373.9 1.4 collective-permute-start.47
  375.5 1.9 pick_slots.1
  379.0 4.4 %collective-permute-done.55 = f32[8,128]{1,0:T(8,128)S(1)} collective-permute-done((f32[8,128]{1,0:T(8,128)S(1)}, f32[8,128]{1,0:T(8,128)S(1)}, u32[]{:S(2)}, u32[]{:S(2)}) %collective-permute-start.55) | collective-permute-done | bytes 4128 | tf_op jit(solution)/shard_map/ppermute | solution.py:1139
  387.8 3.2 collective-permute-done.48
  393.8 1.5 maximum_convert_fusion.1
  395.4 2.4 convert_multiply_fusion
  398.2 2.3 convert_multiply_fusion.6
  400.5 1.4 slice_select_fusion.1
  (310 shorter events, 75.6 us)
Async XLA Ops:
  0.6 21.6 %copy-start = (bf16[32,16]{0,1:T(8,128)(2,1)S(1)}, bf16[32,16]{0,1:T(8,128)(2,1)}, u32[]{:S(2)}) copy-start(bf16[32,16]{0,1:T(8,128)(2,1)} %param.28) | copy-start | bytes 3076
  3.8 17.6 %copy-start.58 = (s32[2047]{0:T(1024)S(1)}, s32[2047]{0:T(1024)}, u32[]{:S(2)}) copy-start(s32[2047]{0:T(1024)} %param.19) | copy-start | bytes 24568
  3.8 3.7 collective-permute-start.2
  10.0 29.5 %collective-permute-start.3 = (bf16[2,128,2048]{2,1,0:T(8,128)(2,1)}, bf16[2,128,2048]{2,1,0:T(8,128)(2,1)S(1)}, u32[]{:S(2)}, u32[]{:S(2)}) collective-permute-start(bf16[2,128,2048]{2,1,0:T(8,128)(2,1)} %get-tuple-element.160.refs_2_.refs_3_.refs_5_.refs_13_), channel_id=1, source_target_pairs={{0,2},{1,5},{2,0},{3,7},{4,6},{5,1},{6,4},{7,3},{8,10},{9,13},{10,... | collective-permute-start | bytes 3145736 | tf_op jit(solution)/shard_map/ppermute | solution.py:1075
  12.9 26.5 %collective-permute-start.4 = (bf16[2,128,2048]{2,1,0:T(8,128)(2,1)}, bf16[2,128,2048]{2,1,0:T(8,128)(2,1)S(1)}, u32[]{:S(2)}, u32[]{:S(2)}) collective-permute-start(bf16[2,128,2048]{2,1,0:T(8,128)(2,1)} %get-tuple-element.160.refs_2_.refs_3_.refs_5_.refs_13_), channel_id=1, source_target_pairs={{0,4},{1,3},{2,6},{3,1},{4,0},{5,7},{6,2},{7,5},{8,12},{9,11},{10,... | collective-permute-start | bytes 3145736 | tf_op jit(solution)/shard_map/ppermute | solution.py:1075
  14.4 16.5 %collective-permute-start = (bf16[256,1024]{1,0:T(8,128)(2,1)}, bf16[256,1024]{1,0:T(8,128)(2,1)}, u32[]{:S(2)}, u32[]{:S(2)}) collective-permute-start(bf16[256,1024]{1,0:T(8,128)(2,1)} %get-tuple-element.153), channel_id=1, source_target_pairs={{0,0},{1,16},{2,2},{3,18},{4,4},{5,20},{6,6},{7,22},{8,8},{9,24},{... | collective-permute-start | bytes 1572872 | tf_op jit(solution)/shard_map/ppermute | solution.py:1174
  19.8 19.6 %collective-permute-start.1 = (bf16[256,1024]{1,0:T(8,128)(2,1)}, bf16[256,1024]{1,0:T(8,128)(2,1)}, u32[]{:S(2)}, u32[]{:S(2)}) collective-permute-start(bf16[256,1024]{1,0:T(8,128)(2,1)} %get-tuple-element.154), channel_id=1, source_target_pairs={{0,8},{1,24},{2,10},{3,26},{4,12},{5,28},{6,14},{7,30},{8,0},{9,16... | collective-permute-start | bytes 1572872 | tf_op jit(solution)/shard_map/ppermute | solution.py:1174
  41.1 3.4 collective-permute-start.5
  41.2 18.0 %collective-permute-start.6 = (bf16[2,128,2048]{2,1,0:T(8,128)(2,1)S(1)}, bf16[2,128,2048]{2,1,0:T(8,128)(2,1)}, u32[]{:S(2)}, u32[]{:S(2)}) collective-permute-start(bf16[2,128,2048]{2,1,0:T(8,128)(2,1)S(1)} %collective-permute-done.3.refs_3_.refs_4_.refs_6_.refs_14_), channel_id=1, source_target_pairs={{0,4},{1,3},{2,6},{3,1},{4,0},{5,7},{6,2},{7,5},{8,12},{9,11},{10,... | collective-permute-start | bytes 3145736 | tf_op jit(solution)/shard_map/ppermute | solution.py:1075
  44.5 46.8 %copy-start.33 = (s32[13]{0:T(128)}, s32[13]{0:T(128)S(1)}, u32[]{:S(2)}) copy-start(s32[13]{0:T(128)S(1)} %stack.175.refs_0_) | copy-start | bytes 160
  48.2 17.3 %slice-start = ((s8[8388608]{0:T(1024)(128)(4,1)}), s8[4194304]{0:T(1024)(128)(4,1)S(1)}, s32[]{:S(2)}) async-start(s8[8388608]{0:T(1024)(128)(4,1)} %bitcast.67), calls=%async_computation | async-start | bytes 8388608
  50.4 26.2 %collective-permute-start.9 = (bf16[2,2,128,1024]{3,2,1,0:T(8,128)(2,1)S(1)}, bf16[2,2,128,1024]{3,2,1,0:T(8,128)(2,1)S(1)}, u32[]{:S(2)}, u32[]{:S(2)}) collective-permute-start(bf16[2,2,128,1024]{3,2,1,0:T(8,128)(2,1)S(1)} %get-tuple-element.176.refs_5_), channel_id=1, source_target_pairs={{0,2},{1,5},{2,0},{3,7},{4,6},{5,1},{6,4},{7,3},{8,10},{9,13},{10,... | collective-permute-start | bytes 3145736 | tf_op jit(solution)/shard_map/ppermute | solution.py:1075
  50.6 28.0 %collective-permute-start.10 = (bf16[2,2,128,1024]{3,2,1,0:T(8,128)(2,1)S(1)}, bf16[2,2,128,1024]{3,2,1,0:T(8,128)(2,1)S(1)}, u32[]{:S(2)}, u32[]{:S(2)}) collective-permute-start(bf16[2,2,128,1024]{3,2,1,0:T(8,128)(2,1)S(1)} %get-tuple-element.176.refs_5_), channel_id=1, source_target_pairs={{0,4},{1,3},{2,6},{3,1},{4,0},{5,7},{6,2},{7,5},{8,12},{9,11},{10,... | collective-permute-start | bytes 3145736 | tf_op jit(solution)/shard_map/ppermute | solution.py:1075
  53.8 22.5 %collective-permute-start.7 = (bf16[256,1024]{1,0:T(8,128)(2,1)S(1)}, bf16[256,1024]{1,0:T(8,128)(2,1)S(1)}, u32[]{:S(2)}, u32[]{:S(2)}) collective-permute-start(bf16[256,1024]{1,0:T(8,128)(2,1)S(1)} %get-tuple-element.172), channel_id=1, source_target_pairs={{0,0},{1,16},{2,2},{3,18},{4,4},{5,20},{6,6},{7,22},{8,8},{9,24},{... | collective-permute-start | bytes 1572872 | tf_op jit(solution)/shard_map/ppermute | solution.py:1174
  54.8 21.5 %collective-permute-start.8 = (bf16[256,1024]{1,0:T(8,128)(2,1)S(1)}, bf16[256,1024]{1,0:T(8,128)(2,1)S(1)}, u32[]{:S(2)}, u32[]{:S(2)}) collective-permute-start(bf16[256,1024]{1,0:T(8,128)(2,1)S(1)} %get-tuple-element.173), channel_id=1, source_target_pairs={{0,8},{1,24},{2,10},{3,26},{4,12},{5,28},{6,14},{7,30},{8,0},{9,16... | collective-permute-start | bytes 1572872 | tf_op jit(solution)/shard_map/ppermute | solution.py:1174
  76.2 15.1 %copy-start.31 = (bf16[1024,256]{1,0:T(8,128)(2,1)}, bf16[1024,256]{1,0:T(8,128)(2,1)S(1)}, u32[]{:S(2)}) copy-start(bf16[1024,256]{1,0:T(8,128)(2,1)S(1)} %get-tuple-element.171.refs_1_.refs_4_.refs_2_) | copy-start | bytes 1572868
  76.5 14.8 %collective-permute-start.11 = (bf16[2,2,128,1024]{3,2,1,0:T(8,128)(2,1)S(1)}, bf16[2,2,128,1024]{3,2,1,0:T(8,128)(2,1)S(1)}, u32[]{:S(2)}, u32[]{:S(2)}) collective-permute-start(bf16[2,2,128,1024]{3,2,1,0:T(8,128)(2,1)S(1)} %collective-permute-done.9.refs_6_), channel_id=1, source_target_pairs={{0,4},{1,3},{2,6},{3,1},{4,0},{5,7},{6,2},{7,5},{8,12},{9,11},{10,... | collective-permute-start | bytes 3145736 | tf_op jit(solution)/shard_map/ppermute | solution.py:1075
  95.2 12.0 %collective-permute-start.12 = (bf16[1024,1024]{1,0:T(8,128)(2,1)S(1)}, bf16[1024,1024]{1,0:T(8,128)(2,1)S(1)}, u32[]{:S(2)}, u32[]{:S(2)}) collective-permute-start(bf16[1024,1024]{1,0:T(8,128)(2,1)S(1)} %get-tuple-element.179.refs_2_), channel_id=1, source_target_pairs={{0,1},{1,0},{2,3},{3,2},{4,5},{5,4},{6,7},{7,6},{8,9},{9,8},{10,11... | collective-permute-start | bytes 6291464 | tf_op jit(solution)/shard_map/ppermute | solution.py:1063
  97.6 5.3 %collective-permute-start.13 = (bf16[2,256,1024]{2,1,0:T(8,128)(2,1)S(1)}, bf16[2,256,1024]{2,1,0:T(8,128)(2,1)S(1)}, u32[]{:S(2)}, u32[]{:S(2)}) collective-permute-start(bf16[2,256,1024]{2,1,0:T(8,128)(2,1)S(1)} %get-tuple-element.180.refs_1_), channel_id=1, source_target_pairs={{0,1},{1,0},{2,3},{3,2},{4,5},{5,4},{6,7},{7,6},{8,9},{9,8},{10,11... | collective-permute-start | bytes 3145736 | tf_op jit(solution)/shard_map/ppermute | solution.py:1063
  97.6 14.8 %collective-permute-start.14 = (bf16[2,2,128,1024]{3,2,1,0:T(8,128)(2,1)S(1)}, bf16[2,2,128,1024]{3,2,1,0:T(8,128)(2,1)S(1)}, u32[]{:S(2)}, u32[]{:S(2)}) collective-permute-start(bf16[2,2,128,1024]{3,2,1,0:T(8,128)(2,1)S(1)} %copy-done.25), channel_id=1, source_target_pairs={{0,2},{1,5},{2,0},{3,7},{4,6},{5,1},{6,4},{7,3},{8,10},{9,13},{10,... | collective-permute-start | bytes 3145736 | tf_op jit(solution)/shard_map/ppermute | solution.py:1075
  114.4 26.7 %collective-permute-start.15 = (bf16[2,2,128,1024]{3,2,1,0:T(8,128)(2,1)}, bf16[2,2,128,1024]{3,2,1,0:T(8,128)(2,1)S(1)}, u32[]{:S(2)}, u32[]{:S(2)}) collective-permute-start(bf16[2,2,128,1024]{3,2,1,0:T(8,128)(2,1)} %get-tuple-element.189), channel_id=1, source_target_pairs={{0,4},{1,3},{2,6},{3,1},{4,0},{5,7},{6,2},{7,5},{8,12},{9,11},{10,... | collective-permute-start | bytes 3145736 | tf_op jit(solution)/shard_map/ppermute | solution.py:1075
  115.7 25.5 %collective-permute-start.16 = (bf16[2,2,128,1024]{3,2,1,0:T(8,128)(2,1)}, bf16[2,2,128,1024]{3,2,1,0:T(8,128)(2,1)}, u32[]{:S(2)}, u32[]{:S(2)}) collective-permute-start(bf16[2,2,128,1024]{3,2,1,0:T(8,128)(2,1)} %get-tuple-element.190), channel_id=1, source_target_pairs={{0,4},{1,3},{2,6},{3,1},{4,0},{5,7},{6,2},{7,5},{8,12},{9,11},{10,... | collective-permute-start | bytes 3145736 | tf_op jit(solution)/shard_map/ppermute | solution.py:1075
  139.9 28.8 %collective-permute-start.19 = (bf16[2,512,1024]{2,1,0:T(8,128)(2,1)}, bf16[2,512,1024]{2,1,0:T(8,128)(2,1)}, u32[]{:S(2)}, u32[]{:S(2)}) collective-permute-start(bf16[2,512,1024]{2,1,0:T(8,128)(2,1)} %get-tuple-element.200), channel_id=1, source_target_pairs={{0,4},{1,3},{2,6},{3,1},{4,0},{5,7},{6,2},{7,5},{8,12},{9,11},{10,... | collective-permute-start | bytes 6291464 | tf_op jit(solution)/shard_map/ppermute | solution.py:1075
  166.7 7.2 %collective-permute-start.18 = (bf16[1024,1024]{1,0:T(8,128)(2,1)}, bf16[1024,1024]{1,0:T(8,128)(2,1)S(1)}, u32[]{:S(2)}, u32[]{:S(2)}) collective-permute-start(bf16[1024,1024]{1,0:T(8,128)(2,1)} %get-tuple-element.198.refs_1_), channel_id=1, source_target_pairs={{0,1},{1,0},{2,3},{3,2},{4,5},{5,4},{6,7},{7,6},{8,9},{9,8},{10,11... | collective-permute-start | bytes 6291464 | tf_op jit(solution)/shard_map/ppermute | solution.py:1063
  166.7 15.9 %collective-permute-start.17 = (bf16[512,1024]{1,0:T(8,128)(2,1)}, bf16[512,1024]{1,0:T(8,128)(2,1)S(1)}, u32[]{:S(2)}, u32[]{:S(2)}) collective-permute-start(bf16[512,1024]{1,0:T(8,128)(2,1)} %get-tuple-element.196), channel_id=1, source_target_pairs={{0,1},{1,0},{2,3},{3,2},{4,5},{5,4},{6,7},{7,6},{8,9},{9,8},{10,11... | collective-permute-start | bytes 3145736 | tf_op jit(solution)/shard_map/ppermute | solution.py:1063
  167.2 49.0 %collective-permute-start.25 = (bf16[2,512,1024]{2,1,0:T(8,128)(2,1)}, bf16[2,512,1024]{2,1,0:T(8,128)(2,1)S(1)}, u32[]{:S(2)}, u32[]{:S(2)}) collective-permute-start(bf16[2,512,1024]{2,1,0:T(8,128)(2,1)} %get-tuple-element.220), channel_id=1, source_target_pairs={{0,4},{1,3},{2,6},{3,1},{4,0},{5,7},{6,2},{7,5},{8,12},{9,11},{10,... | collective-permute-start | bytes 6291464 | tf_op jit(solution)/shard_map/ppermute | solution.py:1075
  172.6 41.6 %collective-permute-start.26 = (bf16[2,256,1024]{2,1,0:T(8,128)(2,1)S(1)}, bf16[2,256,1024]{2,1,0:T(8,128)(2,1)S(1)}, u32[]{:S(2)}, u32[]{:S(2)}) collective-permute-start(bf16[2,256,1024]{2,1,0:T(8,128)(2,1)S(1)} %get-tuple-element.221), channel_id=1, source_target_pairs={{0,2},{1,5},{2,0},{3,7},{4,6},{5,1},{6,4},{7,3},{8,10},{9,13},{10,... | collective-permute-start | bytes 3145736 | tf_op jit(solution)/shard_map/ppermute | solution.py:1075
  184.8 29.4 %collective-permute-start.20 = (bf16[256,1024]{1,0:T(8,128)(2,1)S(1)}, bf16[256,1024]{1,0:T(8,128)(2,1)S(1)}, u32[]{:S(2)}, u32[]{:S(2)}) collective-permute-start(bf16[256,1024]{1,0:T(8,128)(2,1)S(1)} %get-tuple-element.204), channel_id=1, source_target_pairs={{0,0},{16,1},{2,2},{18,3},{4,4},{20,5},{6,6},{22,7},{8,8},{24,9},{... | collective-permute-start | bytes 1572872 | tf_op jit(solution)/shard_map/ppermute | solution.py:1174
  185.6 28.6 %collective-permute-start.21 = (bf16[256,1024]{1,0:T(8,128)(2,1)S(1)}, bf16[256,1024]{1,0:T(8,128)(2,1)S(1)}, u32[]{:S(2)}, u32[]{:S(2)}) collective-permute-start(bf16[256,1024]{1,0:T(8,128)(2,1)S(1)} %get-tuple-element.205), channel_id=1, source_target_pairs={{8,0},{24,1},{10,2},{26,3},{12,4},{28,5},{14,6},{30,7},{0,8},{16,9... | collective-permute-start | bytes 1572872 | tf_op jit(solution)/shard_map/ppermute | solution.py:1174
  217.0 19.8 %collective-permute-start.27 = (bf16[2,256,1024]{2,1,0:T(8,128)(2,1)S(1)}, bf16[2,256,1024]{2,1,0:T(8,128)(2,1)S(1)}, u32[]{:S(2)}, u32[]{:S(2)}) collective-permute-start(bf16[2,256,1024]{2,1,0:T(8,128)(2,1)S(1)} %get-tuple-element.229), channel_id=1, source_target_pairs={{0,2},{1,5},{2,0},{3,7},{4,6},{5,1},{6,4},{7,3},{8,10},{9,13},{10,... | collective-permute-start | bytes 3145736 | tf_op jit(solution)/shard_map/ppermute | solution.py:1075
  221.4 30.6 %collective-permute-start.28 = (bf16[512,1280]{1,0:T(8,128)(2,1)S(1)}, bf16[512,1280]{1,0:T(8,128)(2,1)S(1)}, u32[]{:S(2)}, u32[]{:S(2)}) collective-permute-start(bf16[512,1280]{1,0:T(8,128)(2,1)S(1)} %get-tuple-element.236), channel_id=1, source_target_pairs={{0,4},{1,3},{2,6},{3,1},{4,0},{5,7},{6,2},{7,5},{8,12},{9,11},{10,... | collective-permute-start | bytes 3932168 | tf_op jit(solution)/shard_map/ppermute | solution.py:1075
  222.3 28.5 %collective-permute-start.29 = (bf16[2,256,1024]{2,1,0:T(8,128)(2,1)S(1)}, bf16[2,256,1024]{2,1,0:T(8,128)(2,1)S(1)}, u32[]{:S(2)}, u32[]{:S(2)}) collective-permute-start(bf16[2,256,1024]{2,1,0:T(8,128)(2,1)S(1)} %get-tuple-element.237.refs_0_), channel_id=1, source_target_pairs={{0,8},{24,16},{1,9},{25,17},{2,10},{26,18},{3,11},{27,19},{4,12},{... | collective-permute-start | bytes 3145736 | tf_op jit(solution)/shard_map/ppermute | solution.py:1126
  237.6 33.8 %collective-permute-start.31 = (bf16[2,256,1024]{2,1,0:T(8,128)(2,1)S(1)}, bf16[2,256,1024]{2,1,0:T(8,128)(2,1)S(1)}, u32[]{:S(2)}, u32[]{:S(2)}) collective-permute-start(bf16[2,256,1024]{2,1,0:T(8,128)(2,1)S(1)} %get-tuple-element.243.refs_0_), channel_id=1, source_target_pairs={{0,8},{24,16},{1,9},{25,17},{2,10},{26,18},{3,11},{27,19},{4,12},{... | collective-permute-start | bytes 3145736 | tf_op jit(solution)/shard_map/ppermute | solution.py:1126
  251.3 24.0 %collective-permute-start.34 = (bf16[2,256,1024]{2,1,0:T(8,128)(2,1)S(1)}, bf16[2,256,1024]{2,1,0:T(8,128)(2,1)S(1)}, u32[]{:S(2)}, u32[]{:S(2)}) collective-permute-start(bf16[2,256,1024]{2,1,0:T(8,128)(2,1)S(1)} %get-tuple-element.250.refs_0_), channel_id=1, source_target_pairs={{8,16},{16,8},{9,17},{17,9},{10,18},{18,10},{11,19},{19,11},{12,20... | collective-permute-start | bytes 3145736 | tf_op jit(solution)/shard_map/ppermute | solution.py:1146
  254.3 20.1 %copy-start.9 = (bf16[512,768]{1,0:T(8,128)(2,1)}, bf16[512,768]{1,0:T(8,128)(2,1)S(1)}, u32[]{:S(2)}) copy-start(bf16[512,768]{1,0:T(8,128)(2,1)S(1)} %get-tuple-element.241.refs_0_) | copy-start | bytes 2359300
  254.3 20.1 %collective-permute-start.30 = (bf16[512,768]{1,0:T(8,128)(2,1)S(1)}, bf16[512,768]{1,0:T(8,128)(2,1)S(1)}, u32[]{:S(2)}, u32[]{:S(2)}) collective-permute-start(bf16[512,768]{1,0:T(8,128)(2,1)S(1)} %get-tuple-element.242), channel_id=1, source_target_pairs={{0,4},{1,3},{2,6},{3,1},{4,0},{5,7},{6,2},{7,5},{8,12},{9,11},{10,... | collective-permute-start | bytes 2359304 | tf_op jit(solution)/shard_map/ppermute | solution.py:1075
  255.2 15.2 %collective-permute-start.32 = (bf16[256,1280]{1,0:T(8,128)(2,1)S(1)}, bf16[256,1280]{1,0:T(8,128)(2,1)S(1)}, u32[]{:S(2)}, u32[]{:S(2)}) collective-permute-start(bf16[256,1280]{1,0:T(8,128)(2,1)S(1)} %get-tuple-element.244), channel_id=1, source_target_pairs={{0,2},{1,5},{2,0},{3,7},{4,6},{5,1},{6,4},{7,3},{8,10},{9,13},{10,... | collective-permute-start | bytes 1966088 | tf_op jit(solution)/shard_map/ppermute | solution.py:1075
  264.6 47.6 %collective-permute-start.37 = (bf16[512,1024]{1,0:T(8,128)(2,1)}, bf16[512,1024]{1,0:T(8,128)(2,1)}, u32[]{:S(2)}, u32[]{:S(2)}) collective-permute-start(bf16[512,1024]{1,0:T(8,128)(2,1)} %get-tuple-element.256), channel_id=1, source_target_pairs={{0,1},{1,0},{2,3},{3,2},{4,5},{5,4},{6,7},{7,6},{8,9},{9,8},{10,11... | collective-permute-start | bytes 3145736 | tf_op jit(solution)/shard_map/ppermute | solution.py:1063
  272.6 43.9 %collective-permute-start.36 = (bf16[2,256,1024]{2,1,0:T(8,128)(2,1)}, bf16[2,256,1024]{2,1,0:T(8,128)(2,1)}, u32[]{:S(2)}, u32[]{:S(2)}) collective-permute-start(bf16[2,256,1024]{2,1,0:T(8,128)(2,1)} %get-tuple-element.254.refs_0_), channel_id=1, source_target_pairs={{8,16},{16,8},{9,17},{17,9},{10,18},{18,10},{11,19},{19,11},{12,20... | collective-permute-start | bytes 3145736 | tf_op jit(solution)/shard_map/ppermute | solution.py:1146
  276.6 40.7 %collective-permute-start.39 = (bf16[2,256,1024]{2,1,0:T(8,128)(2,1)}, bf16[2,256,1024]{2,1,0:T(8,128)(2,1)}, u32[]{:S(2)}, u32[]{:S(2)}) collective-permute-start(bf16[2,256,1024]{2,1,0:T(8,128)(2,1)} %get-tuple-element.262), channel_id=1, source_target_pairs={{8,0},{16,24},{9,1},{17,25},{10,2},{18,26},{11,3},{19,27},{12,4},{... | collective-permute-start | bytes 3145736 | tf_op jit(solution)/shard_map/ppermute | solution.py:1150
  277.9 15.8 %collective-permute-start.33 = (bf16[256,768]{1,0:T(8,128)(2,1)}, bf16[256,768]{1,0:T(8,128)(2,1)S(1)}, u32[]{:S(2)}, u32[]{:S(2)}) collective-permute-start(bf16[256,768]{1,0:T(8,128)(2,1)} %copy-done.45), channel_id=1, source_target_pairs={{0,2},{1,5},{2,0},{3,7},{4,6},{5,1},{6,4},{7,3},{8,10},{9,13},{10,... | collective-permute-start | bytes 1179656 | tf_op jit(solution)/shard_map/ppermute | solution.py:1075
  279.1 26.0 %collective-permute-start.38 = (bf16[256,1280]{1,0:T(8,128)(2,1)}, bf16[256,1280]{1,0:T(8,128)(2,1)}, u32[]{:S(2)}, u32[]{:S(2)}) collective-permute-start(bf16[256,1280]{1,0:T(8,128)(2,1)} %get-tuple-element.258.refs_0_), channel_id=1, source_target_pairs={{0,8},{24,16},{1,9},{25,17},{2,10},{26,18},{3,11},{27,19},{4,12},{... | collective-permute-start | bytes 1966088 | tf_op jit(solution)/shard_map/ppermute | solution.py:1126
  293.7 27.6 %collective-permute-start.22 = (bf16[2,256,1024]{2,1,0:T(8,128)(2,1)S(1)}, bf16[2,256,1024]{2,1,0:T(8,128)(2,1)}, u32[]{:S(2)}, u32[]{:S(2)}) collective-permute-start(bf16[2,256,1024]{2,1,0:T(8,128)(2,1)S(1)} %pad_maximum_fusion.refs_1_), channel_id=1, source_target_pairs={{0,2},{1,5},{2,0},{3,7},{4,6},{5,1},{6,4},{7,3},{8,10},{9,13},{10,... | collective-permute-start | bytes 3145736 | tf_op jit(solution)/shard_map/ppermute | solution.py:1075
  305.2 17.5 %collective-permute-start.35 = (bf16[256,768]{1,0:T(8,128)(2,1)S(1)}, bf16[256,768]{1,0:T(8,128)(2,1)S(1)}, u32[]{:S(2)}, u32[]{:S(2)}) collective-permute-start(bf16[256,768]{1,0:T(8,128)(2,1)S(1)} %get-tuple-element.253.refs_0_), channel_id=1, source_target_pairs={{0,8},{24,16},{1,9},{25,17},{2,10},{26,18},{3,11},{27,19},{4,12},{... | collective-permute-start | bytes 1179656 | tf_op jit(solution)/shard_map/ppermute | solution.py:1126
  312.2 19.0 %collective-permute-start.41 = (bf16[256,1280]{1,0:T(8,128)(2,1)S(1)}, bf16[256,1280]{1,0:T(8,128)(2,1)S(1)}, u32[]{:S(2)}, u32[]{:S(2)}) collective-permute-start(bf16[256,1280]{1,0:T(8,128)(2,1)S(1)} %get-tuple-element.269.refs_0_), channel_id=1, source_target_pairs={{8,16},{16,8},{9,17},{17,9},{10,18},{18,10},{11,19},{19,11},{12,20... | collective-permute-start | bytes 1966088 | tf_op jit(solution)/shard_map/ppermute | solution.py:1146
  316.6 9.0 %collective-permute-start.43 = (bf16[256,1024]{1,0:T(8,128)(2,1)S(1)}, bf16[256,1024]{1,0:T(8,128)(2,1)S(1)}, u32[]{:S(2)}, u32[]{:S(2)}) collective-permute-start(bf16[256,1024]{1,0:T(8,128)(2,1)S(1)} %get-tuple-element.273), channel_id=1, source_target_pairs={{0,0},{16,1},{2,2},{18,3},{4,4},{20,5},{6,6},{22,7},{8,8},{24,9},{... | collective-permute-start | bytes 1572872 | tf_op jit(solution)/shard_map/ppermute | solution.py:1174
  317.3 11.5 %collective-permute-start.44 = (bf16[256,1024]{1,0:T(8,128)(2,1)S(1)}, bf16[256,1024]{1,0:T(8,128)(2,1)S(1)}, u32[]{:S(2)}, u32[]{:S(2)}) collective-permute-start(bf16[256,1024]{1,0:T(8,128)(2,1)S(1)} %get-tuple-element.274), channel_id=1, source_target_pairs={{8,0},{24,1},{10,2},{26,3},{12,4},{28,5},{14,6},{30,7},{0,8},{16,9... | collective-permute-start | bytes 1572872 | tf_op jit(solution)/shard_map/ppermute | solution.py:1174
  321.3 37.5 %collective-permute-start.42 = (bf16[2,256,1024]{2,1,0:T(8,128)(2,1)S(1)}, bf16[2,256,1024]{2,1,0:T(8,128)(2,1)S(1)}, u32[]{:S(2)}, u32[]{:S(2)}) collective-permute-start(bf16[2,256,1024]{2,1,0:T(8,128)(2,1)S(1)} %get-tuple-element.272), channel_id=1, source_target_pairs={{8,0},{16,24},{9,1},{17,25},{10,2},{18,26},{11,3},{19,27},{12,4},{... | collective-permute-start | bytes 3145736 | tf_op jit(solution)/shard_map/ppermute | solution.py:1150
  322.6 9.5 %collective-permute-start.50 = (bf16[2,128,1024]{2,1,0:T(8,128)(2,1)S(1)}, bf16[2,128,1024]{2,1,0:T(8,128)(2,1)S(1)}, u32[]{:S(2)}, u32[]{:S(2)}) collective-permute-start(bf16[2,128,1024]{2,1,0:T(8,128)(2,1)S(1)} %constant_dynamic-slice_fusion.1), channel_id=1, source_target_pairs={{0,1},{1,0},{2,3},{3,2},{4,5},{5,4},{6,7},{7,6},{8,9},{9,8},{10,11... | collective-permute-start | bytes 1572872 | tf_op jit(solution)/shard_map/ppermute | solution.py:1063
  325.6 49.9 %collective-permute-start.23 = (bf16[2,256,1024]{2,1,0:T(8,128)(2,1)S(1)}, bf16[2,256,1024]{2,1,0:T(8,128)(2,1)S(1)}, u32[]{:S(2)}, u32[]{:S(2)}) collective-permute-start(bf16[2,256,1024]{2,1,0:T(8,128)(2,1)S(1)} %pad_maximum_fusion.refs_1_), channel_id=1, source_target_pairs={{0,4},{1,3},{2,6},{3,1},{4,0},{5,7},{6,2},{7,5},{8,12},{9,11},{10,... | collective-permute-start | bytes 3145736 | tf_op jit(solution)/shard_map/ppermute | solution.py:1075
  328.7 46.8 %collective-permute-start.24 = (bf16[2,256,1024]{2,1,0:T(8,128)(2,1)}, bf16[2,256,1024]{2,1,0:T(8,128)(2,1)S(1)}, u32[]{:S(2)}, u32[]{:S(2)}) collective-permute-start(bf16[2,256,1024]{2,1,0:T(8,128)(2,1)} %collective-permute-done.22.refs_2_), channel_id=1, source_target_pairs={{0,4},{1,3},{2,6},{3,1},{4,0},{5,7},{6,2},{7,5},{8,12},{9,11},{10,... | collective-permute-start | bytes 3145736 | tf_op jit(solution)/shard_map/ppermute | solution.py:1075
  331.2 44.2 %collective-permute-start.40 = (bf16[256,768]{1,0:T(8,128)(2,1)S(1)}, bf16[256,768]{1,0:T(8,128)(2,1)S(1)}, u32[]{:S(2)}, u32[]{:S(2)}) collective-permute-start(bf16[256,768]{1,0:T(8,128)(2,1)S(1)} %get-tuple-element.264.refs_0_), channel_id=1, source_target_pairs={{8,16},{16,8},{9,17},{17,9},{10,18},{18,10},{11,19},{19,11},{12,20... | collective-permute-start | bytes 1179656 | tf_op jit(solution)/shard_map/ppermute | solution.py:1146
  331.9 27.0 %copy-start.14 = (f32[2,128,2048]{2,1,0:T(8,128)S(1)}, f32[2,128,2048]{2,1,0:T(8,128)}, u32[]{:S(2)}) copy-start(f32[2,128,2048]{2,1,0:T(8,128)} %get-tuple-element.268.refs_0_) | copy-start | bytes 6291460
  332.1 40.8 %collective-permute-start.46 = (bf16[256,1280]{1,0:T(8,128)(2,1)S(1)}, bf16[256,1280]{1,0:T(8,128)(2,1)S(1)}, u32[]{:S(2)}, u32[]{:S(2)}) collective-permute-start(bf16[256,1280]{1,0:T(8,128)(2,1)S(1)} %get-tuple-element.282), channel_id=1, source_target_pairs={{8,0},{16,24},{9,1},{17,25},{10,2},{18,26},{11,3},{19,27},{12,4},{... | collective-permute-start | bytes 1966088 | tf_op jit(solution)/shard_map/ppermute | solution.py:1150
  365.0 3.6 collective-permute-start.52
  368.7 4.3 %collective-permute-start.53 = (f32[8,128]{1,0:T(8,128)S(1)}, f32[8,128]{1,0:T(8,128)S(1)}, u32[]{:S(2)}, u32[]{:S(2)}) collective-permute-start(f32[8,128]{1,0:T(8,128)S(1)} %maximum_select_fusion.3), channel_id=1, source_target_pairs={{0,4},{1,5},{2,6},{3,7},{4,0},{5,1},{6,2},{7,3},{8,12},{9,13},{10,... | collective-permute-start | bytes 12296 | tf_op jit(solution)/shard_map/ppermute | solution.py:1139
  373.0 5.8 %collective-permute-start.54 = (f32[8,128]{1,0:T(8,128)S(1)}, f32[8,128]{1,0:T(8,128)S(1)}, u32[]{:S(2)}, u32[]{:S(2)}) collective-permute-start(f32[8,128]{1,0:T(8,128)S(1)} %maximum_select_fusion.2), channel_id=1, source_target_pairs={{0,8},{8,0},{16,24},{24,16},{1,9},{9,1},{17,25},{25,17},{2,10},{10... | collective-permute-start | bytes 12296 | tf_op jit(solution)/shard_map/ppermute | solution.py:1139
  373.9 11.8 %collective-permute-start.47 = (bf16[128,1280]{1,0:T(8,128)(2,1)}, bf16[128,1280]{1,0:T(8,128)(2,1)}, u32[]{:S(2)}, u32[]{:S(2)}) collective-permute-start(bf16[128,1280]{1,0:T(8,128)(2,1)} %constant_dynamic-slice_fusion.3), channel_id=1, source_target_pairs={{0,1},{1,0},{2,3},{3,2},{4,5},{5,4},{6,7},{7,6},{8,9},{9,8},{10,11... | collective-permute-start | bytes 983048 | tf_op jit(solution)/shard_map/ppermute | solution.py:1063
  377.4 23.1 %collective-permute-start.45 = (bf16[2,256,1024]{2,1,0:T(8,128)(2,1)}, bf16[2,256,1024]{2,1,0:T(8,128)(2,1)}, u32[]{:S(2)}, u32[]{:S(2)}) collective-permute-start(bf16[2,256,1024]{2,1,0:T(8,128)(2,1)} %get-tuple-element.281), channel_id=1, source_target_pairs={{0,1},{1,0},{2,3},{3,2},{4,5},{5,4},{6,7},{7,6},{8,9},{9,8},{10,11... | collective-permute-start | bytes 3145736 | tf_op jit(solution)/shard_map/ppermute | solution.py:1063
  377.5 13.6 %collective-permute-start.48 = (bf16[256,768]{1,0:T(8,128)(2,1)S(1)}, bf16[256,768]{1,0:T(8,128)(2,1)}, u32[]{:S(2)}, u32[]{:S(2)}) collective-permute-start(bf16[256,768]{1,0:T(8,128)(2,1)S(1)} %get-tuple-element.283), channel_id=1, source_target_pairs={{8,0},{16,24},{9,1},{17,25},{10,2},{18,26},{11,3},{19,27},{12,4},{... | collective-permute-start | bytes 1179656 | tf_op jit(solution)/shard_map/ppermute | solution.py:1150
  378.8 4.6 %collective-permute-start.55 = (f32[8,128]{1,0:T(8,128)S(1)}, f32[8,128]{1,0:T(8,128)S(1)}, u32[]{:S(2)}, u32[]{:S(2)}) collective-permute-start(f32[8,128]{1,0:T(8,128)S(1)} %maximum_select_fusion.1), channel_id=1, source_target_pairs={{0,16},{8,24},{16,0},{24,8},{1,17},{9,25},{17,1},{25,9},{2,18},{10... | collective-permute-start | bytes 12296 | tf_op jit(solution)/shard_map/ppermute | solution.py:1139
  383.4 1.2 collective-permute-start.56
  383.5 8.8 %collective-permute-start.51 = (bf16[2,128,1024]{2,1,0:T(8,128)(2,1)S(1)}, bf16[2,128,1024]{2,1,0:T(8,128)(2,1)}, u32[]{:S(2)}, u32[]{:S(2)}) collective-permute-start(bf16[2,128,1024]{2,1,0:T(8,128)(2,1)S(1)} %constant_dynamic-slice_fusion), channel_id=1, source_target_pairs={{0,1},{1,0},{2,3},{3,2},{4,5},{5,4},{6,7},{7,6},{8,9},{9,8},{10,11... | collective-permute-start | bytes 1572872 | tf_op jit(solution)/shard_map/ppermute | solution.py:1063
  392.2 5.6 %collective-permute-start.49 = (bf16[128,768]{1,0:T(8,128)(2,1)S(1)}, bf16[128,768]{1,0:T(8,128)(2,1)S(1)}, u32[]{:S(2)}, u32[]{:S(2)}) collective-permute-start(bf16[128,768]{1,0:T(8,128)(2,1)S(1)} %constant_dynamic-slice_fusion.2), channel_id=1, source_target_pairs={{0,1},{1,0},{2,3},{3,2},{4,5},{5,4},{6,7},{7,6},{8,9},{9,8},{10,11... | collective-permute-start | bytes 589832 | tf_op jit(solution)/shard_map/ppermute | solution.py:1063
  (63 other events, 283.5 us)
